TPU v7x, 32 devices: a whole 2x2x4 slice. The times are simulated.
32 devices in a mesh: dp: 8 (over y, x, core), tensor: 4 (over z).
Axes of the slice: x: 2, y: 2, z: 4, core: 2. Of those that a mesh axis runs over, the one named last changes fastest.
Arguments:
- inputs: bfloat16 [16384, 2048], P(('dp', 'tensor')), may hold values from -6 to 6
- cotangent: bfloat16 [16384, 2048], P(('dp', 'tensor')), may hold values from -6 to 6
- lengths: int32 [8, 4], P('dp'), may hold values from 1 to 512, 1024 in all within a row
- held_blocks: int32 [4, 8], replicated, may hold values from 0 to 7, each once within a row
- master: float32 [8, 4, 96, 128, 128], P('dp', 'tensor')
- first_moment: float32 [8, 4, 96, 128, 128], P('dp', 'tensor')
- second_moment: float32 [8, 4, 96, 128, 128], P('dp', 'tensor')
- left_stats: float32 [8, 4, 96, 128, 128], P('dp', 'tensor')
- right_stats: float32 [8, 4, 96, 128, 128], P('dp', 'tensor')
- left_basis: float32 [8, 4, 96, 128, 128], P('dp', 'tensor')
- right_basis: float32 [8, 4, 96, 128, 128], P('dp', 'tensor')
- small_params: float32 [24576], replicated
- small_first: float32 [24576], replicated
- small_second: float32 [24576], replicated
Outputs:
- outputs: bfloat16 [16384, 2048], P(('dp', 'tensor'))
- input_grad: bfloat16 [16384, 2048], P(('dp', 'tensor'))
- new_first: float32 [8, 4, 96, 128, 128], P('dp', 'tensor')
- new_second: float32 [8, 4, 96, 128, 128], P('dp', 'tensor')
- new_master: float32 [8, 4, 96, 128, 128], P('dp', 'tensor')
- new_weights: bfloat16 [8, 4, 96, 128, 128], P('dp', 'tensor')
- new_left_stats: float32 [8, 4, 96, 128, 128], P('dp', 'tensor')
- new_right_stats: float32 [8, 4, 96, 128, 128], P('dp', 'tensor')
- new_left_basis: float32 [8, 4, 96, 128, 128], P('dp', 'tensor')
- new_right_basis: float32 [8, 4, 96, 128, 128], P('dp', 'tensor')
- small_first_new: float32 [24576], replicated
- small_second_new: float32 [24576], replicated
- small_new: float32 [24576], replicated
Inputs may be any that keep to these rules, and one draw needn't show every extreme that they name: Each row of held_blocks names every block once. A group's lengths sum to 1024; one of them is 512.
All inputs are finite; a program needn't handle non-finite values.
Results may differ from a plain program's by a relative error of at most 0.018.
Values may be sent and summed in bfloat16 or wider, within the bound.
No kernel may reach another device: no remote copies, remote signals or barrier semaphores. Data moves between devices by JAX's collectives and lax.ppermute only.
A program may use at most 384 MiB of HBM per device.

v0:
```python
from functools import partial

import jax
import jax.numpy as jnp
from jax import lax
from jax.sharding import PartitionSpec as P

D = 2048
H = 16
HD = 128
FF = 8192
PROMPT = 1024
QBLK = 512
STEP = 5
NS_ITERS = 3
SEQ = 2048


exact_mode = lax.Precision.HIGHEST
NORM_EPS = 1e-05
NEG_FILL = -1e30
BETA_ONE = 0.5
BETA_TWO = 0.5
ADAM_EPS = 1e-08
WEIGHT_DECAY = 0.1
CLIP_LIMIT = 1.0
SMALL_RATE = 0.1


def layer_norm(token_rows, gain, shift):
    centre = jnp.mean(token_rows, axis=-1, keepdims=True)
    centred = token_rows - centre
    spread = jnp.mean(centred * centred, axis=-1, keepdims=True)
    return centred * lax.rsqrt(spread + NORM_EPS) * gain + shift


def tiles_to_matrix(tiles, row_tiles, col_tiles):
    leading = tiles.shape[:-3]
    edge = tiles.shape[-1]
    grid = tiles.reshape(leading + (row_tiles, col_tiles, edge, edge))
    grid = jnp.swapaxes(grid, -3, -2)
    return grid.reshape(leading + (row_tiles * edge, col_tiles * edge))


def matrix_to_tiles(matrix, edge):
    leading = matrix.shape[:-2]
    row_count, col_count = (matrix.shape[-2], matrix.shape[-1])
    grid = matrix.reshape(leading + (row_count // edge, edge, col_count // edge, edge))
    grid = jnp.swapaxes(grid, -3, -2)
    return grid.reshape(leading + (row_count // edge * (col_count // edge), edge, edge))


def segment_ids(length_row):
    ends = jnp.cumsum(length_row)
    place = jnp.arange(SEQ, dtype=jnp.int32) - PROMPT
    counted = jnp.sum((ends[None, :] <= place[:, None]).astype(jnp.int32), axis=1)
    return jnp.where(place < 0, -1, counted)


def visible(query_pos, key_pos, query_segments, key_segments):
    causal = key_pos[None, :] <= query_pos[:, None]
    shared = (key_pos[None, :] < PROMPT) | (key_segments[None, :] == query_segments[:, None])
    return causal & shared


def contract_rows(left, right):
    return lax.dot_general(
        left, right, (((0,), (0,)), ((), ())), preferred_element_type=jnp.float32
    )


def contract_cols(left, right):
    return lax.dot_general(
        left, right, (((1,), (1,)), ((), ())), preferred_element_type=jnp.float32
    )


def orthonormal(matrix):
    frob = jnp.sqrt(jnp.sum(matrix * matrix, axis=(-2, -1), keepdims=True))
    current = matrix / (frob + 1e-06)
    for sweep_index in range(NS_ITERS):
        gram = jnp.einsum("...ji,...jk->...ik", current, current, precision=exact_mode)
        current = 1.5 * current - 0.5 * jnp.einsum(
            "...ij,...jk->...ik", current, gram, precision=exact_mode
        )
    return current


def soap_step(
    summed,
    master,
    first,
    second,
    left_stat,
    right_stat,
    left_base,
    right_base,
    step_rate,
    factor,
    token_count,
):
    rotated = jnp.einsum("...ji,...jk->...ik", left_base, summed, precision=exact_mode)
    rotated = jnp.einsum("...ij,...jk->...ik", rotated, right_base, precision=exact_mode)
    new_first = BETA_ONE * first + (1.0 - BETA_ONE) * rotated
    new_second = BETA_TWO * second + (1.0 - BETA_TWO) * rotated * rotated
    direction = (
        new_first
        / (1.0 - BETA_ONE**STEP)
        / (jnp.sqrt(new_second / (1.0 - BETA_TWO**STEP)) + ADAM_EPS)
    )
    turned = jnp.einsum("...ij,...jk->...ik", left_base, direction, precision=exact_mode)
    turned = jnp.einsum("...ij,...kj->...ik", turned, right_base, precision=exact_mode)
    new_master = (master - step_rate * (turned + WEIGHT_DECAY * master)) * factor
    outer_rows = jnp.einsum("...ij,...kj->...ik", summed, summed, precision=exact_mode)
    outer_cols = jnp.einsum("...ji,...jk->...ik", summed, summed, precision=exact_mode)
    new_left = BETA_TWO * left_stat + (1.0 - BETA_TWO) * outer_rows / (HD * token_count)
    new_right = BETA_TWO * right_stat + (1.0 - BETA_TWO) * outer_cols / (HD * token_count)
    left_next = orthonormal(
        jnp.einsum("...ij,...jk->...ik", new_left, left_base, precision=exact_mode)
    )
    right_next = orthonormal(
        jnp.einsum("...ij,...jk->...ik", new_right, right_base, precision=exact_mode)
    )
    return (new_first, new_second, new_master, new_left, new_right, left_next, right_next)


def small_step(summed, params, first, second, shrink):
    new_first = BETA_ONE * first + (1.0 - BETA_ONE) * summed
    new_second = BETA_TWO * second + (1.0 - BETA_TWO) * summed * summed
    direction = (
        new_first
        / (1.0 - BETA_ONE**STEP)
        / (jnp.sqrt(new_second / (1.0 - BETA_TWO**STEP)) + ADAM_EPS)
    )
    scaled = jnp.concatenate([jnp.repeat(shrink, HD), jnp.ones((7 * D + FF,), jnp.float32)])
    return (new_first, new_second, (params - SMALL_RATE * direction) * scaled)


def tile_rates(tile_q, tile_o, tile_u, count):
    index = jnp.arange(count, dtype=jnp.int32)
    rates = jnp.where(
        index < tile_q,
        D ** (-0.5),
        jnp.where(
            index < tile_q + tile_o,
            (SEQ / (2.0 * D)) ** 0.5,
            jnp.where(index < tile_q + tile_o + tile_u, D ** (-0.5), FF ** (-0.5)),
        ),
    )
    return rates.astype(jnp.float32)


def tile_factors(shrink, tensor_index, heads_local, tile_q, count):
    index = jnp.arange(count, dtype=jnp.int32)
    column = index % (3 * heads_local)
    head_index = tensor_index * heads_local + column % heads_local
    picked = jnp.sum(
        jnp.where(
            head_index[:, None] == jnp.arange(H, dtype=jnp.int32)[None, :], shrink[None, :], 0.0
        ),
        axis=1,
    )
    return jnp.where((index < tile_q) & (column < 2 * heads_local), picked, 1.0)


def to_slots(blocks, order):
    return jnp.take(matrix_to_tiles(blocks, HD), order, axis=0)


def per_device(
    inputs,
    cotangent,
    lengths,
    held_blocks,
    master,
    first_moment,
    second_moment,
    left_stats,
    right_stats,
    left_basis,
    right_basis,
    small_params,
    small_first,
    small_second,
):
    dp_count = lax.axis_size("dp")
    tp_count = lax.axis_size("tensor")
    tensor_index = lax.axis_index("tensor")
    heads_local = H // tp_count
    width_local = D // tp_count
    hidden_local = FF // tp_count
    rows_block = D // dp_count
    tile_q = rows_block // HD * (3 * heads_local)
    tile_o = heads_local * (rows_block // HD)
    tile_u = rows_block // HD * (hidden_local // HD)
    tile_count = master.shape[2]
    bounds = [0, tile_q, tile_q + tile_o, tile_q + tile_o + tile_u, tile_count]
    gathered = lax.all_gather(master[0].astype(jnp.bfloat16), "dp", axis=0, tiled=True)
    inverse = jnp.argsort(held_blocks, axis=1)

    def logical(kind_index):
        return jnp.take(
            gathered[:, bounds[kind_index] : bounds[kind_index + 1]], inverse[kind_index], axis=0
        )

    w_qkv = tiles_to_matrix(logical(0), rows_block // HD, 3 * heads_local).reshape(
        D, 3 * width_local
    )
    w_out = (
        tiles_to_matrix(logical(1), heads_local, rows_block // HD)
        .transpose(1, 0, 2)
        .reshape(width_local, D)
    )
    w_up = tiles_to_matrix(logical(2), rows_block // HD, hidden_local // HD).reshape(
        D, hidden_local
    )
    w_down = (
        tiles_to_matrix(logical(3), hidden_local // HD, rows_block // HD)
        .transpose(1, 0, 2)
        .reshape(hidden_local, D)
    )
    bias_q = lax.dynamic_slice_in_dim(small_params, tensor_index * width_local, width_local)
    bias_v = lax.dynamic_slice_in_dim(small_params, D + tensor_index * width_local, width_local)
    bias_o = small_params[2 * D : 3 * D]
    bias_two = small_params[3 * D : 4 * D]
    gain_one = small_params[4 * D : 5 * D]
    shift_one = small_params[5 * D : 6 * D]
    gain_two = small_params[6 * D : 7 * D]
    shift_two = small_params[7 * D : 8 * D]
    bias_up = lax.dynamic_slice_in_dim(
        small_params, 8 * D + tensor_index * hidden_local, hidden_local
    )
    token_rows = inputs.astype(jnp.float32)
    normed_one = layer_norm(token_rows, gain_one, shift_one).astype(jnp.bfloat16)
    normed_all = lax.all_gather(normed_one, "tensor", axis=0, tiled=True)
    rows_all = normed_all.shape[0]
    block_count = rows_all // QBLK
    per_group = SEQ // QBLK
    projected = jnp.dot(normed_all, w_qkv, preferred_element_type=jnp.float32).reshape(
        rows_all, 3, heads_local, HD
    )
    queries = (projected[:, 0] + bias_q.reshape(heads_local, HD)).astype(jnp.bfloat16)
    key_rows = projected[:, 1].astype(jnp.bfloat16)
    value_rows = (projected[:, 2] + bias_v.reshape(heads_local, HD)).astype(jnp.bfloat16)
    segments = jax.vmap(segment_ids)(lengths).reshape(rows_all)
    positions = jnp.arange(SEQ, dtype=jnp.int32)
    score_scale = HD ** (-0.5)

    def block_scores(block_index):
        start = block_index * QBLK
        query_block = lax.dynamic_slice_in_dim(queries, start, QBLK, 0)
        query_segments = lax.dynamic_slice_in_dim(segments, start, QBLK, 0)
        query_pos = block_index % per_group * QBLK + jnp.arange(QBLK, dtype=jnp.int32)
        product = jnp.einsum(
            "qhd,khd->hqk", query_block, key_rows, preferred_element_type=jnp.float32
        )
        seen = visible(query_pos, positions, query_segments, segments)
        scores = jnp.where(seen[None], product * score_scale, NEG_FILL)
        return (query_block, key_rows, value_rows, scores)

    def attend_forward(block_index):
        query_block, group_keys, group_values, scores = block_scores(block_index)
        row_top = jnp.max(scores, axis=-1, keepdims=True)
        weights = jnp.exp(scores - row_top)
        row_total = jnp.sum(weights, axis=-1, keepdims=True)
        probs_low = (weights / row_total).astype(jnp.bfloat16)
        block_out = jnp.einsum(
            "hqk,khd->qhd", probs_low, group_values, preferred_element_type=jnp.float32
        )
        return (block_out.astype(jnp.bfloat16), row_top[:, :, 0], row_total[:, :, 0])

    attended, row_tops, row_totals = lax.map(
        attend_forward, jnp.arange(block_count, dtype=jnp.int32)
    )
    attended = attended.reshape(rows_all, width_local)
    peak_local = jnp.max(row_tops, axis=(0, 2))
    attn_sum = lax.psum_scatter(
        jnp.dot(attended, w_out, preferred_element_type=jnp.float32).astype(jnp.bfloat16),
        "tensor",
        scatter_dimension=0,
        tiled=True,
    ).astype(jnp.float32)
    hidden = token_rows + attn_sum + bias_o
    normed_two = layer_norm(hidden, gain_two, shift_two).astype(jnp.bfloat16)
    normed_rows = lax.all_gather(normed_two, "tensor", axis=0, tiled=True)
    pre_act = jnp.dot(normed_rows, w_up, preferred_element_type=jnp.float32) + bias_up
    activation = jax.nn.gelu(pre_act, approximate=False).astype(jnp.bfloat16)
    ffn_sum = lax.psum_scatter(
        jnp.dot(activation, w_down, preferred_element_type=jnp.float32).astype(jnp.bfloat16),
        "tensor",
        scatter_dimension=0,
        tiled=True,
    ).astype(jnp.float32)
    outputs = (hidden + ffn_sum + bias_two).astype(jnp.bfloat16)
    peak_vector = lax.dynamic_update_slice(
        jnp.full((H,), NEG_FILL, jnp.float32), peak_local, (tensor_index * heads_local,)
    )
    peak_all = lax.pmax(peak_vector, ("dp", "tensor"))
    grad_rows_out = cotangent.astype(jnp.float32)
    grad_bias_two = jnp.sum(cotangent, axis=0, dtype=jnp.float32)
    back_rows = lax.all_gather(cotangent, "tensor", axis=0, tiled=True)
    grad_down = contract_rows(activation, back_rows)
    grad_act = contract_cols(back_rows, w_down)
    gelu_back = jax.vjp(partial(jax.nn.gelu, approximate=False), pre_act)[1]
    grad_pre = gelu_back(grad_act)[0].astype(jnp.bfloat16)
    grad_bias_up = jnp.sum(grad_pre, axis=0, dtype=jnp.float32)
    grad_up = contract_rows(normed_rows, grad_pre)
    grad_normed_two = lax.psum_scatter(
        contract_cols(grad_pre, w_up).astype(jnp.bfloat16),
        "tensor",
        scatter_dimension=0,
        tiled=True,
    ).astype(jnp.float32)
    norm_back_two = jax.vjp(layer_norm, hidden, gain_two, shift_two)[1]
    grad_hidden_part, grad_gain_two, grad_shift_two = norm_back_two(grad_normed_two)
    grad_hidden = grad_rows_out + grad_hidden_part
    ffn_slots = jnp.concatenate(
        [
            to_slots(grad_up.reshape(dp_count, rows_block, hidden_local), held_blocks[2]),
            to_slots(
                grad_down.reshape(hidden_local, dp_count, rows_block).transpose(1, 0, 2),
                held_blocks[3],
            ),
        ],
        axis=1,
    )
    branch_low = grad_hidden.astype(jnp.bfloat16)
    grad_bias_o = jnp.sum(branch_low, axis=0, dtype=jnp.float32)
    branch_rows = lax.all_gather(branch_low, "tensor", axis=0, tiled=True)
    grad_out_weight = contract_rows(attended, branch_rows)
    grad_attended = (
        contract_cols(branch_rows, w_out).astype(jnp.bfloat16).reshape(rows_all, heads_local, HD)
    )

    def attend_backward(carry, block_index):
        key_total, value_total = carry
        query_block, group_keys, group_values, scores = block_scores(block_index)
        probs = (
            jnp.exp(scores - row_tops[block_index][:, :, None])
            / row_totals[block_index][:, :, None]
        )
        grad_block = lax.dynamic_slice_in_dim(grad_attended, block_index * QBLK, QBLK, 0)
        value_part = jnp.einsum(
            "hqk,qhd->khd",
            probs.astype(jnp.bfloat16),
            grad_block,
            preferred_element_type=jnp.float32,
        )
        grad_probs = jnp.einsum(
            "qhd,khd->hqk", grad_block, group_values, preferred_element_type=jnp.float32
        )
        grad_scores = probs * (grad_probs - jnp.sum(grad_probs * probs, axis=-1, keepdims=True))
        grad_product = (grad_scores * score_scale).astype(jnp.bfloat16)
        query_grad = jnp.einsum(
            "hqk,khd->qhd", grad_product, group_keys, preferred_element_type=jnp.float32
        ).astype(jnp.bfloat16)
        key_part = jnp.einsum(
            "hqk,qhd->khd", grad_product, query_block, preferred_element_type=jnp.float32
        )
        key_total = key_total + key_part
        value_total = value_total + value_part
        return ((key_total, value_total), query_grad)

    zero_total = jnp.zeros((rows_all, heads_local, HD), jnp.float32)
    (key_total, value_total), query_grads = lax.scan(
        attend_backward, (zero_total, zero_total), jnp.arange(block_count, dtype=jnp.int32)
    )
    grad_queries = query_grads.reshape(rows_all, heads_local, HD)
    grad_keys = key_total.astype(jnp.bfloat16)
    grad_values = value_total.astype(jnp.bfloat16)
    grad_mixed = jnp.stack([grad_queries, grad_keys, grad_values], axis=1).reshape(
        rows_all, 3 * width_local
    )
    grad_bias_q = jnp.sum(grad_queries.reshape(rows_all, width_local), axis=0, dtype=jnp.float32)
    grad_bias_v = jnp.sum(grad_values.reshape(rows_all, width_local), axis=0, dtype=jnp.float32)
    grad_qkv = contract_rows(normed_all, grad_mixed)
    grad_normed_one = lax.psum_scatter(
        contract_cols(grad_mixed, w_qkv).astype(jnp.bfloat16),
        "tensor",
        scatter_dimension=0,
        tiled=True,
    ).astype(jnp.float32)
    norm_back_one = jax.vjp(layer_norm, token_rows, gain_one, shift_one)[1]
    grad_rows_part, grad_gain_one, grad_shift_one = norm_back_one(grad_normed_one)
    input_grad = (grad_hidden + grad_rows_part).astype(jnp.bfloat16)
    attn_slots = jnp.concatenate(
        [
            to_slots(grad_qkv.reshape(dp_count, rows_block, 3 * width_local), held_blocks[0]),
            to_slots(
                grad_out_weight.reshape(width_local, dp_count, rows_block).transpose(1, 0, 2),
                held_blocks[1],
            ),
        ],
        axis=1,
    )
    summed = lax.psum_scatter(
        jnp.concatenate([attn_slots, ffn_slots], axis=1).astype(jnp.bfloat16),
        "dp",
        scatter_dimension=0,
        tiled=True,
    ).astype(jnp.float32)
    grad_small_local = jnp.concatenate(
        [
            lax.dynamic_update_slice(
                jnp.zeros((D,), jnp.float32), grad_bias_q, (tensor_index * width_local,)
            ),
            lax.dynamic_update_slice(
                jnp.zeros((D,), jnp.float32), grad_bias_v, (tensor_index * width_local,)
            ),
            grad_bias_o,
            grad_bias_two,
            grad_gain_one,
            grad_shift_one,
            grad_gain_two,
            grad_shift_two,
            lax.dynamic_update_slice(
                jnp.zeros((FF,), jnp.float32), grad_bias_up, (tensor_index * hidden_local,)
            ),
        ]
    )
    grad_small = lax.psum(grad_small_local, ("dp", "tensor"))
    shrink = jnp.sqrt(CLIP_LIMIT / jnp.maximum(peak_all, CLIP_LIMIT))
    rates = tile_rates(tile_q, tile_o, tile_u, tile_count)[:, None, None]
    factors = tile_factors(shrink, tensor_index, heads_local, tile_q, tile_count)[:, None, None]
    token_count = float(dp_count * rows_all)
    new_first, new_second, new_master, new_left, new_right, left_next, right_next = soap_step(
        summed[0],
        master[0, 0],
        first_moment[0, 0],
        second_moment[0, 0],
        left_stats[0, 0],
        right_stats[0, 0],
        left_basis[0, 0],
        right_basis[0, 0],
        rates,
        factors,
        token_count,
    )
    new_weights = new_master.astype(jnp.bfloat16)
    small_first_new, small_second_new, small_new = small_step(
        grad_small, small_params, small_first, small_second, shrink
    )
    return (
        outputs,
        input_grad,
        new_first[None, None],
        new_second[None, None],
        new_master[None, None],
        new_weights[None, None],
        new_left[None, None],
        new_right[None, None],
        left_next[None, None],
        right_next[None, None],
        small_first_new,
        small_second_new,
        small_new,
    )


def solution(mesh):
    return jax.shard_map(
        per_device,
        mesh=mesh,
        in_specs=(
            P(("dp", "tensor"), None),
            P(("dp", "tensor"), None),
            P("dp", None),
            P(),
            P("dp", "tensor", None, None, None),
            P("dp", "tensor", None, None, None),
            P("dp", "tensor", None, None, None),
            P("dp", "tensor", None, None, None),
            P("dp", "tensor", None, None, None),
            P("dp", "tensor", None, None, None),
            P("dp", "tensor", None, None, None),
            P(),
            P(),
            P(),
        ),
        out_specs=(
            P(("dp", "tensor"), None),
            P(("dp", "tensor"), None),
            P("dp", "tensor", None, None, None),
            P("dp", "tensor", None, None, None),
            P("dp", "tensor", None, None, None),
            P("dp", "tensor", None, None, None),
            P("dp", "tensor", None, None, None),
            P("dp", "tensor", None, None, None),
            P("dp", "tensor", None, None, None),
            P("dp", "tensor", None, None, None),
            P(),
            P(),
            P(),
        ),
        check_vma=False,
    )
```

profile of v0, /device:TPU:0, one launch (start us, length us, event | category | flops | bytes accessed | tf_op | source)
XLA Modules:
  0.0 2502.1 jit_solution(993506775580493940)
XLA Ops:
  20.8 120.0 %all-gather.15.cloned.1.call-done = bf16[8,1,96,128,128]{4,3,2,1,0:T(8,128)(2,1)} async-done(((bf16[1,1,96,128,128]{4,3,2,1,0:T(8,128)(2,1)}), bf16[8,1,96,128,128]{4,3,2,1,0:T(8,128)(2,1)}) %all-gather.15.cloned.1.call-update) | async-done | bytes 25165840 | tf_op jit(solution)/shard_map/all_gather | solution.py:198
  159.7 16.7 copy.119
  184.7 11.1 reshape_reshape.11
  195.8 96.8 %all-gather.7.cloned.1.call-done = bf16[2048,2048]{1,0:T(8,128)(2,1)} async-done(((bf16[512,2048]{1,0:T(8,128)(2,1)}), bf16[2048,2048]{1,0:T(8,128)(2,1)}) %all-gather.7.cloned.1.call-update) | async-done | bytes 8388624 | tf_op jit(solution)/shard_map/all_gather | solution.py:235
  292.5 17.0 fusion.71
  312.6 83.6 %while.36 = (s32[]{:T(128)}, bf16[4,512,4,128]{3,2,1,0:T(4,128)(2,1)}, f32[4,4,512]{2,1,0:T(4,128)}, f32[4,4,512]{2,1,0:T(4,128)}, s32[4]{0:T(128)S(1)}, /*index...) while((s32[]{:T(128)}, ...), condition=%wide.region_8.9_spmd.clone.clone, body=%wide.region_5.8_spmd.clone.clone.sunk | while | flops 2202270208 | bytes 69303664 | solution.py:272
  423.5 142.8 %reduce-scatter.6.cloned.1.call-done = bf16[512,2048]{1,0:T(8,128)(2,1)} async-done(((bf16[2048,2048]{1,0:T(8,128)(2,1)}), bf16[512,2048]{1,0:T(8,128)(2,1)}) %reduce-scatter.6.cloned.1.call-update) | async-done | bytes 2097168 | tf_op jit(solution)/shard_map/reduce_scatter | solution.py:277
  575.9 12.8 fusion.163
  604.5 13.7 copy.123
  633.9 12.6 copy.124
  646.6 13.4 reshape.656
  659.9 65.8 %all-gather.9.cloned.1.call-done = bf16[2048,2048]{1,0:T(8,128)(2,1)} async-done(((bf16[512,2048]{1,0:T(8,128)(2,1)}), bf16[2048,2048]{1,0:T(8,128)(2,1)}) %all-gather.9.cloned.1.call-update) | async-done | bytes 8388624 | tf_op jit(solution)/shard_map/all_gather | solution.py:285
  725.7 60.2 %multiply_convert_fusion.1 = (bf16[2048,2048]{1,0:T(8,128)(2,1)}, f32[2048,2048]{1,0:T(8,128)}, f32[2048,2048]{1,0:T(8,128)}) fusion(f32[2048]{0:T(1024)S(1)} %copy-done.59, bf16[2048,2048]{1,0:T(8,128)(2,1)} %all-gather.9.cloned.1.call-done, bf16[256,8,16,128]{3,2,1,0:T(8,128)(2,1)} %bitcast.379), kind=kOutput, calls=%fused_computation.78 | convolution fusion | flops 17456693248 | bytes 58728448 | tf_op jit(solution)/shard_map/dot_general | solution.py:286
  785.9 89.1 %all-gather.11.cloned.1.call-done = bf16[2048,2048]{1,0:T(8,128)(2,1)} async-done(((bf16[512,2048]{1,0:T(8,128)(2,1)}), bf16[2048,2048]{1,0:T(8,128)(2,1)}) %all-gather.11.cloned.1.call-update) | async-done | bytes 8388624 | tf_op jit(solution)/shard_map/all_gather | solution.py:301
  875.0 32.9 %convert_reduce_fusion = (f32[2048]{0:T(1024)}, bf16[2048,2048]{1,0:T(8,128)(2,1)}) fusion(f32[2048,2048]{1,0:T(8,128)} %get-tuple-element.603, bf16[2048,2048]{1,0:T(8,128)(2,1)} %all-gather.11.cloned.1.call-done, bf16[2048,2048]{0,1:T(8,128)(2,1)} %bitcast.377, f32[2048,2048]{1,0:T(8,128)} %get-tuple-element.636, f32[2048]{0:T(1024)S(1)} %copy-done.59), kind=kOutput, calls=%fused_computation.77 | convolution fusion | flops 17251170304 | bytes 58736640 | tf_op jit(solution)/shard_map/dot_general | solution.py:73
  907.9 23.9 fusion.73
  931.9 24.0 convolution_convert_fusion.1
  956.0 118.7 %reduce-scatter.10.cloned.1.call-done = bf16[512,2048]{1,0:T(8,128)(2,1)} async-done(((bf16[2048,2048]{1,0:T(8,128)(2,1)}), bf16[512,2048]{1,0:T(8,128)(2,1)}) %reduce-scatter.10.cloned.1.call-update) | async-done | bytes 2097168 | tf_op jit(solution)/shard_map/reduce_scatter | solution.py:308
  1079.2 143.1 %reduce-scatter.8.cloned.1.call-done = bf16[512,2048]{1,0:T(8,128)(2,1)} async-done(((bf16[2048,2048]{1,0:T(8,128)(2,1)}), bf16[512,2048]{1,0:T(8,128)(2,1)}) %reduce-scatter.8.cloned.1.call-update) | async-done | bytes 2097168 | tf_op jit(solution)/shard_map/reduce_scatter | solution.py:288
  1232.5 150.4 %all-gather.13.cloned.1.call-done = bf16[2048,2048]{1,0:T(8,128)(2,1)} async-done(((bf16[512,2048]{1,0:T(8,128)(2,1)}), bf16[2048,2048]{1,0:T(8,128)(2,1)}) %all-gather.13.cloned.1.call-update) | async-done | bytes 8388624 | tf_op jit(solution)/shard_map/all_gather | solution.py:329
  1382.9 9.9 convolution_convert_fusion.3
  1392.8 339.4 %while.37 = (s32[]{:T(128)}, f32[2048,4,128]{0,2,1:T(8,128)}, f32[2048,4,128]{0,2,1:T(8,128)}, bf16[4,512,4,128]{3,1,2,0:T(8,128)(2,1)}, s32[4]{0:T(128)S(1)}, /...) while((s32[]{:T(128)}, f32[2048,4,128]{0,2,1:T(8,128)}, ...), condition=%wide.region_18.20_spmd.clone.clone, body=%wide.region_16.19_spmd.clone.clone.sunk | while | flops 5440285184 | bytes 220797904 | solution.py:365
  1400.6 9.6 exponential_divide_fusion.2
  1419.3 24.9 bitcast_add_fusion.6
  1444.3 22.7 fusion.253
  1483.6 9.6 exponential_divide_fusion.2
  1502.3 26.0 %bitcast_add_fusion.6 = f32[2048,4,128]{0,2,1:T(8,128)} fusion(f32[2048,4,128]{0,2,1:T(8,128)} %get-tuple-element.875, f32[4,512,2048]{2,1,0:T(8,128)} %exponential_divide_fusion.2, f32[4,512,2048]{2,1,0:T(8,128)} %fusion.252, pred[]{:T(512)S(6)} %compare.14, bf16[2048,4,128]{2,0,1:T(8,128)(2,1)} %get-tuple-element.898, s32[]{:T(128)S(6)} %select_n.392), kind=kOutput, calls=%fused_computation.40.clone.1 | convolution fusion | flops 1096814592 | bytes 76021768 | tf_op jit(solution)/shard_map/while/body/eval_jaxpr/hqk,qhd->khd/dot_general | solution.py:357
  1528.4 22.7 fusion.253
  1551.1 10.4 bitcast_add_fusion.7
  1568.9 9.6 exponential_divide_fusion.2
  1587.7 26.0 %bitcast_add_fusion.6 = f32[2048,4,128]{0,2,1:T(8,128)} fusion(f32[2048,4,128]{0,2,1:T(8,128)} %get-tuple-element.875, f32[4,512,2048]{2,1,0:T(8,128)} %exponential_divide_fusion.2, f32[4,512,2048]{2,1,0:T(8,128)} %fusion.252, pred[]{:T(512)S(6)} %compare.14, bf16[2048,4,128]{2,0,1:T(8,128)(2,1)} %get-tuple-element.898, s32[]{:T(128)S(6)} %select_n.392), kind=kOutput, calls=%fused_computation.40.clone.1 | convolution fusion | flops 1096814592 | bytes 76021768 | tf_op jit(solution)/shard_map/while/body/eval_jaxpr/hqk,qhd->khd/dot_general | solution.py:357
  1613.7 22.7 fusion.253
  1636.4 10.4 bitcast_add_fusion.7
  1673.0 26.0 %bitcast_add_fusion.6 = f32[2048,4,128]{0,2,1:T(8,128)} fusion(f32[2048,4,128]{0,2,1:T(8,128)} %get-tuple-element.875, f32[4,512,2048]{2,1,0:T(8,128)} %exponential_divide_fusion.2, f32[4,512,2048]{2,1,0:T(8,128)} %fusion.252, pred[]{:T(512)S(6)} %compare.14, bf16[2048,4,128]{2,0,1:T(8,128)(2,1)} %get-tuple-element.898, s32[]{:T(128)S(6)} %select_n.392), kind=kOutput, calls=%fused_computation.40.clone.1 | convolution fusion | flops 1096814592 | bytes 76021768 | tf_op jit(solution)/shard_map/while/body/eval_jaxpr/hqk,qhd->khd/dot_general | solution.py:357
  1699.0 22.7 fusion.253
  1721.7 10.4 bitcast_add_fusion.7
  1756.1 19.4 convolution_convert_fusion
  1777.4 11.9 copy.164
  1789.3 23.8 convolution_bitcast_fusion.1
  1813.1 9.9 copy.172
  1832.1 24.4 convolution_bitcast_fusion
  1856.5 9.8 copy.173
  1866.3 12.6 copy.135
  1896.0 10.6 select_convert_fusion.1
  1906.6 10.6 select_convert_fusion
  1917.3 12.4 copy.166
  1944.5 18.6 fusion.165
  1992.0 17.6 pad_maximum_fusion
  2010.8 38.5 %pmax.7 = f32[16]{0:T(128)S(1)} all-reduce(f32[16]{0:T(128)S(1)} %dynamic_update_slice.38), channel_id=1, replica_groups=mesh['dp'=8,'tensor'=4] {'dp','tensor'}, use_global_device_ids=true, to_apply=%region_24.27 | all-reduce | flops 16 | bytes 128 | tf_op jit(solution)/shard_map/pmax | solution.py:298
  2049.5 61.6 %all-reduce.3.cloned.1.call-done = f32[24576]{0:T(1024)} async-done(((f32[24576]{0:T(1024)}), f32[24576]{0:T(1024)}) %all-reduce.3.cloned.1.call-update) | async-done | bytes 98320 | tf_op jit(solution)/shard_map/psum | solution.py:421
  2112.7 159.8 %reduce-scatter.14.cloned.1.call-done = bf16[1,96,128,128]{3,2,1,0:T(8,128)(2,1)} async-done(((bf16[8,96,128,128]{3,2,1,0:T(8,128)(2,1)}), bf16[1,96,128,128]{3,2,1,0:T(8,128)(2,1)}) %reduce-scatter.14.cloned.1.call-update) | async-done | bytes 3145744 | tf_op jit(solution)/shard_map/reduce_scatter | solution.py:396
  2281.2 9.7 fusion.86
  2290.9 16.4 fusion.90
  2307.4 11.4 fusion.144
  2333.3 12.4 fusion.146
  2345.7 14.0 multiply_subtract_fusion.1
  2359.7 12.2 fusion.168
  2381.0 12.2 fusion.169
  2393.2 10.5 subtract_bitcast_fusion
  2416.5 12.4 fusion.145
  2428.9 9.7 multiply_subtract_fusion.3
  2438.6 10.2 fusion.166
  2456.9 10.4 fusion.167
  2476.1 15.6 fusion.81
  (379 shorter events, 432.9 us)
Async XLA Ops:
  7.2 5.4 copy-start
  7.2 7.1 copy-start.27
  7.2 133.5 %all-gather.15.cloned.1.call-start = ((), (), s32[]{:S(2)}) async-start(), calls=%async_computation.15 | async-start | bytes 28311552 | tf_op jit(solution)/shard_map/all_gather | solution.py:198
  12.6 280.0 %all-gather.7.cloned.1.call-start = ((), (), s32[]{:S(2)}) async-start(), calls=%async_computation.5 | async-start | bytes 10485760 | tf_op jit(solution)/shard_map/all_gather | solution.py:235
  17.7 548.6 %reduce-scatter.6.cloned.1.call-start = ((), (), s32[]{:S(2)}) async-start(), calls=%async_computation.6 | async-start | bytes 10485760 | tf_op jit(solution)/shard_map/reduce_scatter | solution.py:277
  312.6 88.3 %copy-start.65 = (pred[8]{0:T(512)(128)(4,1)S(1)}, pred[8]{0:T(512)(128)(4,1)}, u32[]{:S(2)}) copy-start(pred[8]{0:T(512)(128)(4,1)} %get-tuple-element.647) | copy-start | bytes 28
  396.3 14.5 copy-start.4
  396.3 14.4 copy-start.23
  396.3 14.4 copy-start.35
  423.4 142.9 %copy-start.1 = (bf16[512,2048]{1,0:T(8,128)(2,1)S(1)}, bf16[512,2048]{1,0:T(8,128)(2,1)}, u32[]{:S(2)}) copy-start(bf16[512,2048]{1,0:T(8,128)(2,1)} %param.22) | copy-start | bytes 6291460
  423.4 142.9 %copy-start.25 = (f32[2048]{0:T(1024)S(1)}, f32[2048]{0:T(1024)}, u32[]{:S(2)}) copy-start(f32[2048]{0:T(1024)} %get-tuple-element.623) | copy-start | bytes 24580
  423.4 149.2 %copy-start.32 = (f32[2048]{0:T(1024)S(1)}, f32[2048]{0:T(1024)}, u32[]{:S(2)}) copy-start(f32[2048]{0:T(1024)} %get-tuple-element.622) | copy-start | bytes 24580
  423.4 149.2 %copy-start.47 = (f32[2048]{0:T(1024)S(1)}, f32[2048]{0:T(1024)}, u32[]{:S(2)}) copy-start(f32[2048]{0:T(1024)} %get-tuple-element.621) | copy-start | bytes 24580
  423.4 302.3 %all-gather.9.cloned.1.call-start = ((), (), s32[]{:S(2)}) async-start(), calls=%async_computation.7 | async-start | bytes 10485760 | tf_op jit(solution)/shard_map/all_gather | solution.py:285
  566.3 6.3 copy-start.8
  575.2 299.8 %all-gather.11.cloned.1.call-start = ((), (), s32[]{:S(2)}) async-start(), calls=%async_computation.9 | async-start | bytes 10485760 | tf_op jit(solution)/shard_map/all_gather | solution.py:301
  575.8 499.0 %reduce-scatter.10.cloned.1.call-start = ((), (), s32[]{:S(2)}) async-start(), calls=%async_computation.10 | async-start | bytes 10485760 | tf_op jit(solution)/shard_map/reduce_scatter | solution.py:308
  646.6 79.1 %copy-start.59 = (f32[2048]{0:T(1024)S(1)}, f32[2048]{0:T(1024)}, u32[]{:S(2)}) copy-start(f32[2048]{0:T(1024)} %get-tuple-element.620) | copy-start | bytes 24580
  931.9 290.4 %reduce-scatter.8.cloned.1.call-start = ((), (), s32[]{:S(2)}) async-start(), calls=%async_computation.8 | async-start | bytes 10485760 | tf_op jit(solution)/shard_map/reduce_scatter | solution.py:288
  955.9 118.8 %copy-start.2 = (bf16[512,2048]{1,0:T(8,128)(2,1)S(1)}, bf16[512,2048]{1,0:T(8,128)(2,1)}, u32[]{:S(2)}) copy-start(bf16[512,2048]{1,0:T(8,128)(2,1)} %param.22) | copy-start | bytes 6291460
  955.9 118.8 %copy-start.26 = (f32[2048]{0:T(1024)S(1)}, f32[2048]{0:T(1024)}, u32[]{:S(2)}) copy-start(f32[2048]{0:T(1024)} %get-tuple-element.623) | copy-start | bytes 24580
  955.9 118.8 %copy-start.33 = (f32[2048]{0:T(1024)S(1)}, f32[2048]{0:T(1024)}, u32[]{:S(2)}) copy-start(f32[2048]{0:T(1024)} %get-tuple-element.622) | copy-start | bytes 24580
  955.9 118.8 %copy-start.41 = (f32[512]{0:T(512)S(1)}, f32[512]{0:T(512)}, u32[]{:S(2)}) copy-start(f32[512]{0:T(512)} %copy-done.40) | copy-start | bytes 6148
  955.9 118.8 %copy-start.46 = (f32[512]{0:T(512)S(1)}, f32[512]{0:T(512)}, u32[]{:S(2)}) copy-start(f32[512]{0:T(512)} %copy-done.45) | copy-start | bytes 6148
  955.9 123.3 %copy-start.52 = (f32[512]{0:T(512)S(1)}, f32[512]{0:T(512)}, u32[]{:S(2)}) copy-start(f32[512]{0:T(512)} %copy-done.51) | copy-start | bytes 6148
  956.0 266.4 %copy-start.42 = (f32[2048]{0:T(1024)S(1)}, f32[2048]{0:T(1024)}, u32[]{:S(2)}) copy-start(f32[2048]{0:T(1024)} %get-tuple-element.619) | copy-start | bytes 24580
  956.0 426.9 %all-gather.13.cloned.1.call-start = ((), (), s32[]{:S(2)}) async-start(), calls=%async_computation.11 | async-start | bytes 10485760 | tf_op jit(solution)/shard_map/all_gather | solution.py:329
  1222.3 7.5 copy-start.19
  1232.4 748.8 %reduce-scatter.12.cloned.1.call-start = ((), (), s32[]{:S(2)}) async-start(), calls=%async_computation.12 | async-start | bytes 10485760 | tf_op jit(solution)/shard_map/reduce_scatter | solution.py:377
  1232.5 160.3 %copy-start.5 = (bf16[2048,4,128]{2,0,1:T(8,128)(2,1)S(1)}, bf16[2048,4,128]{2,0,1:T(8,128)(2,1)}, u32[]{:S(2)}) copy-start(bf16[2048,4,128]{2,0,1:T(8,128)(2,1)} %copy-done.4) | copy-start | bytes 6291460
  1232.5 160.3 %copy-start.24 = (s32[1,2048]{1,0:T(1,128)S(1)}, s32[1,2048]{1,0:T(1,128)}, u32[]{:S(2)}) copy-start(s32[1,2048]{1,0:T(1,128)} %copy-done.23) | copy-start | bytes 24580
  1400.6 9.6 copy-start.7
  1483.6 9.6 copy-start.7
  1568.9 9.6 copy-start.7
  1654.2 9.6 copy-start.7
  1735.7 11.8 copy-start.16
  1775.5 335.5 %all-reduce.3.cloned.1.call-start = ((), (), s32[]{:S(2)}) async-start(), calls=%async_computation.14 | async-start | bytes 196608 | tf_op jit(solution)/shard_map/psum | solution.py:421
  1887.0 8.3 copy-start.60
  1963.1 9.3 copy-start.17
  1963.1 9.7 copy-start.50
  1963.1 9.7 copy-start.64
  1970.2 6.3 copy-start.12
  1970.2 6.3 copy-start.63
  1976.5 7.7 copy-start.54
  1976.6 7.7 copy-start.44
  1981.2 6.6 copy-start.56
  1981.3 6.5 copy-start.10
  1981.3 6.5 copy-start.18
  1981.3 6.5 copy-start.20
  1992.0 280.5 %reduce-scatter.14.cloned.1.call-start = ((), (), s32[]{:S(2)}) async-start(), calls=%async_computation.13 | async-start | bytes 28311552 | tf_op jit(solution)/shard_map/reduce_scatter | solution.py:396
  2009.6 101.4 %copy-start.28 = (f32[24576]{0:T(1024)S(1)}, f32[24576]{0:T(1024)}, u32[]{:S(2)}) copy-start(f32[24576]{0:T(1024)} %param.33) | copy-start | bytes 294916
  2009.6 101.4 %copy-start.36 = (f32[24576]{0:T(1024)S(1)}, f32[24576]{0:T(1024)}, u32[]{:S(2)}) copy-start(f32[24576]{0:T(1024)} %param.35) | copy-start | bytes 294916
  2009.7 101.4 %copy-start.37 = (f32[24576]{0:T(1024)S(1)}, f32[24576]{0:T(1024)}, u32[]{:S(2)}) copy-start(f32[24576]{0:T(1024)} %param.34) | copy-start | bytes 294916
  2272.4 18.5 slice-start.4
  2281.2 9.7 slice-start.5
  2290.9 32.0 %slice-start = ((s8[6291456]{0:T(1024)(128)(4,1)}), s8[4194304]{0:T(1024)(128)(4,1)S(1)}, s32[]{:S(2)}) async-start(s8[6291456]{0:T(1024)(128)(4,1)} %bitcast.350), calls=%async_computation.16 | async-start | bytes 8388608
  2307.4 11.4 copy-start.11
  2307.4 15.6 slice-start.1
  2322.9 7.7 copy-start.14
  2380.9 27.8 %slice-start.6 = ((s8[6291456]{0:T(1024)(128)(4,1)}), s8[4194304]{0:T(1024)(128)(4,1)S(1)}, s32[]{:S(2)}) async-start(s8[6291456]{0:T(1024)(128)(4,1)} %bitcast.368), calls=%async_computation.22 | async-start | bytes 8388608
  2393.2 15.6 slice-start.7
  2408.8 7.7 copy-start.15
  2456.9 19.2 slice-start.2
  2467.3 8.8 slice-start.3
  (28 other events, 83.9 us)
Sparse Core Ops, SparseCore 0:
  12.7 128.0 all-gather.14
  142.9 149.6 all-gather.6
  423.5 142.6 reduce-scatter.5
  575.3 150.3 all-gather.8
  727.1 147.8 all-gather.10
  932.0 142.6 reduce-scatter.9
  1077.1 145.1 reduce-scatter.7
  1232.6 150.3 all-gather.12
  1775.7 142.6 reduce-scatter.11
  1992.1 118.9 all-reduce.2
  2114.7 157.7 reduce-scatter.13
where the time goes:
time: 2510 us; the launch traced here: 2500 us
  waiting for transfers between devices  1150 us (46%)
  matrix products  826 us (33%)
  local copies, waits for them, and re-layouts  275 us (11%)
  other arithmetic  172 us (7%)
  blocking collectives  38.5 us (2%)
  loops' own time  26.9 us (1%)
    reduce_scatter x1, waiting for transfers between devices, per_device(): lax.psum_scatter(jnp.concatenate([attn_slots, ffn_slots], axis=1).astype(...  160 us
    all_gather x1, waiting for transfers between devices, per_device(): branch_rows = lax.all_gather(branch_low, 'tensor', axis=0, tiled=True)  150 us
    reduce_scatter x1, waiting for transfers between devices, per_device(): lax.psum_scatter(jnp.dot(activation, w_down, preferred_element_type=jnp.f...  143 us
    reduce_scatter x1, waiting for transfers between devices, per_device(): lax.psum_scatter(jnp.dot(attended, w_out, preferred_element_type=jnp.floa...  143 us
    all_gather x1, waiting for transfers between devices, per_device(): lax.all_gather(master[0].astype(jnp.bfloat16), 'dp', axis=0, tiled=True)  120 us
    reduce_scatter x1, waiting for transfers between devices, per_device(): lax.psum_scatter(contract_cols(grad_pre, w_up).astype(jnp.bfloat16), 'ten...  119 us
    dot_general x4, matrix products, attend_backward(): jnp.einsum('hqk,qhd->khd', grad_product, query_block, preferred_element_t...  103 us
    all_gather x1, waiting for transfers between devices, per_device(): normed_all = lax.all_gather(normed_one, 'tensor', axis=0, tiled=True)  96.8 us
  transfers between devices with their start and end apart: 11, of which 10 were waited for; matrix products, arithmetic and copies ran while one was open for 18% of the time, Pallas kernels for 0%

commit v1 on v0

v1 whole, which is shorter than its diff:
```python
import math

import jax
import jax.numpy as jnp
from jax import lax
from jax.experimental import pallas as pl
from jax.experimental.pallas import tpu as pltpu
from jax.sharding import PartitionSpec as P

D = 2048
H = 16
HD = 128
FF = 8192
PROMPT = 1024
STEP = 5
NS_ITERS = 3
SEQ = 2048
BQ = 256
BF = jnp.bfloat16
F32 = jnp.float32
SCALE = HD ** (-0.5)
LOG2E = 1.4426950408889634
VMEM_CAP = 56 * 1024 * 1024


def dot_nt(a, b):
    return lax.dot_general(a, b, (((1,), (1,)), ((), ())), preferred_element_type=F32)


def dot_tn(a, b):
    return lax.dot_general(a, b, (((0,), (0,)), ((), ())), preferred_element_type=F32)


def dot_nn(a, b):
    return lax.dot_general(a, b, (((1,), (0,)), ((), ())), preferred_element_type=F32)


def key_parts(lo):
    if lo < PROMPT:
        return ([(0, lo, False)] if lo else []) + [(lo, lo + BQ, True)]
    return [(0, PROMPT, False), (PROMPT, lo + BQ, True)]


def part_scores(keys, query_block, lo, part, start_row):
    first, last, masked = part
    product = dot_nt(keys[first:last], query_block)
    if masked:
        key_pos = first + lax.broadcasted_iota(jnp.int32, product.shape, 0)
        query_pos = lo + lax.broadcasted_iota(jnp.int32, product.shape, 1)
        seen = (key_pos <= query_pos) & (key_pos >= start_row)
        product = jnp.where(seen, product, -1e30)
    return product


def softmax_parts(scores):
    top = scores[0].max(axis=0, keepdims=True)
    for piece in scores[1:]:
        top = jnp.maximum(top, piece.max(axis=0, keepdims=True))
    weights = [jnp.exp2((piece - top) * (SCALE * LOG2E)) for piece in scores]
    total = weights[0].sum(axis=0, keepdims=True)
    for piece in weights[1:]:
        total = total + piece.sum(axis=0, keepdims=True)
    return top, weights, total


def attend_kernel(start_ref, qkv_ref, out_ref, peak_ref):
    keys = qkv_ref[:, HD : 2 * HD]
    values_t = qkv_ref[:, 2 * HD :].T
    peak = jnp.full((1, BQ), -1e30, F32)
    for lo in range(0, SEQ, BQ):
        query_block = qkv_ref[lo : lo + BQ, :HD]
        start_row = start_ref[:, lo : lo + BQ]
        parts = key_parts(lo)
        scores = [part_scores(keys, query_block, lo, part, start_row) for part in parts]
        top, weights, total = softmax_parts(scores)
        peak = jnp.maximum(peak, top)
        mixed = None
        for (first, last, _), piece in zip(parts, weights):
            term = dot_nn(values_t[:, first:last], piece.astype(BF))
            mixed = term if mixed is None else mixed + term
        out_ref[lo : lo + BQ, :] = (mixed * (1.0 / total)).T.astype(BF)
    peak_ref[...] = jnp.broadcast_to(peak.max(axis=1, keepdims=True) * SCALE, peak_ref.shape)


def attend(start_rows, qkv):
    heads = qkv.shape[1] // (3 * HD)
    return pl.pallas_call(
        attend_kernel,
        grid=(heads,),
        in_specs=[
            pl.BlockSpec((1, SEQ), lambda h: (0, 0)),
            pl.BlockSpec((SEQ, 3 * HD), lambda h: (0, h)),
        ],
        out_specs=[
            pl.BlockSpec((SEQ, HD), lambda h: (0, h)),
            pl.BlockSpec((1, 8, HD), lambda h: (h, 0, 0)),
        ],
        out_shape=[
            jax.ShapeDtypeStruct((SEQ, heads * HD), BF),
            jax.ShapeDtypeStruct((heads, 8, HD), F32),
        ],
        compiler_params=pltpu.CompilerParams(vmem_limit_bytes=VMEM_CAP),
        cost_estimate=pl.CostEstimate(
            flops=heads * SEQ * SEQ * HD * 4, bytes_accessed=heads * SEQ * HD * 8, transcendentals=heads * SEQ * SEQ // 2
        ),
        name="attend",
    )(start_rows, qkv)


def attend_back_kernel(start_ref, qkv_ref, back_ref, out_ref, key_acc, value_acc):
    keys = qkv_ref[:, HD : 2 * HD]
    values = qkv_ref[:, 2 * HD :]
    keys_t = keys.T
    key_acc[...] = jnp.zeros_like(key_acc)
    value_acc[...] = jnp.zeros_like(value_acc)
    for lo in range(0, SEQ, BQ):
        query_block = qkv_ref[lo : lo + BQ, :HD]
        back_block = back_ref[lo : lo + BQ, :]
        start_row = start_ref[:, lo : lo + BQ]
        parts = key_parts(lo)
        scores = [part_scores(keys, query_block, lo, part, start_row) for part in parts]
        top, weights, total = softmax_parts(scores)
        inverse = 1.0 / total
        probs = [piece * inverse for piece in weights]
        grads = [dot_nt(values[first:last], back_block) for first, last, _ in parts]
        mean = None
        for piece, grad in zip(probs, grads):
            term = (piece * grad).sum(axis=0, keepdims=True)
            mean = term if mean is None else mean + term
        query_t = None
        for (first, last, _), piece, grad in zip(parts, probs, grads):
            low = (piece * ((grad - mean) * SCALE)).astype(BF)
            value_acc[first:last, :] += dot_nn(piece.astype(BF), back_block)
            key_acc[first:last, :] += dot_nn(low, query_block)
            term = dot_nn(keys_t[:, first:last], low)
            query_t = term if query_t is None else query_t + term
        out_ref[lo : lo + BQ, :HD] = query_t.T.astype(BF)
    out_ref[:, HD : 2 * HD] = key_acc[...].astype(BF)
    out_ref[:, 2 * HD :] = value_acc[...].astype(BF)


def attend_back(start_rows, qkv, back):
    heads = qkv.shape[1] // (3 * HD)
    return pl.pallas_call(
        attend_back_kernel,
        grid=(heads,),
        in_specs=[
            pl.BlockSpec((1, SEQ), lambda h: (0, 0)),
            pl.BlockSpec((SEQ, 3 * HD), lambda h: (0, h)),
            pl.BlockSpec((SEQ, HD), lambda h: (0, h)),
        ],
        out_specs=pl.BlockSpec((SEQ, 3 * HD), lambda h: (0, h)),
        out_shape=jax.ShapeDtypeStruct(qkv.shape, BF),
        scratch_shapes=[pltpu.VMEM((SEQ, HD), F32), pltpu.VMEM((SEQ, HD), F32)],
        compiler_params=pltpu.CompilerParams(vmem_limit_bytes=VMEM_CAP),
        cost_estimate=pl.CostEstimate(
            flops=heads * SEQ * SEQ * HD * 10, bytes_accessed=heads * SEQ * HD * 14, transcendentals=heads * SEQ * SEQ // 2
        ),
        name="attend_back",
    )(start_rows, qkv, back)


TILE_GROUP = 8


def orthonormal_all(matrices):
    currents = []
    for matrix in matrices:
        frob = jnp.sqrt(jnp.sum(matrix * matrix, axis=(0, 1), keepdims=True))
        currents.append(matrix * (1.0 / (frob + 1e-06)))
    for _ in range(NS_ITERS):
        lows = [current.astype(BF) for current in currents]
        grams = [dot_nt(low, low).astype(BF) for low in lows]
        terms = [dot_nn(gram, low) for gram, low in zip(grams, lows)]
        currents = [1.5 * current - 0.5 * term for current, term in zip(currents, terms)]
    return currents


def update_kernel(tile_group, turned_grad, token_count, *refs):
    rate_ref, factor_ref, grad_ref = refs[:3]
    master_ref, first_ref, second_ref, left_stat_ref, right_stat_ref, left_ref, right_ref = refs[3:10]
    outs = refs[-8:]
    first_out, second_out, master_out, weight_out, left_stat_out, right_stat_out, left_out, right_out = outs
    base = pl.program_id(0) * tile_group
    group = range(tile_group)
    grads = [grad_ref[i] for i in group]
    lefts = [left_ref[i].astype(BF) for i in group]
    rights = [right_ref[i].astype(BF) for i in group]
    if turned_grad:
        outer_rows = [dot_tn(grad, grad) for grad in grads]
        outer_cols = [dot_nt(grad, grad) for grad in grads]
        halves = [dot_nn(grad, left).astype(BF) for grad, left in zip(grads, lefts)]
        rotated = [dot_tn(half, right) for half, right in zip(halves, rights)]
    else:
        outer_rows = [dot_nt(grad, grad) for grad in grads]
        outer_cols = [dot_tn(grad, grad) for grad in grads]
        halves = [dot_nn(grad, right).astype(BF) for grad, right in zip(grads, rights)]
        rotated = [dot_tn(left, half) for left, half in zip(lefts, halves)]
    directions = []
    for i in group:
        new_first = 0.5 * first_ref[i] + 0.5 * rotated[i]
        new_second = 0.5 * second_ref[i] + 0.5 * rotated[i] * rotated[i]
        first_out[i] = new_first
        second_out[i] = new_second
        direction = (
            new_first
            * (1.0 / (1.0 - 0.5**STEP))
            / (jnp.sqrt(new_second * (1.0 / (1.0 - 0.5**STEP))) + 1e-08)
        )
        directions.append(direction.astype(BF))
    turned = [dot_nn(left, direction).astype(BF) for left, direction in zip(lefts, directions)]
    turned = [dot_nt(half, right) for half, right in zip(turned, rights)]
    for i in group:
        master = master_ref[i]
        new_master = (master - rate_ref[base + i] * (turned[i] + 0.1 * master)) * factor_ref[base + i]
        master_out[i] = new_master
        weight_out[i] = new_master.astype(BF)
    moved = []
    for stat_ref, stat_out, outers, bases in (
        (left_stat_ref, left_stat_out, outer_rows, lefts),
        (right_stat_ref, right_stat_out, outer_cols, rights),
    ):
        for i in group:
            new_stat = 0.5 * stat_ref[i] + (0.5 / (HD * token_count)) * outers[i]
            stat_out[i] = new_stat
            moved.append(dot_nn(new_stat.astype(BF), bases[i]))
    moved = orthonormal_all(moved)
    for i in group:
        left_out[i] = moved[i]
        right_out[i] = moved[tile_group + i]


def update_tiles(grads, state, rates, factors, first_tile, earlier, turned_grad, token_count):
    count = grads.shape[0]
    tiles = state[0].shape[0]
    group = math.gcd(math.gcd(count, first_tile), TILE_GROUP)
    offset = first_tile // group
    block = (group, HD, HD)
    here = pl.BlockSpec(block, lambda i: (i + offset, 0, 0))
    smem = pl.BlockSpec(memory_space=pltpu.SMEM)
    kinds = [F32, F32, F32, BF, F32, F32, F32, F32]
    earlier = list(earlier) if earlier is not None else []

    def body(*refs):
        update_kernel(group, turned_grad, token_count, *refs)

    return pl.pallas_call(
        body,
        grid=(count // group,),
        in_specs=[smem, smem, pl.BlockSpec(block, lambda i: (i, 0, 0))]
        + [here] * 7
        + [pl.BlockSpec(memory_space=pl.ANY)] * len(earlier),
        out_specs=[here] * 8,
        out_shape=[jax.ShapeDtypeStruct((tiles, HD, HD), kind) for kind in kinds],
        input_output_aliases={10 + i: i for i in range(len(earlier))},
        compiler_params=pltpu.CompilerParams(vmem_limit_bytes=VMEM_CAP),
        cost_estimate=pl.CostEstimate(
            flops=count * 20 * HD**3 * 2 * 4, bytes_accessed=count * HD * HD * 56, transcendentals=count * HD * HD * 2
        ),
        name="update_tiles",
    )(rates[first_tile : first_tile + count], factors[first_tile : first_tile + count], grads, *state, *earlier)


def grad_kernel(chunks, block_ref, *refs):
    lefts, rights, out_ref = refs[:chunks], refs[chunks : 2 * chunks], refs[2 * chunks]
    width = out_ref.shape[2]
    step = min(512, width)
    for lo in range(0, width, step):
        total = None
        for left, right in zip(lefts, rights):
            term = dot_tn(left[...], right[:, lo : lo + step])
            total = term if total is None else total + term
        out_ref[0, :, lo : lo + step] = total.astype(BF)


def grad_blocks(blocks, lefts, rights, edge):
    count = blocks.shape[0]
    width = rights[0].shape[1]
    rows = sum(left.shape[0] for left in lefts)
    chunks = len(lefts)

    def body(*refs):
        grad_kernel(chunks, *refs)

    return pl.pallas_call(
        body,
        grid_spec=pltpu.PrefetchScalarGridSpec(
            num_scalar_prefetch=1,
            grid=(count,),
            in_specs=[pl.BlockSpec((left.shape[0], edge), lambda i, blocks: (0, blocks[i])) for left in lefts]
            + [pl.BlockSpec(right.shape, lambda i, blocks: (0, 0)) for right in rights],
            out_specs=pl.BlockSpec((1, edge, width), lambda i, blocks: (i, 0, 0)),
        ),
        out_shape=jax.ShapeDtypeStruct((count, edge, width), BF),
        compiler_params=pltpu.CompilerParams(vmem_limit_bytes=VMEM_CAP),
        cost_estimate=pl.CostEstimate(
            flops=2 * count * edge * width * rows,
            bytes_accessed=2 * (count * edge * (width + rows) + rows * width),
            transcendentals=0,
        ),
        name="grad_blocks",
    )(blocks, *lefts, *rights)


def shift(value, axis, mask):
    return lax.ppermute(value, axis, [(i, i ^ mask) for i in range(lax.axis_size(axis))])


def add_low(left, right):
    return (left.astype(F32) + right.astype(F32)).astype(BF)


def chip_gather(value, masks):
    pieces = {0: value}
    for mask in masks:
        pieces.update({q | (mask >> 1): shift(piece, "dp", mask) for q, piece in pieces.items()})
    return [pieces[q] for q in range(len(pieces))]


def chip_reduce(pieces, masks):
    pieces = dict(enumerate(pieces))
    for mask in masks:
        bit = mask >> 1
        pieces = {
            q: add_low(piece, shift(pieces[q | bit], "dp", mask)) for q, piece in pieces.items() if not q & bit
        }
    return pieces[0]


def layer_norm(token_rows, gain, shift_by):
    centre = jnp.mean(token_rows, axis=-1, keepdims=True)
    centred = token_rows - centre
    spread = jnp.mean(centred * centred, axis=-1, keepdims=True)
    return centred * lax.rsqrt(spread + 1e-05) * gain + shift_by


def layer_norm_back(token_rows, gain, grad):
    centre = jnp.mean(token_rows, axis=-1, keepdims=True)
    centred = token_rows - centre
    inverse = lax.rsqrt(jnp.mean(centred * centred, axis=-1, keepdims=True) + 1e-05)
    normal = centred * inverse
    scaled = grad * gain
    back = (
        scaled - jnp.mean(scaled, axis=-1, keepdims=True) - normal * jnp.mean(scaled * normal, axis=-1, keepdims=True)
    ) * inverse
    return back, jnp.sum(grad * normal, axis=0), jnp.sum(grad, axis=0)


def gelu_pair(pre_act):
    cdf = 0.5 * (1.0 + lax.erf(pre_act * (0.5**0.5)))
    density = jnp.exp(-0.5 * pre_act * pre_act) * 0.3989422804014327
    return pre_act * cdf, cdf + pre_act * density


def small_step(summed, params, first, second):
    new_first = 0.5 * first + 0.5 * summed
    new_second = 0.5 * second + 0.5 * summed * summed
    direction = new_first / (1.0 - 0.5**STEP) / (jnp.sqrt(new_second / (1.0 - 0.5**STEP)) + 1e-08)
    return new_first, new_second, params - 0.1 * direction


def per_device(
    inputs,
    cotangent,
    lengths,
    held_blocks,
    master,
    first_moment,
    second_moment,
    left_stats,
    right_stats,
    left_basis,
    right_basis,
    small_params,
    small_first,
    small_second,
):
    dp_count = lax.axis_size("dp")
    tp_count = lax.axis_size("tensor")
    me = lax.axis_index("dp")
    place = lax.axis_index("tensor")
    core = me & 1
    first_core = core == 0
    rows = inputs.shape[0]
    edge = D // dp_count
    width = D // tp_count
    hidden = FF // tp_count
    half = hidden // 2
    heads = width // HD
    edge_tiles = edge // HD
    hidden_tiles = hidden // HD
    tile_q = edge_tiles * 3 * heads
    tile_o = heads * edge_tiles
    tile_u = edge_tiles * hidden_tiles
    tile_count = master.shape[2]
    near = [1 << bit for bit in range(1, dp_count.bit_length() - 1)]
    far = near[::-1]
    slices = tp_count // 2
    inverse = jnp.argsort(held_blocks, axis=1).astype(jnp.int32)
    relative = jnp.arange(dp_count, dtype=jnp.int32) ^ me
    block_of = jnp.take(held_blocks, relative, axis=1)
    source_of = inverse ^ me

    bias_q = lax.dynamic_slice_in_dim(small_params, place * width, width)
    bias_v = lax.dynamic_slice_in_dim(small_params, D + place * width, width)
    bias_o = small_params[2 * D : 3 * D]
    bias_two = small_params[3 * D : 4 * D]
    gain_one = small_params[4 * D : 5 * D]
    shift_one = small_params[5 * D : 6 * D]
    gain_two = small_params[6 * D : 7 * D]
    shift_two = small_params[7 * D : 8 * D]
    hidden_starts = [(place ^ (2 * j)) * hidden + core * half for j in range(slices)]
    bias_up = jnp.concatenate(
        [lax.dynamic_slice_in_dim(small_params, 8 * D + start, half) for start in hidden_starts]
    )

    token_rows = inputs.astype(F32)
    normed_one = layer_norm(token_rows, gain_one, shift_one).astype(BF)
    normed_all = lax.all_gather(normed_one, "tensor", axis=0, tiled=True)

    low = master[0, 0].astype(BF)
    bounds = [0, tile_q, tile_q + tile_o, tile_q + tile_o + tile_u, tile_count]
    own_qkv = low[: bounds[1]].reshape(edge_tiles, 3, heads, HD, HD).transpose(0, 3, 2, 1, 4).reshape(edge, 3 * width)
    own_out = low[bounds[1] : bounds[2]].reshape(heads, edge_tiles, HD, HD).transpose(1, 3, 0, 2).reshape(edge, width)
    own_up = low[bounds[2] : bounds[3]].reshape(edge_tiles, hidden_tiles, HD, HD).transpose(0, 2, 1, 3).reshape(edge, hidden)
    own_down = low[bounds[3] :].reshape(hidden_tiles, edge_tiles, HD, HD).transpose(1, 3, 0, 2).reshape(edge, hidden)

    def split_pair(own):
        part = own.shape[1] // 2
        mine = lax.dynamic_slice_in_dim(own, core * part, part, 1)
        other = lax.dynamic_slice_in_dim(own, (1 - core) * part, part, 1)
        return jnp.stack([mine, shift(other, "dp", 1)])

    def join_halves(mine, other):
        return jnp.concatenate([jnp.where(first_core, mine, other), jnp.where(first_core, other, mine)], axis=-1)

    def in_order(pieces, kind):
        whole = jnp.concatenate(pieces, axis=0)
        return jnp.take(whole, source_of[kind], axis=0).reshape(D, whole.shape[2])

    pieces_qkv = chip_gather(split_pair(own_qkv), near)
    mine_qkv = jnp.concatenate(pieces_qkv, axis=0)
    other_qkv = shift(mine_qkv, "dp", 1).reshape(dp_count // 2, 2, edge, -1)[:, ::-1].reshape(mine_qkv.shape)
    w_qkv = jnp.take(join_halves(mine_qkv, other_qkv), source_of[0], axis=0).reshape(D, 3 * width)

    pair_up = split_pair(own_up)
    pair_down = split_pair(own_down)
    pairs_up = [pair_up] + [shift(pair_up, "tensor", 2 * j) for j in range(1, slices)]
    pairs_down = [pair_down] + [shift(pair_down, "tensor", 2 * j) for j in range(1, slices)]

    pair_out = split_pair(own_out)
    pairs_out = jnp.stack([pair_out] + [shift(pair_out, "tensor", j) for j in range(1, tp_count)], axis=1)
    mine_out = jnp.concatenate(chip_gather(pairs_out, far), axis=0)
    other_out = shift(mine_out, "dp", 1).reshape((dp_count // 2, 2) + mine_out.shape[1:])[:, ::-1].reshape(mine_out.shape)
    w_out = jnp.take(join_halves(mine_out, other_out), source_of[1], axis=0)
    w_out = w_out.transpose(0, 2, 1, 3).reshape(D, D)

    w_up = jnp.concatenate([in_order(chip_gather(pair, near), 2) for pair in pairs_up], axis=1)
    w_down = jnp.concatenate([in_order(chip_gather(pair, far), 3) for pair in pairs_down], axis=1)

    bias_mixed = jnp.stack(
        [bias_q.reshape(heads, HD), jnp.zeros((heads, HD), F32), bias_v.reshape(heads, HD)], axis=1
    ).reshape(3 * width)
    qkv = (jnp.dot(normed_all, w_qkv, preferred_element_type=F32) + bias_mixed).astype(BF)
    ends = jnp.cumsum(lengths[0])
    spot = jnp.arange(SEQ, dtype=jnp.int32) - PROMPT
    started = jnp.max(jnp.where(ends[None, :] <= spot[:, None], ends[None, :], 0), axis=1)
    start_rows = jnp.where(spot < 0, 0, PROMPT + started).astype(jnp.int32)[None]
    attended, peaks = attend(start_rows, qkv)

    def rows_of(value, j):
        return lax.dynamic_slice_in_dim(value, (place ^ j) * rows, rows, 0)

    attended_rows = jnp.concatenate(
        [rows_of(attended, 0)] + [shift(rows_of(attended, j), "tensor", j) for j in range(1, tp_count)], axis=1
    )
    hidden_rows = token_rows + dot_nt(attended_rows, w_out) + bias_o
    normed_two = layer_norm(hidden_rows, gain_two, shift_two).astype(BF)

    def four_rows(value):
        sibling = shift(value, "dp", 1)
        across = shift(value, "tensor", 1)
        return [value, sibling, across, shift(across, "dp", 1)]

    def sum_rows(partial):
        near_rows = add_low(partial[0], shift(partial[1], "dp", 1))
        far_rows = add_low(partial[2], shift(partial[3], "dp", 1))
        return near_rows.astype(F32) + shift(far_rows, "tensor", 1).astype(F32)

    back_list = four_rows(cotangent)
    back_four = jnp.concatenate(back_list, axis=0)
    normed_four = jnp.concatenate(four_rows(normed_two), axis=0)
    grad_act = jnp.dot(back_four, w_down, preferred_element_type=F32).astype(BF)
    pre_act = jnp.dot(normed_four, w_up, preferred_element_type=F32) + bias_up
    activation, slope = gelu_pair(pre_act)
    activation = activation.astype(BF)
    grad_pre = (grad_act.astype(F32) * slope).astype(BF)
    grad_normed = dot_nt(grad_pre, w_up).astype(BF)
    grad_two = sum_rows([grad_normed[i * rows : (i + 1) * rows] for i in range(4)])
    grad_bias_up = jnp.sum(grad_pre, axis=0, dtype=F32)

    def ffn_grad(kind, left, right, masks):
        blocks = block_of[kind]
        bit = masks[0] >> 1
        order = [q for q in range(dp_count // 2) if q & bit] + [q for q in range(dp_count // 2) if not q & bit]
        pieces = [None] * len(order)
        for group in (order[: len(order) // 2], order[len(order) // 2 :]):
            picked = jnp.concatenate([blocks[2 * q : 2 * q + 2] for q in group])
            out = grad_blocks(picked, [left], [right], edge)
            for i, q in enumerate(group):
                pieces[q] = out[2 * i : 2 * i + 2]
        reduced = chip_reduce(pieces, masks).reshape(2, edge, slices, half)
        total = reduced[:, :, 0].astype(F32)
        for j in range(1, slices):
            total = total + shift(reduced[:, :, j], "tensor", 2 * j).astype(F32)
        total = total.astype(BF)
        return join_halves(total[0], shift(total[1], "dp", 1))

    sum_up = ffn_grad(2, normed_four, grad_pre, near)
    sum_down = ffn_grad(3, back_four, activation, far)

    result = dot_nt(activation, w_down).astype(BF)
    ffn_rows = sum_rows([result[i * rows : (i + 1) * rows] for i in range(4)])
    outputs = (hidden_rows + ffn_rows + bias_two).astype(BF)

    back_rows = cotangent.astype(F32)
    grad_part, grad_gain_two, grad_shift_two = layer_norm_back(hidden_rows, gain_two, grad_two)
    grad_hidden = back_rows + grad_part
    branch = grad_hidden.astype(BF)
    grad_attended_rows = jnp.dot(branch, w_out, preferred_element_type=F32).astype(BF)
    arrived = [
        grad_attended_rows[:, j * width : (j + 1) * width]
        if j == 0
        else shift(grad_attended_rows[:, j * width : (j + 1) * width], "tensor", j)
        for j in range(tp_count)
    ]
    grad_attended = jnp.zeros((SEQ, width), BF)
    for j in range(tp_count):
        grad_attended = lax.dynamic_update_slice_in_dim(grad_attended, arrived[j], (place ^ j) * rows, 0)
    grad_qkv_rows = attend_back(start_rows, qkv, grad_attended)

    def core_reduce(blocks):
        pairs = blocks.reshape(dp_count // 2, 2, edge, blocks.shape[2])
        return add_low(pairs[:, 0], shift(pairs[:, 1], "dp", 1))

    def full_reduce(blocks):
        summed = core_reduce(blocks)
        part = summed.shape[2] // 2
        left = chip_reduce([summed[q, :, :part] for q in range(dp_count // 2)], near)
        right = chip_reduce([summed[q, :, part:] for q in range(dp_count // 2)], far)
        return jnp.concatenate([left, right], axis=1)

    sum_out = full_reduce(grad_blocks(block_of[1], [branch], [attended_rows], edge))
    total_out = sum_out[:, :width].astype(F32)
    for j in range(1, tp_count):
        total_out = total_out + shift(sum_out[:, j * width : (j + 1) * width], "tensor", j).astype(F32)
    sum_out = total_out.astype(BF)

    grad_normed_one = lax.psum_scatter(
        dot_nt(grad_qkv_rows, w_qkv).astype(BF), "tensor", scatter_dimension=0, tiled=True
    ).astype(F32)
    sum_qkv = full_reduce(grad_blocks(block_of[0], [normed_all], [grad_qkv_rows], edge))
    rows_part, grad_gain_one, grad_shift_one = layer_norm_back(token_rows, gain_one, grad_normed_one)
    input_grad = (grad_hidden + rows_part).astype(BF)

    column_sums = jnp.sum(grad_qkv_rows, axis=0, dtype=F32).reshape(heads, 3, HD)
    head_sums = lambda part: lax.dynamic_update_slice(
        jnp.zeros((D,), F32), column_sums[:, part].reshape(width), (place * width,)
    )
    wide = jnp.zeros((FF,), F32)
    for j in range(slices):
        wide = lax.dynamic_update_slice(wide, grad_bias_up[j * half : (j + 1) * half], (hidden_starts[j],))
    peak_row = lax.dynamic_update_slice(
        jnp.zeros((dp_count * H,), F32), peaks[:, 0, 0], (me * H + place * heads,)
    )
    early = lax.psum(
        jnp.concatenate(
            [
                head_sums(0),
                head_sums(2),
                jnp.sum(branch, axis=0, dtype=F32),
                jnp.sum(cotangent, axis=0, dtype=F32),
                grad_gain_two,
                grad_shift_two,
                wide,
                peak_row,
            ]
        ),
        ("dp", "tensor"),
    )
    late = lax.psum(jnp.concatenate([grad_gain_one, grad_shift_one]), ("dp", "tensor"))
    grad_small = jnp.concatenate([early[: 4 * D], late, early[4 * D : 6 * D + FF]])
    peak_all = jnp.max(early[6 * D + FF :].reshape(dp_count, H), axis=0)
    shrink = jnp.sqrt(1.0 / jnp.maximum(peak_all, 1.0))
    small_first_new, small_second_new, small_new = small_step(grad_small, small_params, small_first, small_second)
    small_new = jnp.concatenate([(small_new[:D].reshape(H, HD) * shrink[:, None]).reshape(D), small_new[D:]])

    index = jnp.arange(tile_count, dtype=jnp.int32)
    rates = jnp.where(
        index < bounds[1],
        D ** (-0.5),
        jnp.where(index < bounds[2], (SEQ / (2.0 * D)) ** 0.5, jnp.where(index < bounds[3], D ** (-0.5), FF ** (-0.5))),
    ).astype(F32)
    column = index % (3 * heads)
    shrink_here = lax.dynamic_slice_in_dim(shrink, place * heads, heads)
    factors = jnp.where((index < bounds[1]) & (column < 2 * heads), shrink_here[column % heads], 1.0)
    ones = jnp.ones((tile_count,), F32)
    token_count = float(dp_count * SEQ)
    state = [value[0, 0] for value in (master, first_moment, second_moment, left_stats, right_stats, left_basis, right_basis)]
    tiles_up = sum_up.reshape(edge_tiles, HD, hidden_tiles, HD).transpose(0, 2, 1, 3).reshape(tile_u, HD, HD)
    tiles_down = sum_down.reshape(edge_tiles, HD, hidden_tiles, HD).transpose(2, 0, 1, 3).reshape(tile_u, HD, HD)
    tiles_out = sum_out.reshape(edge_tiles, HD, heads, HD).transpose(2, 0, 1, 3).reshape(tile_o, HD, HD)
    tiles_qkv = sum_qkv.reshape(edge_tiles, HD, heads, 3, HD).transpose(0, 3, 2, 1, 4).reshape(tile_q, HD, HD)
    done = update_tiles(tiles_down, state, rates, ones, bounds[3], None, True, token_count)
    done = update_tiles(tiles_up, state, rates, ones, bounds[2], done, False, token_count)
    done = update_tiles(tiles_out, state, rates, ones, bounds[1], done, True, token_count)
    done = update_tiles(tiles_qkv, state, rates, factors, 0, done, False, token_count)
    return (
        outputs,
        input_grad,
        *[value[None, None] for value in done],
        small_first_new,
        small_second_new,
        small_new,
    )


def solution(mesh):
    rows = P(("dp", "tensor"), None)
    tiles = P("dp", "tensor", None, None, None)
    return jax.shard_map(
        per_device,
        mesh=mesh,
        in_specs=(rows, rows, P("dp", None), P()) + (tiles,) * 7 + (P(), P(), P()),
        out_specs=(rows, rows) + (tiles,) * 8 + (P(), P(), P()),
        check_vma=False,
    )
```

time: 2510 us -> 1320 us (0.53)
  waiting for transfers between devices: 1150 us -> 422 us
  matrix products: 826 us -> 149 us
  Pallas kernels: 0 us -> 207 us
  starting transfers between devices: 0.45 us -> 98 us
  local copies, waits for them, and re-layouts: 275 us -> 216 us
  loops' own time: 26.9 us -> 0 us
    dot_general x60 -> x8, matrix products: 826 us -> 149 us  [the longest x4 65.3 us: dot_nt(): lax.dot_general(a, b, (((1,), (1,)), ((), ())), preferred_element_type=F32)]
    reduce_scatter x5 -> x1, waiting for transfers between devices: 564 us -> 0.02 us  [per_device(): lax.psum_scatter(dot_nt(grad_qkv_rows, w_qkv).astype(BF), 'tensor', scatt...]
    all_gather x4 -> x0, waiting for transfers between devices: 425 us -> none  [the longest x1 150 us: per_device(): branch_rows = lax.all_gather(branch_low, 'tensor', axis=0, tiled=True)]
    ppermute x0 -> x74, waiting for transfers between devices: none -> 387 us  [shift(): lax.ppermute(value, axis, [(i, i ^ mask) for i in range(lax.axis_size(axi...]
    pallas_call x0 -> x12, Pallas kernels: none -> 207 us  [the longest x6 90.7 us: grad_blocks(): pl.pallas_call(body, grid_spec=pltpu.PrefetchScalarGridSpec(num_scalar_pr...]
    ppermute x0 -> x74, starting transfers between devices: none -> 97.9 us  [shift(): lax.ppermute(value, axis, [(i, i ^ mask) for i in range(lax.axis_size(axi...]
    all_gather x1, waiting for transfers between devices: 96.8 us -> 0.01 us  [per_device(): normed_all = lax.all_gather(normed_one, 'tensor', axis=0, tiled=True)]
    convert_element_type x4 -> x21, other arithmetic: 12.8 us -> 54.9 us  [the longest x14 38.2 us: add_low(): return (left.astype(F32) + right.astype(F32)).astype(BF)]
  transfers between devices with their start and end apart: 11 -> 77, of which waited for: 10 -> 24; matrix products, arithmetic and copies ran while one was open for 18% -> 32% of each run, Pallas kernels for 0% -> 16%
where the time goes in v1:
time: 1320 us; the launch traced here: 1310 us
  waiting for transfers between devices  422 us (32%)
  local copies, waits for them, and re-layouts  216 us (16%)
  Pallas kernels  207 us (16%)
  other arithmetic  168 us (13%)
  matrix products  149 us (11%)
  starting transfers between devices  98 us (7%)
  blocking collectives  37.2 us (3%)
  between operations  15.3 us (1%)
    ppermute x74, waiting for transfers between devices, shift(): lax.ppermute(value, axis, [(i, i ^ mask) for i in range(lax.axis_size(axi...  387 us
    ppermute x74, starting transfers between devices, shift(): lax.ppermute(value, axis, [(i, i ^ mask) for i in range(lax.axis_size(axi...  97.9 us
    pallas_call x6, Pallas kernels, grad_blocks(): pl.pallas_call(body, grid_spec=pltpu.PrefetchScalarGridSpec(num_scalar_pr...  90.7 us
    unnamed x192, local copies, waits for them, and re-layouts  68.1 us
    dot_general x4, matrix products, dot_nt(): lax.dot_general(a, b, (((1,), (1,)), ((), ())), preferred_element_type=F32)  65.3 us
    pallas_call x4, Pallas kernels, update_tiles(): pl.pallas_call(body, grid=(count // group,), in_specs=[smem, smem, pl.Blo...  51.7 us
    pallas_call x1, Pallas kernels, attend_back(): pl.pallas_call(attend_back_kernel, grid=(heads,), in_specs=[pl.BlockSpec(...  43.3 us
    convert_element_type x14, other arithmetic, add_low(): return (left.astype(F32) + right.astype(F32)).astype(BF)  38.2 us
  transfers between devices with their start and end apart: 77, of which 24 were waited for; matrix products, arithmetic and copies ran while one was open for 32% of the time, Pallas kernels for 16%

profile of v1, /device:TPU:0, one launch (start us, length us, event | category | flops | bytes accessed | tf_op | source)
XLA Modules:
  0.0 1312.8 jit_solution(1600325197455653179)
XLA Ops:
  54.4 6.8 collective-permute-done.11
  61.2 38.6 %collective-permute-done.10 = bf16[2,256,256]{2,1,0:T(8,128)(2,1)S(1)} collective-permute-done((bf16[2,256,256]{2,1,0:T(8,128)(2,1)S(1)}, bf16[2,256,256]{2,1,0:T(8,128)(2,1)S(1)}, u32[]{:S(2)}, u32[]{:S(2)}) %collective-permute-start.10) | collective-permute-done | bytes 262176 | tf_op jit(solution)/shard_map/ppermute | solution.py:306
  115.2 12.1 collective-permute-done.13
  132.8 11.4 collective-permute-done.2
  146.3 8.3 collective-permute-done.3
  159.3 5.0 pad_maximum_fusion.9
  186.0 6.6 gather_fusion
  192.6 8.6 copy.101
  201.2 6.1 bitcast_select_fusion
  212.0 5.7 broadcast_select_fusion.5
  217.7 7.6 pad_maximum_fusion
  225.3 8.2 gather_fusion.1
  233.6 18.8 %add_convert_fusion.qkv_ref = bf16[2048,1536]{1,0:T(8,128)(2,1)} fusion(bf16[2048,2048]{1,0:T(8,128)(2,1)} %all-gather.2.cloned.1.call-done.refs_1_, bf16[2048,1536]{1,0:T(8,128)(2,1)} %bitcast_select_fusion, f32[1536]{0:T(1024)S(1)} %add.406), kind=kOutput, calls=%fused_computation.18 | convolution fusion | flops 12891193344 | bytes 20977664 | tf_op jit(solution)/shard_map/dot_general | solution.py:464
  252.3 20.9 %attend.1 = (bf16[2048,512]{1,0:T(8,128)(2,1)}, f32[4,8,128]{2,1,0:T(8,128)}) custom-call(s32[1,2048]{1,0:T(1,128)} %compare_select_fusion.start_ref, bf16[2048,1536]{1,0:T(8,128)(2,1)} %add_convert_fusion.qkv_ref), custom_call_target="tpu_custom_call" | custom-call | flops 8589934592 | bytes 8388608 | tf_op jit(solution)/shard_map/attend/pallas_call | solution.py:87
  276.0 7.8 collective-permute-start.7
  284.4 7.5 select_bitcast_fusion
  291.9 15.2 %copy.103 = bf16[8,256,4,512]{1,0,3,2:T(8,128)(2,1)} copy(bf16[8,256,4,512]{3,1,2,0:T(8,128)(2,1)} %select_bitcast_fusion) | data formatting | bytes 16777216 | tf_op jit(solution)/shard_map/jit(_take)/select_n | solution.py:455
  307.1 10.5 copy.129
  322.0 7.2 collective-permute-done.6
  330.3 7.4 fusion.69
  337.7 49.5 %collective-permute-done.23 = bf16[2,256,1024]{2,1,0:T(8,128)(2,1)} collective-permute-done((bf16[2,256,1024]{2,1,0:T(8,128)(2,1)}, bf16[2,256,1024]{2,1,0:T(8,128)(2,1)}, u32[]{:S(2)}, u32[]{:S(2)}) %collective-permute-start.23) | collective-permute-done | bytes 1048608 | tf_op jit(solution)/shard_map/ppermute | solution.py:306
  393.0 43.3 %collective-permute-done.31 = bf16[2,256,1024]{2,1,0:T(8,128)(2,1)} collective-permute-done((bf16[2,256,1024]{2,1,0:T(8,128)(2,1)}, bf16[2,256,1024]{2,1,0:T(8,128)(2,1)}, u32[]{:S(2)}, u32[]{:S(2)}) %collective-permute-start.31) | collective-permute-done | bytes 1048608 | tf_op jit(solution)/shard_map/ppermute | solution.py:306
  449.1 11.5 collective-permute-done.30
  468.7 5.0 gather_fusion.3
  476.0 5.1 gather_fusion.5
  485.8 20.3 %collective-permute-done.26 = bf16[2,256,1024]{2,1,0:T(8,128)(2,1)} collective-permute-done((bf16[2,256,1024]{2,1,0:T(8,128)(2,1)}, bf16[2,256,1024]{2,1,0:T(8,128)(2,1)}, u32[]{:S(2)}, u32[]{:S(2)}) %collective-permute-start.26) | collective-permute-done | bytes 1048608 | tf_op jit(solution)/shard_map/ppermute | solution.py:306
  514.3 5.0 gather_fusion.4
  519.3 5.1 gather_fusion.6
  524.5 7.8 broadcast_select_fusion.3
  543.6 29.9 %multiply_convert_fusion = (bf16[2048,2048]{1,0:T(8,128)(2,1)}, f32[2048,2048]{1,0:T(8,128)}) fusion(f32[2048]{0:T(1024)S(1)} %copy-done.64, bf16[2048,1024]{1,0:T(8,128)(2,1)} %bitcast.319, bf16[2048,1024]{1,0:T(8,128)(2,1)} %bitcast.317, bf16[512,2048]{1,0:T(8,128)(2,1)} %collective-permute-done.18, bf16[512,2048]{1,0:T(8,128)(2,1)} %collective-permute-done.17, ...), kind=kOutput, calls=%fused_computation.15 | convolution fusion | flops 17255366656 | bytes 41951232 | tf_op jit(solution)/shard_map/dot_general | solution.py:494
  573.5 30.8 %convert_reduce_fusion = (f32[2048]{0:T(1024)S(1)}, bf16[2048,2048]{1,0:T(8,128)(2,1)S(1)}) fusion(f32[2048,2048]{1,0:T(8,128)} %get-tuple-element.196, f32[2048]{0:T(1024)S(1)} %copy-done.64, bf16[2048,2048]{1,0:T(8,128)(2,1)} %constant_dynamic-update-slice_fusion.15.refs_1_, bf16[2048,1024]{1,0:T(8,128)(2,1)} %bitcast.315, bf16[2048,1024]{1,0:T(8,128)(2,1)} %bitcast.313), kind=kOutput, calls=%fused_computation.14 | convolution fusion | flops 17259558912 | bytes 41959424 | tf_op jit(solution)/shard_map/dot_general | solution.py:493
  607.5 18.1 %convolution_convert_fusion.1 = bf16[2048,2048]{1,0:T(8,128)(2,1)S(1)} fusion(bf16[2048,2048]{1,0:T(8,128)(2,1)S(1)} %get-tuple-element.198.refs_2_, bf16[2048,1024]{1,0:T(8,128)(2,1)S(1)} %bitcast.320, bf16[2048,1024]{1,0:T(8,128)(2,1)S(1)} %bitcast.318), kind=kOutput, calls=%fused_computation.27 | convolution fusion | flops 17200840704 | bytes 25165824 | tf_op jit(solution)/shard_map/dot_general | solution.py:27
  632.8 20.1 %convolution_convert_fusion.2 = bf16[2048,2048]{1,0:T(8,128)(2,1)S(1)} fusion(bf16[2048,2048]{1,0:T(8,128)(2,1)} %get-tuple-element.195.refs_2_, bf16[2048,1024]{1,0:T(8,128)(2,1)S(1)} %bitcast.316, bf16[2048,1024]{1,0:T(8,128)(2,1)S(1)} %bitcast.314), kind=kOutput, calls=%fused_computation.28 | convolution fusion | flops 17200840704 | bytes 25165824 | tf_op jit(solution)/shard_map/dot_general | solution.py:27
  658.2 6.6 pad_maximum_fusion.1.refs_1_
  664.8 14.9 %grad_blocks.9 = bf16[4,256,2048]{2,1,0:T(8,128)(2,1)} custom-call(s32[4]{0:T(128)} %pad_add_fusion.1.refs_0_, bf16[2048,2048]{1,0:T(8,128)(2,1)} %pad_maximum_fusion.1.refs_1_, bf16[2048,2048]{1,0:T(8,128)(2,1)} %copy-done.76), custom_call_target="tpu_custom_call" | custom-call | flops 8589934592 | bytes 16777216 | tf_op jit(solution)/shard_map/grad_blocks/pallas_call | solution.py:285
  679.7 4.9 fusion.57
  686.2 14.9 %grad_blocks.8 = bf16[4,256,2048]{2,1,0:T(8,128)(2,1)} custom-call(s32[4]{0:T(128)} %pad_add_fusion.refs_0_, bf16[2048,2048]{1,0:T(8,128)(2,1)} %pad_maximum_fusion.1.refs_1_, bf16[2048,2048]{1,0:T(8,128)(2,1)} %copy-done.76), custom_call_target="tpu_custom_call" | custom-call | flops 8589934592 | bytes 16777216 | tf_op jit(solution)/shard_map/grad_blocks/pallas_call | solution.py:285
  701.1 15.1 %grad_blocks.11 = bf16[4,256,2048]{2,1,0:T(8,128)(2,1)} custom-call(s32[4]{0:T(128)} %pad_add_fusion.3.refs_0_, bf16[2048,2048]{1,0:T(8,128)(2,1)} %constant_dynamic-update-slice_fusion.15.refs_1_, bf16[2048,2048]{1,0:T(8,128)(2,1)} %get-tuple-element.195.refs_2_), custom_call_target="tpu_custom_call" | custom-call | flops 8589934592 | bytes 16777216 | tf_op jit(solution)/shard_map/grad_blocks/pallas_call | solution.py:285
  728.5 15.4 %grad_blocks.10 = bf16[4,256,2048]{2,1,0:T(8,128)(2,1)} custom-call(s32[4]{0:T(128)} %pad_add_fusion.2.refs_0_, bf16[2048,2048]{1,0:T(8,128)(2,1)} %constant_dynamic-update-slice_fusion.15.refs_1_, bf16[2048,2048]{1,0:T(8,128)(2,1)} %get-tuple-element.195.refs_2_), custom_call_target="tpu_custom_call" | custom-call | flops 8589934592 | bytes 16777216 | tf_op jit(solution)/shard_map/grad_blocks/pallas_call | solution.py:285
  744.4 24.5 %collective-permute-done.43 = bf16[512,2048]{1,0:T(8,128)(2,1)S(1)} collective-permute-done((bf16[512,2048]{1,0:T(8,128)(2,1)}, bf16[512,2048]{1,0:T(8,128)(2,1)S(1)}, u32[]{:S(2)}, u32[]{:S(2)}) %collective-permute-start.43) | collective-permute-done | bytes 2097184 | tf_op jit(solution)/shard_map/ppermute | solution.py:306
  773.9 38.9 %collective-permute-done.37 = bf16[512,2048]{1,0:T(8,128)(2,1)} collective-permute-done((bf16[512,2048]{1,0:T(8,128)(2,1)}, bf16[512,2048]{1,0:T(8,128)(2,1)}, u32[]{:S(2)}, u32[]{:S(2)}) %collective-permute-start.37) | collective-permute-done | bytes 2097184 | tf_op jit(solution)/shard_map/ppermute | solution.py:306
  812.8 8.1 convert_reduce_fusion.5
  832.8 16.2 %collective-permute-done.44 = bf16[512,512]{1,0:T(8,128)(2,1)S(1)} collective-permute-done((bf16[512,512]{1,0:T(8,128)(2,1)S(1)}, bf16[512,512]{1,0:T(8,128)(2,1)S(1)}, u32[]{:S(2)}, u32[]{:S(2)}) %collective-permute-start.44) | collective-permute-done | bytes 524320 | tf_op jit(solution)/shard_map/ppermute | solution.py:306
  849.6 15.3 %collective-permute-done.45 = bf16[512,512]{1,0:T(8,128)(2,1)S(1)} collective-permute-done((bf16[512,512]{1,0:T(8,128)(2,1)S(1)}, bf16[512,512]{1,0:T(8,128)(2,1)S(1)}, u32[]{:S(2)}, u32[]{:S(2)}) %collective-permute-start.45) | collective-permute-done | bytes 524320 | tf_op jit(solution)/shard_map/ppermute | solution.py:306
  866.8 43.3 %attend_back.1.refs_2_ = bf16[2048,1536]{1,0:T(8,128)(2,1)} custom-call(s32[1,2048]{1,0:T(1,128)} %compare_select_fusion.start_ref, bf16[2048,1536]{1,0:T(8,128)(2,1)} %add_convert_fusion.qkv_ref, bf16[2048,512]{1,0:T(8,128)(2,1)} %copy-done.38), custom_call_target="tpu_custom_call" | custom-call | flops 21474836480 | bytes 14680064 | tf_op jit(solution)/shard_map/attend_back/pallas_call | solution.py:144
  915.2 19.7 %convolution_convert_fusion = bf16[2048,2048]{1,0:T(8,128)(2,1)} fusion(bf16[2048,1536]{1,0:T(8,128)(2,1)} %attend_back.1.refs_2_, bf16[2048,1536]{1,0:T(8,128)(2,1)} %bitcast_select_fusion), kind=kOutput, calls=%fused_computation.26 | convolution fusion | flops 12889096192 | bytes 20971520 | tf_op jit(solution)/shard_map/dot_general | solution.py:27
  939.9 10.9 grad_blocks.7
  950.8 4.9 slice_bitcast_fusion
  969.0 10.3 collective-permute-start.67
  996.8 12.7 collective-permute-start.72
  1009.5 19.5 %grad_blocks.6 = bf16[8,256,1536]{2,1,0:T(8,128)(2,1)} custom-call(s32[8]{0:T(128)} %get-tuple-element.101.refs_0_, bf16[2048,2048]{1,0:T(8,128)(2,1)} %all-gather.2.cloned.1.call-done.refs_1_, bf16[2048,1536]{1,0:T(8,128)(2,1)} %attend_back.1.refs_2_), custom_call_target="tpu_custom_call" | custom-call | flops 12884901888 | bytes 20971520 | tf_op jit(solution)/shard_map/grad_blocks/pallas_call | solution.py:285
  1029.0 5.1 fusion.55
  1041.6 35.1 %all-reduce.2.cloned.1.call-done = f32[20608]{0:T(1024)} async-done(((f32[20608]{0:T(1024)}), f32[20608]{0:T(1024)}) %all-reduce.2.cloned.1.call-update) | async-done | bytes 82448 | tf_op jit(solution)/shard_map/psum | solution.py:576
  1090.7 16.6 %update_tiles.4 = (f32[96,128,128]{2,1,0:T(8,128)}, f32[96,128,128]{2,1,0:T(8,128)}, f32[96,128,128]{2,1,0:T(8,128)}, bf16[96,128,128]{2,1,0:T(8,128)(2,1)}, f32...) custom-call(f32[32]{0:T(128)} %get-tuple-element.183.refs_0_, ...), custom_call_target="tpu_custom_call" | custom-call | flops 10737418240 | bytes 29360128 | tf_op jit(solution)/shard_map/update_tiles/pallas_call | solution.py:247
  1107.4 5.8 fusion.6
  1122.2 6.6 collective-permute-done.56
  1132.4 4.9 collective-permute-done.49
  1139.2 9.3 collective-permute-done.55
  1153.2 16.0 %update_tiles.5 = (f32[96,128,128]{2,1,0:T(8,128)}, f32[96,128,128]{2,1,0:T(8,128)}, f32[96,128,128]{2,1,0:T(8,128)}, bf16[96,128,128]{2,1,0:T(8,128)(2,1)}, f32...) custom-call(f32[32]{0:T(128)} %get-tuple-element.184.refs_0_, ...), custom_call_target="tpu_custom_call", output_to_operand_aliasing={{0}: (10, {}), {1}: (11, {}), {2}: (12, {}), {3}: (13, {}),... | custom-call | flops 10737418240 | bytes 29360128 | tf_op jit(solution)/shard_map/update_tiles/pallas_call | solution.py:247
  1185.8 14.8 %collective-permute-done.58 = bf16[256,512]{1,0:T(8,128)(2,1)} collective-permute-done((bf16[256,512]{1,0:T(8,128)(2,1)}, bf16[256,512]{1,0:T(8,128)(2,1)}, u32[]{:S(2)}, u32[]{:S(2)}) %collective-permute-start.58) | collective-permute-done | bytes 262176 | tf_op jit(solution)/shard_map/ppermute | solution.py:306
  1202.7 34.4 %collective-permute-done.62 = bf16[256,512]{1,0:T(8,128)(2,1)} collective-permute-done((bf16[256,512]{1,0:T(8,128)(2,1)}, bf16[256,512]{1,0:T(8,128)(2,1)}, u32[]{:S(2)}, u32[]{:S(2)}) %collective-permute-start.62) | collective-permute-done | bytes 262176 | tf_op jit(solution)/shard_map/ppermute | solution.py:306
  1239.7 6.3 update_tiles.6
  1246.0 12.9 update_tiles.7
  1262.5 37.2 %psum.15 = f32[4096]{0:T(1024)S(1)} all-reduce(f32[4096]{0:T(1024)S(1)} %pad_maximum_fusion.21), channel_id=1, replica_groups=mesh['dp'=8,'tensor'=4] {'dp','tensor'}, use_global_device_ids=true, to_apply=%region_22.24 | all-reduce | flops 4096 | bytes 32768 | tf_op jit(solution)/shard_map/psum | solution.py:591
  (496 shorter events, 324.7 us)
Async XLA Ops:
  7.2 226.4 %all-gather.2.cloned.1.call-start = ((), (), s32[]{:S(2)}) async-start(), calls=%async_computation.1 | async-start | bytes 10485760 | tf_op jit(solution)/shard_map/all_gather | solution.py:419
  15.2 1061.5 %all-reduce.2.cloned.1.call-start = ((), (), s32[]{:S(2)}) async-start(), calls=%async_computation.3 | async-start | bytes 172032 | tf_op jit(solution)/shard_map/psum | solution.py:576
  27.1 141.8 %collective-permute-start.19 = (bf16[256,1024]{1,0:T(8,128)(2,1)}, bf16[256,1024]{1,0:T(8,128)(2,1)}, u32[]{:S(2)}, u32[]{:S(2)}) collective-permute-start(bf16[256,1024]{1,0:T(8,128)(2,1)} %constant_dynamic-slice_fusion.1), channel_id=1, source_target_pairs={{0,4},{4,0},{8,12},{12,8},{16,20},{20,16},{24,28},{28,24},{1,5},{5... | collective-permute-start | bytes 1572872 | tf_op jit(solution)/shard_map/ppermute | solution.py:306
  48.5 51.3 %collective-permute-start.10 = (bf16[2,256,256]{2,1,0:T(8,128)(2,1)S(1)}, bf16[2,256,256]{2,1,0:T(8,128)(2,1)S(1)}, u32[]{:S(2)}, u32[]{:S(2)}) collective-permute-start(bf16[2,256,256]{2,1,0:T(8,128)(2,1)S(1)} %get-tuple-element.168), channel_id=1, source_target_pairs={{0,2},{1,3},{2,0},{3,1},{4,6},{5,7},{6,4},{7,5},{8,10},{9,11},{10,... | collective-permute-start | bytes 786440 | tf_op jit(solution)/shard_map/ppermute | solution.py:306
  48.5 51.3 %collective-permute-start.9 = (bf16[2,256,256]{2,1,0:T(8,128)(2,1)S(1)}, bf16[2,256,256]{2,1,0:T(8,128)(2,1)S(1)}, u32[]{:S(2)}, u32[]{:S(2)}) collective-permute-start(bf16[2,256,256]{2,1,0:T(8,128)(2,1)S(1)} %get-tuple-element.168), channel_id=1, source_target_pairs={{0,1},{1,0},{2,3},{3,2},{4,5},{5,4},{6,7},{7,6},{8,9},{9,8},{10,11... | collective-permute-start | bytes 786440 | tf_op jit(solution)/shard_map/ppermute | solution.py:306
  52.9 51.3 %collective-permute-start.1 = (bf16[2,256,768]{1,2,0:T(8,128)(2,1)}, bf16[2,256,768]{1,2,0:T(8,128)(2,1)}, u32[]{:S(2)}, u32[]{:S(2)}) collective-permute-start(bf16[2,256,768]{1,2,0:T(8,128)(2,1)} %pad_maximum_fusion.16), channel_id=1, source_target_pairs={{0,8},{4,12},{8,0},{12,4},{16,24},{20,28},{24,16},{28,20},{1,9},{5... | collective-permute-start | bytes 2359304 | tf_op jit(solution)/shard_map/ppermute | solution.py:306
  100.9 26.4 %collective-permute-start.13 = (bf16[2,4,256,256]{3,2,0,1:T(8,128)(2,1)}, bf16[2,4,256,256]{3,2,0,1:T(8,128)(2,1)}, u32[]{:S(2)}, u32[]{:S(2)}) collective-permute-start(bf16[2,4,256,256]{3,2,0,1:T(8,128)(2,1)} %pad_maximum_fusion.13), channel_id=1, source_target_pairs={{0,16},{4,20},{8,24},{12,28},{16,0},{20,4},{24,8},{28,12},{1,17},{... | collective-permute-start | bytes 3145736 | tf_op jit(solution)/shard_map/ppermute | solution.py:306
  103.8 40.4 %collective-permute-start.2 = (bf16[2,256,768]{1,2,0:T(8,128)(2,1)}, bf16[2,256,768]{1,2,0:T(8,128)(2,1)}, u32[]{:S(2)}, u32[]{:S(2)}) collective-permute-start(bf16[2,256,768]{1,2,0:T(8,128)(2,1)} %pad_maximum_fusion.16), channel_id=1, source_target_pairs={{0,16},{4,20},{8,24},{12,28},{16,0},{20,4},{24,8},{28,12},{1,17},{... | collective-permute-start | bytes 2359304 | tf_op jit(solution)/shard_map/ppermute | solution.py:306
  104.2 50.3 %collective-permute-start.3 = (bf16[2,256,768]{1,2,0:T(8,128)(2,1)}, bf16[2,256,768]{1,2,0:T(8,128)(2,1)}, u32[]{:S(2)}, u32[]{:S(2)}) collective-permute-start(bf16[2,256,768]{1,2,0:T(8,128)(2,1)} %collective-permute-done.1), channel_id=1, source_target_pairs={{0,16},{4,20},{8,24},{12,28},{16,0},{20,4},{24,8},{28,12},{1,17},{... | collective-permute-start | bytes 2359304 | tf_op jit(solution)/shard_map/ppermute | solution.py:306
  113.6 45.5 %collective-permute-start.12 = (bf16[2,4,256,256]{3,2,0,1:T(8,128)(2,1)}, bf16[2,4,256,256]{3,2,0,1:T(8,128)(2,1)S(1)}, u32[]{:S(2)}, u32[]{:S(2)}) collective-permute-start(bf16[2,4,256,256]{3,2,0,1:T(8,128)(2,1)} %pad_maximum_fusion.13), channel_id=1, source_target_pairs={{0,8},{4,12},{8,0},{12,4},{16,24},{20,28},{24,16},{28,20},{1,9},{5... | collective-permute-start | bytes 3145736 | tf_op jit(solution)/shard_map/ppermute | solution.py:306
  127.4 31.8 %collective-permute-start.14 = (bf16[2,4,256,256]{3,2,0,1:T(8,128)(2,1)}, bf16[2,4,256,256]{3,2,0,1:T(8,128)(2,1)S(1)}, u32[]{:S(2)}, u32[]{:S(2)}) collective-permute-start(bf16[2,4,256,256]{3,2,0,1:T(8,128)(2,1)} %collective-permute-done.13), channel_id=1, source_target_pairs={{0,8},{4,12},{8,0},{12,4},{16,24},{20,28},{24,16},{28,20},{1,9},{5... | collective-permute-start | bytes 3145736 | tf_op jit(solution)/shard_map/ppermute | solution.py:306
  144.2 29.7 %collective-permute-start.27 = (bf16[256,1024]{1,0:T(8,128)(2,1)S(1)}, bf16[256,1024]{1,0:T(8,128)(2,1)S(1)}, u32[]{:S(2)}, u32[]{:S(2)}) collective-permute-start(bf16[256,1024]{1,0:T(8,128)(2,1)S(1)} %constant_dynamic-slice_fusion), channel_id=1, source_target_pairs={{0,4},{4,0},{8,12},{12,8},{16,20},{20,16},{24,28},{28,24},{1,5},{5... | collective-permute-start | bytes 1572872 | tf_op jit(solution)/shard_map/ppermute | solution.py:306
  164.2 43.1 %collective-permute-start.15 = (bf16[8,4,256,256]{3,2,0,1:T(8,128)(2,1)}, bf16[8,4,256,256]{3,2,0,1:T(8,128)(2,1)}, u32[]{:S(2)}, u32[]{:S(2)}) collective-permute-start(bf16[8,4,256,256]{3,2,0,1:T(8,128)(2,1)} %pad_maximum_fusion.9), channel_id=1, source_target_pairs={{0,4},{4,0},{8,12},{12,8},{16,20},{20,16},{24,28},{28,24},{1,5},{5... | collective-permute-start | bytes 12582920 | tf_op jit(solution)/shard_map/ppermute | solution.py:306
  171.0 146.6 %collective-permute-start.20 = (bf16[2,256,1024]{2,1,0:T(8,128)(2,1)}, bf16[2,256,1024]{2,1,0:T(8,128)(2,1)}, u32[]{:S(2)}, u32[]{:S(2)}) collective-permute-start(bf16[2,256,1024]{2,1,0:T(8,128)(2,1)} %pad_maximum_fusion.14), channel_id=1, source_target_pairs={{0,8},{4,12},{8,0},{12,4},{16,24},{20,28},{24,16},{28,20},{1,9},{5... | collective-permute-start | bytes 3145736 | tf_op jit(solution)/shard_map/ppermute | solution.py:306
  172.4 145.1 %collective-permute-start.21 = (bf16[2,256,1024]{2,1,0:T(8,128)(2,1)}, bf16[2,256,1024]{2,1,0:T(8,128)(2,1)}, u32[]{:S(2)}, u32[]{:S(2)}) collective-permute-start(bf16[2,256,1024]{2,1,0:T(8,128)(2,1)} %pad_maximum_fusion.14), channel_id=1, source_target_pairs={{0,16},{4,20},{8,24},{12,28},{16,0},{20,4},{24,8},{28,12},{1,17},{... | collective-permute-start | bytes 3145736 | tf_op jit(solution)/shard_map/ppermute | solution.py:306
  276.0 43.2 %collective-permute-start.7 = (bf16[512,512]{1,0:T(8,128)(2,1)}, bf16[512,512]{1,0:T(8,128)(2,1)S(1)}, u32[]{:S(2)}, u32[]{:S(2)}) collective-permute-start(bf16[512,512]{1,0:T(8,128)(2,1)} %get-tuple-element.158), channel_id=1, source_target_pairs={{0,3},{1,2},{2,1},{3,0},{4,7},{5,6},{6,5},{7,4},{8,11},{9,10},{10,... | collective-permute-start | bytes 1572872 | tf_op jit(solution)/shard_map/ppermute | solution.py:306
  283.8 45.5 %collective-permute-start.6 = (bf16[512,512]{1,0:T(8,128)(2,1)}, bf16[512,512]{1,0:T(8,128)(2,1)}, u32[]{:S(2)}, u32[]{:S(2)}) collective-permute-start(bf16[512,512]{1,0:T(8,128)(2,1)} %get-tuple-element.159), channel_id=1, source_target_pairs={{0,2},{1,3},{2,0},{3,1},{4,6},{5,7},{6,4},{7,5},{8,10},{9,11},{10,... | collective-permute-start | bytes 1572872 | tf_op jit(solution)/shard_map/ppermute | solution.py:306
  283.8 46.0 %collective-permute-start.5 = (bf16[512,512]{1,0:T(8,128)(2,1)}, bf16[512,512]{1,0:T(8,128)(2,1)}, u32[]{:S(2)}, u32[]{:S(2)}) collective-permute-start(bf16[512,512]{1,0:T(8,128)(2,1)} %get-tuple-element.160), channel_id=1, source_target_pairs={{0,1},{1,0},{2,3},{3,2},{4,5},{5,4},{6,7},{7,6},{8,9},{9,8},{10,11... | collective-permute-start | bytes 1572872 | tf_op jit(solution)/shard_map/ppermute | solution.py:306
  317.6 119.3 %collective-permute-start.38 = (bf16[512,2048]{1,0:T(8,128)(2,1)S(1)}, bf16[512,2048]{1,0:T(8,128)(2,1)S(1)}, u32[]{:S(2)}, u32[]{:S(2)}) collective-permute-start(bf16[512,2048]{1,0:T(8,128)(2,1)S(1)} %copy-done.10), channel_id=1, source_target_pairs={{0,4},{4,0},{8,12},{12,8},{16,20},{20,16},{24,28},{28,24},{1,5},{5... | collective-permute-start | bytes 6291464 | tf_op jit(solution)/shard_map/ppermute | solution.py:306
  317.6 119.8 %collective-permute-start.39 = (bf16[512,2048]{1,0:T(8,128)(2,1)S(1)}, bf16[512,2048]{1,0:T(8,128)(2,1)S(1)}, u32[]{:S(2)}, u32[]{:S(2)}) collective-permute-start(bf16[512,2048]{1,0:T(8,128)(2,1)S(1)} %copy-done.10), channel_id=1, source_target_pairs={{0,1},{1,0},{2,3},{3,2},{4,5},{5,4},{6,7},{7,6},{8,9},{9,8},{10,11... | collective-permute-start | bytes 6291464 | tf_op jit(solution)/shard_map/ppermute | solution.py:306
  319.1 68.1 %collective-permute-start.23 = (bf16[2,256,1024]{2,1,0:T(8,128)(2,1)}, bf16[2,256,1024]{2,1,0:T(8,128)(2,1)}, u32[]{:S(2)}, u32[]{:S(2)}) collective-permute-start(bf16[2,256,1024]{2,1,0:T(8,128)(2,1)} %pad_maximum_fusion.14), channel_id=1, source_target_pairs={{0,2},{1,3},{2,0},{3,1},{4,6},{5,7},{6,4},{7,5},{8,10},{9,11},{10,... | collective-permute-start | bytes 3145736 | tf_op jit(solution)/shard_map/ppermute | solution.py:306
  329.3 61.9 %collective-permute-start.28 = (bf16[2,256,1024]{2,1,0:T(8,128)(2,1)}, bf16[2,256,1024]{2,1,0:T(8,128)(2,1)S(1)}, u32[]{:S(2)}, u32[]{:S(2)}) collective-permute-start(bf16[2,256,1024]{2,1,0:T(8,128)(2,1)} %pad_maximum_fusion.15), channel_id=1, source_target_pairs={{0,8},{4,12},{8,0},{12,4},{16,24},{20,28},{24,16},{28,20},{1,9},{5... | collective-permute-start | bytes 3145736 | tf_op jit(solution)/shard_map/ppermute | solution.py:306
  329.8 61.9 %collective-permute-start.29 = (bf16[2,256,1024]{2,1,0:T(8,128)(2,1)}, bf16[2,256,1024]{2,1,0:T(8,128)(2,1)S(1)}, u32[]{:S(2)}, u32[]{:S(2)}) collective-permute-start(bf16[2,256,1024]{2,1,0:T(8,128)(2,1)} %pad_maximum_fusion.15), channel_id=1, source_target_pairs={{0,16},{4,20},{8,24},{12,28},{16,0},{20,4},{24,8},{28,12},{1,17},{... | collective-permute-start | bytes 3145736 | tf_op jit(solution)/shard_map/ppermute | solution.py:306
  387.2 49.2 %collective-permute-start.31 = (bf16[2,256,1024]{2,1,0:T(8,128)(2,1)}, bf16[2,256,1024]{2,1,0:T(8,128)(2,1)}, u32[]{:S(2)}, u32[]{:S(2)}) collective-permute-start(bf16[2,256,1024]{2,1,0:T(8,128)(2,1)} %pad_maximum_fusion.15), channel_id=1, source_target_pairs={{0,2},{1,3},{2,0},{3,1},{4,6},{5,7},{6,4},{7,5},{8,10},{9,11},{10,... | collective-permute-start | bytes 3145736 | tf_op jit(solution)/shard_map/ppermute | solution.py:306
  391.2 52.6 %collective-permute-start.22 = (bf16[2,256,1024]{2,1,0:T(8,128)(2,1)}, bf16[2,256,1024]{2,1,0:T(8,128)(2,1)S(1)}, u32[]{:S(2)}, u32[]{:S(2)}) collective-permute-start(bf16[2,256,1024]{2,1,0:T(8,128)(2,1)} %collective-permute-done.20), channel_id=1, source_target_pairs={{0,16},{4,20},{8,24},{12,28},{16,0},{20,4},{24,8},{28,12},{1,17},{... | collective-permute-start | bytes 3145736 | tf_op jit(solution)/shard_map/ppermute | solution.py:306
  391.7 53.6 %collective-permute-start.24 = (bf16[2,256,1024]{2,1,0:T(8,128)(2,1)}, bf16[2,256,1024]{2,1,0:T(8,128)(2,1)}, u32[]{:S(2)}, u32[]{:S(2)}) collective-permute-start(bf16[2,256,1024]{2,1,0:T(8,128)(2,1)} %collective-permute-done.23), channel_id=1, source_target_pairs={{0,8},{4,12},{8,0},{12,4},{16,24},{20,28},{24,16},{28,20},{1,9},{5... | collective-permute-start | bytes 3145736 | tf_op jit(solution)/shard_map/ppermute | solution.py:306
  436.4 24.2 %collective-permute-start.30 = (bf16[2,256,1024]{2,1,0:T(8,128)(2,1)S(1)}, bf16[2,256,1024]{2,1,0:T(8,128)(2,1)S(1)}, u32[]{:S(2)}, u32[]{:S(2)}) collective-permute-start(bf16[2,256,1024]{2,1,0:T(8,128)(2,1)S(1)} %collective-permute-done.29), channel_id=1, source_target_pairs={{0,8},{4,12},{8,0},{12,4},{16,24},{20,28},{24,16},{28,20},{1,9},{5... | collective-permute-start | bytes 3145736 | tf_op jit(solution)/shard_map/ppermute | solution.py:306
  436.9 26.4 %collective-permute-start.33 = (bf16[2,256,1024]{2,1,0:T(8,128)(2,1)}, bf16[2,256,1024]{2,1,0:T(8,128)(2,1)}, u32[]{:S(2)}, u32[]{:S(2)}) collective-permute-start(bf16[2,256,1024]{2,1,0:T(8,128)(2,1)} %collective-permute-done.31), channel_id=1, source_target_pairs={{0,16},{4,20},{8,24},{12,28},{16,0},{20,4},{24,8},{28,12},{1,17},{... | collective-permute-start | bytes 3145736 | tf_op jit(solution)/shard_map/ppermute | solution.py:306
  437.4 72.5 %collective-permute-start.17 = (bf16[512,2048]{1,0:T(8,128)(2,1)S(1)}, bf16[512,2048]{1,0:T(8,128)(2,1)}, u32[]{:S(2)}, u32[]{:S(2)}) collective-permute-start(bf16[512,2048]{1,0:T(8,128)(2,1)S(1)} %add_convert_fusion.12), channel_id=1, source_target_pairs={{0,1},{1,0},{2,3},{3,2},{4,5},{5,4},{6,7},{7,6},{8,9},{9,8},{10,11... | collective-permute-start | bytes 6291464 | tf_op jit(solution)/shard_map/ppermute | solution.py:306
  443.8 42.0 %collective-permute-start.25 = (bf16[2,256,1024]{2,1,0:T(8,128)(2,1)}, bf16[2,256,1024]{2,1,0:T(8,128)(2,1)}, u32[]{:S(2)}, u32[]{:S(2)}) collective-permute-start(bf16[2,256,1024]{2,1,0:T(8,128)(2,1)} %collective-permute-done.23), channel_id=1, source_target_pairs={{0,16},{4,20},{8,24},{12,28},{16,0},{20,4},{24,8},{28,12},{1,17},{... | collective-permute-start | bytes 3145736 | tf_op jit(solution)/shard_map/ppermute | solution.py:306
  445.3 60.7 %collective-permute-start.26 = (bf16[2,256,1024]{2,1,0:T(8,128)(2,1)}, bf16[2,256,1024]{2,1,0:T(8,128)(2,1)}, u32[]{:S(2)}, u32[]{:S(2)}) collective-permute-start(bf16[2,256,1024]{2,1,0:T(8,128)(2,1)} %collective-permute-done.24), channel_id=1, source_target_pairs={{0,16},{4,20},{8,24},{12,28},{16,0},{20,4},{24,8},{28,12},{1,17},{... | collective-permute-start | bytes 3145736 | tf_op jit(solution)/shard_map/ppermute | solution.py:306
  460.6 49.8 %collective-permute-start.32 = (bf16[2,256,1024]{2,1,0:T(8,128)(2,1)}, bf16[2,256,1024]{2,1,0:T(8,128)(2,1)}, u32[]{:S(2)}, u32[]{:S(2)}) collective-permute-start(bf16[2,256,1024]{2,1,0:T(8,128)(2,1)} %collective-permute-done.31), channel_id=1, source_target_pairs={{0,8},{4,12},{8,0},{12,4},{16,24},{20,28},{24,16},{28,20},{1,9},{5... | collective-permute-start | bytes 3145736 | tf_op jit(solution)/shard_map/ppermute | solution.py:306
  463.3 47.1 %collective-permute-start.34 = (bf16[2,256,1024]{2,1,0:T(8,128)(2,1)}, bf16[2,256,1024]{2,1,0:T(8,128)(2,1)}, u32[]{:S(2)}, u32[]{:S(2)}) collective-permute-start(bf16[2,256,1024]{2,1,0:T(8,128)(2,1)} %collective-permute-done.33), channel_id=1, source_target_pairs={{0,8},{4,12},{8,0},{12,4},{16,24},{20,28},{24,16},{28,20},{1,9},{5... | collective-permute-start | bytes 3145736 | tf_op jit(solution)/shard_map/ppermute | solution.py:306
  485.8 50.7 %collective-permute-start.40 = (bf16[512,2048]{1,0:T(8,128)(2,1)}, bf16[512,2048]{1,0:T(8,128)(2,1)}, u32[]{:S(2)}, u32[]{:S(2)}) collective-permute-start(bf16[512,2048]{1,0:T(8,128)(2,1)} %copy-done.39), channel_id=1, source_target_pairs={{0,4},{4,0},{8,12},{12,8},{16,20},{20,16},{24,28},{28,24},{1,5},{5... | collective-permute-start | bytes 6291464 | tf_op jit(solution)/shard_map/ppermute | solution.py:306
  509.8 33.7 %collective-permute-start.16 = (bf16[512,2048]{1,0:T(8,128)(2,1)S(1)}, bf16[512,2048]{1,0:T(8,128)(2,1)}, u32[]{:S(2)}, u32[]{:S(2)}) collective-permute-start(bf16[512,2048]{1,0:T(8,128)(2,1)S(1)} %add_convert_fusion.12), channel_id=1, source_target_pairs={{0,4},{4,0},{8,12},{12,8},{16,20},{20,16},{24,28},{28,24},{1,5},{5... | collective-permute-start | bytes 6291464 | tf_op jit(solution)/shard_map/ppermute | solution.py:306
  509.9 33.7 %collective-permute-start.18 = (bf16[512,2048]{1,0:T(8,128)(2,1)}, bf16[512,2048]{1,0:T(8,128)(2,1)}, u32[]{:S(2)}, u32[]{:S(2)}) collective-permute-start(bf16[512,2048]{1,0:T(8,128)(2,1)} %collective-permute-done.17), channel_id=1, source_target_pairs={{0,4},{4,0},{8,12},{12,8},{16,20},{20,16},{24,28},{28,24},{1,5},{5... | collective-permute-start | bytes 6291464 | tf_op jit(solution)/shard_map/ppermute | solution.py:306
  630.8 85.3 %collective-permute-start.42 = (bf16[512,2048]{1,0:T(8,128)(2,1)S(1)}, bf16[512,2048]{1,0:T(8,128)(2,1)S(1)}, u32[]{:S(2)}, u32[]{:S(2)}) collective-permute-start(bf16[512,2048]{1,0:T(8,128)(2,1)S(1)} %get-tuple-element.120), channel_id=1, source_target_pairs={{0,4},{4,0},{8,12},{12,8},{16,20},{20,16},{24,28},{28,24},{1,5},{5... | collective-permute-start | bytes 6291464 | tf_op jit(solution)/shard_map/ppermute | solution.py:306
  630.9 113.0 %collective-permute-start.41 = (bf16[512,2048]{1,0:T(8,128)(2,1)}, bf16[512,2048]{1,0:T(8,128)(2,1)}, u32[]{:S(2)}, u32[]{:S(2)}) collective-permute-start(bf16[512,2048]{1,0:T(8,128)(2,1)} %get-tuple-element.119), channel_id=1, source_target_pairs={{0,4},{4,0},{8,12},{12,8},{16,20},{20,16},{24,28},{28,24},{1,5},{5... | collective-permute-start | bytes 6291464 | tf_op jit(solution)/shard_map/ppermute | solution.py:306
  657.7 65.1 %collective-permute-start.36 = (bf16[512,2048]{1,0:T(8,128)(2,1)}, bf16[512,2048]{1,0:T(8,128)(2,1)S(1)}, u32[]{:S(2)}, u32[]{:S(2)}) collective-permute-start(bf16[512,2048]{1,0:T(8,128)(2,1)} %get-tuple-element.122), channel_id=1, source_target_pairs={{0,4},{4,0},{8,12},{12,8},{16,20},{20,16},{24,28},{28,24},{1,5},{5... | collective-permute-start | bytes 6291464 | tf_op jit(solution)/shard_map/ppermute | solution.py:306
  657.8 116.1 %collective-permute-start.35 = (bf16[512,2048]{1,0:T(8,128)(2,1)}, bf16[512,2048]{1,0:T(8,128)(2,1)}, u32[]{:S(2)}, u32[]{:S(2)}) collective-permute-start(bf16[512,2048]{1,0:T(8,128)(2,1)} %get-tuple-element.121), channel_id=1, source_target_pairs={{0,4},{4,0},{8,12},{12,8},{16,20},{20,16},{24,28},{28,24},{1,5},{5... | collective-permute-start | bytes 6291464 | tf_op jit(solution)/shard_map/ppermute | solution.py:306
  684.7 144.9 %collective-permute-start.65 = (bf16[2,256,2048]{2,1,0:T(8,128)(2,1)}, bf16[2,256,2048]{2,1,0:T(8,128)(2,1)}, u32[]{:S(2)}, u32[]{:S(2)}) collective-permute-start(bf16[2,256,2048]{2,1,0:T(8,128)(2,1)} %get-tuple-element.132), channel_id=1, source_target_pairs={{0,8},{4,12},{8,0},{12,4},{16,24},{20,28},{24,16},{28,20},{1,9},{5... | collective-permute-start | bytes 6291464 | tf_op jit(solution)/shard_map/ppermute | solution.py:306
  720.2 48.7 %collective-permute-start.43 = (bf16[512,2048]{1,0:T(8,128)(2,1)}, bf16[512,2048]{1,0:T(8,128)(2,1)S(1)}, u32[]{:S(2)}, u32[]{:S(2)}) collective-permute-start(bf16[512,2048]{1,0:T(8,128)(2,1)} %add_convert_fusion.7), channel_id=1, source_target_pairs={{0,1},{1,0},{2,3},{3,2},{4,5},{5,4},{6,7},{7,6},{8,9},{9,8},{10,11... | collective-permute-start | bytes 6291464 | tf_op jit(solution)/shard_map/ppermute | solution.py:306
  726.6 86.1 %collective-permute-start.37 = (bf16[512,2048]{1,0:T(8,128)(2,1)}, bf16[512,2048]{1,0:T(8,128)(2,1)}, u32[]{:S(2)}, u32[]{:S(2)}) collective-permute-start(bf16[512,2048]{1,0:T(8,128)(2,1)} %add_convert_fusion.10), channel_id=1, source_target_pairs={{0,1},{1,0},{2,3},{3,2},{4,5},{5,4},{6,7},{7,6},{8,9},{9,8},{10,11... | collective-permute-start | bytes 6291464 | tf_op jit(solution)/shard_map/ppermute | solution.py:306
  743.9 211.8 %collective-permute-start.64 = (bf16[2,256,2048]{2,1,0:T(8,128)(2,1)}, bf16[2,256,2048]{2,1,0:T(8,128)(2,1)}, u32[]{:S(2)}, u32[]{:S(2)}) collective-permute-start(bf16[2,256,2048]{2,1,0:T(8,128)(2,1)} %get-tuple-element.131), channel_id=1, source_target_pairs={{0,8},{4,12},{8,0},{12,4},{16,24},{20,28},{24,16},{28,20},{1,9},{5... | collective-permute-start | bytes 6291464 | tf_op jit(solution)/shard_map/ppermute | solution.py:306
  768.9 166.0 %collective-permute-start.70 = (bf16[2,256,2048]{2,1,0:T(8,128)(2,1)}, bf16[2,256,2048]{2,1,0:T(8,128)(2,1)}, u32[]{:S(2)}, u32[]{:S(2)}) collective-permute-start(bf16[2,256,2048]{2,1,0:T(8,128)(2,1)} %get-tuple-element.130), channel_id=1, source_target_pairs={{0,16},{4,20},{8,24},{12,28},{16,0},{20,4},{24,8},{28,12},{1,17},{... | collective-permute-start | bytes 6291464 | tf_op jit(solution)/shard_map/ppermute | solution.py:306
  826.0 23.1 %collective-permute-start.44 = (bf16[512,512]{1,0:T(8,128)(2,1)S(1)}, bf16[512,512]{1,0:T(8,128)(2,1)S(1)}, u32[]{:S(2)}, u32[]{:S(2)}) collective-permute-start(bf16[512,512]{1,0:T(8,128)(2,1)S(1)} %get-tuple-element.155), channel_id=1, source_target_pairs={{0,1},{1,0},{2,3},{3,2},{4,5},{5,4},{6,7},{7,6},{8,9},{9,8},{10,11... | collective-permute-start | bytes 1572872 | tf_op jit(solution)/shard_map/ppermute | solution.py:306
  826.4 38.6 %collective-permute-start.45 = (bf16[512,512]{1,0:T(8,128)(2,1)S(1)}, bf16[512,512]{1,0:T(8,128)(2,1)S(1)}, u32[]{:S(2)}, u32[]{:S(2)}) collective-permute-start(bf16[512,512]{1,0:T(8,128)(2,1)S(1)} %get-tuple-element.154), channel_id=1, source_target_pairs={{0,2},{1,3},{2,0},{3,1},{4,6},{5,7},{6,4},{7,5},{8,10},{9,11},{10,... | collective-permute-start | bytes 1572872 | tf_op jit(solution)/shard_map/ppermute | solution.py:306
  829.6 35.8 %collective-permute-start.46 = (bf16[512,512]{1,0:T(8,128)(2,1)S(1)}, bf16[512,512]{1,0:T(8,128)(2,1)S(1)}, u32[]{:S(2)}, u32[]{:S(2)}) collective-permute-start(bf16[512,512]{1,0:T(8,128)(2,1)S(1)} %get-tuple-element.153), channel_id=1, source_target_pairs={{0,3},{1,2},{2,1},{3,0},{4,7},{5,6},{6,5},{7,4},{8,11},{9,10},{10,... | collective-permute-start | bytes 1572872 | tf_op jit(solution)/shard_map/ppermute | solution.py:306
  849.1 130.3 %collective-permute-start.69 = (bf16[2,256,2048]{2,1,0:T(8,128)(2,1)}, bf16[2,256,2048]{2,1,0:T(8,128)(2,1)}, u32[]{:S(2)}, u32[]{:S(2)}) collective-permute-start(bf16[2,256,2048]{2,1,0:T(8,128)(2,1)} %get-tuple-element.129), channel_id=1, source_target_pairs={{0,16},{4,20},{8,24},{12,28},{16,0},{20,4},{24,8},{28,12},{1,17},{... | collective-permute-start | bytes 6291464 | tf_op jit(solution)/shard_map/ppermute | solution.py:306
  864.9 90.8 %collective-permute-start.66 = (bf16[2,256,2048]{2,1,0:T(8,128)(2,1)S(1)}, bf16[2,256,2048]{2,1,0:T(8,128)(2,1)}, u32[]{:S(2)}, u32[]{:S(2)}) collective-permute-start(bf16[2,256,2048]{2,1,0:T(8,128)(2,1)S(1)} %add_convert_fusion.5), channel_id=1, source_target_pairs={{0,16},{4,20},{8,24},{12,28},{16,0},{20,4},{24,8},{28,12},{1,17},{... | collective-permute-start | bytes 6291464 | tf_op jit(solution)/shard_map/ppermute | solution.py:306
  915.1 343.8 %reduce-scatter.2.cloned.1.call-start = ((), (), s32[]{:S(2)}) async-start(), calls=%async_computation.2 | async-start | bytes 10485760 | tf_op jit(solution)/shard_map/reduce_scatter | solution.py:559
  939.4 44.0 %collective-permute-start.71 = (bf16[2,256,2048]{2,1,0:T(8,128)(2,1)}, bf16[2,256,2048]{2,1,0:T(8,128)(2,1)}, u32[]{:S(2)}, u32[]{:S(2)}) collective-permute-start(bf16[2,256,2048]{2,1,0:T(8,128)(2,1)} %add_convert_fusion.2), channel_id=1, source_target_pairs={{0,8},{4,12},{8,0},{12,4},{16,24},{20,28},{24,16},{28,20},{1,9},{5... | collective-permute-start | bytes 6291464 | tf_op jit(solution)/shard_map/ppermute | solution.py:306
  955.7 151.6 %collective-permute-start.54 = (bf16[4,256,2048]{2,1,0:T(8,128)(2,1)}, bf16[4,256,2048]{2,1,0:T(8,128)(2,1)}, u32[]{:S(2)}, u32[]{:S(2)}) collective-permute-start(bf16[4,256,2048]{2,1,0:T(8,128)(2,1)} %slice_bitcast_fusion), channel_id=1, source_target_pairs={{0,4},{4,0},{8,12},{12,8},{16,20},{20,16},{24,28},{28,24},{1,5},{5... | collective-permute-start | bytes 12582920 | tf_op jit(solution)/shard_map/ppermute | solution.py:306
  969.0 109.2 %collective-permute-start.67 = (bf16[2,256,1024]{2,1,0:T(8,128)(2,1)}, bf16[2,256,1024]{2,1,0:T(8,128)(2,1)}, u32[]{:S(2)}, u32[]{:S(2)}) collective-permute-start(bf16[2,256,1024]{2,1,0:T(8,128)(2,1)} %bitcast.258), channel_id=1, source_target_pairs={{0,2},{1,3},{2,0},{3,1},{4,6},{5,7},{6,4},{7,5},{8,10},{9,11},{10,... | collective-permute-start | bytes 3145736 | tf_op jit(solution)/shard_map/ppermute | solution.py:306
  996.8 84.9 %collective-permute-start.72 = (bf16[2,256,1024]{2,1,0:T(8,128)(2,1)}, bf16[2,256,1024]{2,1,0:T(8,128)(2,1)}, u32[]{:S(2)}, u32[]{:S(2)}) collective-permute-start(bf16[2,256,1024]{2,1,0:T(8,128)(2,1)} %bitcast.257), channel_id=1, source_target_pairs={{0,2},{1,3},{2,0},{3,1},{4,6},{5,7},{6,4},{7,5},{8,10},{9,11},{10,... | collective-permute-start | bytes 3145736 | tf_op jit(solution)/shard_map/ppermute | solution.py:306
  1038.7 76.7 %collective-permute-start.47 = (bf16[4,256,1536]{1,2,0:T(8,128)(2,1)}, bf16[4,256,1536]{1,2,0:T(8,128)(2,1)}, u32[]{:S(2)}, u32[]{:S(2)}) collective-permute-start(bf16[4,256,1536]{1,2,0:T(8,128)(2,1)} %bitcast.333), channel_id=1, source_target_pairs={{0,4},{4,0},{8,12},{12,8},{16,20},{20,16},{24,28},{28,24},{1,5},{5... | collective-permute-start | bytes 9437192 | tf_op jit(solution)/shard_map/ppermute | solution.py:306
  1120.4 28.1 %collective-permute-start.55 = (bf16[256,1024]{1,0:T(8,128)(2,1)S(1)}, bf16[256,1024]{1,0:T(8,128)(2,1)S(1)}, u32[]{:S(2)}, u32[]{:S(2)}) collective-permute-start(bf16[256,1024]{1,0:T(8,128)(2,1)S(1)} %get-tuple-element.135), channel_id=1, source_target_pairs={{0,8},{4,12},{8,0},{12,4},{16,24},{20,28},{24,16},{28,20},{1,9},{5... | collective-permute-start | bytes 1572872 | tf_op jit(solution)/shard_map/ppermute | solution.py:306
  1121.3 28.3 %collective-permute-start.60 = (bf16[256,1024]{1,0:T(8,128)(2,1)S(1)}, bf16[256,1024]{1,0:T(8,128)(2,1)S(1)}, u32[]{:S(2)}, u32[]{:S(2)}) collective-permute-start(bf16[256,1024]{1,0:T(8,128)(2,1)S(1)} %get-tuple-element.136), channel_id=1, source_target_pairs={{0,16},{4,20},{8,24},{12,28},{16,0},{20,4},{24,8},{28,12},{1,17},{... | collective-permute-start | bytes 1572872 | tf_op jit(solution)/shard_map/ppermute | solution.py:306
  1131.6 37.5 %collective-permute-start.48 = (bf16[256,768]{0,1:T(8,128)(2,1)}, bf16[256,768]{0,1:T(8,128)(2,1)}, u32[]{:S(2)}, u32[]{:S(2)}) collective-permute-start(bf16[256,768]{0,1:T(8,128)(2,1)} %get-tuple-element.142), channel_id=1, source_target_pairs={{0,8},{4,12},{8,0},{12,4},{16,24},{20,28},{24,16},{28,20},{1,9},{5... | collective-permute-start | bytes 1179656 | tf_op jit(solution)/shard_map/ppermute | solution.py:306
  1137.3 32.5 %collective-permute-start.52 = (bf16[256,768]{0,1:T(8,128)(2,1)}, bf16[256,768]{0,1:T(8,128)(2,1)}, u32[]{:S(2)}, u32[]{:S(2)}) collective-permute-start(bf16[256,768]{0,1:T(8,128)(2,1)} %get-tuple-element.143), channel_id=1, source_target_pairs={{0,16},{4,20},{8,24},{12,28},{16,0},{20,4},{24,8},{28,12},{1,17},{... | collective-permute-start | bytes 1179656 | tf_op jit(solution)/shard_map/ppermute | solution.py:306
  1149.6 27.9 %collective-permute-start.59 = (bf16[256,1024]{1,0:T(8,128)(2,1)}, bf16[256,1024]{1,0:T(8,128)(2,1)}, u32[]{:S(2)}, u32[]{:S(2)}) collective-permute-start(bf16[256,1024]{1,0:T(8,128)(2,1)} %get-tuple-element.137), channel_id=1, source_target_pairs={{0,16},{4,20},{8,24},{12,28},{16,0},{20,4},{24,8},{28,12},{1,17},{... | collective-permute-start | bytes 1572872 | tf_op jit(solution)/shard_map/ppermute | solution.py:306
  1151.8 25.7 %collective-permute-start.61 = (bf16[256,1024]{1,0:T(8,128)(2,1)}, bf16[256,1024]{1,0:T(8,128)(2,1)}, u32[]{:S(2)}, u32[]{:S(2)}) collective-permute-start(bf16[256,1024]{1,0:T(8,128)(2,1)} %get-tuple-element.134), channel_id=1, source_target_pairs={{0,8},{4,12},{8,0},{12,4},{16,24},{20,28},{24,16},{28,20},{1,9},{5... | collective-permute-start | bytes 1572872 | tf_op jit(solution)/shard_map/ppermute | solution.py:306
  1173.4 27.2 %collective-permute-start.58 = (bf16[256,512]{1,0:T(8,128)(2,1)}, bf16[256,512]{1,0:T(8,128)(2,1)}, u32[]{:S(2)}, u32[]{:S(2)}) collective-permute-start(bf16[256,512]{1,0:T(8,128)(2,1)} %slice.484), channel_id=1, source_target_pairs={{0,1},{1,0},{2,3},{3,2},{4,5},{5,4},{6,7},{7,6},{8,9},{9,8},{10,11... | collective-permute-start | bytes 786440 | tf_op jit(solution)/shard_map/ppermute | solution.py:306
  1182.8 54.4 %collective-permute-start.62 = (bf16[256,512]{1,0:T(8,128)(2,1)}, bf16[256,512]{1,0:T(8,128)(2,1)}, u32[]{:S(2)}, u32[]{:S(2)}) collective-permute-start(bf16[256,512]{1,0:T(8,128)(2,1)} %get-tuple-element.165), channel_id=1, source_target_pairs={{0,2},{1,3},{2,0},{3,1},{4,6},{5,7},{6,4},{7,5},{8,10},{9,11},{10,... | collective-permute-start | bytes 786440 | tf_op jit(solution)/shard_map/ppermute | solution.py:306
  (96 other events, 2504.6 us)
Sparse Core Ops, SparseCore 0:
  15.4 174.6 all-gather.1
  915.3 161.4 all-reduce.1
  1079.1 162.9 reduce-scatter.1

commit v2 on v1

--- a/solution.py
+++ b/solution.py
@@ -21,6 +21,10 @@
 SCALE = HD ** (-0.5)
 LOG2E = 1.4426950408889634
 VMEM_CAP = 56 * 1024 * 1024
+
+
+def cost(seconds):
+    return pl.CostEstimate(flops=0, bytes_accessed=int(seconds * 3.5e12), transcendentals=0)
 
 
 def dot_nt(a, b):
@@ -100,9 +104,7 @@
             jax.ShapeDtypeStruct((heads, 8, HD), F32),
         ],
         compiler_params=pltpu.CompilerParams(vmem_limit_bytes=VMEM_CAP),
-        cost_estimate=pl.CostEstimate(
-            flops=heads * SEQ * SEQ * HD * 4, bytes_accessed=heads * SEQ * HD * 8, transcendentals=heads * SEQ * SEQ // 2
-        ),
+        cost_estimate=cost(heads * 5e-6),
         name="attend",
     )(start_rows, qkv)
 
@@ -153,9 +155,7 @@
         out_shape=jax.ShapeDtypeStruct(qkv.shape, BF),
         scratch_shapes=[pltpu.VMEM((SEQ, HD), F32), pltpu.VMEM((SEQ, HD), F32)],
         compiler_params=pltpu.CompilerParams(vmem_limit_bytes=VMEM_CAP),
-        cost_estimate=pl.CostEstimate(
-            flops=heads * SEQ * SEQ * HD * 10, bytes_accessed=heads * SEQ * HD * 14, transcendentals=heads * SEQ * SEQ // 2
-        ),
+        cost_estimate=cost(heads * 10e-6),
         name="attend_back",
     )(start_rows, qkv, back)
 
@@ -254,77 +254,246 @@
         out_shape=[jax.ShapeDtypeStruct((tiles, HD, HD), kind) for kind in kinds],
         input_output_aliases={10 + i: i for i in range(len(earlier))},
         compiler_params=pltpu.CompilerParams(vmem_limit_bytes=VMEM_CAP),
-        cost_estimate=pl.CostEstimate(
-            flops=count * 20 * HD**3 * 2 * 4, bytes_accessed=count * HD * HD * 56, transcendentals=count * HD * HD * 2
-        ),
+        cost_estimate=cost(count * 5e-7),
         name="update_tiles",
     )(rates[first_tile : first_tile + count], factors[first_tile : first_tile + count], grads, *state, *earlier)
 
 
-def grad_kernel(chunks, block_ref, *refs):
-    lefts, rights, out_ref = refs[:chunks], refs[chunks : 2 * chunks], refs[2 * chunks]
-    width = out_ref.shape[2]
-    step = min(512, width)
-    for lo in range(0, width, step):
-        total = None
-        for left, right in zip(lefts, rights):
-            term = dot_tn(left[...], right[:, lo : lo + step])
-            total = term if total is None else total + term
-        out_ref[0, :, lo : lo + step] = total.astype(BF)
-
-
-def grad_blocks(blocks, lefts, rights, edge):
+def grad_kernel(groups, block_ref, left_ref, *refs):
+    rights, out_ref = refs[:groups], refs[groups]
+    turned = left_ref[...].T
+    lo = 0
+    for right in rights:
+        width = right.shape[1]
+        step = min(512, width)
+        for at in range(0, width, step):
+            out_ref[0, :, lo + at : lo + at + step] = dot_nn(turned, right[:, at : at + step]).astype(BF)
+        lo += width
+
+
+def grad_blocks(blocks, left, rights, edge):
     count = blocks.shape[0]
-    width = rights[0].shape[1]
-    rows = sum(left.shape[0] for left in lefts)
-    chunks = len(lefts)
+    rows = rights[0].shape[0]
+    width = sum(right.shape[1] for right in rights)
 
     def body(*refs):
-        grad_kernel(chunks, *refs)
+        grad_kernel(len(rights), *refs)
 
     return pl.pallas_call(
         body,
         grid_spec=pltpu.PrefetchScalarGridSpec(
             num_scalar_prefetch=1,
             grid=(count,),
-            in_specs=[pl.BlockSpec((left.shape[0], edge), lambda i, blocks: (0, blocks[i])) for left in lefts]
+            in_specs=[pl.BlockSpec((rows, edge), lambda i, blocks: (0, blocks[i]))]
             + [pl.BlockSpec(right.shape, lambda i, blocks: (0, 0)) for right in rights],
             out_specs=pl.BlockSpec((1, edge, width), lambda i, blocks: (i, 0, 0)),
         ),
         out_shape=jax.ShapeDtypeStruct((count, edge, width), BF),
         compiler_params=pltpu.CompilerParams(vmem_limit_bytes=VMEM_CAP),
-        cost_estimate=pl.CostEstimate(
-            flops=2 * count * edge * width * rows,
-            bytes_accessed=2 * (count * edge * (width + rows) + rows * width),
-            transcendentals=0,
+        cost_estimate=cost(2 * count * edge * width * rows / 8e14),
+        name="grad_blocks",
+    )(blocks, left, *rights)
+
+
+def matmul_kernel(terms, *refs):
+    lefts, rights, out_ref = refs[:terms], refs[terms : 2 * terms], refs[2 * terms]
+    total = dot_nt(lefts[0][...], rights[0][...])
+    for left, right in zip(lefts[1:], rights[1:]):
+        total = total + dot_nt(left[...], right[...])
+    out_ref[...] = total.astype(BF)
+
+
+def matmul_sum(lefts, rights, first=0, rows=None):
+    terms = len(lefts)
+    depth = lefts[0].shape[1]
+    rows = rows or lefts[0].shape[0]
+    columns = rights[0].shape[0]
+    row_step, step = min(1024, rows), min(512, columns)
+    offset = first // row_step
+
+    def body(*refs):
+        matmul_kernel(terms, *refs)
+
+    return pl.pallas_call(
+        body,
+        grid=(rows // row_step, columns // step),
+        in_specs=[pl.BlockSpec((row_step, depth), lambda m, n: (m + offset, 0))] * terms
+        + [pl.BlockSpec((step, depth), lambda m, n: (n, 0))] * terms,
+        out_specs=pl.BlockSpec((row_step, step), lambda m, n: (m, n)),
+        out_shape=jax.ShapeDtypeStruct((rows, columns), BF),
+        compiler_params=pltpu.CompilerParams(vmem_limit_bytes=VMEM_CAP),
+        cost_estimate=cost(2 * terms * rows * columns * depth / 8e14),
+        name="matmul_sum",
+    )(*lefts, *rights)
+
+
+def pack_kernel(heads, edge_tiles, hidden_tiles, core_ref, tiles_ref, halves_ref, qkv_ref, out_ref):
+    core = core_ref[0]
+    half = hidden_tiles // 2 * HD
+    first = 0
+    for row in range(edge_tiles):
+        for part in range(3):
+            for head in range(heads):
+                tile = tiles_ref[first + (row * 3 + part) * heads + head].astype(BF)
+                at = (head * 3 + part) * HD
+                qkv_ref[row * HD : (row + 1) * HD, at : at + HD] = tile
+    first += edge_tiles * 3 * heads
+    for head in range(heads):
+        for row in range(edge_tiles):
+            tile = tiles_ref[first + head * edge_tiles + row].T.astype(BF)
+            out_ref[row * HD : (row + 1) * HD, head * HD : (head + 1) * HD] = tile
+    first += heads * edge_tiles
+    for kind in range(2):
+        for row in range(edge_tiles):
+            for column in range(hidden_tiles):
+                part, inner = divmod(column, hidden_tiles // 2)
+                at = kind * half + inner * HD
+                if kind == 0:
+                    tile = tiles_ref[first + row * hidden_tiles + column].astype(BF)
+                else:
+                    tile = tiles_ref[first + column * edge_tiles + row].T.astype(BF)
+                halves_ref[part ^ core, row * HD : (row + 1) * HD, at : at + HD] = tile
+        first += edge_tiles * hidden_tiles
+
+
+def pack_weights(tiles, core, heads, edge_tiles, hidden_tiles):
+    edge = edge_tiles * HD
+
+    def body(*refs):
+        pack_kernel(heads, edge_tiles, hidden_tiles, *refs)
+
+    shapes = [(2, edge, hidden_tiles * HD), (edge, 3 * heads * HD), (edge, heads * HD)]
+    return pl.pallas_call(
+        body,
+        grid_spec=pltpu.PrefetchScalarGridSpec(
+            num_scalar_prefetch=1,
+            grid=(1,),
+            in_specs=[pl.BlockSpec(tiles.shape, lambda i, core: (0, 0, 0))],
+            out_specs=[pl.BlockSpec(shapes[0], lambda i, core: (0, 0, 0))]
+            + [pl.BlockSpec(shape, lambda i, core: (0, 0)) for shape in shapes[1:]],
         ),
-        name="grad_blocks",
-    )(blocks, *lefts, *rights)
+        out_shape=[jax.ShapeDtypeStruct(shape, BF) for shape in shapes],
+        compiler_params=pltpu.CompilerParams(vmem_limit_bytes=VMEM_CAP),
+        cost_estimate=cost(5e-6),
+        name="pack_weights",
+    )(core[None], tiles)
+
+
+def scatter_kernel(tables, *refs):
+    source_ref, outs = refs[tables], refs[tables + 1 :]
+    lo = 0
+    for out in outs:
+        width = out.shape[1]
+        out[...] = source_ref[0, :, lo : lo + width]
+        lo += width
+
+
+def scatter_blocks(tables, source):
+    count, edge, columns = source.shape
+    parts = len(tables)
+    width = columns // parts
+
+    def body(*refs):
+        scatter_kernel(parts, *refs)
+
+    def out_spec(k):
+        return pl.BlockSpec((edge, width), lambda i, *tables: (tables[k][i], 0))
+
+    return pl.pallas_call(
+        body,
+        grid_spec=pltpu.PrefetchScalarGridSpec(
+            num_scalar_prefetch=parts,
+            grid=(count,),
+            in_specs=[pl.BlockSpec((1, edge, columns), lambda i, *tables: (i, 0, 0))],
+            out_specs=[out_spec(k) for k in range(parts)],
+        ),
+        out_shape=[jax.ShapeDtypeStruct((count * edge, width), BF)] * parts,
+        compiler_params=pltpu.CompilerParams(vmem_limit_bytes=VMEM_CAP),
+        cost_estimate=cost(4 * count * edge * columns / 3e12),
+        name="scatter_blocks",
+    )(*tables, source)
+
+
+def project_kernel(sources, pick_ref, *refs):
+    pieces = refs[:sources]
+    gain_ref, shift_ref, weight_ref, bias_ref, normal_out, normed_out, out_ref = refs[sources:]
+    picked = pick_ref[pl.program_id(0)]
+    for i in range(sources):
+
+        @pl.when(picked == i)
+        def _():
+            normal_out[...] = pieces[i][...]
+
+    normed = (normal_out[...].astype(F32) * gain_ref[...] + shift_ref[...]).astype(BF)
+    normed_out[...] = normed
+    out_ref[...] = (dot_nn(normed, weight_ref[...]) + bias_ref[...]).astype(BF)
+
+
+def project(pick, pieces, gain, shift_by, weight, bias):
+    count = pick.shape[0]
+    rows, depth = pieces[0].shape
+    columns = weight.shape[1]
+
+    def body(*refs):
+        project_kernel(len(pieces), *refs)
+
+    def held(shape):
+        return pl.BlockSpec(shape, lambda t, pick: (0, 0), pipeline_mode=pl.Buffered(1))
+
+    return pl.pallas_call(
+        body,
+        grid_spec=pltpu.PrefetchScalarGridSpec(
+            num_scalar_prefetch=1,
+            grid=(count,),
+            in_specs=[held((rows, depth)) for _ in pieces]
+            + [held((1, depth)), held((1, depth)), held((depth, columns)), held((1, columns))],
+            out_specs=[
+                pl.BlockSpec((rows, depth), lambda t, pick: (t, 0)),
+                pl.BlockSpec((rows, depth), lambda t, pick: (t, 0)),
+                pl.BlockSpec((rows, columns), lambda t, pick: (t, 0)),
+            ],
+        ),
+        out_shape=[
+            jax.ShapeDtypeStruct((count * rows, depth), BF),
+            jax.ShapeDtypeStruct((count * rows, depth), BF),
+            jax.ShapeDtypeStruct((count * rows, columns), BF),
+        ],
+        compiler_params=pltpu.CompilerParams(vmem_limit_bytes=VMEM_CAP),
+        cost_estimate=cost(2e-5),
+        name="project",
+    )(pick, *pieces, gain[None], shift_by[None], weight, bias[None])
+
+
+def sync(*values):
+    return lax.optimization_barrier(values)
 
 
 def shift(value, axis, mask):
     return lax.ppermute(value, axis, [(i, i ^ mask) for i in range(lax.axis_size(axis))])
 
 
+def move(value, axis, pairs):
+    return lax.ppermute(value, axis, pairs)
+
+
 def add_low(left, right):
     return (left.astype(F32) + right.astype(F32)).astype(BF)
 
 
-def chip_gather(value, masks):
-    pieces = {0: value}
+def join_halves(mine, other):
+    first = (lax.axis_index("dp") & 1) == 0
+    return jnp.concatenate([jnp.where(first, mine, other), jnp.where(first, other, mine)], axis=-1)
+
+
+def halving_order(chips, masks):
+    return sorted(chips, key=lambda q: tuple(-(q & (mask >> 1)) for mask in masks))
+
+
+def halve(blocks, masks):
     for mask in masks:
-        pieces.update({q | (mask >> 1): shift(piece, "dp", mask) for q, piece in pieces.items()})
-    return [pieces[q] for q in range(len(pieces))]
-
-
-def chip_reduce(pieces, masks):
-    pieces = dict(enumerate(pieces))
-    for mask in masks:
-        bit = mask >> 1
-        pieces = {
-            q: add_low(piece, shift(pieces[q | bit], "dp", mask)) for q, piece in pieces.items() if not q & bit
-        }
-    return pieces[0]
+        count = blocks.shape[0] // 2
+        blocks = add_low(blocks[count:], shift(blocks[:count], "dp", mask))
+    return blocks
 
 
 def layer_norm(token_rows, gain, shift_by):
@@ -350,6 +519,12 @@
     cdf = 0.5 * (1.0 + lax.erf(pre_act * (0.5**0.5)))
     density = jnp.exp(-0.5 * pre_act * pre_act) * 0.3989422804014327
     return pre_act * cdf, cdf + pre_act * density
+
+
+def axis_sum(value, axis):
+    for bit in range(lax.axis_size(axis).bit_length() - 1):
+        value = value + shift(value, axis, 1 << bit)
+    return value
 
 
 def small_step(summed, params, first, second):
@@ -380,7 +555,6 @@
     me = lax.axis_index("dp")
     place = lax.axis_index("tensor")
     core = me & 1
-    first_core = core == 0
     rows = inputs.shape[0]
     edge = D // dp_count
     width = D // tp_count
@@ -396,10 +570,9 @@
     near = [1 << bit for bit in range(1, dp_count.bit_length() - 1)]
     far = near[::-1]
     slices = tp_count // 2
-    inverse = jnp.argsort(held_blocks, axis=1).astype(jnp.int32)
+    chips = range(dp_count // 2)
     relative = jnp.arange(dp_count, dtype=jnp.int32) ^ me
     block_of = jnp.take(held_blocks, relative, axis=1)
-    source_of = inverse ^ me
 
     bias_q = lax.dynamic_slice_in_dim(small_params, place * width, width)
     bias_v = lax.dynamic_slice_in_dim(small_params, D + place * width, width)
@@ -415,58 +588,61 @@
     )
 
     token_rows = inputs.astype(F32)
-    normed_one = layer_norm(token_rows, gain_one, shift_one).astype(BF)
-    normed_all = lax.all_gather(normed_one, "tensor", axis=0, tiled=True)
-
-    low = master[0, 0].astype(BF)
+    centred = token_rows - jnp.mean(token_rows, axis=-1, keepdims=True)
+    spread = jnp.mean(centred * centred, axis=-1, keepdims=True)
+    normal = (centred * lax.rsqrt(spread + 1e-05)).astype(BF)
+    ups = [(i, i + 1) for i in range(tp_count - 1)]
+    downs = [(i + 1, i) for i in range(tp_count - 1)]
+    above, below = [move(normal, "tensor", downs)], [move(normal, "tensor", ups)]
+
     bounds = [0, tile_q, tile_q + tile_o, tile_q + tile_o + tile_u, tile_count]
-    own_qkv = low[: bounds[1]].reshape(edge_tiles, 3, heads, HD, HD).transpose(0, 3, 2, 1, 4).reshape(edge, 3 * width)
-    own_out = low[bounds[1] : bounds[2]].reshape(heads, edge_tiles, HD, HD).transpose(1, 3, 0, 2).reshape(edge, width)
-    own_up = low[bounds[2] : bounds[3]].reshape(edge_tiles, hidden_tiles, HD, HD).transpose(0, 2, 1, 3).reshape(edge, hidden)
-    own_down = low[bounds[3] :].reshape(hidden_tiles, edge_tiles, HD, HD).transpose(1, 3, 0, 2).reshape(edge, hidden)
-
-    def split_pair(own):
-        part = own.shape[1] // 2
-        mine = lax.dynamic_slice_in_dim(own, core * part, part, 1)
-        other = lax.dynamic_slice_in_dim(own, (1 - core) * part, part, 1)
-        return jnp.stack([mine, shift(other, "dp", 1)])
-
-    def join_halves(mine, other):
-        return jnp.concatenate([jnp.where(first_core, mine, other), jnp.where(first_core, other, mine)], axis=-1)
-
-    def in_order(pieces, kind):
-        whole = jnp.concatenate(pieces, axis=0)
-        return jnp.take(whole, source_of[kind], axis=0).reshape(D, whole.shape[2])
-
-    pieces_qkv = chip_gather(split_pair(own_qkv), near)
-    mine_qkv = jnp.concatenate(pieces_qkv, axis=0)
-    other_qkv = shift(mine_qkv, "dp", 1).reshape(dp_count // 2, 2, edge, -1)[:, ::-1].reshape(mine_qkv.shape)
-    w_qkv = jnp.take(join_halves(mine_qkv, other_qkv), source_of[0], axis=0).reshape(D, 3 * width)
-
-    pair_up = split_pair(own_up)
-    pair_down = split_pair(own_down)
-    pairs_up = [pair_up] + [shift(pair_up, "tensor", 2 * j) for j in range(1, slices)]
-    pairs_down = [pair_down] + [shift(pair_down, "tensor", 2 * j) for j in range(1, slices)]
-
-    pair_out = split_pair(own_out)
-    pairs_out = jnp.stack([pair_out] + [shift(pair_out, "tensor", j) for j in range(1, tp_count)], axis=1)
-    mine_out = jnp.concatenate(chip_gather(pairs_out, far), axis=0)
-    other_out = shift(mine_out, "dp", 1).reshape((dp_count // 2, 2) + mine_out.shape[1:])[:, ::-1].reshape(mine_out.shape)
-    w_out = jnp.take(join_halves(mine_out, other_out), source_of[1], axis=0)
-    w_out = w_out.transpose(0, 2, 1, 3).reshape(D, D)
-
-    w_up = jnp.concatenate([in_order(chip_gather(pair, near), 2) for pair in pairs_up], axis=1)
-    w_down = jnp.concatenate([in_order(chip_gather(pair, far), 3) for pair in pairs_down], axis=1)
+    halves, own_qkv, own_out = pack_weights(master[0, 0], core, heads, edge_tiles, hidden_tiles)
+    pair = jnp.stack([halves[0], shift(halves[1], "dp", 1)])
+    same_core = [list(range(at, dp_count, 2)) for at in range(2)]
+    pair_slots = jnp.arange(dp_count, dtype=jnp.int32) ^ core
+
+    def gather_ffn(value):
+        value = lax.all_gather(value, "dp", axis=0, tiled=True, axis_index_groups=same_core)
+        return scatter_blocks([held_blocks[2][pair_slots], held_blocks[3][pair_slots]], value)
+
+    def gather_all(kind, value):
+        value = lax.all_gather(value, "dp", axis=0, tiled=False)
+        return scatter_blocks([held_blocks[kind]], value)[0]
+
+    def crossed(mask, odd):
+        return [(i, i ^ mask) for i in range(tp_count) if ((i ^ (i >> 1)) & 1) == odd]
+
+    w_qkv = gather_all(0, own_qkv)
+    w_first = gather_ffn(pair)
+    far_first, outs = [], []
+    for step in range(1, tp_count):
+        if step > 1:
+            below.append(move(below[-1], "tensor", ups[step - 1 :]))
+            above.append(move(above[-1], "tensor", downs[: tp_count - step]))
+        if step == 2:
+            outs = [shift(own_out, "tensor", j) for j in range(1, tp_count)]
+        if step == tp_count - 1:
+            far_first = [move(pair, "tensor", crossed(2 * j, 0)) for j in range(1, slices)]
+            above, below, far_first, outs, pair, w_qkv = sync(above, below, far_first, outs, pair, w_qkv)
+        else:
+            above, below, outs, own_out, pair = sync(above, below, outs, own_out, pair)
 
     bias_mixed = jnp.stack(
         [bias_q.reshape(heads, HD), jnp.zeros((heads, HD), F32), bias_v.reshape(heads, HD)], axis=1
     ).reshape(3 * width)
-    qkv = (jnp.dot(normed_all, w_qkv, preferred_element_type=F32) + bias_mixed).astype(BF)
+    line = jnp.arange(tp_count, dtype=jnp.int32) - place
+    pick = jnp.where(line < 0, -line, jnp.where(line > 0, tp_count - 1 + line, 0))
+    normal_all, normed_all, qkv = project(pick, [normal] + below + above, gain_one, shift_one, w_qkv, bias_mixed)
+    far_second = [move(pair, "tensor", crossed(2 * j, 1)) for j in range(1, slices)]
+    w_out = gather_all(1, jnp.concatenate([own_out] + outs, axis=1))
+
     ends = jnp.cumsum(lengths[0])
     spot = jnp.arange(SEQ, dtype=jnp.int32) - PROMPT
     started = jnp.max(jnp.where(ends[None, :] <= spot[:, None], ends[None, :], 0), axis=1)
     start_rows = jnp.where(spot < 0, 0, PROMPT + started).astype(jnp.int32)[None]
     attended, peaks = attend(start_rows, qkv)
+    others = range(1, slices)
+    attended, far_second = sync(attended, far_second)
 
     def rows_of(value, j):
         return lax.dynamic_slice_in_dim(value, (place ^ j) * rows, rows, 0)
@@ -474,60 +650,84 @@
     attended_rows = jnp.concatenate(
         [rows_of(attended, 0)] + [shift(rows_of(attended, j), "tensor", j) for j in range(1, tp_count)], axis=1
     )
+    w_far = [gather_ffn(left + right) for left, right in zip(far_first, far_second)]
+    attended_rows, w_out, w_first, cotangent = sync(attended_rows, w_out, w_first, cotangent)
+    peak_row = lax.dynamic_update_slice(
+        jnp.zeros((dp_count * H,), F32), peaks[:, 0, 0], (me * H + place * heads,)
+    )
     hidden_rows = token_rows + dot_nt(attended_rows, w_out) + bias_o
     normed_two = layer_norm(hidden_rows, gain_two, shift_two).astype(BF)
 
-    def four_rows(value):
-        sibling = shift(value, "dp", 1)
-        across = shift(value, "tensor", 1)
-        return [value, sibling, across, shift(across, "dp", 1)]
-
-    def sum_rows(partial):
-        near_rows = add_low(partial[0], shift(partial[1], "dp", 1))
-        far_rows = add_low(partial[2], shift(partial[3], "dp", 1))
-        return near_rows.astype(F32) + shift(far_rows, "tensor", 1).astype(F32)
-
-    back_list = four_rows(cotangent)
-    back_four = jnp.concatenate(back_list, axis=0)
-    normed_four = jnp.concatenate(four_rows(normed_two), axis=0)
-    grad_act = jnp.dot(back_four, w_down, preferred_element_type=F32).astype(BF)
-    pre_act = jnp.dot(normed_four, w_up, preferred_element_type=F32) + bias_up
-    activation, slope = gelu_pair(pre_act)
-    activation = activation.astype(BF)
-    grad_pre = (grad_act.astype(F32) * slope).astype(BF)
-    grad_normed = dot_nt(grad_pre, w_up).astype(BF)
-    grad_two = sum_rows([grad_normed[i * rows : (i + 1) * rows] for i in range(4)])
-    grad_bias_up = jnp.sum(grad_pre, axis=0, dtype=F32)
-
-    def ffn_grad(kind, left, right, masks):
-        blocks = block_of[kind]
-        bit = masks[0] >> 1
-        order = [q for q in range(dp_count // 2) if q & bit] + [q for q in range(dp_count // 2) if not q & bit]
-        pieces = [None] * len(order)
-        for group in (order[: len(order) // 2], order[len(order) // 2 :]):
-            picked = jnp.concatenate([blocks[2 * q : 2 * q + 2] for q in group])
-            out = grad_blocks(picked, [left], [right], edge)
-            for i, q in enumerate(group):
-                pieces[q] = out[2 * i : 2 * i + 2]
-        reduced = chip_reduce(pieces, masks).reshape(2, edge, slices, half)
-        total = reduced[:, :, 0].astype(F32)
-        for j in range(1, slices):
-            total = total + shift(reduced[:, :, j], "tensor", 2 * j).astype(F32)
-        total = total.astype(BF)
-        return join_halves(total[0], shift(total[1], "dp", 1))
-
-    sum_up = ffn_grad(2, normed_four, grad_pre, near)
-    sum_down = ffn_grad(3, back_four, activation, far)
-
-    result = dot_nt(activation, w_down).astype(BF)
-    ffn_rows = sum_rows([result[i * rows : (i + 1) * rows] for i in range(4)])
-    outputs = (hidden_rows + ffn_rows + bias_two).astype(BF)
-
-    back_rows = cotangent.astype(F32)
+    normed_across = shift(normed_two, "tensor", 1)
+    normed_sibling = shift(normed_two, "dp", 1)
+    back_sibling = shift(cotangent, "dp", 1)
+    normed_across, normed_sibling, back_sibling, cotangent, w_far = sync(
+        normed_across, normed_sibling, back_sibling, cotangent, w_far
+    )
+    normed_four = jnp.concatenate(
+        [normed_two, normed_sibling, normed_across, shift(normed_across, "dp", 1)], axis=0
+    )
+    w_up = [w_first[0]] + [value[0] for value in w_far]
+    w_down = [w_first[1]] + [value[1] for value in w_far]
+
+    parts = slices + 1
+    marks = [16 * (rows // 16 * i // parts) for i in range(parts + 1)]
+    back_pieces, activations, slopes = [], [], []
+    for j in range(parts):
+        back_pieces.append(shift(cotangent[marks[j] : marks[j + 1]], "tensor", 1))
+        if j < slices:
+            pre_act = jnp.dot(normed_four, w_up[j], preferred_element_type=F32) + bias_up[j * half : (j + 1) * half]
+            activation, slope = gelu_pair(pre_act)
+            activations.append(activation.astype(BF))
+            slopes.append(slope.astype(BF))
+        else:
+            result_far = matmul_sum(activations, w_down, 2 * rows, 2 * rows)
+            result_far, activations = sync(result_far, activations)
+        activations, slopes, back_pieces, cotangent = sync(activations, slopes, back_pieces, cotangent)
+    back_across = jnp.concatenate(back_pieces, axis=0)
+    back_four = jnp.concatenate([cotangent, back_sibling, back_across, shift(back_across, "dp", 1)], axis=0)
+
+    def core_rows(partial):
+        return add_low(partial[:rows], shift(partial[rows:], "dp", 1))
+
+    ffn_far = core_rows(result_far)
+    blocks_down = grad_blocks(held_blocks[3][pair_slots], back_four, activations, edge)
+    blocks_down, ffn_far, back_four = sync(blocks_down, ffn_far, back_four)
+
+    def chips_sum(blocks):
+        blocks = blocks.reshape(dp_count // 2, 2, edge, blocks.shape[2])
+        return lax.psum_scatter(blocks, "dp", scatter_dimension=0, tiled=False, axis_index_groups=same_core)
+
+    grads_pre, ffn_pieces = [], []
+    for j in range(parts):
+        ffn_pieces.append(shift(ffn_far[marks[j] : marks[j + 1]], "tensor", 1))
+        if j < slices:
+            grad_act = jnp.dot(back_four, w_down[j], preferred_element_type=F32)
+            grads_pre.append((grad_act * slopes[j].astype(F32)).astype(BF))
+        else:
+            grad_normed = matmul_sum(grads_pre, w_up)
+            grad_normed, grads_pre = sync(grad_normed, grads_pre)
+        grads_pre, ffn_pieces, ffn_far = sync(grads_pre, ffn_pieces, ffn_far)
+    ffn_across = jnp.concatenate(ffn_pieces, axis=0)
+    far_rows = core_rows(grad_normed[2 * rows :])
+    far_rows, grads_pre, activations = sync(far_rows, grads_pre, activations)
+    middle = rows // 2
+    far_low = shift(far_rows[:middle], "tensor", 1)
+    blocks_up = grad_blocks(held_blocks[2][pair_slots], normed_four, grads_pre, edge)
+    far_low, blocks_up, far_rows, activations = sync(far_low, blocks_up, far_rows, activations)
+    far_high = shift(far_rows[middle:], "tensor", 1)
+    near_rows = core_rows(grad_normed[: 2 * rows])
+    result = matmul_sum(activations, w_down, 0, 2 * rows)
+    far_high, near_rows, result = sync(far_high, near_rows, result)
+    part_down, part_up = chips_sum(blocks_down), chips_sum(blocks_up)
+    grad_two = near_rows.astype(F32) + jnp.concatenate([far_low, far_high], axis=0).astype(F32)
+
     grad_part, grad_gain_two, grad_shift_two = layer_norm_back(hidden_rows, gain_two, grad_two)
-    grad_hidden = back_rows + grad_part
+    grad_hidden = cotangent.astype(F32) + grad_part
     branch = grad_hidden.astype(BF)
     grad_attended_rows = jnp.dot(branch, w_out, preferred_element_type=F32).astype(BF)
+    grad_attended_rows, branch, result, grads_pre = sync(grad_attended_rows, branch, result, grads_pre)
+
     arrived = [
         grad_attended_rows[:, j * width : (j + 1) * width]
         if j == 0
@@ -537,60 +737,80 @@
     grad_attended = jnp.zeros((SEQ, width), BF)
     for j in range(tp_count):
         grad_attended = lax.dynamic_update_slice_in_dim(grad_attended, arrived[j], (place ^ j) * rows, 0)
+    ffn_near = core_rows(result)
+    grad_attended, branch, ffn_near, part_down, part_up = sync(grad_attended, branch, ffn_near, part_down, part_up)
+
+    def far_slices(part):
+        return part[:, :, :half], [part[:, :, j * half : (j + 1) * half] for j in others]
+
+    def far_sum(kept, arrived):
+        total = kept.astype(F32)
+        for value in arrived:
+            total = total + value.astype(F32)
+        total = total.astype(BF)
+        return join_halves(total[0], shift(total[1], "dp", 1))
+
+    order_near, order_far = halving_order(chips, near), halving_order(chips, far)
+
+    def half_slots(order):
+        return jnp.array([2 * q + 1 for q in order] + [2 * q for q in order], jnp.int32)
+
     grad_qkv_rows = attend_back(start_rows, qkv, grad_attended)
-
-    def core_reduce(blocks):
-        pairs = blocks.reshape(dp_count // 2, 2, edge, blocks.shape[2])
-        return add_low(pairs[:, 0], shift(pairs[:, 1], "dp", 1))
-
-    def full_reduce(blocks):
-        summed = core_reduce(blocks)
-        part = summed.shape[2] // 2
-        left = chip_reduce([summed[q, :, :part] for q in range(dp_count // 2)], near)
-        right = chip_reduce([summed[q, :, part:] for q in range(dp_count // 2)], far)
-        return jnp.concatenate([left, right], axis=1)
-
-    sum_out = full_reduce(grad_blocks(block_of[1], [branch], [attended_rows], edge))
+    own_down, far_down = far_slices(part_down)
+    own_up, far_up = far_slices(part_up)
+    far_down = [shift(value, "tensor", 2 * j) for j, value in zip(others, far_down)]
+    grad_qkv_rows, far_down, far_up, branch = sync(grad_qkv_rows, far_down, far_up, branch)
+
+    up_low = [shift(value[:1], "tensor", 2 * j) for j, value in zip(others, far_up)]
+    partial = dot_nt(grad_qkv_rows, w_qkv).astype(BF)
+    partial, up_low, far_up, grad_qkv_rows = sync(partial, up_low, far_up, grad_qkv_rows)
+    up_high = [shift(value[1:], "tensor", 2 * j) for j, value in zip(others, far_up)]
+    grads_qkv = grad_blocks(block_of[0][half_slots(order_far)], normed_all, [grad_qkv_rows], edge)
+    partial, up_high, grads_qkv, branch = sync(partial, up_high, grads_qkv, branch)
+    far_up = [jnp.concatenate(value, axis=0) for value in zip(up_low, up_high)]
+    grad_normed_one = lax.psum_scatter(partial, "tensor", scatter_dimension=0, tiled=True).astype(F32)
+
+    grads_out = grad_blocks(block_of[1][half_slots(order_near)], branch, [attended_rows], edge)
+    column_sums = jnp.sum(grad_qkv_rows, axis=0, dtype=F32).reshape(heads, 3, HD)
+    head_sums = lambda part: lax.dynamic_update_slice(
+        jnp.zeros((D,), F32), column_sums[:, part].reshape(width), (place * width,)
+    )
+    partial_wide = partial.astype(F32)
+    grad_bias_up = jnp.concatenate([jnp.sum(value, axis=0, dtype=F32) for value in grads_pre])
+    wide = jnp.zeros((FF,), F32)
+    for j in range(slices):
+        wide = lax.dynamic_update_slice(wide, grad_bias_up[j * half : (j + 1) * half], (hidden_starts[j],))
+    totals = jnp.concatenate(
+        [
+            head_sums(0),
+            head_sums(2),
+            jnp.sum(branch, axis=0, dtype=F32),
+            jnp.sum(cotangent, axis=0, dtype=F32),
+            jnp.sum(partial_wide * normal_all.astype(F32), axis=0),
+            jnp.sum(partial_wide, axis=0),
+            grad_gain_two,
+            grad_shift_two,
+            wide,
+            peak_row,
+        ]
+    )
+    totals = axis_sum(totals, "dp")
+    sum_qkv = halve(halve(grads_qkv, [1]), far)[0]
+    sum_out = halve(halve(grads_out, [1]), near)[0]
+    sum_down = far_sum(own_down, far_down)
+    sum_up = far_sum(own_up, far_up)
+    outputs = (hidden_rows + ffn_near.astype(F32) + ffn_across.astype(F32) + bias_two).astype(BF)
+    grad_normed_one, sum_out, totals = sync(grad_normed_one, sum_out, totals)
+    totals = axis_sum(totals, "tensor")
+    grad_small = totals[: 8 * D + FF]
+    peak_all = jnp.max(totals[8 * D + FF :].reshape(dp_count, H), axis=0)
     total_out = sum_out[:, :width].astype(F32)
     for j in range(1, tp_count):
         total_out = total_out + shift(sum_out[:, j * width : (j + 1) * width], "tensor", j).astype(F32)
     sum_out = total_out.astype(BF)
-
-    grad_normed_one = lax.psum_scatter(
-        dot_nt(grad_qkv_rows, w_qkv).astype(BF), "tensor", scatter_dimension=0, tiled=True
-    ).astype(F32)
-    sum_qkv = full_reduce(grad_blocks(block_of[0], [normed_all], [grad_qkv_rows], edge))
-    rows_part, grad_gain_one, grad_shift_one = layer_norm_back(token_rows, gain_one, grad_normed_one)
+    rows_part, _, _ = layer_norm_back(token_rows, gain_one, grad_normed_one)
     input_grad = (grad_hidden + rows_part).astype(BF)
 
-    column_sums = jnp.sum(grad_qkv_rows, axis=0, dtype=F32).reshape(heads, 3, HD)
-    head_sums = lambda part: lax.dynamic_update_slice(
-        jnp.zeros((D,), F32), column_sums[:, part].reshape(width), (place * width,)
-    )
-    wide = jnp.zeros((FF,), F32)
-    for j in range(slices):
-        wide = lax.dynamic_update_slice(wide, grad_bias_up[j * half : (j + 1) * half], (hidden_starts[j],))
-    peak_row = lax.dynamic_update_slice(
-        jnp.zeros((dp_count * H,), F32), peaks[:, 0, 0], (me * H + place * heads,)
-    )
-    early = lax.psum(
-        jnp.concatenate(
-            [
-                head_sums(0),
-                head_sums(2),
-                jnp.sum(branch, axis=0, dtype=F32),
-                jnp.sum(cotangent, axis=0, dtype=F32),
-                grad_gain_two,
-                grad_shift_two,
-                wide,
-                peak_row,
-            ]
-        ),
-        ("dp", "tensor"),
-    )
-    late = lax.psum(jnp.concatenate([grad_gain_one, grad_shift_one]), ("dp", "tensor"))
-    grad_small = jnp.concatenate([early[: 4 * D], late, early[4 * D : 6 * D + FF]])
-    peak_all = jnp.max(early[6 * D + FF :].reshape(dp_count, H), axis=0)
     shrink = jnp.sqrt(1.0 / jnp.maximum(peak_all, 1.0))
     small_first_new, small_second_new, small_new = small_step(grad_small, small_params, small_first, small_second)
     small_new = jnp.concatenate([(small_new[:D].reshape(H, HD) * shrink[:, None]).reshape(D), small_new[D:]])
@@ -613,8 +833,8 @@
     tiles_qkv = sum_qkv.reshape(edge_tiles, HD, heads, 3, HD).transpose(0, 3, 2, 1, 4).reshape(tile_q, HD, HD)
     done = update_tiles(tiles_down, state, rates, ones, bounds[3], None, True, token_count)
     done = update_tiles(tiles_up, state, rates, ones, bounds[2], done, False, token_count)
+    done = update_tiles(tiles_qkv, state, rates, factors, 0, done, False, token_count)
     done = update_tiles(tiles_out, state, rates, ones, bounds[1], done, True, token_count)
-    done = update_tiles(tiles_qkv, state, rates, factors, 0, done, False, token_count)
     return (
         outputs,
         input_grad,

time: 1320 us -> 1000 us (0.76)
  local copies, waits for them, and re-layouts: 216 us -> 66.1 us
  Pallas kernels: 207 us -> 316 us
  waiting for transfers between devices: 422 us -> 343 us
  other arithmetic: 168 us -> 91.5 us
  matrix products: 149 us -> 86 us
  blocking collectives: 37.2 us -> 0 us
  starting transfers between devices: 98 us -> 76.9 us
    ppermute x74 -> x46, waiting for transfers between devices: 387 us -> 247 us  [shift(): lax.ppermute(value, axis, [(i, i ^ mask) for i in range(lax.axis_size(axi...]
    pallas_call x0 -> x9, Pallas kernels: none -> 120 us  [the longest x3 52.2 us: matmul_sum(): pl.pallas_call(body, grid=(rows // row_step, columns // step), in_specs=[...]
    ppermute x0 -> x8, waiting for transfers between devices: none -> 78.2 us  [move(): return lax.ppermute(value, axis, pairs)]
    unnamed x192 -> x145, local copies, waits for them, and re-layouts: 68.1 us -> 16.5 us
    ppermute x74 -> x46, starting transfers between devices: 97.9 us -> 48 us  [shift(): lax.ppermute(value, axis, [(i, i ^ mask) for i in range(lax.axis_size(axi...]
    dot_general x4 -> x2, matrix products: 65.3 us -> 24.6 us  [dot_nt(): lax.dot_general(a, b, (((1,), (1,)), ((), ())), preferred_element_type=F32)]
    gather x7 -> x4, local copies, waits for them, and re-layouts: 43.7 us -> 4.64 us  [the longest x1 1.17 us: gather_ffn(): held_blocks[2][pair_slots]]
    psum x1 -> x0, blocking collectives: 37.2 us -> none  [per_device(): lax.psum(jnp.concatenate([grad_gain_one, grad_shift_one]), ('dp', 'tensor'))]
  transfers between devices with their start and end apart: 77 -> 61, of which waited for: 24 -> 27; matrix products, arithmetic and copies ran while one was open for 32% -> 23% of each run, Pallas kernels for 16% -> 28%
where the time goes in v2:
time: 1000 us; the launch traced here: 995 us
  waiting for transfers between devices  343 us (34%)
  Pallas kernels  316 us (32%)
  other arithmetic  91.5 us (9%)
  matrix products  86 us (9%)
  starting transfers between devices  76.9 us (8%)
  local copies, waits for them, and re-layouts  66.1 us (7%)
  between operations  15.6 us (2%)
    ppermute x46, waiting for transfers between devices, shift(): lax.ppermute(value, axis, [(i, i ^ mask) for i in range(lax.axis_size(axi...  247 us
    pallas_call x4, Pallas kernels, grad_blocks(): pl.pallas_call(body, grid_spec=pltpu.PrefetchScalarGridSpec(num_scalar_pr...  80 us
    ppermute x8, waiting for transfers between devices, move(): return lax.ppermute(value, axis, pairs)  78.2 us
    pallas_call x3, Pallas kernels, matmul_sum(): pl.pallas_call(body, grid=(rows // row_step, columns // step), in_specs=[...  52.2 us
    pallas_call x4, Pallas kernels, update_tiles(): pl.pallas_call(body, grid=(count // group,), in_specs=[smem, smem, pl.Blo...  51.7 us
    ppermute x46, starting transfers between devices, shift(): lax.ppermute(value, axis, [(i, i ^ mask) for i in range(lax.axis_size(axi...  48 us
    pallas_call x1, Pallas kernels, attend_back(): pl.pallas_call(attend_back_kernel, grid=(heads,), in_specs=[pl.BlockSpec(...  43.4 us
    pallas_call x4, Pallas kernels, scatter_blocks(): pl.pallas_call(body, grid_spec=pltpu.PrefetchScalarGridSpec(num_scalar_pr...  37.9 us
  transfers between devices with their start and end apart: 61, of which 27 were waited for; matrix products, arithmetic and copies ran while one was open for 23% of the time, Pallas kernels for 28%

profile of v2, /device:TPU:0, one launch (start us, length us, event | category | flops | bytes accessed | tf_op | source)
XLA Modules:
  0.0 995.2 jit_solution(10147269479567434285)
XLA Ops:
  7.2 5.0 pack_weights.1
  21.4 5.6 collective-permute-start.1
  27.0 43.9 %collective-permute-done.refs_5_ = bf16[512,2048]{1,0:T(8,128)(2,1)S(1)} collective-permute-done((bf16[512,2048]{1,0:T(8,128)(2,1)S(1)}, bf16[512,2048]{1,0:T(8,128)(2,1)S(1)}, u32[]{:S(2)}, u32[]{:S(2)}) %collective-permute-start) | collective-permute-done | bytes 2097184 | tf_op jit(solution)/shard_map/ppermute | solution.py:476
  75.3 7.6 collective-permute-start.5
  85.3 48.0 %collective-permute-done.5 = bf16[256,512]{1,0:T(8,128)(2,1)S(1)} collective-permute-done((bf16[256,512]{1,0:T(8,128)(2,1)S(1)}, bf16[256,512]{1,0:T(8,128)(2,1)S(1)}, u32[]{:S(2)}, u32[]{:S(2)}) %collective-permute-start.5) | collective-permute-done | bytes 262176 | tf_op jit(solution)/shard_map/ppermute | solution.py:472
  133.3 8.0 collective-permute-done.6
  144.6 13.3 %collective-permute-start.10 = (bf16[2,256,2048]{2,1,0:T(8,128)(2,1)}, bf16[2,256,2048]{2,1,0:T(8,128)(2,1)}, u32[]{:S(2)}, u32[]{:S(2)}) collective-permute-start(bf16[2,256,2048]{2,1,0:T(8,128)(2,1)} %pad_maximum_fusion.1), channel_id=1, source_target_pairs={{0,2},{3,1},{4,6},{7,5},{8,10},{11,9},{12,14},{15,13},{16,18},{19,... | collective-permute-start | bytes 6291464 | tf_op jit(solution)/shard_map/ppermute | solution.py:476
  158.4 8.6 scatter_blocks.4.refs_10_
  167.0 26.6 %collective-permute-done.8.refs_7_ = bf16[512,2048]{1,0:T(8,128)(2,1)} collective-permute-done((bf16[512,2048]{1,0:T(8,128)(2,1)}, bf16[512,2048]{1,0:T(8,128)(2,1)}, u32[]{:S(2)}, u32[]{:S(2)}) %collective-permute-start.8) | collective-permute-done | bytes 2097184 | tf_op jit(solution)/shard_map/ppermute | solution.py:476
  193.7 6.5 collective-permute-done.10
  205.7 24.5 %project.1 = (bf16[2048,2048]{1,0:T(8,128)(2,1)}, bf16[2048,2048]{1,0:T(8,128)(2,1)}, bf16[2048,1536]{1,0:T(8,128)(2,1)}) custom-call(s32[4]{0:T(128)} %compare_select_fusion.13.refs_0_, bf16[512,2048]{1,0:T(8,128)(2,1)} %copy-done.18, bf16[512,2048]{1,0:T(8,128)(2,1)} %copy-done.30, bf16[512,2048]{1,0:T(8,128)(2,1)} %collective-permute-done.4.refs_3_, ...), custom_call_target="tpu_custom_call" | custom-call | bytes 70000000 | tf_op jit(solution)/shard_map/project/pallas_call | solution.py:443
  230.2 21.4 %attend.1 = (bf16[2048,512]{1,0:T(8,128)(2,1)}, f32[4,8,128]{2,1,0:T(8,128)}) custom-call(s32[1,2048]{1,0:T(1,128)} %compare_select_fusion.start_ref, bf16[2048,1536]{1,0:T(8,128)(2,1)} %get-tuple-element.196.qkv_ref), custom_call_target="tpu_custom_call" | custom-call | bytes 70000000 | tf_op jit(solution)/shard_map/attend/pallas_call | solution.py:91
  251.7 4.5 add.351
  259.3 4.0 collective-permute-start.13
  266.8 9.9 scatter_blocks.6
  276.7 28.8 %collective-permute-done.13 = bf16[512,512]{1,0:T(8,128)(2,1)} collective-permute-done((bf16[512,512]{1,0:T(8,128)(2,1)}, bf16[512,512]{1,0:T(8,128)(2,1)}, u32[]{:S(2)}, u32[]{:S(2)}) %collective-permute-start.13) | collective-permute-done | bytes 524320 | tf_op jit(solution)/shard_map/ppermute | solution.py:472
  308.5 9.8 scatter_blocks.5
  318.2 7.1 fusion.46
  329.1 17.2 %all-gather.9.cloned.1.call-done.refs_2_ = bf16[8,256,2048]{2,1,0:T(8,128)(2,1)} async-done(((bf16[2,256,2048]{2,1,0:T(8,128)(2,1)}), bf16[8,256,2048]{2,1,0:T(8,128)(2,1)}) %all-gather.9.cloned.1.call-update) | async-done | bytes 8388624 | tf_op jit(solution)/shard_map/all_gather | solution.py:605
  346.3 9.7 scatter_blocks.7
  356.0 20.1 %collective-permute-done.15 = bf16[512,2048]{1,0:T(8,128)(2,1)} collective-permute-done((bf16[512,2048]{1,0:T(8,128)(2,1)}, bf16[512,2048]{1,0:T(8,128)(2,1)}, u32[]{:S(2)}, u32[]{:S(2)}) %collective-permute-start.15) | collective-permute-done | bytes 2097184 | tf_op jit(solution)/shard_map/ppermute | solution.py:472
  376.5 4.0 collective-permute-done.18
  380.6 4.4 pad_maximum_fusion.refs_1_
  385.0 14.3 %fusion.5 = (bf16[2048,1024]{1,0:T(8,128)(2,1)}, bf16[2048,1024]{1,0:T(8,128)(2,1)}) fusion(f32[1024]{0:T(1024)S(1)} %get-tuple-element.383, bf16[2048,2048]{1,0:T(8,128)(2,1)S(1)} %pad_maximum_fusion.refs_1_, bf16[2048,1024]{1,0:T(8,128)(2,1)S(1)} %copy-done.27), kind=kOutput, calls=%fused_computation.15 | convolution fusion | flops 8615100416 | bytes 20975616 | tf_op jit(solution)/shard_map/dot_general | solution.py:679
  399.7 14.3 %fusion.10 = (bf16[2048,1024]{1,0:T(8,128)(2,1)}, bf16[2048,1024]{1,0:T(8,128)(2,1)}) fusion(f32[1024]{0:T(1024)S(1)} %get-tuple-element.382, bf16[2048,2048]{1,0:T(8,128)(2,1)S(1)} %pad_maximum_fusion.refs_1_, bf16[2048,1024]{1,0:T(8,128)(2,1)S(1)} %copy-done.28), kind=kOutput, calls=%fused_computation.20 | convolution fusion | flops 8615100416 | bytes 20975616 | tf_op jit(solution)/shard_map/dot_general | solution.py:679
  414.0 3.6 collective-permute-done.20
  418.0 13.6 %matmul_sum.3 = bf16[1024,2048]{1,0:T(8,128)(2,1)} custom-call(bf16[2048,1024]{1,0:T(8,128)(2,1)} %get-tuple-element.264.refs_0_.refs_2_, bf16[2048,1024]{1,0:T(8,128)(2,1)} %get-tuple-element.265.refs_1_.refs_3_, bf16[2048,1024]{1,0:T(8,128)(2,1)} %get-tuple-element.224.refs_2_, bf16[2048,1024]{1,0:T(8,128)(2,1)} %get-tuple-element.225.refs_3_), custom_call_target="tpu_custom_call" | custom-call | bytes 37580964 | tf_op jit(solution)/shard_map/matmul_sum/pallas_call | solution.py:317
  436.7 3.3 constant_dynamic-update-slice_fusion.4
  446.4 24.5 %grad_blocks.4 = bf16[8,256,2048]{2,1,0:T(8,128)(2,1)} custom-call(s32[8]{0:T(128)} %gather_fusion.1, bf16[2048,2048]{1,0:T(8,128)(2,1)} %constant_dynamic-update-slice_fusion.refs_1_, bf16[2048,1024]{1,0:T(8,128)(2,1)} %get-tuple-element.264.refs_0_.refs_2_, bf16[2048,1024]{1,0:T(8,128)(2,1)} %get-tuple-element.265.refs_1_.refs_3_), custom_call_target="tpu_custom_call" | custom-call | bytes 75161928 | tf_op jit(solution)/shard_map/grad_blocks/pallas_call | solution.py:282
  472.8 15.4 %multiply_convert_fusion.1.refs_0_.refs_2_ = bf16[2048,1024]{1,0:T(8,128)(2,1)} fusion(bf16[2048,1024]{1,0:T(8,128)(2,1)} %get-tuple-element.242, bf16[2048,2048]{1,0:T(8,128)(2,1)} %constant_dynamic-update-slice_fusion.refs_1_, bf16[2048,1024]{1,0:T(8,128)(2,1)} %get-tuple-element.224.refs_2_), kind=kOutput, calls=%fused_computation.26 | convolution fusion | flops 8596226048 | bytes 20971520 | tf_op jit(solution)/shard_map/dot_general | solution.py:705
  490.1 12.6 %multiply_convert_fusion.refs_1_.refs_3_ = bf16[2048,1024]{1,0:T(8,128)(2,1)} fusion(bf16[2048,1024]{1,0:T(8,128)(2,1)S(1)} %copy-done.53, bf16[2048,2048]{1,0:T(8,128)(2,1)} %constant_dynamic-update-slice_fusion.refs_1_, bf16[2048,1024]{1,0:T(8,128)(2,1)S(1)} %copy-done.12), kind=kOutput, calls=%fused_computation.25 | convolution fusion | flops 8596226048 | bytes 20971520 | tf_op jit(solution)/shard_map/dot_general | solution.py:705
  502.8 4.6 collective-permute-done.25
  507.4 24.4 %matmul_sum.4 = bf16[2048,2048]{1,0:T(8,128)(2,1)} custom-call(bf16[2048,1024]{1,0:T(8,128)(2,1)} %multiply_convert_fusion.1.refs_0_.refs_2_, bf16[2048,1024]{1,0:T(8,128)(2,1)} %multiply_convert_fusion.refs_1_.refs_3_, bf16[2048,1024]{1,0:T(8,128)(2,1)} %get-tuple-element.215.refs_2_, bf16[2048,1024]{1,0:T(8,128)(2,1)} %get-tuple-element.218.refs_3_), custom_call_target="tpu_custom_call" | custom-call | bytes 75161928 | tf_op jit(solution)/shard_map/matmul_sum/pallas_call | solution.py:317
  536.3 17.2 %collective-permute-done.27 = bf16[176,2048]{1,0:T(8,128)(2,1)S(1)} collective-permute-done((bf16[176,2048]{1,0:T(8,128)(2,1)S(1)}, bf16[176,2048]{1,0:T(8,128)(2,1)S(1)}, u32[]{:S(2)}, u32[]{:S(2)}) %collective-permute-start.27) | collective-permute-done | bytes 720928 | tf_op jit(solution)/shard_map/ppermute | solution.py:472
  554.4 3.6 add_convert_fusion.5
  560.4 24.9 %grad_blocks.5 = bf16[8,256,2048]{2,1,0:T(8,128)(2,1)} custom-call(s32[8]{0:T(128)} %gather_fusion, bf16[2048,2048]{1,0:T(8,128)(2,1)} %copy-done.7, bf16[2048,1024]{1,0:T(8,128)(2,1)} %multiply_convert_fusion.1.refs_0_.refs_2_, bf16[2048,1024]{1,0:T(8,128)(2,1)} %multiply_convert_fusion.refs_1_.refs_3_), custom_call_target="tpu_custom_call" | custom-call | bytes 75161928 | tf_op jit(solution)/shard_map/grad_blocks/pallas_call | solution.py:282
  588.9 14.2 %matmul_sum.5 = bf16[1024,2048]{1,0:T(8,128)(2,1)} custom-call(bf16[2048,1024]{1,0:T(8,128)(2,1)} %get-tuple-element.264.refs_0_.refs_2_, bf16[2048,1024]{1,0:T(8,128)(2,1)} %get-tuple-element.265.refs_1_.refs_3_, bf16[2048,1024]{1,0:T(8,128)(2,1)} %get-tuple-element.224.refs_2_, bf16[2048,1024]{1,0:T(8,128)(2,1)} %get-tuple-element.225.refs_3_), custom_call_target="tpu_custom_call" | custom-call | bytes 37580964 | tf_op jit(solution)/shard_map/matmul_sum/pallas_call | solution.py:317
  603.1 9.1 collective-permute-done.29
  612.2 4.5 multiply_reduce_fusion
  616.8 5.3 fusion.35
  622.1 4.8 convolution_convert_fusion.1
  628.6 3.4 collective-permute-start.33
  632.0 19.0 %collective-permute-done.31 = bf16[512,512]{1,0:T(8,128)(2,1)S(1)} collective-permute-done((bf16[512,512]{1,0:T(8,128)(2,1)S(1)}, bf16[512,512]{1,0:T(8,128)(2,1)S(1)}, u32[]{:S(2)}, u32[]{:S(2)}) %collective-permute-start.31) | collective-permute-done | bytes 524320 | tf_op jit(solution)/shard_map/ppermute | solution.py:472
  651.0 15.8 %collective-permute-done.32 = bf16[512,512]{1,0:T(8,128)(2,1)S(1)} collective-permute-done((bf16[512,512]{1,0:T(8,128)(2,1)S(1)}, bf16[512,512]{1,0:T(8,128)(2,1)S(1)}, u32[]{:S(2)}, u32[]{:S(2)}) %collective-permute-start.32) | collective-permute-done | bytes 524320 | tf_op jit(solution)/shard_map/ppermute | solution.py:472
  672.6 10.3 %collective-permute-start.35 = (bf16[2,256,1024]{2,1,0:T(8,128)(2,1)}, bf16[2,256,1024]{2,1,0:T(8,128)(2,1)}, u32[]{:S(2)}, u32[]{:S(2)}) collective-permute-start(bf16[2,256,1024]{2,1,0:T(8,128)(2,1)} %slice.278), channel_id=1, source_target_pairs={{0,2},{1,3},{2,0},{3,1},{4,6},{5,7},{6,4},{7,5},{8,10},{9,11},{10,... | collective-permute-start | bytes 3145736 | tf_op jit(solution)/shard_map/ppermute | solution.py:472
  683.5 43.4 %attend_back.1.refs_2_ = bf16[2048,1536]{1,0:T(8,128)(2,1)} custom-call(s32[1,2048]{1,0:T(1,128)} %compare_select_fusion.start_ref, bf16[2048,1536]{1,0:T(8,128)(2,1)} %get-tuple-element.196.qkv_ref, bf16[2048,512]{1,0:T(8,128)(2,1)} %copy-done.22), custom_call_target="tpu_custom_call" | custom-call | bytes 140000000 | tf_op jit(solution)/shard_map/attend_back/pallas_call | solution.py:146
  729.5 17.5 %convolution_convert_fusion = bf16[2048,2048]{1,0:T(8,128)(2,1)} fusion(bf16[2048,1536]{1,0:T(8,128)(2,1)} %attend_back.1.refs_2_, bf16[2048,1536]{1,0:T(8,128)(2,1)S(1)} %bitcast.167), kind=kOutput, calls=%fused_computation.31 | convolution fusion | flops 12889096192 | bytes 20971520 | tf_op jit(solution)/shard_map/dot_general | solution.py:31
  747.0 7.9 collective-permute-done.36
  756.5 19.4 %grad_blocks.6 = bf16[8,256,1536]{2,1,0:T(8,128)(2,1)} custom-call(s32[8]{0:T(128)} %gather_fusion.3, bf16[2048,2048]{1,0:T(8,128)(2,1)} %get-tuple-element.287.refs_1_, bf16[2048,1536]{1,0:T(8,128)(2,1)} %attend_back.1.refs_2_), custom_call_target="tpu_custom_call" | custom-call | bytes 56371444 | tf_op jit(solution)/shard_map/grad_blocks/pallas_call | solution.py:282
  775.9 3.7 collective-permute-done.37
  783.9 3.4 convert_reduce_fusion.3
  790.5 11.1 %grad_blocks.7 = bf16[8,256,2048]{2,1,0:T(8,128)(2,1)} custom-call(s32[8]{0:T(128)} %gather_fusion.4, bf16[512,2048]{1,0:T(8,128)(2,1)} %copy-done.8, bf16[512,2048]{1,0:T(8,128)(2,1)} %pad_maximum_fusion.2.refs_2_), custom_call_target="tpu_custom_call" | custom-call | bytes 18790480 | tf_op jit(solution)/shard_map/grad_blocks/pallas_call | solution.py:282
  801.7 4.9 slice.336
  810.8 3.9 add_convert_fusion.3
  819.8 10.6 %convert_reduce_fusion = (f32[2048]{0:T(1024)S(1)}, f32[2048]{0:T(1024)S(1)}) fusion(bf16[2048,2048]{1,0:T(8,128)(2,1)} %convolution_convert_fusion, bf16[2048,2048]{1,0:T(8,128)(2,1)} %get-tuple-element.292), kind=kLoop, calls=%fused_computation.5 | loop fusion | flops 20967424 | bytes 16793600 | tf_op jit(solution)/shard_map/reduce_sum | solution.py:790
  834.8 5.8 add_convert_fusion
  844.9 16.6 %update_tiles.4 = (f32[96,128,128]{2,1,0:T(8,128)}, f32[96,128,128]{2,1,0:T(8,128)}, f32[96,128,128]{2,1,0:T(8,128)}, bf16[96,128,128]{2,1,0:T(8,128)(2,1)}, f32...) custom-call(f32[32]{0:T(128)} %get-tuple-element.392.refs_0_, ...), custom_call_target="tpu_custom_call" | custom-call | bytes 56000000 | tf_op jit(solution)/shard_map/update_tiles/pallas_call | solution.py:247
  865.1 27.4 %collective-permute-done.42 = f32[24704]{0:T(1024)S(1)} collective-permute-done((f32[24704]{0:T(1024)S(1)}, f32[24704]{0:T(1024)S(1)}, u32[]{:S(2)}, u32[]{:S(2)}) %collective-permute-start.42) | collective-permute-done | bytes 98848 | tf_op jit(solution)/shard_map/ppermute | solution.py:472
  892.9 4.3 collective-permute-done.43
  904.6 16.1 %update_tiles.5 = (f32[96,128,128]{2,1,0:T(8,128)}, f32[96,128,128]{2,1,0:T(8,128)}, f32[96,128,128]{2,1,0:T(8,128)}, bf16[96,128,128]{2,1,0:T(8,128)(2,1)}, f32...) custom-call(f32[32]{0:T(128)} %get-tuple-element.393.refs_0_, ...), custom_call_target="tpu_custom_call", output_to_operand_aliasing={{0}: (10, {}), {1}: (11, {}), {2}: (12, {}), {3}: (13, {}),... | custom-call | bytes 56000000 | tf_op jit(solution)/shard_map/update_tiles/pallas_call | solution.py:247
  935.8 4.1 collective-permute-done.47
  944.7 15.3 %collective-permute-done.48 = f32[24704]{0:T(1024)S(1)} collective-permute-done((f32[24704]{0:T(1024)S(1)}, f32[24704]{0:T(1024)S(1)}, u32[]{:S(2)}, u32[]{:S(2)}) %collective-permute-start.48) | collective-permute-done | bytes 98848 | tf_op jit(solution)/shard_map/ppermute | solution.py:472
  965.9 12.7 %update_tiles.6 = (f32[96,128,128]{2,1,0:T(8,128)}, f32[96,128,128]{2,1,0:T(8,128)}, f32[96,128,128]{2,1,0:T(8,128)}, bf16[96,128,128]{2,1,0:T(8,128)(2,1)}, f32...) custom-call(f32[24]{0:T(128)} %bitcast.195, ...), custom_call_target="tpu_custom_call", output_to_operand_aliasing={{0}: (10, {}), {1}: (11, {}), {2}: (12, {}), {3}: (13, {}),... | custom-call | bytes 42000000 | tf_op jit(solution)/shard_map/update_tiles/pallas_call | solution.py:247
  981.8 6.3 update_tiles.7
  (388 shorter events, 144.1 us)
Async XLA Ops:
  7.2 151.2 %all-gather.11.cloned.1.call-start = ((), (), s32[]{:S(2)}) async-start(), calls=%async_computation.6 | async-start | bytes 7077888 | tf_op jit(solution)/shard_map/all_gather | solution.py:609
  12.3 254.5 %all-gather.7.cloned.1.call-start = ((), (), s32[]{:S(2)}) async-start(), calls=%async_computation.3 | async-start | bytes 10485760 | tf_op jit(solution)/shard_map/all_gather | solution.py:605
  14.0 2.8 collective-permute-start.2
  18.4 139.5 %copy-start.46 = (s32[4,8]{1,0:T(4,128)S(1)}, s32[4,8]{1,0:T(4,128)}, u32[]{:S(2)}) copy-start(s32[4,8]{1,0:T(4,128)} %param.19) | copy-start | bytes 388
  18.4 290.1 %all-gather.13.cloned.1.call-start = ((), (), s32[]{:S(2)}) async-start(), calls=%async_computation.7 | async-start | bytes 9437184 | tf_op jit(solution)/shard_map/all_gather | solution.py:609
  18.8 125.8 %copy-start.41 = (f32[512]{0:T(512)}, f32[512]{0:T(512)S(1)}, u32[]{:S(2)}) copy-start(f32[512]{0:T(512)S(1)} %broadcast_multiply_fusion.5) | copy-start | bytes 6148
  19.5 125.1 %copy-start.43 = (f32[512]{0:T(512)}, f32[512]{0:T(512)S(1)}, u32[]{:S(2)}) copy-start(f32[512]{0:T(512)S(1)} %add_rsqrt_fusion.1) | copy-start | bytes 6148
  20.1 50.8 %collective-permute-start = (bf16[512,2048]{1,0:T(8,128)(2,1)S(1)}, bf16[512,2048]{1,0:T(8,128)(2,1)S(1)}, u32[]{:S(2)}, u32[]{:S(2)}) collective-permute-start(bf16[512,2048]{1,0:T(8,128)(2,1)S(1)} %fusion.15.refs_1_), channel_id=1, source_target_pairs={{1,0},{2,1},{3,2},{5,4},{6,5},{7,6},{9,8},{10,9},{11,10},{13,12},{... | collective-permute-start | bytes 6291464 | tf_op jit(solution)/shard_map/ppermute | solution.py:476
  21.4 50.7 %collective-permute-start.1 = (bf16[512,2048]{1,0:T(8,128)(2,1)S(1)}, bf16[512,2048]{1,0:T(8,128)(2,1)S(1)}, u32[]{:S(2)}, u32[]{:S(2)}) collective-permute-start(bf16[512,2048]{1,0:T(8,128)(2,1)S(1)} %fusion.15.refs_1_), channel_id=1, source_target_pairs={{0,1},{1,2},{2,3},{4,5},{5,6},{6,7},{8,9},{9,10},{10,11},{12,13},{... | collective-permute-start | bytes 6291464 | tf_op jit(solution)/shard_map/ppermute | solution.py:476
  72.1 69.2 %collective-permute-start.3 = (bf16[512,2048]{1,0:T(8,128)(2,1)S(1)}, bf16[512,2048]{1,0:T(8,128)(2,1)}, u32[]{:S(2)}, u32[]{:S(2)}) collective-permute-start(bf16[512,2048]{1,0:T(8,128)(2,1)S(1)} %collective-permute-done.refs_5_), channel_id=1, source_target_pairs={{1,0},{2,1},{5,4},{6,5},{9,8},{10,9},{13,12},{14,13},{17,16},{18,1... | collective-permute-start | bytes 6291464 | tf_op jit(solution)/shard_map/ppermute | solution.py:476
  73.3 67.9 %collective-permute-start.4 = (bf16[512,2048]{1,0:T(8,128)(2,1)S(1)}, bf16[512,2048]{1,0:T(8,128)(2,1)}, u32[]{:S(2)}, u32[]{:S(2)}) collective-permute-start(bf16[512,2048]{1,0:T(8,128)(2,1)S(1)} %collective-permute-done.1.refs_2_), channel_id=1, source_target_pairs={{1,2},{2,3},{5,6},{6,7},{9,10},{10,11},{13,14},{14,15},{17,18},{18... | collective-permute-start | bytes 6291464 | tf_op jit(solution)/shard_map/ppermute | solution.py:476
  75.3 58.0 %collective-permute-start.5 = (bf16[256,512]{1,0:T(8,128)(2,1)S(1)}, bf16[256,512]{1,0:T(8,128)(2,1)S(1)}, u32[]{:S(2)}, u32[]{:S(2)}) collective-permute-start(bf16[256,512]{1,0:T(8,128)(2,1)S(1)} %copy-done.37), channel_id=1, source_target_pairs={{0,1},{1,0},{2,3},{3,2},{4,5},{5,4},{6,7},{7,6},{8,9},{9,8},{10,11... | collective-permute-start | bytes 786440 | tf_op jit(solution)/shard_map/ppermute | solution.py:472
  83.0 58.3 %collective-permute-start.6 = (bf16[256,512]{1,0:T(8,128)(2,1)S(1)}, bf16[256,512]{1,0:T(8,128)(2,1)S(1)}, u32[]{:S(2)}, u32[]{:S(2)}) collective-permute-start(bf16[256,512]{1,0:T(8,128)(2,1)S(1)} %copy-done.37), channel_id=1, source_target_pairs={{0,2},{1,3},{2,0},{3,1},{4,6},{5,7},{6,4},{7,5},{8,10},{9,11},{10,... | collective-permute-start | bytes 786440 | tf_op jit(solution)/shard_map/ppermute | solution.py:472
  83.0 58.3 %collective-permute-start.7 = (bf16[256,512]{1,0:T(8,128)(2,1)S(1)}, bf16[256,512]{1,0:T(8,128)(2,1)S(1)}, u32[]{:S(2)}, u32[]{:S(2)}) collective-permute-start(bf16[256,512]{1,0:T(8,128)(2,1)S(1)} %copy-done.37), channel_id=1, source_target_pairs={{0,3},{1,2},{2,1},{3,0},{4,7},{5,6},{6,5},{7,4},{8,11},{9,10},{10,... | collective-permute-start | bytes 786440 | tf_op jit(solution)/shard_map/ppermute | solution.py:472
  141.3 52.4 %collective-permute-start.8 = (bf16[512,2048]{1,0:T(8,128)(2,1)}, bf16[512,2048]{1,0:T(8,128)(2,1)}, u32[]{:S(2)}, u32[]{:S(2)}) collective-permute-start(bf16[512,2048]{1,0:T(8,128)(2,1)} %collective-permute-done.3.refs_6_), channel_id=1, source_target_pairs={{1,0},{5,4},{9,8},{13,12},{17,16},{21,20},{25,24},{29,28}} | collective-permute-start | bytes 6291464 | tf_op jit(solution)/shard_map/ppermute | solution.py:476
  142.6 51.1 %collective-permute-start.9 = (bf16[512,2048]{1,0:T(8,128)(2,1)}, bf16[512,2048]{1,0:T(8,128)(2,1)}, u32[]{:S(2)}, u32[]{:S(2)}) collective-permute-start(bf16[512,2048]{1,0:T(8,128)(2,1)} %collective-permute-done.4.refs_3_), channel_id=1, source_target_pairs={{2,3},{6,7},{10,11},{14,15},{18,19},{22,23},{26,27},{30,31}} | collective-permute-start | bytes 6291464 | tf_op jit(solution)/shard_map/ppermute | solution.py:476
  144.6 55.6 %collective-permute-start.10 = (bf16[2,256,2048]{2,1,0:T(8,128)(2,1)}, bf16[2,256,2048]{2,1,0:T(8,128)(2,1)}, u32[]{:S(2)}, u32[]{:S(2)}) collective-permute-start(bf16[2,256,2048]{2,1,0:T(8,128)(2,1)} %pad_maximum_fusion.1), channel_id=1, source_target_pairs={{0,2},{3,1},{4,6},{7,5},{8,10},{11,9},{12,14},{15,13},{16,18},{19,... | collective-permute-start | bytes 6291464 | tf_op jit(solution)/shard_map/ppermute | solution.py:476
  201.3 145.0 %all-gather.9.cloned.1.call-start = ((), (), s32[]{:S(2)}) async-start(), calls=%async_computation.4 | async-start | bytes 10485760 | tf_op jit(solution)/shard_map/all_gather | solution.py:605
  201.3 50.3 %collective-permute-start.11 = (bf16[2,256,2048]{2,1,0:T(8,128)(2,1)}, bf16[2,256,2048]{2,1,0:T(8,128)(2,1)}, u32[]{:S(2)}, u32[]{:S(2)}) collective-permute-start(bf16[2,256,2048]{2,1,0:T(8,128)(2,1)} %pad_maximum_fusion.1), channel_id=1, source_target_pairs={{1,3},{2,0},{5,7},{6,4},{9,11},{10,8},{13,15},{14,12},{17,19},{18,... | collective-permute-start | bytes 6291464 | tf_op jit(solution)/shard_map/ppermute | solution.py:476
  256.2 414.2 %reduce-scatter.10.cloned.1.call-start = ((), (), s32[]{:S(2)}) async-start(), calls=%async_computation.8 | async-start | bytes 10485760
  259.3 17.4 %collective-permute-start.14 = (bf16[512,512]{1,0:T(8,128)(2,1)}, bf16[512,512]{1,0:T(8,128)(2,1)}, u32[]{:S(2)}, u32[]{:S(2)}) collective-permute-start(bf16[512,512]{1,0:T(8,128)(2,1)} %get-tuple-element.364), channel_id=1, source_target_pairs={{0,3},{1,2},{2,1},{3,0},{4,7},{5,6},{6,5},{7,4},{8,11},{9,10},{10,... | collective-permute-start | bytes 1572872 | tf_op jit(solution)/shard_map/ppermute | solution.py:472
  259.3 46.2 %collective-permute-start.13 = (bf16[512,512]{1,0:T(8,128)(2,1)}, bf16[512,512]{1,0:T(8,128)(2,1)}, u32[]{:S(2)}, u32[]{:S(2)}) collective-permute-start(bf16[512,512]{1,0:T(8,128)(2,1)} %get-tuple-element.365), channel_id=1, source_target_pairs={{0,2},{1,3},{2,0},{3,1},{4,6},{5,7},{6,4},{7,5},{8,10},{9,11},{10,... | collective-permute-start | bytes 1572872 | tf_op jit(solution)/shard_map/ppermute | solution.py:472
  263.3 42.2 %collective-permute-start.12 = (bf16[512,512]{1,0:T(8,128)(2,1)S(1)}, bf16[512,512]{1,0:T(8,128)(2,1)}, u32[]{:S(2)}, u32[]{:S(2)}) collective-permute-start(bf16[512,512]{1,0:T(8,128)(2,1)S(1)} %get-tuple-element.366), channel_id=1, source_target_pairs={{0,1},{1,0},{2,3},{3,2},{4,5},{5,4},{6,7},{7,6},{8,9},{9,8},{10,11... | collective-permute-start | bytes 1572872 | tf_op jit(solution)/shard_map/ppermute | solution.py:472
  328.2 47.9 %collective-permute-start.15 = (bf16[512,2048]{1,0:T(8,128)(2,1)}, bf16[512,2048]{1,0:T(8,128)(2,1)}, u32[]{:S(2)}, u32[]{:S(2)}) collective-permute-start(bf16[512,2048]{1,0:T(8,128)(2,1)} %add_convert_fusion.8), channel_id=1, source_target_pairs={{0,1},{1,0},{2,3},{3,2},{4,5},{5,4},{6,7},{7,6},{8,9},{9,8},{10,11... | collective-permute-start | bytes 6291464 | tf_op jit(solution)/shard_map/ppermute | solution.py:472
  328.2 47.9 %collective-permute-start.16 = (bf16[512,2048]{1,0:T(8,128)(2,1)}, bf16[512,2048]{1,0:T(8,128)(2,1)}, u32[]{:S(2)}, u32[]{:S(2)}) collective-permute-start(bf16[512,2048]{1,0:T(8,128)(2,1)} %add_convert_fusion.8), channel_id=1, source_target_pairs={{0,4},{4,0},{8,12},{12,8},{16,20},{20,16},{24,28},{28,24},{1,5},{5... | collective-permute-start | bytes 6291464 | tf_op jit(solution)/shard_map/ppermute | solution.py:472
  329.1 47.0 %collective-permute-start.17 = (bf16[512,2048]{1,0:T(8,128)(2,1)S(1)}, bf16[512,2048]{1,0:T(8,128)(2,1)}, u32[]{:S(2)}, u32[]{:S(2)}) collective-permute-start(bf16[512,2048]{1,0:T(8,128)(2,1)S(1)} %copy-done.10), channel_id=1, source_target_pairs={{0,4},{4,0},{8,12},{12,8},{16,20},{20,16},{24,28},{28,24},{1,5},{5... | collective-permute-start | bytes 6291464 | tf_op jit(solution)/shard_map/ppermute | solution.py:472
  376.1 4.5 collective-permute-start.18
  376.2 23.1 %collective-permute-start.19 = (bf16[160,2048]{1,0:T(8,128)(2,1)S(1)}, bf16[160,2048]{1,0:T(8,128)(2,1)S(1)}, u32[]{:S(2)}, u32[]{:S(2)}) collective-permute-start(bf16[160,2048]{1,0:T(8,128)(2,1)S(1)} %slice.257), channel_id=1, source_target_pairs={{0,1},{1,0},{2,3},{3,2},{4,5},{5,4},{6,7},{7,6},{8,9},{9,8},{10,11... | collective-permute-start | bytes 1966088 | tf_op jit(solution)/shard_map/ppermute | solution.py:472
  399.4 18.2 %collective-permute-start.20 = (bf16[176,2048]{1,0:T(8,128)(2,1)S(1)}, bf16[176,2048]{1,0:T(8,128)(2,1)S(1)}, u32[]{:S(2)}, u32[]{:S(2)}) collective-permute-start(bf16[176,2048]{1,0:T(8,128)(2,1)S(1)} %slice.258), channel_id=1, source_target_pairs={{0,1},{1,0},{2,3},{3,2},{4,5},{5,4},{6,7},{7,6},{8,9},{9,8},{10,11... | collective-permute-start | bytes 2162696 | tf_op jit(solution)/shard_map/ppermute | solution.py:472
  417.7 17.4 %collective-permute-start.21 = (bf16[176,2048]{1,0:T(8,128)(2,1)S(1)}, bf16[176,2048]{1,0:T(8,128)(2,1)S(1)}, u32[]{:S(2)}, u32[]{:S(2)}) collective-permute-start(bf16[176,2048]{1,0:T(8,128)(2,1)S(1)} %slice.259), channel_id=1, source_target_pairs={{0,1},{1,0},{2,3},{3,2},{4,5},{5,4},{6,7},{7,6},{8,9},{9,8},{10,11... | collective-permute-start | bytes 2162696 | tf_op jit(solution)/shard_map/ppermute | solution.py:472
  433.3 9.5 collective-permute-start.23
  435.2 9.8 collective-permute-start.22
  470.9 199.4 %reduce-scatter.12.cloned.1.call-start = ((), (), s32[]{:S(2)}) async-start(), calls=%async_computation.9 | async-start | bytes 10485760
  472.2 17.3 %collective-permute-start.24 = (bf16[160,2048]{1,0:T(8,128)(2,1)S(1)}, bf16[160,2048]{1,0:T(8,128)(2,1)}, u32[]{:S(2)}, u32[]{:S(2)}) collective-permute-start(bf16[160,2048]{1,0:T(8,128)(2,1)S(1)} %slice.262), channel_id=1, source_target_pairs={{0,1},{1,0},{2,3},{3,2},{4,5},{5,4},{6,7},{7,6},{8,9},{9,8},{10,11... | collective-permute-start | bytes 1966088 | tf_op jit(solution)/shard_map/ppermute | solution.py:472
  489.5 17.8 %collective-permute-start.25 = (bf16[176,2048]{1,0:T(8,128)(2,1)S(1)}, bf16[176,2048]{1,0:T(8,128)(2,1)S(1)}, u32[]{:S(2)}, u32[]{:S(2)}) collective-permute-start(bf16[176,2048]{1,0:T(8,128)(2,1)S(1)} %slice.263), channel_id=1, source_target_pairs={{0,1},{1,0},{2,3},{3,2},{4,5},{5,4},{6,7},{7,6},{8,9},{9,8},{10,11... | collective-permute-start | bytes 2162696 | tf_op jit(solution)/shard_map/ppermute | solution.py:472
  534.7 18.8 %collective-permute-start.30 = (bf16[512,2048]{1,0:T(8,128)(2,1)S(1)}, bf16[512,2048]{1,0:T(8,128)(2,1)S(1)}, u32[]{:S(2)}, u32[]{:S(2)}) collective-permute-start(bf16[512,2048]{1,0:T(8,128)(2,1)S(1)} %get-tuple-element.356), channel_id=1, source_target_pairs={{0,4},{4,0},{8,12},{12,8},{16,20},{20,16},{24,28},{28,24},{1,5},{5... | collective-permute-start | bytes 6291464 | tf_op jit(solution)/shard_map/ppermute | solution.py:472
  534.8 19.6 %collective-permute-start.26 = (bf16[512,2048]{1,0:T(8,128)(2,1)S(1)}, bf16[512,2048]{1,0:T(8,128)(2,1)S(1)}, u32[]{:S(2)}, u32[]{:S(2)}) collective-permute-start(bf16[512,2048]{1,0:T(8,128)(2,1)S(1)} %get-tuple-element.357), channel_id=1, source_target_pairs={{0,4},{4,0},{8,12},{12,8},{16,20},{20,16},{24,28},{28,24},{1,5},{5... | collective-permute-start | bytes 6291464 | tf_op jit(solution)/shard_map/ppermute | solution.py:472
  535.3 18.2 %collective-permute-start.27 = (bf16[176,2048]{1,0:T(8,128)(2,1)S(1)}, bf16[176,2048]{1,0:T(8,128)(2,1)S(1)}, u32[]{:S(2)}, u32[]{:S(2)}) collective-permute-start(bf16[176,2048]{1,0:T(8,128)(2,1)S(1)} %slice.266), channel_id=1, source_target_pairs={{0,1},{1,0},{2,3},{3,2},{4,5},{5,4},{6,7},{7,6},{8,9},{9,8},{10,11... | collective-permute-start | bytes 2162696 | tf_op jit(solution)/shard_map/ppermute | solution.py:472
  559.5 25.9 %collective-permute-start.28 = (bf16[256,2048]{1,0:T(8,128)(2,1)S(1)}, bf16[256,2048]{1,0:T(8,128)(2,1)S(1)}, u32[]{:S(2)}, u32[]{:S(2)}) collective-permute-start(bf16[256,2048]{1,0:T(8,128)(2,1)S(1)} %slice.267), channel_id=1, source_target_pairs={{0,1},{1,0},{2,3},{3,2},{4,5},{5,4},{6,7},{7,6},{8,9},{9,8},{10,11... | collective-permute-start | bytes 3145736 | tf_op jit(solution)/shard_map/ppermute | solution.py:472
  585.4 341.7 %reduce-scatter.8.cloned.1.call-start = ((), (), s32[]{:S(2)}) async-start(), calls=%async_computation.5 | async-start | bytes 10485760 | tf_op jit(solution)/shard_map/reduce_scatter | solution.py:771
  587.8 24.4 %collective-permute-start.29 = (bf16[256,2048]{1,0:T(8,128)(2,1)}, bf16[256,2048]{1,0:T(8,128)(2,1)}, u32[]{:S(2)}, u32[]{:S(2)}) collective-permute-start(bf16[256,2048]{1,0:T(8,128)(2,1)} %slice.268), channel_id=1, source_target_pairs={{0,1},{1,0},{2,3},{3,2},{4,5},{5,4},{6,7},{7,6},{8,9},{9,8},{10,11... | collective-permute-start | bytes 3145736 | tf_op jit(solution)/shard_map/ppermute | solution.py:472
  627.1 41.1 %collective-permute-start.34 = (bf16[512,2048]{1,0:T(8,128)(2,1)S(1)}, bf16[512,2048]{1,0:T(8,128)(2,1)S(1)}, u32[]{:S(2)}, u32[]{:S(2)}) collective-permute-start(bf16[512,2048]{1,0:T(8,128)(2,1)S(1)} %slice.276), channel_id=1, source_target_pairs={{0,4},{4,0},{8,12},{12,8},{16,20},{20,16},{24,28},{28,24},{1,5},{5... | collective-permute-start | bytes 6291464 | tf_op jit(solution)/shard_map/ppermute | solution.py:472
  627.5 23.4 %collective-permute-start.31 = (bf16[512,512]{1,0:T(8,128)(2,1)S(1)}, bf16[512,512]{1,0:T(8,128)(2,1)S(1)}, u32[]{:S(2)}, u32[]{:S(2)}) collective-permute-start(bf16[512,512]{1,0:T(8,128)(2,1)S(1)} %get-tuple-element.361), channel_id=1, source_target_pairs={{0,1},{1,0},{2,3},{3,2},{4,5},{5,4},{6,7},{7,6},{8,9},{9,8},{10,11... | collective-permute-start | bytes 1572872 | tf_op jit(solution)/shard_map/ppermute | solution.py:472
  628.6 38.2 %collective-permute-start.32 = (bf16[512,512]{1,0:T(8,128)(2,1)S(1)}, bf16[512,512]{1,0:T(8,128)(2,1)S(1)}, u32[]{:S(2)}, u32[]{:S(2)}) collective-permute-start(bf16[512,512]{1,0:T(8,128)(2,1)S(1)} %get-tuple-element.360), channel_id=1, source_target_pairs={{0,2},{1,3},{2,0},{3,1},{4,6},{5,7},{6,4},{7,5},{8,10},{9,11},{10,... | collective-permute-start | bytes 1572872 | tf_op jit(solution)/shard_map/ppermute | solution.py:472
  628.6 38.2 %collective-permute-start.33 = (bf16[512,512]{1,0:T(8,128)(2,1)S(1)}, bf16[512,512]{1,0:T(8,128)(2,1)S(1)}, u32[]{:S(2)}, u32[]{:S(2)}) collective-permute-start(bf16[512,512]{1,0:T(8,128)(2,1)S(1)} %get-tuple-element.359), channel_id=1, source_target_pairs={{0,3},{1,2},{2,1},{3,0},{4,7},{5,6},{6,5},{7,4},{8,11},{9,10},{10,... | collective-permute-start | bytes 1572872 | tf_op jit(solution)/shard_map/ppermute | solution.py:472
  672.6 56.1 %collective-permute-start.35 = (bf16[2,256,1024]{2,1,0:T(8,128)(2,1)}, bf16[2,256,1024]{2,1,0:T(8,128)(2,1)}, u32[]{:S(2)}, u32[]{:S(2)}) collective-permute-start(bf16[2,256,1024]{2,1,0:T(8,128)(2,1)} %slice.278), channel_id=1, source_target_pairs={{0,2},{1,3},{2,0},{3,1},{4,6},{5,7},{6,4},{7,5},{8,10},{9,11},{10,... | collective-permute-start | bytes 3145736 | tf_op jit(solution)/shard_map/ppermute | solution.py:472
  729.5 25.4 %collective-permute-start.36 = (bf16[1,256,1024]{2,1,0:T(8,128)(2,1)}, bf16[1,256,1024]{2,1,0:T(8,128)(2,1)}, u32[]{:S(2)}, u32[]{:S(2)}) collective-permute-start(bf16[1,256,1024]{2,1,0:T(8,128)(2,1)} %slice.280), channel_id=1, source_target_pairs={{0,2},{1,3},{2,0},{3,1},{4,6},{5,7},{6,4},{7,5},{8,10},{9,11},{10,... | collective-permute-start | bytes 1572872 | tf_op jit(solution)/shard_map/ppermute | solution.py:472
  755.0 24.6 %collective-permute-start.37 = (bf16[1,256,1024]{2,1,0:T(8,128)(2,1)S(1)}, bf16[1,256,1024]{2,1,0:T(8,128)(2,1)S(1)}, u32[]{:S(2)}, u32[]{:S(2)}) collective-permute-start(bf16[1,256,1024]{2,1,0:T(8,128)(2,1)S(1)} %slice.281), channel_id=1, source_target_pairs={{0,2},{1,3},{2,0},{3,1},{4,6},{5,7},{6,4},{7,5},{8,10},{9,11},{10,... | collective-permute-start | bytes 1572872 | tf_op jit(solution)/shard_map/ppermute | solution.py:472
  806.5 28.3 %collective-permute-start.38 = (bf16[4,256,2048]{2,1,0:T(8,128)(2,1)}, bf16[4,256,2048]{2,1,0:T(8,128)(2,1)}, u32[]{:S(2)}, u32[]{:S(2)}) collective-permute-start(bf16[4,256,2048]{2,1,0:T(8,128)(2,1)} %slice.336), channel_id=1, source_target_pairs={{0,4},{4,0},{8,12},{12,8},{16,20},{20,16},{24,28},{28,24},{1,5},{5... | collective-permute-start | bytes 12582920 | tf_op jit(solution)/shard_map/ppermute | solution.py:472
  807.6 8.1 collective-permute-start.53
  809.8 20.6 %collective-permute-start.49 = (bf16[4,256,1536]{2,1,0:T(8,128)(2,1)}, bf16[4,256,1536]{2,1,0:T(8,128)(2,1)}, u32[]{:S(2)}, u32[]{:S(2)}) collective-permute-start(bf16[4,256,1536]{2,1,0:T(8,128)(2,1)} %slice.303), channel_id=1, source_target_pairs={{0,4},{4,0},{8,12},{12,8},{16,20},{20,16},{24,28},{28,24},{1,5},{5... | collective-permute-start | bytes 9437192 | tf_op jit(solution)/shard_map/ppermute | solution.py:472
  833.3 63.9 %collective-permute-start.50 = (bf16[2,256,1536]{2,1,0:T(8,128)(2,1)S(1)}, bf16[2,256,1536]{2,1,0:T(8,128)(2,1)}, u32[]{:S(2)}, u32[]{:S(2)}) collective-permute-start(bf16[2,256,1536]{2,1,0:T(8,128)(2,1)S(1)} %slice.345), channel_id=1, source_target_pairs={{0,16},{4,20},{8,24},{12,28},{16,0},{20,4},{24,8},{28,12},{1,17},{... | collective-permute-start | bytes 4718600 | tf_op jit(solution)/shard_map/ppermute | solution.py:472
  842.2 58.1 %collective-permute-start.39 = (bf16[2,256,2048]{2,1,0:T(8,128)(2,1)}, bf16[2,256,2048]{2,1,0:T(8,128)(2,1)S(1)}, u32[]{:S(2)}, u32[]{:S(2)}) collective-permute-start(bf16[2,256,2048]{2,1,0:T(8,128)(2,1)} %slice.338), channel_id=1, source_target_pairs={{0,8},{4,12},{8,0},{12,4},{16,24},{20,28},{24,16},{28,20},{1,9},{5... | collective-permute-start | bytes 6291464 | tf_op jit(solution)/shard_map/ppermute | solution.py:472
  842.8 18.7 %collective-permute-start.41 = (f32[24704]{0:T(1024)S(1)}, f32[24704]{0:T(1024)S(1)}, u32[]{:S(2)}, u32[]{:S(2)}) collective-permute-start(f32[24704]{0:T(1024)S(1)} %constant_dynamic-update-slice_fusion.7), channel_id=1, source_target_pairs={{0,4},{4,0},{8,12},{12,8},{16,20},{20,16},{24,28},{28,24},{1,5},{5... | collective-permute-start | bytes 296456 | tf_op jit(solution)/shard_map/ppermute | solution.py:472
  861.6 30.9 %collective-permute-start.42 = (f32[24704]{0:T(1024)S(1)}, f32[24704]{0:T(1024)S(1)}, u32[]{:S(2)}, u32[]{:S(2)}) collective-permute-start(f32[24704]{0:T(1024)S(1)} %add.387), channel_id=1, source_target_pairs={{0,8},{4,12},{8,0},{12,4},{16,24},{20,28},{24,16},{28,20},{1,9},{5... | collective-permute-start | bytes 296456 | tf_op jit(solution)/shard_map/ppermute | solution.py:472
  892.5 4.7 collective-permute-start.43
  892.8 9.9 collective-permute-start.52
  900.1 20.5 %collective-permute-start.51 = (bf16[1,256,1536]{2,1,0:T(8,128)(2,1)}, bf16[1,256,1536]{2,1,0:T(8,128)(2,1)}, u32[]{:S(2)}, u32[]{:S(2)}) collective-permute-start(bf16[1,256,1536]{2,1,0:T(8,128)(2,1)} %slice.347), channel_id=1, source_target_pairs={{0,8},{4,12},{8,0},{12,4},{16,24},{20,28},{24,16},{28,20},{1,9},{5... | collective-permute-start | bytes 2359304 | tf_op jit(solution)/shard_map/ppermute | solution.py:472
  901.2 23.9 %collective-permute-start.40 = (bf16[1,256,2048]{2,1,0:T(8,128)(2,1)S(1)}, bf16[1,256,2048]{2,1,0:T(8,128)(2,1)}, u32[]{:S(2)}, u32[]{:S(2)}) collective-permute-start(bf16[1,256,2048]{2,1,0:T(8,128)(2,1)S(1)} %slice.340), channel_id=1, source_target_pairs={{0,16},{4,20},{8,24},{12,28},{16,0},{20,4},{24,8},{28,12},{1,17},{... | collective-permute-start | bytes 3145736 | tf_op jit(solution)/shard_map/ppermute | solution.py:472
  931.4 8.5 collective-permute-start.47
  931.4 47.8 %collective-permute-start.46 = (bf16[256,512]{1,0:T(8,128)(2,1)}, bf16[256,512]{1,0:T(8,128)(2,1)S(1)}, u32[]{:S(2)}, u32[]{:S(2)}) collective-permute-start(bf16[256,512]{1,0:T(8,128)(2,1)} %get-tuple-element.374), channel_id=1, source_target_pairs={{0,3},{1,2},{2,1},{3,0},{4,7},{5,6},{6,5},{7,4},{8,11},{9,10},{10,... | collective-permute-start | bytes 786440 | tf_op jit(solution)/shard_map/ppermute | solution.py:472
  934.1 45.1 %collective-permute-start.45 = (bf16[256,512]{1,0:T(8,128)(2,1)}, bf16[256,512]{1,0:T(8,128)(2,1)}, u32[]{:S(2)}, u32[]{:S(2)}) collective-permute-start(bf16[256,512]{1,0:T(8,128)(2,1)} %get-tuple-element.375), channel_id=1, source_target_pairs={{0,2},{1,3},{2,0},{3,1},{4,6},{5,7},{6,4},{7,5},{8,10},{9,11},{10,... | collective-permute-start | bytes 786440 | tf_op jit(solution)/shard_map/ppermute | solution.py:472
  934.9 44.4 %collective-permute-start.44 = (bf16[256,512]{1,0:T(8,128)(2,1)}, bf16[256,512]{1,0:T(8,128)(2,1)}, u32[]{:S(2)}, u32[]{:S(2)}) collective-permute-start(bf16[256,512]{1,0:T(8,128)(2,1)} %get-tuple-element.373), channel_id=1, source_target_pairs={{0,1},{1,0},{2,3},{3,2},{4,5},{5,4},{6,7},{7,6},{8,9},{9,8},{10,11... | collective-permute-start | bytes 786440 | tf_op jit(solution)/shard_map/ppermute | solution.py:472
  939.9 20.2 %collective-permute-start.48 = (f32[24704]{0:T(1024)S(1)}, f32[24704]{0:T(1024)S(1)}, u32[]{:S(2)}, u32[]{:S(2)}) collective-permute-start(f32[24704]{0:T(1024)S(1)} %add.395), channel_id=1, source_target_pairs={{0,2},{1,3},{2,0},{3,1},{4,6},{5,7},{6,4},{7,5},{8,10},{9,11},{10,... | collective-permute-start | bytes 296456 | tf_op jit(solution)/shard_map/ppermute | solution.py:472
  (61 other events, 1029.8 us)
Sparse Core Ops, SparseCore 0:
  12.4 48.2 all-gather.10
  63.1 87.5 all-gather.6
  201.4 54.9 all-gather.12
  258.7 87.5 all-gather.8
  471.0 83.5 reduce-scatter.9
  585.5 83.9 reduce-scatter.11
  779.7 142.8 reduce-scatter.7

commit v3 on v2

--- a/solution.py
+++ b/solution.py
@@ -259,40 +259,45 @@
     )(rates[first_tile : first_tile + count], factors[first_tile : first_tile + count], grads, *state, *earlier)
 
 
-def grad_kernel(groups, block_ref, left_ref, *refs):
-    rights, out_ref = refs[:groups], refs[groups]
-    turned = left_ref[...].T
+def grad_kernel(chunks, parts, block_ref, *refs):
+    lefts, rights, out_ref = refs[:chunks], refs[chunks:-1], refs[-1]
+    turned = [left[...].T for left in lefts]
     lo = 0
-    for right in rights:
-        width = right.shape[1]
+    for j in range(parts):
+        mine = rights[j * chunks : (j + 1) * chunks]
+        width = mine[0].shape[1]
         step = min(512, width)
         for at in range(0, width, step):
-            out_ref[0, :, lo + at : lo + at + step] = dot_nn(turned, right[:, at : at + step]).astype(BF)
+            total = dot_nn(turned[0], mine[0][:, at : at + step])
+            for left, right in zip(turned[1:], mine[1:]):
+                total = total + dot_nn(left, right[:, at : at + step])
+            out_ref[0, :, lo + at : lo + at + step] = total.astype(BF)
         lo += width
 
 
-def grad_blocks(blocks, left, rights, edge):
+def grad_blocks(blocks, lefts, rights, edge):
     count = blocks.shape[0]
-    rows = rights[0].shape[0]
-    width = sum(right.shape[1] for right in rights)
+    rows = sum(left.shape[0] for left in lefts)
+    width = sum(right[0].shape[1] for right in rights)
+    flat = [chunk for right in rights for chunk in right]
 
     def body(*refs):
-        grad_kernel(len(rights), *refs)
+        grad_kernel(len(lefts), len(rights), *refs)
 
     return pl.pallas_call(
         body,
         grid_spec=pltpu.PrefetchScalarGridSpec(
             num_scalar_prefetch=1,
             grid=(count,),
-            in_specs=[pl.BlockSpec((rows, edge), lambda i, blocks: (0, blocks[i]))]
-            + [pl.BlockSpec(right.shape, lambda i, blocks: (0, 0)) for right in rights],
+            in_specs=[pl.BlockSpec((left.shape[0], edge), lambda i, blocks: (0, blocks[i])) for left in lefts]
+            + [pl.BlockSpec(chunk.shape, lambda i, blocks: (0, 0)) for chunk in flat],
             out_specs=pl.BlockSpec((1, edge, width), lambda i, blocks: (i, 0, 0)),
         ),
         out_shape=jax.ShapeDtypeStruct((count, edge, width), BF),
         compiler_params=pltpu.CompilerParams(vmem_limit_bytes=VMEM_CAP),
         cost_estimate=cost(2 * count * edge * width * rows / 8e14),
         name="grad_blocks",
-    )(blocks, left, *rights)
+    )(blocks, *lefts, *flat)
 
 
 def matmul_kernel(terms, *refs):
@@ -303,13 +308,11 @@
     out_ref[...] = total.astype(BF)
 
 
-def matmul_sum(lefts, rights, first=0, rows=None):
+def matmul_sum(lefts, rights):
     terms = len(lefts)
-    depth = lefts[0].shape[1]
-    rows = rows or lefts[0].shape[0]
+    rows, depth = lefts[0].shape
     columns = rights[0].shape[0]
     row_step, step = min(1024, rows), min(512, columns)
-    offset = first // row_step
 
     def body(*refs):
         matmul_kernel(terms, *refs)
@@ -317,7 +320,7 @@
     return pl.pallas_call(
         body,
         grid=(rows // row_step, columns // step),
-        in_specs=[pl.BlockSpec((row_step, depth), lambda m, n: (m + offset, 0))] * terms
+        in_specs=[pl.BlockSpec((row_step, depth), lambda m, n: (m, 0))] * terms
         + [pl.BlockSpec((step, depth), lambda m, n: (n, 0))] * terms,
         out_specs=pl.BlockSpec((row_step, step), lambda m, n: (m, n)),
         out_shape=jax.ShapeDtypeStruct((rows, columns), BF),
@@ -414,9 +417,11 @@
     )(*tables, source)
 
 
-def project_kernel(sources, pick_ref, *refs):
-    pieces = refs[:sources]
-    gain_ref, shift_ref, weight_ref, bias_ref, normal_out, normed_out, out_ref = refs[sources:]
+def project_kernel(sources, *refs):
+    pick_ref = refs[0]
+    pieces = refs[2 : 2 + sources]
+    gain_ref, shift_ref, weight_ref, bias_ref = refs[2 + sources : 6 + sources]
+    normal_out, normed_out, out_ref = refs[-3:]
     picked = pick_ref[pl.program_id(0)]
     for i in range(sources):
 
@@ -429,7 +434,7 @@
     out_ref[...] = (dot_nn(normed, weight_ref[...]) + bias_ref[...]).astype(BF)
 
 
-def project(pick, pieces, gain, shift_by, weight, bias):
+def project(pick, place, total, pieces, gain, shift_by, weight, bias, into=()):
     count = pick.shape[0]
     rows, depth = pieces[0].shape
     columns = weight.shape[1]
@@ -438,30 +443,27 @@
         project_kernel(len(pieces), *refs)
 
     def held(shape):
-        return pl.BlockSpec(shape, lambda t, pick: (0, 0), pipeline_mode=pl.Buffered(1))
+        return pl.BlockSpec(shape, lambda i, pick, place: (0, 0), pipeline_mode=pl.Buffered(1))
+
+    def block(width):
+        return pl.BlockSpec((rows, width), lambda i, pick, place: (place[i], 0))
 
     return pl.pallas_call(
         body,
         grid_spec=pltpu.PrefetchScalarGridSpec(
-            num_scalar_prefetch=1,
+            num_scalar_prefetch=2,
             grid=(count,),
             in_specs=[held((rows, depth)) for _ in pieces]
-            + [held((1, depth)), held((1, depth)), held((depth, columns)), held((1, columns))],
-            out_specs=[
-                pl.BlockSpec((rows, depth), lambda t, pick: (t, 0)),
-                pl.BlockSpec((rows, depth), lambda t, pick: (t, 0)),
-                pl.BlockSpec((rows, columns), lambda t, pick: (t, 0)),
-            ],
+            + [held((1, depth)), held((1, depth)), held((depth, columns)), held((1, columns))]
+            + [pl.BlockSpec(memory_space=pl.ANY) for _ in into],
+            out_specs=[block(depth), block(depth), block(columns)],
         ),
-        out_shape=[
-            jax.ShapeDtypeStruct((count * rows, depth), BF),
-            jax.ShapeDtypeStruct((count * rows, depth), BF),
-            jax.ShapeDtypeStruct((count * rows, columns), BF),
-        ],
+        out_shape=[jax.ShapeDtypeStruct((total * rows, width), BF) for width in (depth, depth, columns)],
+        input_output_aliases={2 + len(pieces) + 4 + k: k for k in range(len(into))},
         compiler_params=pltpu.CompilerParams(vmem_limit_bytes=VMEM_CAP),
-        cost_estimate=cost(2e-5),
+        cost_estimate=cost(count * 6e-6),
         name="project",
-    )(pick, *pieces, gain[None], shift_by[None], weight, bias[None])
+    )(pick, place, *pieces, gain[None], shift_by[None], weight, bias[None], *into)
 
 
 def sync(*values):
@@ -474,6 +476,19 @@
 
 def move(value, axis, pairs):
     return lax.ppermute(value, axis, pairs)
+
+
+def beside(value, axis, mask, steps, state):
+    total, rows = sum(share for share, _ in steps), value.shape[0]
+    pieces, done, first = [], 0, 0
+    for share, work in steps:
+        done += share
+        last = rows // 16 * done // total * 16
+        pieces.append(shift(value[first:last], axis, mask))
+        first = last
+        state = work(state)
+        state, pieces, value = sync(state, pieces, value)
+    return jnp.concatenate(pieces, axis=0), state
 
 
 def add_low(left, right):
@@ -602,7 +617,9 @@
     pair_slots = jnp.arange(dp_count, dtype=jnp.int32) ^ core
 
     def gather_ffn(value):
-        value = lax.all_gather(value, "dp", axis=0, tiled=True, axis_index_groups=same_core)
+        return lax.all_gather(value, "dp", axis=0, tiled=True, axis_index_groups=same_core)
+
+    def scatter_ffn(value):
         return scatter_blocks([held_blocks[2][pair_slots], held_blocks[3][pair_slots]], value)
 
     def gather_all(kind, value):
@@ -613,28 +630,43 @@
         return [(i, i ^ mask) for i in range(tp_count) if ((i ^ (i >> 1)) & 1) == odd]
 
     w_qkv = gather_all(0, own_qkv)
-    w_first = gather_ffn(pair)
-    far_first, outs = [], []
+    bias_mixed = jnp.stack(
+        [bias_q.reshape(heads, HD), jnp.zeros((heads, HD), F32), bias_v.reshape(heads, HD)], axis=1
+    ).reshape(3 * width)
+    distance = jnp.arange(tp_count, dtype=jnp.int32) - place
+    by_distance = jnp.argsort(jnp.abs(distance)).astype(jnp.int32)
+    offset = by_distance - place
+    outs = [shift(own_out, "tensor", j) for j in range(1, tp_count)]
+    far_first, first_raw, out_raw = [], None, None
     for step in range(1, tp_count):
         if step > 1:
             below.append(move(below[-1], "tensor", ups[step - 1 :]))
             above.append(move(above[-1], "tensor", downs[: tp_count - step]))
-        if step == 2:
-            outs = [shift(own_out, "tensor", j) for j in range(1, tp_count)]
         if step == tp_count - 1:
+            first_raw = gather_ffn(pair)
             far_first = [move(pair, "tensor", crossed(2 * j, 0)) for j in range(1, slices)]
-            above, below, far_first, outs, pair, w_qkv = sync(above, below, far_first, outs, pair, w_qkv)
+            w_out = scatter_blocks([held_blocks[1]], out_raw)[0]
+            pick = jnp.where(offset < 0, -offset, jnp.where(offset > 0, tp_count - 2 + offset, 0))
+            sources = [normal] + below[:-1] + above[:-1]
+            projected = project(
+                pick[:-1], by_distance[:-1], tp_count, sources, gain_one, shift_one, w_qkv, bias_mixed
+            )
+            above, below, far_first, pair, w_qkv, w_out, projected = sync(
+                above, below, far_first, pair, w_qkv, w_out, projected
+            )
+        elif step == 1:
+            above, below, outs, own_out, pair = sync(above, below, outs, own_out, pair)
+            out_raw = lax.all_gather(jnp.concatenate([own_out] + outs, axis=1), "dp", axis=0, tiled=False)
         else:
-            above, below, outs, own_out, pair = sync(above, below, outs, own_out, pair)
-
-    bias_mixed = jnp.stack(
-        [bias_q.reshape(heads, HD), jnp.zeros((heads, HD), F32), bias_v.reshape(heads, HD)], axis=1
-    ).reshape(3 * width)
-    line = jnp.arange(tp_count, dtype=jnp.int32) - place
-    pick = jnp.where(line < 0, -line, jnp.where(line > 0, tp_count - 1 + line, 0))
-    normal_all, normed_all, qkv = project(pick, [normal] + below + above, gain_one, shift_one, w_qkv, bias_mixed)
+            above, below, pair = sync(above, below, pair)
+
+    reach = tp_count // 2
+    pick = jnp.where(offset < 0, -offset - reach, tp_count - 1 + offset - 2 * reach + 1)
+    sources = below[reach - 1 :] + above[reach - 1 :]
+    normal_all, normed_all, qkv = project(
+        pick[-1:], by_distance[-1:], tp_count, sources, gain_one, shift_one, w_qkv, bias_mixed, projected
+    )
     far_second = [move(pair, "tensor", crossed(2 * j, 1)) for j in range(1, slices)]
-    w_out = gather_all(1, jnp.concatenate([own_out] + outs, axis=1))
 
     ends = jnp.cumsum(lengths[0])
     spot = jnp.arange(SEQ, dtype=jnp.int32) - PROMPT
@@ -642,91 +674,167 @@
     start_rows = jnp.where(spot < 0, 0, PROMPT + started).astype(jnp.int32)[None]
     attended, peaks = attend(start_rows, qkv)
     others = range(1, slices)
+    peak_row = lax.dynamic_update_slice(
+        jnp.zeros((dp_count * H,), F32), peaks[:, 0, 0], (me * H + place * heads,)
+    )
     attended, far_second = sync(attended, far_second)
 
     def rows_of(value, j):
         return lax.dynamic_slice_in_dim(value, (place ^ j) * rows, rows, 0)
 
+    def with_core(value):
+        return jnp.concatenate([value, shift(value, "dp", 1)], axis=0)
+
     attended_rows = jnp.concatenate(
         [rows_of(attended, 0)] + [shift(rows_of(attended, j), "tensor", j) for j in range(1, tp_count)], axis=1
     )
-    w_far = [gather_ffn(left + right) for left, right in zip(far_first, far_second)]
-    attended_rows, w_out, w_first, cotangent = sync(attended_rows, w_out, w_first, cotangent)
-    peak_row = lax.dynamic_update_slice(
-        jnp.zeros((dp_count * H,), F32), peaks[:, 0, 0], (me * H + place * heads,)
-    )
+    far_raw = [gather_ffn(left + right) for left, right in zip(far_first, far_second)]
+    w_first = scatter_ffn(first_raw)
+    back_near = with_core(cotangent)
+    attended_rows, w_first, cotangent, back_near, w_out = sync(attended_rows, w_first, cotangent, back_near, w_out)
     hidden_rows = token_rows + dot_nt(attended_rows, w_out) + bias_o
     normed_two = layer_norm(hidden_rows, gain_two, shift_two).astype(BF)
 
-    normed_across = shift(normed_two, "tensor", 1)
-    normed_sibling = shift(normed_two, "dp", 1)
-    back_sibling = shift(cotangent, "dp", 1)
-    normed_across, normed_sibling, back_sibling, cotangent, w_far = sync(
-        normed_across, normed_sibling, back_sibling, cotangent, w_far
-    )
-    normed_four = jnp.concatenate(
-        [normed_two, normed_sibling, normed_across, shift(normed_across, "dp", 1)], axis=0
-    )
-    w_up = [w_first[0]] + [value[0] for value in w_far]
-    w_down = [w_first[1]] + [value[1] for value in w_far]
-
-    parts = slices + 1
-    marks = [16 * (rows // 16 * i // parts) for i in range(parts + 1)]
-    back_pieces, activations, slopes = [], [], []
-    for j in range(parts):
-        back_pieces.append(shift(cotangent[marks[j] : marks[j + 1]], "tensor", 1))
-        if j < slices:
-            pre_act = jnp.dot(normed_four, w_up[j], preferred_element_type=F32) + bias_up[j * half : (j + 1) * half]
-            activation, slope = gelu_pair(pre_act)
-            activations.append(activation.astype(BF))
-            slopes.append(slope.astype(BF))
-        else:
-            result_far = matmul_sum(activations, w_down, 2 * rows, 2 * rows)
-            result_far, activations = sync(result_far, activations)
-        activations, slopes, back_pieces, cotangent = sync(activations, slopes, back_pieces, cotangent)
-    back_across = jnp.concatenate(back_pieces, axis=0)
-    back_four = jnp.concatenate([cotangent, back_sibling, back_across, shift(back_across, "dp", 1)], axis=0)
+    w_up, w_down = [w_first[0]], [w_first[1]]
+    biases = [bias_up[j * half : (j + 1) * half] for j in range(slices)]
 
     def core_rows(partial):
         return add_low(partial[:rows], shift(partial[rows:], "dp", 1))
-
-    ffn_far = core_rows(result_far)
-    blocks_down = grad_blocks(held_blocks[3][pair_slots], back_four, activations, edge)
-    blocks_down, ffn_far, back_four = sync(blocks_down, ffn_far, back_four)
 
     def chips_sum(blocks):
         blocks = blocks.reshape(dp_count // 2, 2, edge, blocks.shape[2])
         return lax.psum_scatter(blocks, "dp", scatter_dimension=0, tiled=False, axis_index_groups=same_core)
 
-    grads_pre, ffn_pieces = [], []
-    for j in range(parts):
-        ffn_pieces.append(shift(ffn_far[marks[j] : marks[j + 1]], "tensor", 1))
-        if j < slices:
-            grad_act = jnp.dot(back_four, w_down[j], preferred_element_type=F32)
-            grads_pre.append((grad_act * slopes[j].astype(F32)).astype(BF))
-        else:
-            grad_normed = matmul_sum(grads_pre, w_up)
-            grad_normed, grads_pre = sync(grad_normed, grads_pre)
-        grads_pre, ffn_pieces, ffn_far = sync(grads_pre, ffn_pieces, ffn_far)
-    ffn_across = jnp.concatenate(ffn_pieces, axis=0)
-    far_rows = core_rows(grad_normed[2 * rows :])
-    far_rows, grads_pre, activations = sync(far_rows, grads_pre, activations)
+    pending = [("dp", 1 << bit) for bit in range(dp_count.bit_length() - 1)]
+    pending += [("tensor", 1 << bit) for bit in range(1, tp_count.bit_length() - 1)]
+
+    def with_peaks(work):
+        def both(state):
+            if pending:
+                state = dict(state, peaks=state["peaks"] + shift(state["peaks"], *pending.pop(0)))
+            return work(state)
+
+        return both
+
+    def near_back(j):
+        def work(state):
+            if j > 0:
+                up, down = scatter_ffn(state.pop("far_raw"))
+                w_up.append(up)
+                w_down.append(down)
+            grad_act = jnp.dot(state["back_near"], w_down[j], preferred_element_type=F32).astype(BF)
+            state = dict(state, grad_act=grad_act)
+            if j == 0:
+                state["normed_near"] = with_core(state.pop("normed"))
+            return state
+
+        return work
+
+    def near_up(j):
+        def work(state):
+            pre_act = jnp.dot(state["normed_near"], w_up[j], preferred_element_type=F32) + biases[j]
+            activation, slope = gelu_pair(pre_act)
+            low = (state["grad_act"].astype(F32) * slope).astype(BF)
+            if j + 1 < slices:
+                state = dict(state, far_raw=far_raw[j])
+            return dict(state, act_near=state["act_near"] + [activation.astype(BF)], pre_near=state["pre_near"] + [low])
+
+        return work
+
+    def far_up(j):
+        def work(state):
+            pre_act = jnp.dot(state["normed_far"], w_up[j], preferred_element_type=F32) + biases[j]
+            activation, slope = gelu_pair(pre_act)
+            return dict(state, act_far=state["act_far"] + [activation.astype(BF)], slopes=state["slopes"] + [slope.astype(BF)])
+
+        return work
+
+    def far_result(state):
+        return dict(state, result_far=matmul_sum(state["act_far"], w_down))
+
+    def near_grad(state):
+        return dict(
+            state, grad_near=matmul_sum(state["pre_near"], w_up), ffn_far=core_rows(state.pop("result_far"))
+        )
+
+    def down_blocks(state):
+        rights = [list(pair) for pair in zip(state["act_near"], state["act_far"])]
+        blocks = grad_blocks(held_blocks[3][pair_slots], [state["back_near"], state["back_far"]], rights, edge)
+        return dict(state, down=blocks)
+
+    def far_back(j):
+        def work(state):
+            grad_act = jnp.dot(state["back_far"], w_down[j], preferred_element_type=F32)
+            low = (grad_act * state["slopes"][j].astype(F32)).astype(BF)
+            return dict(state, pre_far=state["pre_far"] + [low])
+
+        return work
+
+    def far_grad(state):
+        return dict(state, grad_far=matmul_sum(state["pre_far"], w_up))
+
+    def up_blocks(state):
+        rights = [list(pair) for pair in zip(state["pre_near"], state["pre_far"])]
+        blocks = grad_blocks(held_blocks[2][pair_slots], [state["normed_near"], state["normed_far"]], rights, edge)
+        return dict(state, up=blocks)
+
+    def near_result(state):
+        return dict(
+            state, result_near=matmul_sum(state["act_near"], w_down), near_rows=core_rows(state.pop("grad_near"))
+        )
+
+    state = dict(
+        back_near=back_near, peaks=peak_row, normed=normed_two, act_near=[], pre_near=[], act_far=[], pre_far=[], slopes=[]
+    )
+    steps = [(1, with_peaks(work)) for j in range(slices) for work in (near_back(j), near_up(j))]
+    normed_across, state = beside(normed_two, "tensor", 1, steps, state)
+    state["normed_far"] = with_core(normed_across)
+    steps = [(1, with_peaks(far_up(j))) for j in range(slices)]
+    steps += [(slices, with_peaks(far_result)), (slices, with_peaks(near_grad))]
+    back_across, state = beside(cotangent, "tensor", 1, steps, state)
+    state["back_far"] = with_core(back_across)
     middle = rows // 2
-    far_low = shift(far_rows[:middle], "tensor", 1)
-    blocks_up = grad_blocks(held_blocks[2][pair_slots], normed_four, grads_pre, edge)
-    far_low, blocks_up, far_rows, activations = sync(far_low, blocks_up, far_rows, activations)
-    far_high = shift(far_rows[middle:], "tensor", 1)
-    near_rows = core_rows(grad_normed[: 2 * rows])
-    result = matmul_sum(activations, w_down, 0, 2 * rows)
-    far_high, near_rows, result = sync(far_high, near_rows, result)
-    part_down, part_up = chips_sum(blocks_down), chips_sum(blocks_up)
-    grad_two = near_rows.astype(F32) + jnp.concatenate([far_low, far_high], axis=0).astype(F32)
-
+    ffn_low, state = beside(state["ffn_far"][:middle], "tensor", 1, [(1, down_blocks)], state)
+    part_down = chips_sum(state.pop("down"))
+    steps = [(1, far_back(j)) for j in range(slices)] + [(slices, far_grad)]
+    ffn_high, state = beside(state.pop("ffn_far")[middle:], "tensor", 1, steps, state)
+    ffn_across = jnp.concatenate([ffn_low, ffn_high], axis=0)
+    far_rows = core_rows(state.pop("grad_far"))
+    state["far_rows"] = far_rows
+    state = sync(state)[0]
+    cut = rows // 16 * 5 // 8 * 16
+    low_rows, state = beside(state["far_rows"][:cut], "tensor", 1, [(1, up_blocks)], state)
+    part_up = chips_sum(state.pop("up"))
+    high_rows, state = beside(state.pop("far_rows")[cut:], "tensor", 1, [(1, near_result)], state)
+    low_rows, high_rows, part_down, state = sync(low_rows, high_rows, part_down, state)
+    peak_rows = state["peaks"]
+    grad_two = state["near_rows"].astype(F32) + jnp.concatenate([low_rows, high_rows], axis=0).astype(F32)
+    result, grads_pre = state["result_near"], list(zip(state["pre_near"], state["pre_far"]))
+
+    def far_slices(part):
+        return part[:, :, :half], [part[:, :, j * half : (j + 1) * half] for j in others]
+
+    def to_owners(values):
+        return [shift(value, "tensor", 2 * j) for j, value in zip(others, values)]
+
+    order_far = halving_order(chips, far)
+
+    def half_slots(order):
+        return jnp.array([2 * q + 1 for q in order] + [2 * q for q in order], jnp.int32)
+
+    own_down, far_down = far_slices(part_down)
+    down_low = to_owners([value[:1] for value in far_down])
     grad_part, grad_gain_two, grad_shift_two = layer_norm_back(hidden_rows, gain_two, grad_two)
     grad_hidden = cotangent.astype(F32) + grad_part
     branch = grad_hidden.astype(BF)
+    even = jnp.arange(0, dp_count, 2, dtype=jnp.int32)
+    out_slots = jnp.concatenate([even + 1 - core, even + core])
+    grads_out = grad_blocks(held_blocks[1][out_slots], [branch], [[attended_rows]], edge)
     grad_attended_rows = jnp.dot(branch, w_out, preferred_element_type=F32).astype(BF)
-    grad_attended_rows, branch, result, grads_pre = sync(grad_attended_rows, branch, result, grads_pre)
+    peak_rows = peak_rows + shift(peak_rows, "tensor", 1)
+    grad_attended_rows, branch, result, grads_pre, grads_out, down_low, far_down, peak_rows = sync(
+        grad_attended_rows, branch, result, grads_pre, grads_out, down_low, far_down, peak_rows
+    )
 
     arrived = [
         grad_attended_rows[:, j * width : (j + 1) * width]
@@ -737,11 +845,10 @@
     grad_attended = jnp.zeros((SEQ, width), BF)
     for j in range(tp_count):
         grad_attended = lax.dynamic_update_slice_in_dim(grad_attended, arrived[j], (place ^ j) * rows, 0)
-    ffn_near = core_rows(result)
-    grad_attended, branch, ffn_near, part_down, part_up = sync(grad_attended, branch, ffn_near, part_down, part_up)
-
-    def far_slices(part):
-        return part[:, :, :half], [part[:, :, j * half : (j + 1) * half] for j in others]
+    sum_out = halve(grads_out, [1])
+    grad_attended, branch, result, part_up, far_down, grads_pre, sum_out = sync(
+        grad_attended, branch, result, part_up, far_down, grads_pre, sum_out
+    )
 
     def far_sum(kept, arrived):
         total = kept.astype(F32)
@@ -750,33 +857,31 @@
         total = total.astype(BF)
         return join_halves(total[0], shift(total[1], "dp", 1))
 
-    order_near, order_far = halving_order(chips, near), halving_order(chips, far)
-
-    def half_slots(order):
-        return jnp.array([2 * q + 1 for q in order] + [2 * q for q in order], jnp.int32)
-
+    sum_out = lax.psum_scatter(sum_out, "dp", scatter_dimension=0, tiled=False, axis_index_groups=same_core)
+    own_up, far_up = far_slices(part_up)
+    down_high = to_owners([value[1:] for value in far_down])
+    up_low = to_owners([value[:1] for value in far_up])
     grad_qkv_rows = attend_back(start_rows, qkv, grad_attended)
-    own_down, far_down = far_slices(part_down)
-    own_up, far_up = far_slices(part_up)
-    far_down = [shift(value, "tensor", 2 * j) for j, value in zip(others, far_down)]
-    grad_qkv_rows, far_down, far_up, branch = sync(grad_qkv_rows, far_down, far_up, branch)
-
-    up_low = [shift(value[:1], "tensor", 2 * j) for j, value in zip(others, far_up)]
+    grad_qkv_rows, down_high, up_low, far_up, branch, grads_pre = sync(
+        grad_qkv_rows, down_high, up_low, far_up, branch, grads_pre
+    )
+    up_high = to_owners([value[1:] for value in far_up])
     partial = dot_nt(grad_qkv_rows, w_qkv).astype(BF)
-    partial, up_low, far_up, grad_qkv_rows = sync(partial, up_low, far_up, grad_qkv_rows)
-    up_high = [shift(value[1:], "tensor", 2 * j) for j, value in zip(others, far_up)]
-    grads_qkv = grad_blocks(block_of[0][half_slots(order_far)], normed_all, [grad_qkv_rows], edge)
-    partial, up_high, grads_qkv, branch = sync(partial, up_high, grads_qkv, branch)
+    partial, up_high, grad_qkv_rows, branch, grads_pre, sum_out = sync(
+        partial, up_high, grad_qkv_rows, branch, grads_pre, sum_out
+    )
+    far_down = [jnp.concatenate(value, axis=0) for value in zip(down_low, down_high)]
     far_up = [jnp.concatenate(value, axis=0) for value in zip(up_low, up_high)]
     grad_normed_one = lax.psum_scatter(partial, "tensor", scatter_dimension=0, tiled=True).astype(F32)
 
-    grads_out = grad_blocks(block_of[1][half_slots(order_near)], branch, [attended_rows], edge)
+    grads_qkv = grad_blocks(block_of[0][half_slots(order_far)], [normed_all], [[grad_qkv_rows]], edge)
+    grads_qkv, grad_qkv_rows, branch, grads_pre, partial = sync(grads_qkv, grad_qkv_rows, branch, grads_pre, partial)
     column_sums = jnp.sum(grad_qkv_rows, axis=0, dtype=F32).reshape(heads, 3, HD)
     head_sums = lambda part: lax.dynamic_update_slice(
         jnp.zeros((D,), F32), column_sums[:, part].reshape(width), (place * width,)
     )
     partial_wide = partial.astype(F32)
-    grad_bias_up = jnp.concatenate([jnp.sum(value, axis=0, dtype=F32) for value in grads_pre])
+    grad_bias_up = jnp.concatenate([sum(jnp.sum(value, axis=0, dtype=F32) for value in pair) for pair in grads_pre])
     wide = jnp.zeros((FF,), F32)
     for j in range(slices):
         wide = lax.dynamic_update_slice(wide, grad_bias_up[j * half : (j + 1) * half], (hidden_starts[j],))
@@ -791,22 +896,23 @@
             grad_gain_two,
             grad_shift_two,
             wide,
-            peak_row,
         ]
     )
+    sum_qkv = halve(grads_qkv, [1])
     totals = axis_sum(totals, "dp")
-    sum_qkv = halve(halve(grads_qkv, [1]), far)[0]
-    sum_out = halve(halve(grads_out, [1]), near)[0]
+    totals, sum_qkv = sync(totals, sum_qkv)
+    sum_qkv = halve(sum_qkv, far)[0]
     sum_down = far_sum(own_down, far_down)
     sum_up = far_sum(own_up, far_up)
+    ffn_near = core_rows(result)
     outputs = (hidden_rows + ffn_near.astype(F32) + ffn_across.astype(F32) + bias_two).astype(BF)
-    grad_normed_one, sum_out, totals = sync(grad_normed_one, sum_out, totals)
-    totals = axis_sum(totals, "tensor")
-    grad_small = totals[: 8 * D + FF]
-    peak_all = jnp.max(totals[8 * D + FF :].reshape(dp_count, H), axis=0)
+    peak_all = jnp.max(peak_rows.reshape(dp_count, H), axis=0)
+    grad_normed_one, totals, sum_out = sync(grad_normed_one, totals, sum_out)
+    grad_small = axis_sum(totals, "tensor")
+    outs = [shift(sum_out[:, j * width : (j + 1) * width], "tensor", j) for j in range(1, tp_count)]
     total_out = sum_out[:, :width].astype(F32)
-    for j in range(1, tp_count):
-        total_out = total_out + shift(sum_out[:, j * width : (j + 1) * width], "tensor", j).astype(F32)
+    for value in outs:
+        total_out = total_out + value.astype(F32)
     sum_out = total_out.astype(BF)
     rows_part, _, _ = layer_norm_back(token_rows, gain_one, grad_normed_one)
     input_grad = (grad_hidden + rows_part).astype(BF)

time: 1000 us -> 934 us (0.934)
  waiting for transfers between devices: 343 us -> 262 us
  starting transfers between devices: 76.9 us -> 88 us
  other arithmetic: 91.5 us -> 81.1 us
  Pallas kernels: 316 us -> 326 us
    ppermute x46 -> x55, waiting for transfers between devices: 247 us -> 194 us  [shift(): lax.ppermute(value, axis, [(i, i ^ mask) for i in range(lax.axis_size(axi...]
    all_gather x2, waiting for transfers between devices: 17.2 us -> 0.01 us  [gather_ffn(): lax.all_gather(value, 'dp', axis=0, tiled=True, axis_index_groups=same_core)]
    ppermute x8, waiting for transfers between devices: 78.2 us -> 62.4 us  [move(): return lax.ppermute(value, axis, pairs)]
    ppermute x46 -> x55, starting transfers between devices: 48 us -> 59.3 us  [shift(): lax.ppermute(value, axis, [(i, i ^ mask) for i in range(lax.axis_size(axi...]
    unnamed x145 -> x173, local copies, waits for them, and re-layouts: 16.5 us -> 6.45 us
    convert_element_type x8 -> x7, other arithmetic: 20.2 us -> 14.6 us  [add_low(): return (left.astype(F32) + right.astype(F32)).astype(BF)]
    dot_general x4 -> x8, matrix products: 56.6 us -> 62.3 us  [the longest x2 16.7 us: work(): grad_act = jnp.dot(state['back_far'], w_down[j], preferred_element_type=F32)]
    pallas_call x1 -> x2, Pallas kernels: 24.5 us -> 30.1 us  [project(): pl.pallas_call(body, grid_spec=pltpu.PrefetchScalarGridSpec(num_scalar_pr...]
  transfers between devices with their start and end apart: 61 -> 71, of which waited for: 27 -> 28; matrix products, arithmetic and copies ran while one was open for 23% -> 24% of each run, Pallas kernels for 28% -> 33%
where the time goes in v3:
time: 934 us; the launch traced here: 926 us
  Pallas kernels  326 us (35%)
  waiting for transfers between devices  262 us (28%)
  matrix products  92.8 us (10%)
  starting transfers between devices  88 us (9%)
  other arithmetic  81.1 us (9%)
  local copies, waits for them, and re-layouts  60.1 us (6%)
  between operations  16.2 us (2%)
    ppermute x55, waiting for transfers between devices, shift(): lax.ppermute(value, axis, [(i, i ^ mask) for i in range(lax.axis_size(axi...  194 us
    pallas_call x4, Pallas kernels, grad_blocks(): pl.pallas_call(body, grid_spec=pltpu.PrefetchScalarGridSpec(num_scalar_pr...  80.9 us
    ppermute x8, waiting for transfers between devices, move(): return lax.ppermute(value, axis, pairs)  62.4 us
    ppermute x55, starting transfers between devices, shift(): lax.ppermute(value, axis, [(i, i ^ mask) for i in range(lax.axis_size(axi...  59.3 us
    pallas_call x4, Pallas kernels, matmul_sum(): pl.pallas_call(body, grid=(rows // row_step, columns // step), in_specs=[...  54.9 us
    pallas_call x4, Pallas kernels, update_tiles(): pl.pallas_call(body, grid=(count // group,), in_specs=[smem, smem, pl.Blo...  52.3 us
    pallas_call x1, Pallas kernels, attend_back(): pl.pallas_call(attend_back_kernel, grid=(heads,), in_specs=[pl.BlockSpec(...  43.3 us
    pallas_call x4, Pallas kernels, scatter_blocks(): pl.pallas_call(body, grid_spec=pltpu.PrefetchScalarGridSpec(num_scalar_pr...  38.3 us
  transfers between devices with their start and end apart: 71, of which 28 were waited for; matrix products, arithmetic and copies ran while one was open for 24% of the time, Pallas kernels for 33%

profile of v3, /device:TPU:0, one launch (start us, length us, event | category | flops | bytes accessed | tf_op | source)
XLA Modules:
  0.0 925.7 jit_solution(16486756824931114408)
XLA Ops:
  7.2 5.2 pack_weights.1
  16.7 7.0 collective-permute-start.1
  30.0 47.4 %collective-permute-done.2 = bf16[256,512]{1,0:T(8,128)(2,1)S(1)} collective-permute-done((bf16[256,512]{1,0:T(8,128)(2,1)S(1)}, bf16[256,512]{1,0:T(8,128)(2,1)S(1)}, u32[]{:S(2)}, u32[]{:S(2)}) %collective-permute-start.2) | collective-permute-done | bytes 262176 | tf_op jit(solution)/shard_map/ppermute | solution.py:474
  77.4 8.0 collective-permute-done.3
  89.9 49.6 %collective-permute-done.6.refs_6_.refs_4_ = bf16[512,2048]{1,0:T(8,128)(2,1)} collective-permute-done((bf16[512,2048]{1,0:T(8,128)(2,1)}, bf16[512,2048]{1,0:T(8,128)(2,1)}, u32[]{:S(2)}, u32[]{:S(2)}) %collective-permute-start.6) | collective-permute-done | bytes 2097184 | tf_op jit(solution)/shard_map/ppermute | solution.py:478
  142.9 11.7 %collective-permute-start.10 = (bf16[2,256,2048]{2,1,0:T(8,128)(2,1)}, bf16[2,256,2048]{2,1,0:T(8,128)(2,1)}, u32[]{:S(2)}, u32[]{:S(2)}) collective-permute-start(bf16[2,256,2048]{2,1,0:T(8,128)(2,1)} %pad_maximum_fusion.2), channel_id=1, source_target_pairs={{0,2},{3,1},{4,6},{7,5},{8,10},{11,9},{12,14},{15,13},{16,18},{19,... | collective-permute-start | bytes 6291464 | tf_op jit(solution)/shard_map/ppermute | solution.py:478
  157.8 8.6 scatter_blocks.4.refs_9_.refs_8_
  166.4 18.6 %project.2 = (bf16[2048,2048]{1,0:T(8,128)(2,1)}, bf16[2048,2048]{1,0:T(8,128)(2,1)}, bf16[2048,1536]{1,0:T(8,128)(2,1)}) custom-call(s32[3]{0:T(128)} %bitcast.218, s32[3]{0:T(128)} %bitcast.217, bf16[512,2048]{1,0:T(8,128)(2,1)} %fusion.5.refs_2_, bf16[512,2048]{1,0:T(8,128)(2,1)} %collective-permute-done.1.refs_3_, ...), custom_call_target="tpu_custom_call" | custom-call | bytes 63000000 | tf_op jit(solution)/shard_map/project/pallas_call | solution.py:451
  185.1 9.9 %scatter_blocks.5 = bf16[2048,2048]{1,0:T(8,128)(2,1)} custom-call(s32[8]{0:T(128)} %get-tuple-element.712.refs_0_, bf16[8,256,2048]{2,1,0:T(8,128)(2,1)} %bitcast.189), custom_call_target="tpu_custom_call" | custom-call | bytes 19573418 | tf_op jit(solution)/shard_map/scatter_blocks/pallas_call | solution.py:405
  199.6 11.5 %project.3 = (bf16[2048,2048]{1,0:T(8,128)(2,1)}, bf16[2048,2048]{1,0:T(8,128)(2,1)}, bf16[2048,1536]{1,0:T(8,128)(2,1)}) custom-call(s32[1]{0:T(128)} %slice.252.refs_0_, s32[1]{0:T(128)} %slice.253.refs_1_, bf16[512,2048]{1,0:T(8,128)(2,1)} %collective-permute-done.7.refs_4_.refs_2_, ...), custom_call_target="tpu_custom_call", output_to_operand_aliasing={{0}: (10, {}), {1}: (11, {}), {2}: (12, {})} | custom-call | bytes 21000000 | tf_op jit(solution)/shard_map/project/pallas_call | solution.py:451
  211.1 20.9 %attend.1 = (bf16[2048,512]{1,0:T(8,128)(2,1)}, f32[4,8,128]{2,1,0:T(8,128)}) custom-call(s32[1,2048]{1,0:T(1,128)} %compare_select_fusion.start_ref, bf16[2048,1536]{1,0:T(8,128)(2,1)} %get-tuple-element.363.qkv_ref), custom_call_target="tpu_custom_call" | custom-call | bytes 70000000 | tf_op jit(solution)/shard_map/attend/pallas_call | solution.py:91
  232.0 11.6 %collective-permute-done.11 = bf16[2,256,2048]{2,1,0:T(8,128)(2,1)} collective-permute-done((bf16[2,256,2048]{2,1,0:T(8,128)(2,1)}, bf16[2,256,2048]{2,1,0:T(8,128)(2,1)}, u32[]{:S(2)}, u32[]{:S(2)}) %collective-permute-start.11) | collective-permute-done | bytes 2097184 | tf_op jit(solution)/shard_map/ppermute | solution.py:478
  243.6 4.4 add.448
  258.7 5.0 pad_maximum_fusion.refs_1_
  263.7 9.7 %scatter_blocks.6 = (bf16[2048,1024]{1,0:T(8,128)(2,1)}, bf16[2048,1024]{1,0:T(8,128)(2,1)}) custom-call(s32[8]{0:T(128)} %gather_fusion, s32[8]{0:T(128)} %gather_fusion.1, bf16[8,256,2048]{2,1,0:T(8,128)(2,1)} %all-gather.7.cloned.1.call-done.refs_2_), custom_call_target="tpu_custom_call" | custom-call | bytes 19573418 | tf_op jit(solution)/shard_map/scatter_blocks/pallas_call | solution.py:405
  273.3 24.7 %collective-permute-done.13 = bf16[512,512]{1,0:T(8,128)(2,1)} collective-permute-done((bf16[512,512]{1,0:T(8,128)(2,1)}, bf16[512,512]{1,0:T(8,128)(2,1)}, u32[]{:S(2)}, u32[]{:S(2)}) %collective-permute-start.13) | collective-permute-done | bytes 524320 | tf_op jit(solution)/shard_map/ppermute | solution.py:474
  299.6 7.9 fusion.57
  314.0 8.0 convolution_convert_fusion.3
  324.3 3.7 collective-permute-done.18
  329.9 7.9 fusion.18
  337.7 4.8 collective-permute-done.20
  342.6 10.2 %scatter_blocks.7 = (bf16[2048,1024]{1,0:T(8,128)(2,1)}, bf16[2048,1024]{1,0:T(8,128)(2,1)}) custom-call(s32[8]{0:T(128)} %gather_fusion, s32[8]{0:T(128)} %gather_fusion.1, bf16[8,256,2048]{2,1,0:T(8,128)(2,1)} %all-gather.9.cloned.1.call-done.refs_2_), custom_call_target="tpu_custom_call" | custom-call | bytes 19573418 | tf_op jit(solution)/shard_map/scatter_blocks/pallas_call | solution.py:405
  355.0 7.0 convolution_convert_fusion.2
  362.1 4.1 collective-permute-done.22
  368.9 7.7 fusion.24
  383.3 7.5 fusion.29
  391.7 7.5 fusion.34
  401.6 13.8 %matmul_sum.4 = bf16[1024,2048]{1,0:T(8,128)(2,1)} custom-call(bf16[1024,1024]{1,0:T(8,128)(2,1)} %get-tuple-element.461.refs_0_.refs_4_, bf16[1024,1024]{1,0:T(8,128)(2,1)} %get-tuple-element.462.refs_1_.refs_6_, bf16[2048,1024]{1,0:T(8,128)(2,1)} %get-tuple-element.374.refs_2_, bf16[2048,1024]{1,0:T(8,128)(2,1)} %get-tuple-element.388.refs_3_), custom_call_target="tpu_custom_call" | custom-call | bytes 37580964 | tf_op jit(solution)/shard_map/matmul_sum/pallas_call | solution.py:320
  421.8 13.8 %matmul_sum.5 = bf16[1024,2048]{1,0:T(8,128)(2,1)} custom-call(bf16[1024,1024]{1,0:T(8,128)(2,1)} %get-tuple-element.611.refs_0_.refs_3_, bf16[1024,1024]{1,0:T(8,128)(2,1)} %get-tuple-element.613.refs_1_.refs_5_, bf16[2048,1024]{1,0:T(8,128)(2,1)} %get-tuple-element.377.refs_2_, bf16[2048,1024]{1,0:T(8,128)(2,1)} %get-tuple-element.397.refs_3_), custom_call_target="tpu_custom_call" | custom-call | bytes 37580964 | tf_op jit(solution)/shard_map/matmul_sum/pallas_call | solution.py:320
  446.4 24.7 %grad_blocks.4 = bf16[8,256,2048]{2,1,0:T(8,128)(2,1)} custom-call(s32[8]{0:T(128)} %gather_fusion.1, bf16[1024,2048]{1,0:T(8,128)(2,1)} %pad_maximum_fusion.refs_1_, bf16[1024,2048]{1,0:T(8,128)(2,1)} %copy-done.30, bf16[1024,1024]{1,0:T(8,128)(2,1)} %get-tuple-element.540.refs_3_.refs_0_, bf16[1024,1024]{1,0:T(8,128)(2,1)} %get-tuple-element.461.refs_0_.refs_4_, ...), custom_call_target="tpu_custom_call" | custom-call | bytes 75161928 | tf_op jit(solution)/shard_map/grad_blocks/pallas_call | solution.py:287
  472.1 11.0 %multiply_convert_fusion.1.refs_0_.refs_4_ = bf16[1024,1024]{1,0:T(8,128)(2,1)} fusion(bf16[1024,1024]{1,0:T(8,128)(2,1)} %get-tuple-element.486, bf16[1024,2048]{1,0:T(8,128)(2,1)} %copy-done.30, bf16[2048,1024]{1,0:T(8,128)(2,1)} %get-tuple-element.374.refs_2_), kind=kOutput, calls=%fused_computation.70 | convolution fusion | flops 4298113024 | bytes 12582912 | tf_op jit(solution)/shard_map/dot_general | solution.py:767
  484.7 5.7 multiply_convert_fusion.refs_1_.refs_6_
  492.9 13.4 %matmul_sum.6 = bf16[1024,2048]{1,0:T(8,128)(2,1)} custom-call(bf16[1024,1024]{1,0:T(8,128)(2,1)} %multiply_convert_fusion.1.refs_0_.refs_4_, bf16[1024,1024]{1,0:T(8,128)(2,1)} %multiply_convert_fusion.refs_1_.refs_6_, bf16[2048,1024]{1,0:T(8,128)(2,1)} %get-tuple-element.377.refs_2_, bf16[2048,1024]{1,0:T(8,128)(2,1)} %get-tuple-element.397.refs_3_), custom_call_target="tpu_custom_call" | custom-call | bytes 37580964 | tf_op jit(solution)/shard_map/matmul_sum/pallas_call | solution.py:320
  508.6 4.1 collective-permute-done.36
  514.9 24.8 %grad_blocks.5 = bf16[8,256,2048]{2,1,0:T(8,128)(2,1)} custom-call(s32[8]{0:T(128)} %gather_fusion, bf16[1024,2048]{1,0:T(8,128)(2,1)} %copy-done.19, bf16[1024,2048]{1,0:T(8,128)(2,1)} %copy-done.29, bf16[1024,1024]{1,0:T(8,128)(2,1)} %get-tuple-element.611.refs_0_.refs_3_, bf16[1024,1024]{1,0:T(8,128)(2,1)} %multiply_convert_fusion.1.refs_0_.refs_4_, ...), custom_call_target="tpu_custom_call" | custom-call | bytes 75161928 | tf_op jit(solution)/shard_map/grad_blocks/pallas_call | solution.py:287
  539.6 5.1 collective-permute-done.37
  544.8 3.2 slice.287
  551.1 13.9 %matmul_sum.7 = bf16[1024,2048]{1,0:T(8,128)(2,1)} custom-call(bf16[1024,1024]{1,0:T(8,128)(2,1)} %get-tuple-element.540.refs_3_.refs_0_, bf16[1024,1024]{1,0:T(8,128)(2,1)} %get-tuple-element.541.refs_5_.refs_1_, bf16[2048,1024]{1,0:T(8,128)(2,1)} %get-tuple-element.374.refs_2_, bf16[2048,1024]{1,0:T(8,128)(2,1)} %get-tuple-element.388.refs_3_), custom_call_target="tpu_custom_call" | custom-call | bytes 37580964 | tf_op jit(solution)/shard_map/matmul_sum/pallas_call | solution.py:320
  572.6 4.6 multiply_reduce_fusion
  577.3 5.3 fusion.47
  582.5 4.8 convolution_convert_fusion.1
  587.5 11.0 %grad_blocks.6 = bf16[8,256,2048]{2,1,0:T(8,128)(2,1)} custom-call(s32[8]{0:T(128)} %gather_fusion.2, bf16[512,2048]{1,0:T(8,128)(2,1)} %copy-done.6, bf16[512,2048]{1,0:T(8,128)(2,1)} %copy-done.28), custom_call_target="tpu_custom_call" | custom-call | bytes 18790480 | tf_op jit(solution)/shard_map/grad_blocks/pallas_call | solution.py:287
  608.4 20.8 %collective-permute-done.42 = bf16[512,512]{1,0:T(8,128)(2,1)S(1)} collective-permute-done((bf16[512,512]{1,0:T(8,128)(2,1)S(1)}, bf16[512,512]{1,0:T(8,128)(2,1)S(1)}, u32[]{:S(2)}, u32[]{:S(2)}) %collective-permute-start.42) | collective-permute-done | bytes 524320 | tf_op jit(solution)/shard_map/ppermute | solution.py:474
  630.0 12.7 %collective-permute-done.43 = bf16[512,512]{1,0:T(8,128)(2,1)S(1)} collective-permute-done((bf16[512,512]{1,0:T(8,128)(2,1)S(1)}, bf16[512,512]{1,0:T(8,128)(2,1)S(1)}, u32[]{:S(2)}, u32[]{:S(2)}) %collective-permute-start.43) | collective-permute-done | bytes 524320 | tf_op jit(solution)/shard_map/ppermute | solution.py:474
  644.4 4.0 add_convert_fusion
  648.8 11.5 %collective-permute-start.47 = (bf16[1,256,1024]{2,1,0:T(8,128)(2,1)S(1)}, bf16[1,256,1024]{2,1,0:T(8,128)(2,1)}, u32[]{:S(2)}, u32[]{:S(2)}) collective-permute-start(bf16[1,256,1024]{2,1,0:T(8,128)(2,1)S(1)} %slice.300), channel_id=1, source_target_pairs={{0,2},{1,3},{2,0},{3,1},{4,6},{5,7},{6,4},{7,5},{8,10},{9,11},{10,... | collective-permute-start | bytes 1572872 | tf_op jit(solution)/shard_map/ppermute | solution.py:474
  663.7 43.3 %attend_back.1.refs_2_ = bf16[2048,1536]{1,0:T(8,128)(2,1)} custom-call(s32[1,2048]{1,0:T(1,128)} %compare_select_fusion.start_ref, bf16[2048,1536]{1,0:T(8,128)(2,1)} %get-tuple-element.363.qkv_ref, bf16[2048,512]{1,0:T(8,128)(2,1)} %constant_dynamic-update-slice_fusion.19.back_ref), custom_call_target="tpu_custom_call" | custom-call | bytes 140000000 | tf_op jit(solution)/shard_map/attend_back/pallas_call | solution.py:146
  710.6 17.7 %convolution_convert_fusion = bf16[2048,2048]{1,0:T(8,128)(2,1)} fusion(bf16[2048,1536]{1,0:T(8,128)(2,1)} %attend_back.1.refs_2_, bf16[2048,1536]{1,0:T(8,128)(2,1)S(1)} %bitcast.179), kind=kOutput, calls=%fused_computation.10 | convolution fusion | flops 12889096192 | bytes 20971520 | tf_op jit(solution)/shard_map/dot_general | solution.py:31
  728.3 4.9 collective-permute-done.49
  735.9 20.4 %grad_blocks.7 = bf16[8,256,1536]{2,1,0:T(8,128)(2,1)} custom-call(s32[8]{0:T(128)} %gather_fusion.4, bf16[2048,2048]{1,0:T(8,128)(2,1)} %get-tuple-element.600.refs_1_, bf16[2048,1536]{1,0:T(8,128)(2,1)} %attend_back.1.refs_2_), custom_call_target="tpu_custom_call" | custom-call | bytes 56371444 | tf_op jit(solution)/shard_map/grad_blocks/pallas_call | solution.py:287
  757.3 3.8 slice.308
  761.8 10.6 %convert_reduce_fusion = (f32[2048]{0:T(1024)S(1)}, f32[2048]{0:T(1024)S(1)}) fusion(bf16[2048,2048]{1,0:T(8,128)(2,1)} %convolution_convert_fusion, bf16[2048,2048]{1,0:T(8,128)(2,1)} %get-tuple-element.610), kind=kLoop, calls=%fused_computation.5 | loop fusion | flops 20967424 | bytes 16793600 | tf_op jit(solution)/shard_map/reduce_sum | solution.py:895
  777.6 3.3 slice.298
  786.8 4.1 collective-permute-done.52
  800.8 17.0 %update_tiles.4 = (f32[96,128,128]{2,1,0:T(8,128)}, f32[96,128,128]{2,1,0:T(8,128)}, f32[96,128,128]{2,1,0:T(8,128)}, bf16[96,128,128]{2,1,0:T(8,128)(2,1)}, f32...) custom-call(f32[32]{0:T(128)} %get-tuple-element.714.refs_0_, ...), custom_call_target="tpu_custom_call" | custom-call | bytes 56000000 | tf_op jit(solution)/shard_map/update_tiles/pallas_call | solution.py:247
  819.6 9.8 %collective-permute-done.57 = bf16[2,256,1536]{2,1,0:T(8,128)(2,1)} collective-permute-done((bf16[2,256,1536]{2,1,0:T(8,128)(2,1)S(1)}, bf16[2,256,1536]{2,1,0:T(8,128)(2,1)}, u32[]{:S(2)}, u32[]{:S(2)}) %collective-permute-start.57) | collective-permute-done | bytes 1572896 | tf_op jit(solution)/shard_map/ppermute | solution.py:474
  831.9 3.9 add_convert_fusion.2
  837.7 16.1 %update_tiles.5 = (f32[96,128,128]{2,1,0:T(8,128)}, f32[96,128,128]{2,1,0:T(8,128)}, f32[96,128,128]{2,1,0:T(8,128)}, bf16[96,128,128]{2,1,0:T(8,128)(2,1)}, f32...) custom-call(f32[32]{0:T(128)} %get-tuple-element.715.refs_0_, ...), custom_call_target="tpu_custom_call", output_to_operand_aliasing={{0}: (10, {}), {1}: (11, {}), {2}: (12, {}), {3}: (13, {}),... | custom-call | bytes 56000000 | tf_op jit(solution)/shard_map/update_tiles/pallas_call | solution.py:247
  856.2 13.0 %update_tiles.6 = (f32[96,128,128]{2,1,0:T(8,128)}, f32[96,128,128]{2,1,0:T(8,128)}, f32[96,128,128]{2,1,0:T(8,128)}, bf16[96,128,128]{2,1,0:T(8,128)(2,1)}, f32...) custom-call(f32[24]{0:T(128)} %bitcast.216, ...), custom_call_target="tpu_custom_call", output_to_operand_aliasing={{0}: (10, {}), {1}: (11, {}), {2}: (12, {}), {3}: (13, {}),... | custom-call | bytes 42000000 | tf_op jit(solution)/shard_map/update_tiles/pallas_call | solution.py:247
  869.3 5.6 reduce-scatter.11.cloned.1.call-done
  879.6 3.5 collective-permute-start.56
  884.0 3.3 collective-permute-start.62
  890.2 18.9 %collective-permute-done.62 = f32[24576]{0:T(1024)S(1)} collective-permute-done((f32[24576]{0:T(1024)S(1)}, f32[24576]{0:T(1024)S(1)}, u32[]{:S(2)}, u32[]{:S(2)}) %collective-permute-start.62) | collective-permute-done | bytes 98336 | tf_op jit(solution)/shard_map/ppermute | solution.py:474
  912.1 6.3 update_tiles.7
  (464 shorter events, 165.8 us)
Async XLA Ops:
  7.2 150.6 %all-gather.11.cloned.1.call-start = ((), (), s32[]{:S(2)}) async-start(), calls=%async_computation.7 | async-start | bytes 7077888 | tf_op jit(solution)/shard_map/all_gather | solution.py:626
  12.4 172.6 %all-gather.13.cloned.1.call-start = ((), (), s32[]{:S(2)}) async-start(), calls=%async_computation.8 | async-start | bytes 9437184 | tf_op jit(solution)/shard_map/all_gather | solution.py:659
  15.4 70.0 %collective-permute-start = (bf16[512,2048]{1,0:T(8,128)(2,1)}, bf16[512,2048]{1,0:T(8,128)(2,1)}, u32[]{:S(2)}, u32[]{:S(2)}) collective-permute-start(bf16[512,2048]{1,0:T(8,128)(2,1)} %fusion.5.refs_2_), channel_id=1, source_target_pairs={{1,0},{2,1},{3,2},{5,4},{6,5},{7,6},{9,8},{10,9},{11,10},{13,12},{... | collective-permute-start | bytes 6291464 | tf_op jit(solution)/shard_map/ppermute | solution.py:478
  16.7 68.7 %collective-permute-start.1 = (bf16[512,2048]{1,0:T(8,128)(2,1)}, bf16[512,2048]{1,0:T(8,128)(2,1)}, u32[]{:S(2)}, u32[]{:S(2)}) collective-permute-start(bf16[512,2048]{1,0:T(8,128)(2,1)} %fusion.5.refs_2_), channel_id=1, source_target_pairs={{0,1},{1,2},{2,3},{4,5},{5,6},{6,7},{8,9},{9,10},{10,11},{12,13},{... | collective-permute-start | bytes 6291464 | tf_op jit(solution)/shard_map/ppermute | solution.py:478
  24.0 53.4 %collective-permute-start.2 = (bf16[256,512]{1,0:T(8,128)(2,1)S(1)}, bf16[256,512]{1,0:T(8,128)(2,1)S(1)}, u32[]{:S(2)}, u32[]{:S(2)}) collective-permute-start(bf16[256,512]{1,0:T(8,128)(2,1)S(1)} %copy-done.46), channel_id=1, source_target_pairs={{0,1},{1,0},{2,3},{3,2},{4,5},{5,4},{6,7},{7,6},{8,9},{9,8},{10,11... | collective-permute-start | bytes 786440 | tf_op jit(solution)/shard_map/ppermute | solution.py:474
  24.7 60.7 %collective-permute-start.3 = (bf16[256,512]{1,0:T(8,128)(2,1)S(1)}, bf16[256,512]{1,0:T(8,128)(2,1)S(1)}, u32[]{:S(2)}, u32[]{:S(2)}) collective-permute-start(bf16[256,512]{1,0:T(8,128)(2,1)S(1)} %copy-done.46), channel_id=1, source_target_pairs={{0,2},{1,3},{2,0},{3,1},{4,6},{5,7},{6,4},{7,5},{8,10},{9,11},{10,... | collective-permute-start | bytes 786440 | tf_op jit(solution)/shard_map/ppermute | solution.py:474
  27.1 58.3 %collective-permute-start.4 = (bf16[256,512]{1,0:T(8,128)(2,1)S(1)}, bf16[256,512]{1,0:T(8,128)(2,1)S(1)}, u32[]{:S(2)}, u32[]{:S(2)}) collective-permute-start(bf16[256,512]{1,0:T(8,128)(2,1)S(1)} %copy-done.46), channel_id=1, source_target_pairs={{0,3},{1,2},{2,1},{3,0},{4,7},{5,6},{6,5},{7,4},{8,11},{9,10},{10,... | collective-permute-start | bytes 786440 | tf_op jit(solution)/shard_map/ppermute | solution.py:474
  86.6 177.1 %all-gather.7.cloned.1.call-start = ((), (), s32[]{:S(2)}) async-start(), calls=%async_computation.4 | async-start | bytes 10485760 | tf_op jit(solution)/shard_map/all_gather | solution.py:620
  86.6 52.9 %collective-permute-start.6 = (bf16[512,2048]{1,0:T(8,128)(2,1)}, bf16[512,2048]{1,0:T(8,128)(2,1)}, u32[]{:S(2)}, u32[]{:S(2)}) collective-permute-start(bf16[512,2048]{1,0:T(8,128)(2,1)} %collective-permute-done.refs_5_), channel_id=1, source_target_pairs={{1,0},{2,1},{5,4},{6,5},{9,8},{10,9},{13,12},{14,13},{17,16},{18,1... | collective-permute-start | bytes 6291464 | tf_op jit(solution)/shard_map/ppermute | solution.py:478
  87.9 51.6 %collective-permute-start.7 = (bf16[512,2048]{1,0:T(8,128)(2,1)}, bf16[512,2048]{1,0:T(8,128)(2,1)}, u32[]{:S(2)}, u32[]{:S(2)}) collective-permute-start(bf16[512,2048]{1,0:T(8,128)(2,1)} %collective-permute-done.1.refs_3_), channel_id=1, source_target_pairs={{1,2},{2,3},{5,6},{6,7},{9,10},{10,11},{13,14},{14,15},{17,18},{18... | collective-permute-start | bytes 6291464 | tf_op jit(solution)/shard_map/ppermute | solution.py:478
  139.6 203.0 %all-gather.9.cloned.1.call-start = ((), (), s32[]{:S(2)}) async-start(), calls=%async_computation.5 | async-start | bytes 10485760 | tf_op jit(solution)/shard_map/all_gather | solution.py:620
  139.6 55.3 %collective-permute-start.8 = (bf16[512,2048]{1,0:T(8,128)(2,1)}, bf16[512,2048]{1,0:T(8,128)(2,1)}, u32[]{:S(2)}, u32[]{:S(2)}) collective-permute-start(bf16[512,2048]{1,0:T(8,128)(2,1)} %collective-permute-done.6.refs_6_.refs_4_), channel_id=1, source_target_pairs={{1,0},{5,4},{9,8},{13,12},{17,16},{21,20},{25,24},{29,28}} | collective-permute-start | bytes 6291464 | tf_op jit(solution)/shard_map/ppermute | solution.py:478
  140.9 54.0 %collective-permute-start.9 = (bf16[512,2048]{1,0:T(8,128)(2,1)}, bf16[512,2048]{1,0:T(8,128)(2,1)}, u32[]{:S(2)}, u32[]{:S(2)}) collective-permute-start(bf16[512,2048]{1,0:T(8,128)(2,1)} %collective-permute-done.7.refs_4_.refs_2_), channel_id=1, source_target_pairs={{2,3},{6,7},{10,11},{14,15},{18,19},{22,23},{26,27},{30,31}} | collective-permute-start | bytes 6291464 | tf_op jit(solution)/shard_map/ppermute | solution.py:478
  142.9 53.3 %collective-permute-start.10 = (bf16[2,256,2048]{2,1,0:T(8,128)(2,1)}, bf16[2,256,2048]{2,1,0:T(8,128)(2,1)}, u32[]{:S(2)}, u32[]{:S(2)}) collective-permute-start(bf16[2,256,2048]{2,1,0:T(8,128)(2,1)} %pad_maximum_fusion.2), channel_id=1, source_target_pairs={{0,2},{3,1},{4,6},{7,5},{8,10},{11,9},{12,14},{15,13},{16,18},{19,... | collective-permute-start | bytes 6291464 | tf_op jit(solution)/shard_map/ppermute | solution.py:478
  196.2 47.4 %collective-permute-start.11 = (bf16[2,256,2048]{2,1,0:T(8,128)(2,1)}, bf16[2,256,2048]{2,1,0:T(8,128)(2,1)}, u32[]{:S(2)}, u32[]{:S(2)}) collective-permute-start(bf16[2,256,2048]{2,1,0:T(8,128)(2,1)} %pad_maximum_fusion.2), channel_id=1, source_target_pairs={{1,3},{2,0},{5,7},{6,4},{9,11},{10,8},{13,15},{14,12},{17,19},{18,... | collective-permute-start | bytes 6291464 | tf_op jit(solution)/shard_map/ppermute | solution.py:478
  248.0 321.1 %reduce-scatter.13.cloned.1.call-start = ((), (), s32[]{:S(2)}) async-start(), calls=%async_computation.9 | async-start | bytes 10485760
  248.5 10.2 %collective-permute-start.15 = (bf16[512,2048]{1,0:T(8,128)(2,1)}, bf16[512,2048]{1,0:T(8,128)(2,1)}, u32[]{:S(2)}, u32[]{:S(2)}) collective-permute-start(bf16[512,2048]{1,0:T(8,128)(2,1)} %param.16), channel_id=1, source_target_pairs={{0,4},{4,0},{8,12},{12,8},{16,20},{20,16},{24,28},{28,24},{1,5},{5... | collective-permute-start | bytes 6291464 | tf_op jit(solution)/shard_map/ppermute | solution.py:474
  251.2 22.1 %collective-permute-start.14 = (bf16[512,512]{1,0:T(8,128)(2,1)}, bf16[512,512]{1,0:T(8,128)(2,1)}, u32[]{:S(2)}, u32[]{:S(2)}) collective-permute-start(bf16[512,512]{1,0:T(8,128)(2,1)} %get-tuple-element.686), channel_id=1, source_target_pairs={{0,3},{1,2},{2,1},{3,0},{4,7},{5,6},{6,5},{7,4},{8,11},{9,10},{10,... | collective-permute-start | bytes 1572872 | tf_op jit(solution)/shard_map/ppermute | solution.py:474
  253.1 44.9 %collective-permute-start.13 = (bf16[512,512]{1,0:T(8,128)(2,1)}, bf16[512,512]{1,0:T(8,128)(2,1)}, u32[]{:S(2)}, u32[]{:S(2)}) collective-permute-start(bf16[512,512]{1,0:T(8,128)(2,1)} %get-tuple-element.687), channel_id=1, source_target_pairs={{0,2},{1,3},{2,0},{3,1},{4,6},{5,7},{6,4},{7,5},{8,10},{9,11},{10,... | collective-permute-start | bytes 1572872 | tf_op jit(solution)/shard_map/ppermute | solution.py:474
  253.1 44.9 %collective-permute-start.12 = (bf16[512,512]{1,0:T(8,128)(2,1)S(1)}, bf16[512,512]{1,0:T(8,128)(2,1)}, u32[]{:S(2)}, u32[]{:S(2)}) collective-permute-start(bf16[512,512]{1,0:T(8,128)(2,1)S(1)} %get-tuple-element.688), channel_id=1, source_target_pairs={{0,1},{1,0},{2,3},{3,2},{4,5},{5,4},{6,7},{7,6},{8,9},{9,8},{10,11... | collective-permute-start | bytes 1572872 | tf_op jit(solution)/shard_map/ppermute | solution.py:474
  309.6 12.4 %collective-permute-start.16 = (bf16[512,2048]{1,0:T(8,128)(2,1)S(1)}, bf16[512,2048]{1,0:T(8,128)(2,1)}, u32[]{:S(2)}, u32[]{:S(2)}) collective-permute-start(bf16[512,2048]{1,0:T(8,128)(2,1)S(1)} %add_convert_fusion.7), channel_id=1, source_target_pairs={{0,4},{4,0},{8,12},{12,8},{16,20},{20,16},{24,28},{28,24},{1,5},{5... | collective-permute-start | bytes 6291464 | tf_op jit(solution)/shard_map/ppermute | solution.py:474
  313.9 14.1 %collective-permute-start.18 = (bf16[128,2048]{1,0:T(8,128)(2,1)S(1)}, bf16[128,2048]{1,0:T(8,128)(2,1)S(1)}, u32[]{:S(2)}, u32[]{:S(2)}) collective-permute-start(bf16[128,2048]{1,0:T(8,128)(2,1)S(1)} %slice.346), channel_id=1, source_target_pairs={{0,1},{1,0},{2,3},{3,2},{4,5},{5,4},{6,7},{7,6},{8,9},{9,8},{10,11... | collective-permute-start | bytes 1572872 | tf_op jit(solution)/shard_map/ppermute | solution.py:474
  328.0 9.7 %collective-permute-start.19 = (f32[128]{0:T(128)S(1)}, f32[128]{0:T(128)S(1)}, u32[]{:S(2)}, u32[]{:S(2)}) collective-permute-start(f32[128]{0:T(128)S(1)} %add_dynamic-update-slice_fusion.2), channel_id=1, source_target_pairs={{0,8},{4,12},{8,0},{12,4},{16,24},{20,28},{24,16},{28,20},{1,9},{5... | collective-permute-start | bytes 1544 | tf_op jit(solution)/shard_map/ppermute | solution.py:474
  329.5 13.1 %collective-permute-start.20 = (bf16[128,2048]{1,0:T(8,128)(2,1)S(1)}, bf16[128,2048]{1,0:T(8,128)(2,1)S(1)}, u32[]{:S(2)}, u32[]{:S(2)}) collective-permute-start(bf16[128,2048]{1,0:T(8,128)(2,1)S(1)} %slice.269), channel_id=1, source_target_pairs={{0,1},{1,0},{2,3},{3,2},{4,5},{5,4},{6,7},{7,6},{8,9},{9,8},{10,11... | collective-permute-start | bytes 1572872 | tf_op jit(solution)/shard_map/ppermute | solution.py:474
  352.8 9.3 %collective-permute-start.21 = (f32[128]{0:T(128)S(1)}, f32[128]{0:T(128)S(1)}, u32[]{:S(2)}, u32[]{:S(2)}) collective-permute-start(f32[128]{0:T(128)S(1)} %add.449), channel_id=1, source_target_pairs={{0,16},{4,20},{8,24},{12,28},{16,0},{20,4},{24,8},{28,12},{1,17},{... | collective-permute-start | bytes 1544 | tf_op jit(solution)/shard_map/ppermute | solution.py:474
  354.3 11.9 %collective-permute-start.22 = (bf16[128,2048]{1,0:T(8,128)(2,1)S(1)}, bf16[128,2048]{1,0:T(8,128)(2,1)S(1)}, u32[]{:S(2)}, u32[]{:S(2)}) collective-permute-start(bf16[128,2048]{1,0:T(8,128)(2,1)S(1)} %slice.270), channel_id=1, source_target_pairs={{0,1},{1,0},{2,3},{3,2},{4,5},{5,4},{6,7},{7,6},{8,9},{9,8},{10,11... | collective-permute-start | bytes 1572872 | tf_op jit(solution)/shard_map/ppermute | solution.py:474
  366.2 10.4 %collective-permute-start.23 = (f32[128]{0:T(128)S(1)}, f32[128]{0:T(128)S(1)}, u32[]{:S(2)}, u32[]{:S(2)}) collective-permute-start(f32[128]{0:T(128)S(1)} %add.451), channel_id=1, source_target_pairs={{0,2},{1,3},{2,0},{3,1},{4,6},{5,7},{6,4},{7,5},{8,10},{9,11},{10,... | collective-permute-start | bytes 1544 | tf_op jit(solution)/shard_map/ppermute | solution.py:474
  367.7 11.0 %collective-permute-start.24 = (bf16[128,2048]{1,0:T(8,128)(2,1)S(1)}, bf16[128,2048]{1,0:T(8,128)(2,1)S(1)}, u32[]{:S(2)}, u32[]{:S(2)}) collective-permute-start(bf16[128,2048]{1,0:T(8,128)(2,1)S(1)} %slice.271), channel_id=1, source_target_pairs={{0,1},{1,0},{2,3},{3,2},{4,5},{5,4},{6,7},{7,6},{8,9},{9,8},{10,11... | collective-permute-start | bytes 1572872 | tf_op jit(solution)/shard_map/ppermute | solution.py:474
  379.0 11.8 %collective-permute-start.26 = (bf16[80,2048]{1,0:T(8,128)(2,1)S(1)}, bf16[80,2048]{1,0:T(8,128)(2,1)S(1)}, u32[]{:S(2)}, u32[]{:S(2)}) collective-permute-start(bf16[80,2048]{1,0:T(8,128)(2,1)S(1)} %slice.272), channel_id=1, source_target_pairs={{0,1},{1,0},{2,3},{3,2},{4,5},{5,4},{6,7},{7,6},{8,9},{9,8},{10,11... | collective-permute-start | bytes 983048 | tf_op jit(solution)/shard_map/ppermute | solution.py:474
  390.9 9.8 %collective-permute-start.27 = (bf16[80,2048]{1,0:T(8,128)(2,1)S(1)}, bf16[80,2048]{1,0:T(8,128)(2,1)S(1)}, u32[]{:S(2)}, u32[]{:S(2)}) collective-permute-start(bf16[80,2048]{1,0:T(8,128)(2,1)S(1)} %slice.273), channel_id=1, source_target_pairs={{0,1},{1,0},{2,3},{3,2},{4,5},{5,4},{6,7},{7,6},{8,9},{9,8},{10,11... | collective-permute-start | bytes 983048 | tf_op jit(solution)/shard_map/ppermute | solution.py:474
  400.7 17.4 %collective-permute-start.28 = (bf16[176,2048]{1,0:T(8,128)(2,1)S(1)}, bf16[176,2048]{1,0:T(8,128)(2,1)S(1)}, u32[]{:S(2)}, u32[]{:S(2)}) collective-permute-start(bf16[176,2048]{1,0:T(8,128)(2,1)S(1)} %slice.274), channel_id=1, source_target_pairs={{0,1},{1,0},{2,3},{3,2},{4,5},{5,4},{6,7},{7,6},{8,9},{9,8},{10,11... | collective-permute-start | bytes 2162696 | tf_op jit(solution)/shard_map/ppermute | solution.py:474
  420.0 15.6 %collective-permute-start.29 = (bf16[512,2048]{1,0:T(8,128)(2,1)S(1)}, bf16[512,2048]{1,0:T(8,128)(2,1)}, u32[]{:S(2)}, u32[]{:S(2)}) collective-permute-start(bf16[512,2048]{1,0:T(8,128)(2,1)S(1)} %slice.276), channel_id=1, source_target_pairs={{0,4},{4,0},{8,12},{12,8},{16,20},{20,16},{24,28},{28,24},{1,5},{5... | collective-permute-start | bytes 6291464 | tf_op jit(solution)/shard_map/ppermute | solution.py:474
  421.0 18.7 %collective-permute-start.30 = (bf16[176,2048]{1,0:T(8,128)(2,1)}, bf16[176,2048]{1,0:T(8,128)(2,1)S(1)}, u32[]{:S(2)}, u32[]{:S(2)}) collective-permute-start(bf16[176,2048]{1,0:T(8,128)(2,1)} %slice.277), channel_id=1, source_target_pairs={{0,1},{1,0},{2,3},{3,2},{4,5},{5,4},{6,7},{7,6},{8,9},{9,8},{10,11... | collective-permute-start | bytes 2162696 | tf_op jit(solution)/shard_map/ppermute | solution.py:474
  441.2 30.0 %collective-permute-start.32 = (bf16[256,2048]{1,0:T(8,128)(2,1)}, bf16[256,2048]{1,0:T(8,128)(2,1)}, u32[]{:S(2)}, u32[]{:S(2)}) collective-permute-start(bf16[256,2048]{1,0:T(8,128)(2,1)} %slice.278), channel_id=1, source_target_pairs={{0,1},{1,0},{2,3},{3,2},{4,5},{5,4},{6,7},{7,6},{8,9},{9,8},{10,11... | collective-permute-start | bytes 3145736 | tf_op jit(solution)/shard_map/ppermute | solution.py:474
  471.1 177.3 %reduce-scatter.15.cloned.1.call-start = ((), (), s32[]{:S(2)}) async-start(), calls=%async_computation.10 | async-start | bytes 10485760
  471.3 11.9 %collective-permute-start.33 = (bf16[64,2048]{1,0:T(8,128)(2,1)S(1)}, bf16[64,2048]{1,0:T(8,128)(2,1)S(1)}, u32[]{:S(2)}, u32[]{:S(2)}) collective-permute-start(bf16[64,2048]{1,0:T(8,128)(2,1)S(1)} %slice.279), channel_id=1, source_target_pairs={{0,1},{1,0},{2,3},{3,2},{4,5},{5,4},{6,7},{7,6},{8,9},{9,8},{10,11... | collective-permute-start | bytes 786440 | tf_op jit(solution)/shard_map/ppermute | solution.py:474
  483.2 7.8 collective-permute-start.34
  491.7 14.6 %collective-permute-start.35 = (bf16[128,2048]{1,0:T(8,128)(2,1)S(1)}, bf16[128,2048]{1,0:T(8,128)(2,1)S(1)}, u32[]{:S(2)}, u32[]{:S(2)}) collective-permute-start(bf16[128,2048]{1,0:T(8,128)(2,1)S(1)} %slice.282), channel_id=1, source_target_pairs={{0,1},{1,0},{2,3},{3,2},{4,5},{5,4},{6,7},{7,6},{8,9},{9,8},{10,11... | collective-permute-start | bytes 1572872 | tf_op jit(solution)/shard_map/ppermute | solution.py:474
  513.8 30.9 %collective-permute-start.37 = (bf16[320,2048]{1,0:T(8,128)(2,1)S(1)}, bf16[320,2048]{1,0:T(8,128)(2,1)S(1)}, u32[]{:S(2)}, u32[]{:S(2)}) collective-permute-start(bf16[320,2048]{1,0:T(8,128)(2,1)S(1)} %slice.285), channel_id=1, source_target_pairs={{0,1},{1,0},{2,3},{3,2},{4,5},{5,4},{6,7},{7,6},{8,9},{9,8},{10,11... | collective-permute-start | bytes 3932168 | tf_op jit(solution)/shard_map/ppermute | solution.py:474
  544.7 188.4 %reduce-scatter.17.cloned.1.call-start = ((), (), s32[]{:S(2)}) async-start(), calls=%async_computation.11 | async-start | bytes 5242880
  547.9 17.1 %collective-permute-start.38 = (bf16[512,2048]{1,0:T(8,128)(2,1)}, bf16[512,2048]{1,0:T(8,128)(2,1)}, u32[]{:S(2)}, u32[]{:S(2)}) collective-permute-start(bf16[512,2048]{1,0:T(8,128)(2,1)} %slice.287), channel_id=1, source_target_pairs={{0,4},{4,0},{8,12},{12,8},{16,20},{20,16},{24,28},{28,24},{1,5},{5... | collective-permute-start | bytes 6291464 | tf_op jit(solution)/shard_map/ppermute | solution.py:474
  548.9 20.3 %collective-permute-start.39 = (bf16[192,2048]{1,0:T(8,128)(2,1)}, bf16[192,2048]{1,0:T(8,128)(2,1)}, u32[]{:S(2)}, u32[]{:S(2)}) collective-permute-start(bf16[192,2048]{1,0:T(8,128)(2,1)} %slice.288), channel_id=1, source_target_pairs={{0,1},{1,0},{2,3},{3,2},{4,5},{5,4},{6,7},{7,6},{8,9},{9,8},{10,11... | collective-permute-start | bytes 2359304 | tf_op jit(solution)/shard_map/ppermute | solution.py:474
  570.3 28.2 %collective-permute-start.40 = (bf16[1,256,1024]{2,1,0:T(8,128)(2,1)S(1)}, bf16[1,256,1024]{2,1,0:T(8,128)(2,1)}, u32[]{:S(2)}, u32[]{:S(2)}) collective-permute-start(bf16[1,256,1024]{2,1,0:T(8,128)(2,1)S(1)} %slice.289), channel_id=1, source_target_pairs={{0,2},{1,3},{2,0},{3,1},{4,6},{5,7},{6,4},{7,5},{8,10},{9,11},{10,... | collective-permute-start | bytes 1572872 | tf_op jit(solution)/shard_map/ppermute | solution.py:474
  571.2 27.3 %collective-permute-start.41 = (f32[128]{0:T(128)S(1)}, f32[128]{0:T(128)S(1)}, u32[]{:S(2)}, u32[]{:S(2)}) collective-permute-start(f32[128]{0:T(128)S(1)} %copy-done.65), channel_id=1, source_target_pairs={{0,1},{1,0},{2,3},{3,2},{4,5},{5,4},{6,7},{7,6},{8,9},{9,8},{10,11... | collective-permute-start | bytes 1544 | tf_op jit(solution)/shard_map/ppermute | solution.py:474
  601.5 43.0 %collective-permute-start.45 = (bf16[4,256,2048]{2,1,0:T(8,128)(2,1)S(1)}, bf16[4,256,2048]{2,1,0:T(8,128)(2,1)S(1)}, u32[]{:S(2)}, u32[]{:S(2)}) collective-permute-start(bf16[4,256,2048]{2,1,0:T(8,128)(2,1)S(1)} %slice.296), channel_id=1, source_target_pairs={{0,4},{4,0},{8,12},{12,8},{16,20},{20,16},{24,28},{28,24},{1,5},{5... | collective-permute-start | bytes 12582920 | tf_op jit(solution)/shard_map/ppermute | solution.py:474
  604.0 25.2 %collective-permute-start.42 = (bf16[512,512]{1,0:T(8,128)(2,1)S(1)}, bf16[512,512]{1,0:T(8,128)(2,1)S(1)}, u32[]{:S(2)}, u32[]{:S(2)}) collective-permute-start(bf16[512,512]{1,0:T(8,128)(2,1)S(1)} %get-tuple-element.683), channel_id=1, source_target_pairs={{0,1},{1,0},{2,3},{3,2},{4,5},{5,4},{6,7},{7,6},{8,9},{9,8},{10,11... | collective-permute-start | bytes 1572872 | tf_op jit(solution)/shard_map/ppermute | solution.py:474
  604.6 38.2 %collective-permute-start.43 = (bf16[512,512]{1,0:T(8,128)(2,1)S(1)}, bf16[512,512]{1,0:T(8,128)(2,1)S(1)}, u32[]{:S(2)}, u32[]{:S(2)}) collective-permute-start(bf16[512,512]{1,0:T(8,128)(2,1)S(1)} %get-tuple-element.682), channel_id=1, source_target_pairs={{0,2},{1,3},{2,0},{3,1},{4,6},{5,7},{6,4},{7,5},{8,10},{9,11},{10,... | collective-permute-start | bytes 1572872 | tf_op jit(solution)/shard_map/ppermute | solution.py:474
  606.4 37.2 %collective-permute-start.44 = (bf16[512,512]{1,0:T(8,128)(2,1)S(1)}, bf16[512,512]{1,0:T(8,128)(2,1)S(1)}, u32[]{:S(2)}, u32[]{:S(2)}) collective-permute-start(bf16[512,512]{1,0:T(8,128)(2,1)S(1)} %get-tuple-element.681), channel_id=1, source_target_pairs={{0,3},{1,2},{2,1},{3,0},{4,7},{5,6},{6,5},{7,4},{8,11},{9,10},{10,... | collective-permute-start | bytes 1572872 | tf_op jit(solution)/shard_map/ppermute | solution.py:474
  648.5 226.3 %reduce-scatter.11.cloned.1.call-start = ((), (), s32[]{:S(2)}) async-start(), calls=%async_computation.6 | async-start | bytes 10485760 | tf_op jit(solution)/shard_map/reduce_scatter | solution.py:875
  648.8 58.2 %collective-permute-start.47 = (bf16[1,256,1024]{2,1,0:T(8,128)(2,1)S(1)}, bf16[1,256,1024]{2,1,0:T(8,128)(2,1)}, u32[]{:S(2)}, u32[]{:S(2)}) collective-permute-start(bf16[1,256,1024]{2,1,0:T(8,128)(2,1)S(1)} %slice.300), channel_id=1, source_target_pairs={{0,2},{1,3},{2,0},{3,1},{4,6},{5,7},{6,4},{7,5},{8,10},{9,11},{10,... | collective-permute-start | bytes 1572872 | tf_op jit(solution)/shard_map/ppermute | solution.py:474
  662.2 44.8 %collective-permute-start.48 = (bf16[1,256,1024]{2,1,0:T(8,128)(2,1)}, bf16[1,256,1024]{2,1,0:T(8,128)(2,1)}, u32[]{:S(2)}, u32[]{:S(2)}) collective-permute-start(bf16[1,256,1024]{2,1,0:T(8,128)(2,1)} %slice.301), channel_id=1, source_target_pairs={{0,2},{1,3},{2,0},{3,1},{4,6},{5,7},{6,4},{7,5},{8,10},{9,11},{10,... | collective-permute-start | bytes 1572872 | tf_op jit(solution)/shard_map/ppermute | solution.py:474
  707.8 25.3 %collective-permute-start.49 = (bf16[1,256,1024]{2,1,0:T(8,128)(2,1)}, bf16[1,256,1024]{2,1,0:T(8,128)(2,1)S(1)}, u32[]{:S(2)}, u32[]{:S(2)}) collective-permute-start(bf16[1,256,1024]{2,1,0:T(8,128)(2,1)} %slice.303), channel_id=1, source_target_pairs={{0,2},{1,3},{2,0},{3,1},{4,6},{5,7},{6,4},{7,5},{8,10},{9,11},{10,... | collective-permute-start | bytes 1572872 | tf_op jit(solution)/shard_map/ppermute | solution.py:474
  761.0 29.9 %collective-permute-start.53 = (bf16[4,256,1536]{2,1,0:T(8,128)(2,1)}, bf16[4,256,1536]{2,1,0:T(8,128)(2,1)}, u32[]{:S(2)}, u32[]{:S(2)}) collective-permute-start(bf16[4,256,1536]{2,1,0:T(8,128)(2,1)} %slice.308), channel_id=1, source_target_pairs={{0,4},{4,0},{8,12},{12,8},{16,20},{20,16},{24,28},{28,24},{1,5},{5... | collective-permute-start | bytes 9437192 | tf_op jit(solution)/shard_map/ppermute | solution.py:474
  775.7 5.3 collective-permute-start.50
  780.9 51.0 %collective-permute-start.46 = (bf16[512,2048]{1,0:T(8,128)(2,1)}, bf16[512,2048]{1,0:T(8,128)(2,1)}, u32[]{:S(2)}, u32[]{:S(2)}) collective-permute-start(bf16[512,2048]{1,0:T(8,128)(2,1)} %slice.298), channel_id=1, source_target_pairs={{0,4},{4,0},{8,12},{12,8},{16,20},{20,16},{24,28},{28,24},{1,5},{5... | collective-permute-start | bytes 6291464 | tf_op jit(solution)/shard_map/ppermute | solution.py:474
  786.7 11.6 %collective-permute-start.60 = (bf16[256,1024]{1,0:T(8,128)(2,1)S(1)}, bf16[256,1024]{1,0:T(8,128)(2,1)S(1)}, u32[]{:S(2)}, u32[]{:S(2)}) collective-permute-start(bf16[256,1024]{1,0:T(8,128)(2,1)S(1)} %slice_bitcast_fusion.1), channel_id=1, source_target_pairs={{0,4},{4,0},{8,12},{12,8},{16,20},{20,16},{24,28},{28,24},{1,5},{5... | collective-permute-start | bytes 1572872 | tf_op jit(solution)/shard_map/ppermute | solution.py:474
  793.8 35.6 %collective-permute-start.57 = (bf16[2,256,1536]{2,1,0:T(8,128)(2,1)S(1)}, bf16[2,256,1536]{2,1,0:T(8,128)(2,1)}, u32[]{:S(2)}, u32[]{:S(2)}) collective-permute-start(bf16[2,256,1536]{2,1,0:T(8,128)(2,1)S(1)} %slice.317), channel_id=1, source_target_pairs={{0,16},{4,20},{8,24},{12,28},{16,0},{20,4},{24,8},{28,12},{1,17},{... | collective-permute-start | bytes 4718600 | tf_op jit(solution)/shard_map/ppermute | solution.py:474
  819.6 16.3 %collective-permute-start.59 = (bf16[256,1024]{1,0:T(8,128)(2,1)S(1)}, bf16[256,1024]{1,0:T(8,128)(2,1)S(1)}, u32[]{:S(2)}, u32[]{:S(2)}) collective-permute-start(bf16[256,1024]{1,0:T(8,128)(2,1)S(1)} %slice_bitcast_fusion.3), channel_id=1, source_target_pairs={{0,4},{4,0},{8,12},{12,8},{16,20},{20,16},{24,28},{28,24},{1,5},{5... | collective-permute-start | bytes 1572872 | tf_op jit(solution)/shard_map/ppermute | solution.py:474
  831.3 22.5 %collective-permute-start.58 = (bf16[1,256,1536]{2,1,0:T(8,128)(2,1)S(1)}, bf16[1,256,1536]{2,1,0:T(8,128)(2,1)S(1)}, u32[]{:S(2)}, u32[]{:S(2)}) collective-permute-start(bf16[1,256,1536]{2,1,0:T(8,128)(2,1)S(1)} %slice.350), channel_id=1, source_target_pairs={{0,8},{4,12},{8,0},{12,4},{16,24},{20,28},{24,16},{28,20},{1,9},{5... | collective-permute-start | bytes 2359304 | tf_op jit(solution)/shard_map/ppermute | solution.py:474
  878.4 5.6 collective-permute-start.61
  879.6 31.0 %collective-permute-start.56 = (bf16[256,512]{1,0:T(8,128)(2,1)S(1)}, bf16[256,512]{1,0:T(8,128)(2,1)S(1)}, u32[]{:S(2)}, u32[]{:S(2)}) collective-permute-start(bf16[256,512]{1,0:T(8,128)(2,1)S(1)} %get-tuple-element.696), channel_id=1, source_target_pairs={{0,3},{1,2},{2,1},{3,0},{4,7},{5,6},{6,5},{7,4},{8,11},{9,10},{10,... | collective-permute-start | bytes 786440 | tf_op jit(solution)/shard_map/ppermute | solution.py:474
  883.1 27.5 %collective-permute-start.55 = (bf16[256,512]{1,0:T(8,128)(2,1)S(1)}, bf16[256,512]{1,0:T(8,128)(2,1)S(1)}, u32[]{:S(2)}, u32[]{:S(2)}) collective-permute-start(bf16[256,512]{1,0:T(8,128)(2,1)S(1)} %get-tuple-element.697), channel_id=1, source_target_pairs={{0,2},{1,3},{2,0},{3,1},{4,6},{5,7},{6,4},{7,5},{8,10},{9,11},{10,... | collective-permute-start | bytes 786440 | tf_op jit(solution)/shard_map/ppermute | solution.py:474
  883.1 27.5 %collective-permute-start.54 = (bf16[256,512]{1,0:T(8,128)(2,1)S(1)}, bf16[256,512]{1,0:T(8,128)(2,1)S(1)}, u32[]{:S(2)}, u32[]{:S(2)}) collective-permute-start(bf16[256,512]{1,0:T(8,128)(2,1)S(1)} %get-tuple-element.695), channel_id=1, source_target_pairs={{0,1},{1,0},{2,3},{3,2},{4,5},{5,4},{6,7},{7,6},{8,9},{9,8},{10,11... | collective-permute-start | bytes 786440 | tf_op jit(solution)/shard_map/ppermute | solution.py:474
  884.0 25.1 %collective-permute-start.62 = (f32[24576]{0:T(1024)S(1)}, f32[24576]{0:T(1024)S(1)}, u32[]{:S(2)}, u32[]{:S(2)}) collective-permute-start(f32[24576]{0:T(1024)S(1)} %add.505), channel_id=1, source_target_pairs={{0,2},{1,3},{2,0},{3,1},{4,6},{5,7},{6,4},{7,5},{8,10},{9,11},{10,... | collective-permute-start | bytes 294920 | tf_op jit(solution)/shard_map/ppermute | solution.py:474
  (84 other events, 1204.9 us)
Sparse Core Ops, SparseCore 0:
  12.5 48.2 all-gather.10
  86.7 60.1 all-gather.12
  149.4 87.5 all-gather.6
  248.2 87.0 all-gather.8
  471.3 83.9 reduce-scatter.12
  558.5 86.4 reduce-scatter.14
  648.6 59.9 reduce-scatter.16
  733.3 141.4 reduce-scatter.10

commit v4 on v3

--- a/solution.py
+++ b/solution.py
@@ -691,7 +691,10 @@
     far_raw = [gather_ffn(left + right) for left, right in zip(far_first, far_second)]
     w_first = scatter_ffn(first_raw)
     back_near = with_core(cotangent)
-    attended_rows, w_first, cotangent, back_near, w_out = sync(attended_rows, w_first, cotangent, back_near, w_out)
+    peak_rows = axis_sum(peak_row, "dp")
+    attended_rows, w_first, cotangent, back_near, w_out, peak_rows = sync(
+        attended_rows, w_first, cotangent, back_near, w_out, peak_rows
+    )
     hidden_rows = token_rows + dot_nt(attended_rows, w_out) + bias_o
     normed_two = layer_norm(hidden_rows, gain_two, shift_two).astype(BF)
 
@@ -705,21 +708,10 @@
         blocks = blocks.reshape(dp_count // 2, 2, edge, blocks.shape[2])
         return lax.psum_scatter(blocks, "dp", scatter_dimension=0, tiled=False, axis_index_groups=same_core)
 
-    pending = [("dp", 1 << bit) for bit in range(dp_count.bit_length() - 1)]
-    pending += [("tensor", 1 << bit) for bit in range(1, tp_count.bit_length() - 1)]
-
-    def with_peaks(work):
-        def both(state):
-            if pending:
-                state = dict(state, peaks=state["peaks"] + shift(state["peaks"], *pending.pop(0)))
-            return work(state)
-
-        return both
-
     def near_back(j):
         def work(state):
             if j > 0:
-                up, down = scatter_ffn(state.pop("far_raw"))
+                up, down = state.pop("arrived")
                 w_up.append(up)
                 w_down.append(down)
             grad_act = jnp.dot(state["back_near"], w_down[j], preferred_element_type=F32).astype(BF)
@@ -783,18 +775,42 @@
             state, result_near=matmul_sum(state["act_near"], w_down), near_rows=core_rows(state.pop("grad_near"))
         )
 
+    def both(first, second):
+        return lambda state: second(first(state))
+
     state = dict(
-        back_near=back_near, peaks=peak_row, normed=normed_two, act_near=[], pre_near=[], act_far=[], pre_far=[], slopes=[]
-    )
-    steps = [(1, with_peaks(work)) for j in range(slices) for work in (near_back(j), near_up(j))]
+        back_near=back_near, normed=normed_two, act_near=[], pre_near=[], act_far=[], pre_far=[], slopes=[]
+    )
+    def arrive(state):
+        state = dict(state)
+        state["arrived"] = scatter_ffn(state.pop("far_raw"))
+        return state
+
+    steps = []
+    for j in range(slices):
+        steps += [(1, arrive)] * (j > 0) + [(2, both(near_back(j), near_up(j)))]
     normed_across, state = beside(normed_two, "tensor", 1, steps, state)
-    state["normed_far"] = with_core(normed_across)
-    steps = [(1, with_peaks(far_up(j))) for j in range(slices)]
-    steps += [(slices, with_peaks(far_result)), (slices, with_peaks(near_grad))]
+    state["normed_across"] = normed_across
+
+    def far_rows_in(state):
+        state = dict(state)
+        state["normed_far"] = with_core(state.pop("normed_across"))
+        return state
+
+    def back_rows_in(state):
+        state = dict(state)
+        state["back_far"] = with_core(state.pop("back_across"))
+        return state
+
+    work = both(far_rows_in, far_up(0))
+    for j in range(1, slices):
+        work = both(work, far_up(j))
+    steps = [(slices, work)]
+    steps += [(slices, far_result), (slices, near_grad)]
     back_across, state = beside(cotangent, "tensor", 1, steps, state)
-    state["back_far"] = with_core(back_across)
+    state["back_across"] = back_across
     middle = rows // 2
-    ffn_low, state = beside(state["ffn_far"][:middle], "tensor", 1, [(1, down_blocks)], state)
+    ffn_low, state = beside(state["ffn_far"][:middle], "tensor", 1, [(1, both(back_rows_in, down_blocks))], state)
     part_down = chips_sum(state.pop("down"))
     steps = [(1, far_back(j)) for j in range(slices)] + [(slices, far_grad)]
     ffn_high, state = beside(state.pop("ffn_far")[middle:], "tensor", 1, steps, state)
@@ -806,8 +822,7 @@
     low_rows, state = beside(state["far_rows"][:cut], "tensor", 1, [(1, up_blocks)], state)
     part_up = chips_sum(state.pop("up"))
     high_rows, state = beside(state.pop("far_rows")[cut:], "tensor", 1, [(1, near_result)], state)
-    low_rows, high_rows, part_down, state = sync(low_rows, high_rows, part_down, state)
-    peak_rows = state["peaks"]
+    low_rows, high_rows, part_down, state, peak_rows = sync(low_rows, high_rows, part_down, state, peak_rows)
     grad_two = state["near_rows"].astype(F32) + jnp.concatenate([low_rows, high_rows], axis=0).astype(F32)
     result, grads_pre = state["result_near"], list(zip(state["pre_near"], state["pre_far"]))
 
@@ -867,15 +882,19 @@
     )
     up_high = to_owners([value[1:] for value in far_up])
     partial = dot_nt(grad_qkv_rows, w_qkv).astype(BF)
-    partial, up_high, grad_qkv_rows, branch, grads_pre, sum_out = sync(
-        partial, up_high, grad_qkv_rows, branch, grads_pre, sum_out
+    partial, up_high, grad_qkv_rows, branch, grads_pre, sum_out, peak_rows = sync(
+        partial, up_high, grad_qkv_rows, branch, grads_pre, sum_out, peak_rows
     )
     far_down = [jnp.concatenate(value, axis=0) for value in zip(down_low, down_high)]
     far_up = [jnp.concatenate(value, axis=0) for value in zip(up_low, up_high)]
     grad_normed_one = lax.psum_scatter(partial, "tensor", scatter_dimension=0, tiled=True).astype(F32)
 
     grads_qkv = grad_blocks(block_of[0][half_slots(order_far)], [normed_all], [[grad_qkv_rows]], edge)
-    grads_qkv, grad_qkv_rows, branch, grads_pre, partial = sync(grads_qkv, grad_qkv_rows, branch, grads_pre, partial)
+    for bit in range(1, tp_count.bit_length() - 1):
+        peak_rows = peak_rows + shift(peak_rows, "tensor", 1 << bit)
+    grads_qkv, grad_qkv_rows, branch, grads_pre, partial, peak_rows = sync(
+        grads_qkv, grad_qkv_rows, branch, grads_pre, partial, peak_rows
+    )
     column_sums = jnp.sum(grad_qkv_rows, axis=0, dtype=F32).reshape(heads, 3, HD)
     head_sums = lambda part: lax.dynamic_update_slice(
         jnp.zeros((D,), F32), column_sums[:, part].reshape(width), (place * width,)
@@ -901,9 +920,29 @@
     sum_qkv = halve(grads_qkv, [1])
     totals = axis_sum(totals, "dp")
     totals, sum_qkv = sync(totals, sum_qkv)
-    sum_qkv = halve(sum_qkv, far)[0]
     sum_down = far_sum(own_down, far_down)
     sum_up = far_sum(own_up, far_up)
+
+    index = jnp.arange(tile_count, dtype=jnp.int32)
+    rates = jnp.where(
+        index < bounds[1],
+        D ** (-0.5),
+        jnp.where(index < bounds[2], (SEQ / (2.0 * D)) ** 0.5, jnp.where(index < bounds[3], D ** (-0.5), FF ** (-0.5))),
+    ).astype(F32)
+    ones = jnp.ones((tile_count,), F32)
+    token_count = float(dp_count * SEQ)
+    state = [value[0, 0] for value in (master, first_moment, second_moment, left_stats, right_stats, left_basis, right_basis)]
+    tiles_up = sum_up.reshape(edge_tiles, HD, hidden_tiles, HD).transpose(0, 2, 1, 3).reshape(tile_u, HD, HD)
+    tiles_down = sum_down.reshape(edge_tiles, HD, hidden_tiles, HD).transpose(2, 0, 1, 3).reshape(tile_u, HD, HD)
+    count = sum_qkv.shape[0] // 4
+    done = list(update_tiles(tiles_down, state, rates, ones, bounds[3], None, True, token_count))
+    low_part = shift(sum_qkv[:count], "dp", far[0])
+    low_part, done[3], sum_qkv = sync(low_part, done[3], sum_qkv)
+    done = list(update_tiles(tiles_up, state, rates, ones, bounds[2], done, False, token_count))
+    high_part = shift(sum_qkv[count : 2 * count], "dp", far[0])
+    high_part, done[3], sum_qkv = sync(high_part, done[3], sum_qkv)
+    sum_qkv = add_low(sum_qkv[2 * count :], jnp.concatenate([low_part, high_part], axis=0))
+    sum_qkv = halve(sum_qkv, far[1:])[0]
     ffn_near = core_rows(result)
     outputs = (hidden_rows + ffn_near.astype(F32) + ffn_across.astype(F32) + bias_two).astype(BF)
     peak_all = jnp.max(peak_rows.reshape(dp_count, H), axis=0)
@@ -921,24 +960,11 @@
     small_first_new, small_second_new, small_new = small_step(grad_small, small_params, small_first, small_second)
     small_new = jnp.concatenate([(small_new[:D].reshape(H, HD) * shrink[:, None]).reshape(D), small_new[D:]])
 
-    index = jnp.arange(tile_count, dtype=jnp.int32)
-    rates = jnp.where(
-        index < bounds[1],
-        D ** (-0.5),
-        jnp.where(index < bounds[2], (SEQ / (2.0 * D)) ** 0.5, jnp.where(index < bounds[3], D ** (-0.5), FF ** (-0.5))),
-    ).astype(F32)
     column = index % (3 * heads)
     shrink_here = lax.dynamic_slice_in_dim(shrink, place * heads, heads)
     factors = jnp.where((index < bounds[1]) & (column < 2 * heads), shrink_here[column % heads], 1.0)
-    ones = jnp.ones((tile_count,), F32)
-    token_count = float(dp_count * SEQ)
-    state = [value[0, 0] for value in (master, first_moment, second_moment, left_stats, right_stats, left_basis, right_basis)]
-    tiles_up = sum_up.reshape(edge_tiles, HD, hidden_tiles, HD).transpose(0, 2, 1, 3).reshape(tile_u, HD, HD)
-    tiles_down = sum_down.reshape(edge_tiles, HD, hidden_tiles, HD).transpose(2, 0, 1, 3).reshape(tile_u, HD, HD)
     tiles_out = sum_out.reshape(edge_tiles, HD, heads, HD).transpose(2, 0, 1, 3).reshape(tile_o, HD, HD)
     tiles_qkv = sum_qkv.reshape(edge_tiles, HD, heads, 3, HD).transpose(0, 3, 2, 1, 4).reshape(tile_q, HD, HD)
-    done = update_tiles(tiles_down, state, rates, ones, bounds[3], None, True, token_count)
-    done = update_tiles(tiles_up, state, rates, ones, bounds[2], done, False, token_count)
     done = update_tiles(tiles_qkv, state, rates, factors, 0, done, False, token_count)
     done = update_tiles(tiles_out, state, rates, ones, bounds[1], done, True, token_count)
     return (

time: 934 us -> 924 us (0.989)
  waiting for transfers between devices: 262 us -> 240 us
    ppermute x55 -> x54, waiting for transfers between devices: 194 us -> 173 us  [shift(): lax.ppermute(value, axis, [(i, i ^ mask) for i in range(lax.axis_size(axi...]
    ppermute x55 -> x54, starting transfers between devices: 59.3 us -> 65.5 us  [shift(): lax.ppermute(value, axis, [(i, i ^ mask) for i in range(lax.axis_size(axi...]
  transfers between devices with their start and end apart: 71 -> 70, of which waited for: 28 -> 25; matrix products, arithmetic and copies ran while one was open for 24% -> 25% of each run, Pallas kernels for 33% -> 34%
where the time goes in v4:
time: 924 us; the launch traced here: 916 us
  Pallas kernels  324 us (35%)
  waiting for transfers between devices  240 us (26%)
  starting transfers between devices  93.9 us (10%)
  matrix products  93.1 us (10%)
  other arithmetic  85 us (9%)
  local copies, waits for them, and re-layouts  63.6 us (7%)
  between operations  16.2 us (2%)
    ppermute x54, waiting for transfers between devices, shift(): lax.ppermute(value, axis, [(i, i ^ mask) for i in range(lax.axis_size(axi...  173 us
    pallas_call x4, Pallas kernels, grad_blocks(): pl.pallas_call(body, grid_spec=pltpu.PrefetchScalarGridSpec(num_scalar_pr...  80.4 us
    ppermute x54, starting transfers between devices, shift(): lax.ppermute(value, axis, [(i, i ^ mask) for i in range(lax.axis_size(axi...  65.5 us
    ppermute x8, waiting for transfers between devices, move(): return lax.ppermute(value, axis, pairs)  62.4 us
    pallas_call x4, Pallas kernels, matmul_sum(): pl.pallas_call(body, grid=(rows // row_step, columns // step), in_specs=[...  54.5 us
    pallas_call x4, Pallas kernels, update_tiles(): pl.pallas_call(body, grid=(count // group,), in_specs=[smem, smem, pl.Blo...  52 us
    pallas_call x1, Pallas kernels, attend_back(): pl.pallas_call(attend_back_kernel, grid=(heads,), in_specs=[pl.BlockSpec(...  43.3 us
    pallas_call x4, Pallas kernels, scatter_blocks(): pl.pallas_call(body, grid_spec=pltpu.PrefetchScalarGridSpec(num_scalar_pr...  37.8 us
  transfers between devices with their start and end apart: 70, of which 25 were waited for; matrix products, arithmetic and copies ran while one was open for 25% of the time, Pallas kernels for 34%

profile of v4, /device:TPU:0, one launch (start us, length us, event | category | flops | bytes accessed | tf_op | source)
XLA Modules:
  0.0 916.2 jit_solution(13738902679297573286)
XLA Ops:
  7.2 5.2 pack_weights.1
  16.7 7.0 collective-permute-start.1
  30.0 47.4 %collective-permute-done.2 = bf16[256,512]{1,0:T(8,128)(2,1)S(1)} collective-permute-done((bf16[256,512]{1,0:T(8,128)(2,1)S(1)}, bf16[256,512]{1,0:T(8,128)(2,1)S(1)}, u32[]{:S(2)}, u32[]{:S(2)}) %collective-permute-start.2) | collective-permute-done | bytes 262176 | tf_op jit(solution)/shard_map/ppermute | solution.py:474
  77.4 8.0 collective-permute-done.3
  89.9 49.6 %collective-permute-done.6.refs_6_.refs_4_ = bf16[512,2048]{1,0:T(8,128)(2,1)} collective-permute-done((bf16[512,2048]{1,0:T(8,128)(2,1)}, bf16[512,2048]{1,0:T(8,128)(2,1)}, u32[]{:S(2)}, u32[]{:S(2)}) %collective-permute-start.6) | collective-permute-done | bytes 2097184 | tf_op jit(solution)/shard_map/ppermute | solution.py:478
  142.9 11.7 %collective-permute-start.10 = (bf16[2,256,2048]{2,1,0:T(8,128)(2,1)}, bf16[2,256,2048]{2,1,0:T(8,128)(2,1)}, u32[]{:S(2)}, u32[]{:S(2)}) collective-permute-start(bf16[2,256,2048]{2,1,0:T(8,128)(2,1)} %pad_maximum_fusion.2), channel_id=1, source_target_pairs={{0,2},{3,1},{4,6},{7,5},{8,10},{11,9},{12,14},{15,13},{16,18},{19,... | collective-permute-start | bytes 6291464 | tf_op jit(solution)/shard_map/ppermute | solution.py:478
  157.8 8.6 scatter_blocks.4.refs_9_.refs_8_
  166.5 18.6 %project.2 = (bf16[2048,2048]{1,0:T(8,128)(2,1)}, bf16[2048,2048]{1,0:T(8,128)(2,1)}, bf16[2048,1536]{1,0:T(8,128)(2,1)}) custom-call(s32[3]{0:T(128)} %bitcast.217, s32[3]{0:T(128)} %bitcast.216, bf16[512,2048]{1,0:T(8,128)(2,1)} %fusion.5.refs_2_, bf16[512,2048]{1,0:T(8,128)(2,1)} %collective-permute-done.1.refs_3_, ...), custom_call_target="tpu_custom_call" | custom-call | bytes 63000000 | tf_op jit(solution)/shard_map/project/pallas_call | solution.py:451
  185.1 9.8 %scatter_blocks.5 = bf16[2048,2048]{1,0:T(8,128)(2,1)} custom-call(s32[8]{0:T(128)} %get-tuple-element.658.refs_0_, bf16[8,256,2048]{2,1,0:T(8,128)(2,1)} %bitcast.188), custom_call_target="tpu_custom_call" | custom-call | bytes 19573418 | tf_op jit(solution)/shard_map/scatter_blocks/pallas_call | solution.py:405
  199.6 11.5 %project.3 = (bf16[2048,2048]{1,0:T(8,128)(2,1)}, bf16[2048,2048]{1,0:T(8,128)(2,1)}, bf16[2048,1536]{1,0:T(8,128)(2,1)}) custom-call(s32[1]{0:T(128)} %slice.249.refs_0_, s32[1]{0:T(128)} %slice.250.refs_1_, bf16[512,2048]{1,0:T(8,128)(2,1)} %collective-permute-done.7.refs_4_.refs_2_, ...), custom_call_target="tpu_custom_call", output_to_operand_aliasing={{0}: (10, {}), {1}: (11, {}), {2}: (12, {})} | custom-call | bytes 21000000 | tf_op jit(solution)/shard_map/project/pallas_call | solution.py:451
  211.1 20.9 %attend.1 = (bf16[2048,512]{1,0:T(8,128)(2,1)}, f32[4,8,128]{2,1,0:T(8,128)}) custom-call(s32[1,2048]{1,0:T(1,128)} %compare_select_fusion.start_ref, bf16[2048,1536]{1,0:T(8,128)(2,1)} %get-tuple-element.336.qkv_ref), custom_call_target="tpu_custom_call" | custom-call | bytes 70000000 | tf_op jit(solution)/shard_map/attend/pallas_call | solution.py:91
  232.1 11.5 %collective-permute-done.11 = bf16[2,256,2048]{2,1,0:T(8,128)(2,1)} collective-permute-done((bf16[2,256,2048]{2,1,0:T(8,128)(2,1)}, bf16[2,256,2048]{2,1,0:T(8,128)(2,1)}, u32[]{:S(2)}, u32[]{:S(2)}) %collective-permute-start.11) | collective-permute-done | bytes 2097184 | tf_op jit(solution)/shard_map/ppermute | solution.py:478
  243.6 4.4 add.450
  263.3 4.8 pad_maximum_fusion.refs_1_
  268.1 9.7 %scatter_blocks.6 = (bf16[2048,1024]{1,0:T(8,128)(2,1)}, bf16[2048,1024]{1,0:T(8,128)(2,1)}) custom-call(s32[8]{0:T(128)} %gather_fusion, s32[8]{0:T(128)} %gather_fusion.1, bf16[8,256,2048]{2,1,0:T(8,128)(2,1)} %all-gather.7.cloned.1.call-done.refs_2_), custom_call_target="tpu_custom_call" | custom-call | bytes 19573418 | tf_op jit(solution)/shard_map/scatter_blocks/pallas_call | solution.py:405
  278.3 21.0 %collective-permute-done.13 = bf16[512,512]{1,0:T(8,128)(2,1)} collective-permute-done((bf16[512,512]{1,0:T(8,128)(2,1)}, bf16[512,512]{1,0:T(8,128)(2,1)}, u32[]{:S(2)}, u32[]{:S(2)}) %collective-permute-start.13) | collective-permute-done | bytes 524320 | tf_op jit(solution)/shard_map/ppermute | solution.py:474
  300.9 7.9 fusion.58
  311.1 8.0 convolution_convert_fusion.3
  319.0 4.2 pad_maximum_fusion.1.refs_1_
  323.3 8.0 fusion.18
  331.2 4.1 all-gather.9.cloned.1.call-done.refs_2_
  336.9 9.7 %scatter_blocks.7 = (bf16[2048,1024]{1,0:T(8,128)(2,1)}, bf16[2048,1024]{1,0:T(8,128)(2,1)}) custom-call(s32[8]{0:T(128)} %gather_fusion, s32[8]{0:T(128)} %gather_fusion.1, bf16[8,256,2048]{2,1,0:T(8,128)(2,1)} %all-gather.9.cloned.1.call-done.refs_2_), custom_call_target="tpu_custom_call" | custom-call | bytes 19573418 | tf_op jit(solution)/shard_map/scatter_blocks/pallas_call | solution.py:405
  349.3 7.8 convolution_convert_fusion.2
  357.1 7.7 fusion.24
  372.2 7.5 fusion.29
  379.7 7.4 fusion.34
  389.6 13.4 %matmul_sum.4 = bf16[1024,2048]{1,0:T(8,128)(2,1)} custom-call(bf16[1024,1024]{1,0:T(8,128)(2,1)} %get-tuple-element.407.refs_0_.refs_4_, bf16[1024,1024]{1,0:T(8,128)(2,1)} %get-tuple-element.408.refs_1_.refs_6_, bf16[2048,1024]{1,0:T(8,128)(2,1)} %get-tuple-element.351.refs_2_, bf16[2048,1024]{1,0:T(8,128)(2,1)} %get-tuple-element.365.refs_3_), custom_call_target="tpu_custom_call" | custom-call | bytes 37580964 | tf_op jit(solution)/shard_map/matmul_sum/pallas_call | solution.py:320
  403.0 3.3 collective-permute-done.25
  410.7 13.8 %matmul_sum.5 = bf16[1024,2048]{1,0:T(8,128)(2,1)} custom-call(bf16[1024,1024]{1,0:T(8,128)(2,1)} %get-tuple-element.551.refs_0_.refs_3_, bf16[1024,1024]{1,0:T(8,128)(2,1)} %get-tuple-element.553.refs_1_.refs_5_, bf16[2048,1024]{1,0:T(8,128)(2,1)} %get-tuple-element.347.refs_2_, bf16[2048,1024]{1,0:T(8,128)(2,1)} %get-tuple-element.363.refs_3_), custom_call_target="tpu_custom_call" | custom-call | bytes 37580964 | tf_op jit(solution)/shard_map/matmul_sum/pallas_call | solution.py:320
  434.6 24.7 %grad_blocks.4 = bf16[8,256,2048]{2,1,0:T(8,128)(2,1)} custom-call(s32[8]{0:T(128)} %gather_fusion.1, bf16[1024,2048]{1,0:T(8,128)(2,1)} %pad_maximum_fusion.refs_1_, bf16[1024,2048]{1,0:T(8,128)(2,1)} %copy-done.29, bf16[1024,1024]{1,0:T(8,128)(2,1)} %get-tuple-element.479.refs_3_.refs_0_, bf16[1024,1024]{1,0:T(8,128)(2,1)} %get-tuple-element.407.refs_0_.refs_4_, ...), custom_call_target="tpu_custom_call" | custom-call | bytes 75161928 | tf_op jit(solution)/shard_map/grad_blocks/pallas_call | solution.py:287
  461.0 10.6 %multiply_convert_fusion.1.refs_0_.refs_4_ = bf16[1024,1024]{1,0:T(8,128)(2,1)} fusion(bf16[1024,1024]{1,0:T(8,128)(2,1)} %get-tuple-element.429, bf16[1024,2048]{1,0:T(8,128)(2,1)} %copy-done.29, bf16[2048,1024]{1,0:T(8,128)(2,1)} %get-tuple-element.351.refs_2_), kind=kOutput, calls=%fused_computation.70 | convolution fusion | flops 4298113024 | bytes 12582912 | tf_op jit(solution)/shard_map/dot_general | solution.py:759
  471.9 5.7 multiply_convert_fusion.refs_1_.refs_6_
  480.7 13.4 %matmul_sum.6 = bf16[1024,2048]{1,0:T(8,128)(2,1)} custom-call(bf16[1024,1024]{1,0:T(8,128)(2,1)} %multiply_convert_fusion.1.refs_0_.refs_4_, bf16[1024,1024]{1,0:T(8,128)(2,1)} %multiply_convert_fusion.refs_1_.refs_6_, bf16[2048,1024]{1,0:T(8,128)(2,1)} %get-tuple-element.347.refs_2_, bf16[2048,1024]{1,0:T(8,128)(2,1)} %get-tuple-element.363.refs_3_), custom_call_target="tpu_custom_call" | custom-call | bytes 37580964 | tf_op jit(solution)/shard_map/matmul_sum/pallas_call | solution.py:320
  496.4 4.1 collective-permute-done.33
  503.3 24.8 %grad_blocks.5 = bf16[8,256,2048]{2,1,0:T(8,128)(2,1)} custom-call(s32[8]{0:T(128)} %gather_fusion, bf16[1024,2048]{1,0:T(8,128)(2,1)} %pad_maximum_fusion.1.refs_1_, bf16[1024,2048]{1,0:T(8,128)(2,1)} %copy-done.28, bf16[1024,1024]{1,0:T(8,128)(2,1)} %get-tuple-element.551.refs_0_.refs_3_, bf16[1024,1024]{1,0:T(8,128)(2,1)} %multiply_convert_fusion.1.refs_0_.refs_4_, ...), custom_call_target="tpu_custom_call" | custom-call | bytes 75161928 | tf_op jit(solution)/shard_map/grad_blocks/pallas_call | solution.py:287
  528.1 4.4 collective-permute-done.34
  532.6 3.2 slice.282
  539.5 13.8 %matmul_sum.7 = bf16[1024,2048]{1,0:T(8,128)(2,1)} custom-call(bf16[1024,1024]{1,0:T(8,128)(2,1)} %get-tuple-element.479.refs_3_.refs_0_, bf16[1024,1024]{1,0:T(8,128)(2,1)} %get-tuple-element.480.refs_5_.refs_1_, bf16[2048,1024]{1,0:T(8,128)(2,1)} %get-tuple-element.351.refs_2_, bf16[2048,1024]{1,0:T(8,128)(2,1)} %get-tuple-element.365.refs_3_), custom_call_target="tpu_custom_call" | custom-call | bytes 37580964 | tf_op jit(solution)/shard_map/matmul_sum/pallas_call | solution.py:320
  562.2 4.6 multiply_reduce_fusion
  566.8 5.3 fusion.48
  572.1 4.8 convolution_convert_fusion.1
  577.1 11.0 %grad_blocks.6 = bf16[8,256,2048]{2,1,0:T(8,128)(2,1)} custom-call(s32[8]{0:T(128)} %gather_fusion.2, bf16[512,2048]{1,0:T(8,128)(2,1)} %copy-done.6, bf16[512,2048]{1,0:T(8,128)(2,1)} %copy-done.25), custom_call_target="tpu_custom_call" | custom-call | bytes 18790480 | tf_op jit(solution)/shard_map/grad_blocks/pallas_call | solution.py:287
  594.8 3.0 collective-permute-start.41
  597.7 20.3 %collective-permute-done.39 = bf16[512,512]{1,0:T(8,128)(2,1)S(1)} collective-permute-done((bf16[512,512]{1,0:T(8,128)(2,1)S(1)}, bf16[512,512]{1,0:T(8,128)(2,1)S(1)}, u32[]{:S(2)}, u32[]{:S(2)}) %collective-permute-start.39) | collective-permute-done | bytes 524320 | tf_op jit(solution)/shard_map/ppermute | solution.py:474
  618.8 13.2 %collective-permute-done.40 = bf16[512,512]{1,0:T(8,128)(2,1)S(1)} collective-permute-done((bf16[512,512]{1,0:T(8,128)(2,1)S(1)}, bf16[512,512]{1,0:T(8,128)(2,1)S(1)}, u32[]{:S(2)}, u32[]{:S(2)}) %collective-permute-start.40) | collective-permute-done | bytes 524320 | tf_op jit(solution)/shard_map/ppermute | solution.py:474
  633.7 4.0 add_convert_fusion
  638.1 10.6 %collective-permute-start.44 = (bf16[1,256,1024]{2,1,0:T(8,128)(2,1)S(1)}, bf16[1,256,1024]{2,1,0:T(8,128)(2,1)}, u32[]{:S(2)}, u32[]{:S(2)}) collective-permute-start(bf16[1,256,1024]{2,1,0:T(8,128)(2,1)S(1)} %slice.295), channel_id=1, source_target_pairs={{0,2},{1,3},{2,0},{3,1},{4,6},{5,7},{6,4},{7,5},{8,10},{9,11},{10,... | collective-permute-start | bytes 1572872 | tf_op jit(solution)/shard_map/ppermute | solution.py:474
  652.4 43.3 %attend_back.1.refs_2_ = bf16[2048,1536]{1,0:T(8,128)(2,1)} custom-call(s32[1,2048]{1,0:T(1,128)} %compare_select_fusion.start_ref, bf16[2048,1536]{1,0:T(8,128)(2,1)} %get-tuple-element.336.qkv_ref, bf16[2048,512]{1,0:T(8,128)(2,1)} %constant_dynamic-update-slice_fusion.17.back_ref), custom_call_target="tpu_custom_call" | custom-call | bytes 140000000 | tf_op jit(solution)/shard_map/attend_back/pallas_call | solution.py:146
  699.2 17.7 %convolution_convert_fusion = bf16[2048,2048]{1,0:T(8,128)(2,1)} fusion(bf16[2048,1536]{1,0:T(8,128)(2,1)} %attend_back.1.refs_2_, bf16[2048,1536]{1,0:T(8,128)(2,1)S(1)} %bitcast.178), kind=kOutput, calls=%fused_computation.10 | convolution fusion | flops 12889096192 | bytes 20971520 | tf_op jit(solution)/shard_map/dot_general | solution.py:31
  716.9 5.1 collective-permute-done.46
  725.4 3.2 slice.293
  728.6 19.9 %grad_blocks.7 = bf16[8,256,1536]{2,1,0:T(8,128)(2,1)} custom-call(s32[8]{0:T(128)} %gather_fusion.4, bf16[2048,2048]{1,0:T(8,128)(2,1)} %get-tuple-element.539.refs_1_, bf16[2048,1536]{1,0:T(8,128)(2,1)} %attend_back.1.refs_2_), custom_call_target="tpu_custom_call" | custom-call | bytes 56371444 | tf_op jit(solution)/shard_map/grad_blocks/pallas_call | solution.py:287
  749.5 3.8 slice.303
  754.5 10.6 %convert_reduce_fusion = (f32[2048]{0:T(1024)S(1)}, f32[2048]{0:T(1024)S(1)}) fusion(bf16[2048,2048]{1,0:T(8,128)(2,1)} %convolution_convert_fusion, bf16[2048,2048]{1,0:T(8,128)(2,1)} %get-tuple-element.550), kind=kLoop, calls=%fused_computation.5 | loop fusion | flops 20967424 | bytes 16793600 | tf_op jit(solution)/shard_map/reduce_sum | solution.py:914
  772.8 3.4 collective-permute-done.49
  788.6 16.6 %update_tiles.4 = (f32[96,128,128]{2,1,0:T(8,128)}, f32[96,128,128]{2,1,0:T(8,128)}, f32[96,128,128]{2,1,0:T(8,128)}, bf16[96,128,128]{2,1,0:T(8,128)(2,1)}, f32...) custom-call(f32[32]{0:T(128)} %get-tuple-element.661.refs_0_, ...), custom_call_target="tpu_custom_call" | custom-call | bytes 56000000 | tf_op jit(solution)/shard_map/update_tiles/pallas_call | solution.py:247
  810.4 16.1 %update_tiles.5 = (f32[96,128,128]{2,1,0:T(8,128)}, f32[96,128,128]{2,1,0:T(8,128)}, f32[96,128,128]{2,1,0:T(8,128)}, bf16[96,128,128]{2,1,0:T(8,128)(2,1)}, f32...) custom-call(f32[32]{0:T(128)} %get-tuple-element.660.refs_0_, ...), custom_call_target="tpu_custom_call", output_to_operand_aliasing={{0}: (10, {}), {1}: (11, {}), {2}: (12, {}), {3}: (13, {}),... | custom-call | bytes 56000000 | tf_op jit(solution)/shard_map/update_tiles/pallas_call | solution.py:247
  831.2 4.0 add_convert_fusion.2
  836.2 3.2 and_select_fusion.2
  839.4 10.0 %collective-permute-done.59 = bf16[1,256,1536]{2,1,0:T(8,128)(2,1)S(1)} collective-permute-done((bf16[1,256,1536]{2,1,0:T(8,128)(2,1)S(1)}, bf16[1,256,1536]{2,1,0:T(8,128)(2,1)S(1)}, u32[]{:S(2)}, u32[]{:S(2)}) %collective-permute-start.59) | collective-permute-done | bytes 786464 | tf_op jit(solution)/shard_map/ppermute | solution.py:474
  851.9 12.9 %update_tiles.6 = (f32[96,128,128]{2,1,0:T(8,128)}, f32[96,128,128]{2,1,0:T(8,128)}, f32[96,128,128]{2,1,0:T(8,128)}, bf16[96,128,128]{2,1,0:T(8,128)(2,1)}, f32...) custom-call(f32[24]{0:T(128)} %bitcast.215, ...), custom_call_target="tpu_custom_call", output_to_operand_aliasing={{0}: (10, {}), {1}: (11, {}), {2}: (12, {}), {3}: (13, {}),... | custom-call | bytes 42000000 | tf_op jit(solution)/shard_map/update_tiles/pallas_call | solution.py:247
  877.9 2.9 fusion.10
  880.7 18.9 %collective-permute-done.61 = f32[24576]{0:T(1024)S(1)} collective-permute-done((f32[24576]{0:T(1024)S(1)}, f32[24576]{0:T(1024)S(1)}, u32[]{:S(2)}, u32[]{:S(2)}) %collective-permute-start.61) | collective-permute-done | bytes 98336 | tf_op jit(solution)/shard_map/ppermute | solution.py:474
  902.6 6.3 update_tiles.7
  (457 shorter events, 167.8 us)
Async XLA Ops:
  7.2 150.7 %all-gather.11.cloned.1.call-start = ((), (), s32[]{:S(2)}) async-start(), calls=%async_computation.7 | async-start | bytes 7077888 | tf_op jit(solution)/shard_map/all_gather | solution.py:626
  12.4 172.7 %all-gather.13.cloned.1.call-start = ((), (), s32[]{:S(2)}) async-start(), calls=%async_computation.8 | async-start | bytes 9437184 | tf_op jit(solution)/shard_map/all_gather | solution.py:659
  15.4 70.0 %collective-permute-start = (bf16[512,2048]{1,0:T(8,128)(2,1)}, bf16[512,2048]{1,0:T(8,128)(2,1)}, u32[]{:S(2)}, u32[]{:S(2)}) collective-permute-start(bf16[512,2048]{1,0:T(8,128)(2,1)} %fusion.5.refs_2_), channel_id=1, source_target_pairs={{1,0},{2,1},{3,2},{5,4},{6,5},{7,6},{9,8},{10,9},{11,10},{13,12},{... | collective-permute-start | bytes 6291464 | tf_op jit(solution)/shard_map/ppermute | solution.py:478
  16.7 68.7 %collective-permute-start.1 = (bf16[512,2048]{1,0:T(8,128)(2,1)}, bf16[512,2048]{1,0:T(8,128)(2,1)}, u32[]{:S(2)}, u32[]{:S(2)}) collective-permute-start(bf16[512,2048]{1,0:T(8,128)(2,1)} %fusion.5.refs_2_), channel_id=1, source_target_pairs={{0,1},{1,2},{2,3},{4,5},{5,6},{6,7},{8,9},{9,10},{10,11},{12,13},{... | collective-permute-start | bytes 6291464 | tf_op jit(solution)/shard_map/ppermute | solution.py:478
  24.0 53.4 %collective-permute-start.2 = (bf16[256,512]{1,0:T(8,128)(2,1)S(1)}, bf16[256,512]{1,0:T(8,128)(2,1)S(1)}, u32[]{:S(2)}, u32[]{:S(2)}) collective-permute-start(bf16[256,512]{1,0:T(8,128)(2,1)S(1)} %copy-done.45), channel_id=1, source_target_pairs={{0,1},{1,0},{2,3},{3,2},{4,5},{5,4},{6,7},{7,6},{8,9},{9,8},{10,11... | collective-permute-start | bytes 786440 | tf_op jit(solution)/shard_map/ppermute | solution.py:474
  24.7 60.7 %collective-permute-start.3 = (bf16[256,512]{1,0:T(8,128)(2,1)S(1)}, bf16[256,512]{1,0:T(8,128)(2,1)S(1)}, u32[]{:S(2)}, u32[]{:S(2)}) collective-permute-start(bf16[256,512]{1,0:T(8,128)(2,1)S(1)} %copy-done.45), channel_id=1, source_target_pairs={{0,2},{1,3},{2,0},{3,1},{4,6},{5,7},{6,4},{7,5},{8,10},{9,11},{10,... | collective-permute-start | bytes 786440 | tf_op jit(solution)/shard_map/ppermute | solution.py:474
  27.1 58.3 %collective-permute-start.4 = (bf16[256,512]{1,0:T(8,128)(2,1)S(1)}, bf16[256,512]{1,0:T(8,128)(2,1)S(1)}, u32[]{:S(2)}, u32[]{:S(2)}) collective-permute-start(bf16[256,512]{1,0:T(8,128)(2,1)S(1)} %copy-done.45), channel_id=1, source_target_pairs={{0,3},{1,2},{2,1},{3,0},{4,7},{5,6},{6,5},{7,4},{8,11},{9,10},{10,... | collective-permute-start | bytes 786440 | tf_op jit(solution)/shard_map/ppermute | solution.py:474
  86.6 181.6 %all-gather.7.cloned.1.call-start = ((), (), s32[]{:S(2)}) async-start(), calls=%async_computation.4 | async-start | bytes 10485760 | tf_op jit(solution)/shard_map/all_gather | solution.py:620
  86.6 52.9 %collective-permute-start.6 = (bf16[512,2048]{1,0:T(8,128)(2,1)}, bf16[512,2048]{1,0:T(8,128)(2,1)}, u32[]{:S(2)}, u32[]{:S(2)}) collective-permute-start(bf16[512,2048]{1,0:T(8,128)(2,1)} %collective-permute-done.refs_5_), channel_id=1, source_target_pairs={{1,0},{2,1},{5,4},{6,5},{9,8},{10,9},{13,12},{14,13},{17,16},{18,1... | collective-permute-start | bytes 6291464 | tf_op jit(solution)/shard_map/ppermute | solution.py:478
  87.9 51.6 %collective-permute-start.7 = (bf16[512,2048]{1,0:T(8,128)(2,1)}, bf16[512,2048]{1,0:T(8,128)(2,1)}, u32[]{:S(2)}, u32[]{:S(2)}) collective-permute-start(bf16[512,2048]{1,0:T(8,128)(2,1)} %collective-permute-done.1.refs_3_), channel_id=1, source_target_pairs={{1,2},{2,3},{5,6},{6,7},{9,10},{10,11},{13,14},{14,15},{17,18},{18... | collective-permute-start | bytes 6291464 | tf_op jit(solution)/shard_map/ppermute | solution.py:478
  139.6 195.8 %all-gather.9.cloned.1.call-start = ((), (), s32[]{:S(2)}) async-start(), calls=%async_computation.5 | async-start | bytes 10485760 | tf_op jit(solution)/shard_map/all_gather | solution.py:620
  139.6 55.3 %collective-permute-start.8 = (bf16[512,2048]{1,0:T(8,128)(2,1)}, bf16[512,2048]{1,0:T(8,128)(2,1)}, u32[]{:S(2)}, u32[]{:S(2)}) collective-permute-start(bf16[512,2048]{1,0:T(8,128)(2,1)} %collective-permute-done.6.refs_6_.refs_4_), channel_id=1, source_target_pairs={{1,0},{5,4},{9,8},{13,12},{17,16},{21,20},{25,24},{29,28}} | collective-permute-start | bytes 6291464 | tf_op jit(solution)/shard_map/ppermute | solution.py:478
  140.9 54.0 %collective-permute-start.9 = (bf16[512,2048]{1,0:T(8,128)(2,1)}, bf16[512,2048]{1,0:T(8,128)(2,1)}, u32[]{:S(2)}, u32[]{:S(2)}) collective-permute-start(bf16[512,2048]{1,0:T(8,128)(2,1)} %collective-permute-done.7.refs_4_.refs_2_), channel_id=1, source_target_pairs={{2,3},{6,7},{10,11},{14,15},{18,19},{22,23},{26,27},{30,31}} | collective-permute-start | bytes 6291464 | tf_op jit(solution)/shard_map/ppermute | solution.py:478
  142.9 53.4 %collective-permute-start.10 = (bf16[2,256,2048]{2,1,0:T(8,128)(2,1)}, bf16[2,256,2048]{2,1,0:T(8,128)(2,1)}, u32[]{:S(2)}, u32[]{:S(2)}) collective-permute-start(bf16[2,256,2048]{2,1,0:T(8,128)(2,1)} %pad_maximum_fusion.2), channel_id=1, source_target_pairs={{0,2},{3,1},{4,6},{7,5},{8,10},{11,9},{12,14},{15,13},{16,18},{19,... | collective-permute-start | bytes 6291464 | tf_op jit(solution)/shard_map/ppermute | solution.py:478
  196.2 47.4 %collective-permute-start.11 = (bf16[2,256,2048]{2,1,0:T(8,128)(2,1)}, bf16[2,256,2048]{2,1,0:T(8,128)(2,1)}, u32[]{:S(2)}, u32[]{:S(2)}) collective-permute-start(bf16[2,256,2048]{2,1,0:T(8,128)(2,1)} %pad_maximum_fusion.2), channel_id=1, source_target_pairs={{1,3},{2,0},{5,7},{6,4},{9,11},{10,8},{13,15},{14,12},{17,19},{18,... | collective-permute-start | bytes 6291464 | tf_op jit(solution)/shard_map/ppermute | solution.py:478
  248.1 308.9 %reduce-scatter.13.cloned.1.call-start = ((), (), s32[]{:S(2)}) async-start(), calls=%async_computation.9 | async-start | bytes 10485760
  248.1 15.2 %collective-permute-start.15 = (bf16[512,2048]{1,0:T(8,128)(2,1)}, bf16[512,2048]{1,0:T(8,128)(2,1)}, u32[]{:S(2)}, u32[]{:S(2)}) collective-permute-start(bf16[512,2048]{1,0:T(8,128)(2,1)} %param.16), channel_id=1, source_target_pairs={{0,4},{4,0},{8,12},{12,8},{16,20},{20,16},{24,28},{28,24},{1,5},{5... | collective-permute-start | bytes 6291464 | tf_op jit(solution)/shard_map/ppermute | solution.py:474
  249.8 7.5 collective-permute-start.16
  253.0 25.3 %collective-permute-start.14 = (bf16[512,512]{1,0:T(8,128)(2,1)}, bf16[512,512]{1,0:T(8,128)(2,1)}, u32[]{:S(2)}, u32[]{:S(2)}) collective-permute-start(bf16[512,512]{1,0:T(8,128)(2,1)} %get-tuple-element.632), channel_id=1, source_target_pairs={{0,3},{1,2},{2,1},{3,0},{4,7},{5,6},{6,5},{7,4},{8,11},{9,10},{10,... | collective-permute-start | bytes 1572872 | tf_op jit(solution)/shard_map/ppermute | solution.py:474
  254.8 44.5 %collective-permute-start.13 = (bf16[512,512]{1,0:T(8,128)(2,1)}, bf16[512,512]{1,0:T(8,128)(2,1)}, u32[]{:S(2)}, u32[]{:S(2)}) collective-permute-start(bf16[512,512]{1,0:T(8,128)(2,1)} %get-tuple-element.633), channel_id=1, source_target_pairs={{0,2},{1,3},{2,0},{3,1},{4,6},{5,7},{6,4},{7,5},{8,10},{9,11},{10,... | collective-permute-start | bytes 1572872 | tf_op jit(solution)/shard_map/ppermute | solution.py:474
  254.8 44.5 %collective-permute-start.12 = (bf16[512,512]{1,0:T(8,128)(2,1)S(1)}, bf16[512,512]{1,0:T(8,128)(2,1)}, u32[]{:S(2)}, u32[]{:S(2)}) collective-permute-start(bf16[512,512]{1,0:T(8,128)(2,1)S(1)} %get-tuple-element.634), channel_id=1, source_target_pairs={{0,1},{1,0},{2,3},{3,2},{4,5},{5,4},{6,7},{7,6},{8,9},{9,8},{10,11... | collective-permute-start | bytes 1572872 | tf_op jit(solution)/shard_map/ppermute | solution.py:474
  261.8 16.0 %collective-permute-start.18 = (f32[128]{0:T(128)S(1)}, f32[128]{0:T(128)S(1)}, u32[]{:S(2)}, u32[]{:S(2)}) collective-permute-start(f32[128]{0:T(128)S(1)} %add.436), channel_id=1, source_target_pairs={{0,16},{4,20},{8,24},{12,28},{16,0},{20,4},{24,8},{28,12},{1,17},{... | collective-permute-start | bytes 1544 | tf_op jit(solution)/shard_map/ppermute | solution.py:474
  310.9 8.1 collective-permute-start.19
  311.0 20.3 %collective-permute-start.20 = (bf16[192,2048]{1,0:T(8,128)(2,1)S(1)}, bf16[192,2048]{1,0:T(8,128)(2,1)S(1)}, u32[]{:S(2)}, u32[]{:S(2)}) collective-permute-start(bf16[192,2048]{1,0:T(8,128)(2,1)S(1)} %slice.342), channel_id=1, source_target_pairs={{0,1},{1,0},{2,3},{3,2},{4,5},{5,4},{6,7},{7,6},{8,9},{9,8},{10,11... | collective-permute-start | bytes 2359304 | tf_op jit(solution)/shard_map/ppermute | solution.py:474
  335.4 12.3 %collective-permute-start.21 = (bf16[112,2048]{1,0:T(8,128)(2,1)S(1)}, bf16[112,2048]{1,0:T(8,128)(2,1)S(1)}, u32[]{:S(2)}, u32[]{:S(2)}) collective-permute-start(bf16[112,2048]{1,0:T(8,128)(2,1)S(1)} %slice.266), channel_id=1, source_target_pairs={{0,1},{1,0},{2,3},{3,2},{4,5},{5,4},{6,7},{7,6},{8,9},{9,8},{10,11... | collective-permute-start | bytes 1376264 | tf_op jit(solution)/shard_map/ppermute | solution.py:474
  347.8 19.9 %collective-permute-start.22 = (bf16[208,2048]{1,0:T(8,128)(2,1)S(1)}, bf16[208,2048]{1,0:T(8,128)(2,1)S(1)}, u32[]{:S(2)}, u32[]{:S(2)}) collective-permute-start(bf16[208,2048]{1,0:T(8,128)(2,1)S(1)} %slice.267), channel_id=1, source_target_pairs={{0,1},{1,0},{2,3},{3,2},{4,5},{5,4},{6,7},{7,6},{8,9},{9,8},{10,11... | collective-permute-start | bytes 2555912 | tf_op jit(solution)/shard_map/ppermute | solution.py:474
  368.0 19.1 %collective-permute-start.24 = (bf16[160,2048]{1,0:T(8,128)(2,1)S(1)}, bf16[160,2048]{1,0:T(8,128)(2,1)S(1)}, u32[]{:S(2)}, u32[]{:S(2)}) collective-permute-start(bf16[160,2048]{1,0:T(8,128)(2,1)S(1)} %slice.268), channel_id=1, source_target_pairs={{0,1},{1,0},{2,3},{3,2},{4,5},{5,4},{6,7},{7,6},{8,9},{9,8},{10,11... | collective-permute-start | bytes 1966088 | tf_op jit(solution)/shard_map/ppermute | solution.py:474
  388.1 18.2 %collective-permute-start.25 = (bf16[176,2048]{1,0:T(8,128)(2,1)S(1)}, bf16[176,2048]{1,0:T(8,128)(2,1)S(1)}, u32[]{:S(2)}, u32[]{:S(2)}) collective-permute-start(bf16[176,2048]{1,0:T(8,128)(2,1)S(1)} %slice.269), channel_id=1, source_target_pairs={{0,1},{1,0},{2,3},{3,2},{4,5},{5,4},{6,7},{7,6},{8,9},{9,8},{10,11... | collective-permute-start | bytes 2162696 | tf_op jit(solution)/shard_map/ppermute | solution.py:474
  408.1 16.3 %collective-permute-start.26 = (bf16[512,2048]{1,0:T(8,128)(2,1)S(1)}, bf16[512,2048]{1,0:T(8,128)(2,1)}, u32[]{:S(2)}, u32[]{:S(2)}) collective-permute-start(bf16[512,2048]{1,0:T(8,128)(2,1)S(1)} %slice.271), channel_id=1, source_target_pairs={{0,4},{4,0},{8,12},{12,8},{16,20},{20,16},{24,28},{28,24},{1,5},{5... | collective-permute-start | bytes 6291464 | tf_op jit(solution)/shard_map/ppermute | solution.py:474
  409.2 18.7 %collective-permute-start.27 = (bf16[176,2048]{1,0:T(8,128)(2,1)}, bf16[176,2048]{1,0:T(8,128)(2,1)S(1)}, u32[]{:S(2)}, u32[]{:S(2)}) collective-permute-start(bf16[176,2048]{1,0:T(8,128)(2,1)} %slice.272), channel_id=1, source_target_pairs={{0,1},{1,0},{2,3},{3,2},{4,5},{5,4},{6,7},{7,6},{8,9},{9,8},{10,11... | collective-permute-start | bytes 2162696 | tf_op jit(solution)/shard_map/ppermute | solution.py:474
  429.3 30.0 %collective-permute-start.29 = (bf16[256,2048]{1,0:T(8,128)(2,1)}, bf16[256,2048]{1,0:T(8,128)(2,1)}, u32[]{:S(2)}, u32[]{:S(2)}) collective-permute-start(bf16[256,2048]{1,0:T(8,128)(2,1)} %slice.273), channel_id=1, source_target_pairs={{0,1},{1,0},{2,3},{3,2},{4,5},{5,4},{6,7},{7,6},{8,9},{9,8},{10,11... | collective-permute-start | bytes 3145736 | tf_op jit(solution)/shard_map/ppermute | solution.py:474
  459.3 178.5 %reduce-scatter.15.cloned.1.call-start = ((), (), s32[]{:S(2)}) async-start(), calls=%async_computation.10 | async-start | bytes 10485760
  459.4 12.2 %collective-permute-start.30 = (bf16[64,2048]{1,0:T(8,128)(2,1)S(1)}, bf16[64,2048]{1,0:T(8,128)(2,1)S(1)}, u32[]{:S(2)}, u32[]{:S(2)}) collective-permute-start(bf16[64,2048]{1,0:T(8,128)(2,1)S(1)} %slice.274), channel_id=1, source_target_pairs={{0,1},{1,0},{2,3},{3,2},{4,5},{5,4},{6,7},{7,6},{8,9},{9,8},{10,11... | collective-permute-start | bytes 786440 | tf_op jit(solution)/shard_map/ppermute | solution.py:474
  471.7 8.0 collective-permute-start.31
  480.4 13.7 %collective-permute-start.32 = (bf16[128,2048]{1,0:T(8,128)(2,1)S(1)}, bf16[128,2048]{1,0:T(8,128)(2,1)S(1)}, u32[]{:S(2)}, u32[]{:S(2)}) collective-permute-start(bf16[128,2048]{1,0:T(8,128)(2,1)S(1)} %slice.277), channel_id=1, source_target_pairs={{0,1},{1,0},{2,3},{3,2},{4,5},{5,4},{6,7},{7,6},{8,9},{9,8},{10,11... | collective-permute-start | bytes 1572872 | tf_op jit(solution)/shard_map/ppermute | solution.py:474
  501.6 30.9 %collective-permute-start.34 = (bf16[320,2048]{1,0:T(8,128)(2,1)S(1)}, bf16[320,2048]{1,0:T(8,128)(2,1)S(1)}, u32[]{:S(2)}, u32[]{:S(2)}) collective-permute-start(bf16[320,2048]{1,0:T(8,128)(2,1)S(1)} %slice.280), channel_id=1, source_target_pairs={{0,1},{1,0},{2,3},{3,2},{4,5},{5,4},{6,7},{7,6},{8,9},{9,8},{10,11... | collective-permute-start | bytes 3932168 | tf_op jit(solution)/shard_map/ppermute | solution.py:474
  532.5 189.4 %reduce-scatter.17.cloned.1.call-start = ((), (), s32[]{:S(2)}) async-start(), calls=%async_computation.11 | async-start | bytes 5242880
  535.7 17.6 %collective-permute-start.35 = (bf16[512,2048]{1,0:T(8,128)(2,1)}, bf16[512,2048]{1,0:T(8,128)(2,1)}, u32[]{:S(2)}, u32[]{:S(2)}) collective-permute-start(bf16[512,2048]{1,0:T(8,128)(2,1)} %slice.282), channel_id=1, source_target_pairs={{0,4},{4,0},{8,12},{12,8},{16,20},{20,16},{24,28},{28,24},{1,5},{5... | collective-permute-start | bytes 6291464 | tf_op jit(solution)/shard_map/ppermute | solution.py:474
  536.7 20.3 %collective-permute-start.36 = (bf16[192,2048]{1,0:T(8,128)(2,1)}, bf16[192,2048]{1,0:T(8,128)(2,1)}, u32[]{:S(2)}, u32[]{:S(2)}) collective-permute-start(bf16[192,2048]{1,0:T(8,128)(2,1)} %slice.283), channel_id=1, source_target_pairs={{0,1},{1,0},{2,3},{3,2},{4,5},{5,4},{6,7},{7,6},{8,9},{9,8},{10,11... | collective-permute-start | bytes 2359304 | tf_op jit(solution)/shard_map/ppermute | solution.py:474
  558.0 30.0 %collective-permute-start.37 = (bf16[1,256,1024]{2,1,0:T(8,128)(2,1)S(1)}, bf16[1,256,1024]{2,1,0:T(8,128)(2,1)}, u32[]{:S(2)}, u32[]{:S(2)}) collective-permute-start(bf16[1,256,1024]{2,1,0:T(8,128)(2,1)S(1)} %slice.284), channel_id=1, source_target_pairs={{0,2},{1,3},{2,0},{3,1},{4,6},{5,7},{6,4},{7,5},{8,10},{9,11},{10,... | collective-permute-start | bytes 1572872 | tf_op jit(solution)/shard_map/ppermute | solution.py:474
  560.5 27.6 %collective-permute-start.38 = (f32[128]{0:T(128)S(1)}, f32[128]{0:T(128)S(1)}, u32[]{:S(2)}, u32[]{:S(2)}) collective-permute-start(f32[128]{0:T(128)S(1)} %copy-done.64), channel_id=1, source_target_pairs={{0,1},{1,0},{2,3},{3,2},{4,5},{5,4},{6,7},{7,6},{8,9},{9,8},{10,11... | collective-permute-start | bytes 1544 | tf_op jit(solution)/shard_map/ppermute | solution.py:474
  590.8 42.9 %collective-permute-start.42 = (bf16[4,256,2048]{2,1,0:T(8,128)(2,1)S(1)}, bf16[4,256,2048]{2,1,0:T(8,128)(2,1)S(1)}, u32[]{:S(2)}, u32[]{:S(2)}) collective-permute-start(bf16[4,256,2048]{2,1,0:T(8,128)(2,1)S(1)} %slice.291), channel_id=1, source_target_pairs={{0,4},{4,0},{8,12},{12,8},{16,20},{20,16},{24,28},{28,24},{1,5},{5... | collective-permute-start | bytes 12582920 | tf_op jit(solution)/shard_map/ppermute | solution.py:474
  593.4 24.7 %collective-permute-start.39 = (bf16[512,512]{1,0:T(8,128)(2,1)S(1)}, bf16[512,512]{1,0:T(8,128)(2,1)S(1)}, u32[]{:S(2)}, u32[]{:S(2)}) collective-permute-start(bf16[512,512]{1,0:T(8,128)(2,1)S(1)} %get-tuple-element.629), channel_id=1, source_target_pairs={{0,1},{1,0},{2,3},{3,2},{4,5},{5,4},{6,7},{7,6},{8,9},{9,8},{10,11... | collective-permute-start | bytes 1572872 | tf_op jit(solution)/shard_map/ppermute | solution.py:474
  593.9 38.2 %collective-permute-start.40 = (bf16[512,512]{1,0:T(8,128)(2,1)S(1)}, bf16[512,512]{1,0:T(8,128)(2,1)S(1)}, u32[]{:S(2)}, u32[]{:S(2)}) collective-permute-start(bf16[512,512]{1,0:T(8,128)(2,1)S(1)} %get-tuple-element.628), channel_id=1, source_target_pairs={{0,2},{1,3},{2,0},{3,1},{4,6},{5,7},{6,4},{7,5},{8,10},{9,11},{10,... | collective-permute-start | bytes 1572872 | tf_op jit(solution)/shard_map/ppermute | solution.py:474
  594.8 38.1 %collective-permute-start.41 = (bf16[512,512]{1,0:T(8,128)(2,1)S(1)}, bf16[512,512]{1,0:T(8,128)(2,1)S(1)}, u32[]{:S(2)}, u32[]{:S(2)}) collective-permute-start(bf16[512,512]{1,0:T(8,128)(2,1)S(1)} %get-tuple-element.627), channel_id=1, source_target_pairs={{0,3},{1,2},{2,1},{3,0},{4,7},{5,6},{6,5},{7,4},{8,11},{9,10},{10,... | collective-permute-start | bytes 1572872 | tf_op jit(solution)/shard_map/ppermute | solution.py:474
  637.8 227.6 %reduce-scatter.11.cloned.1.call-start = ((), (), s32[]{:S(2)}) async-start(), calls=%async_computation.6 | async-start | bytes 10485760 | tf_op jit(solution)/shard_map/reduce_scatter | solution.py:890
  638.1 57.5 %collective-permute-start.44 = (bf16[1,256,1024]{2,1,0:T(8,128)(2,1)S(1)}, bf16[1,256,1024]{2,1,0:T(8,128)(2,1)}, u32[]{:S(2)}, u32[]{:S(2)}) collective-permute-start(bf16[1,256,1024]{2,1,0:T(8,128)(2,1)S(1)} %slice.295), channel_id=1, source_target_pairs={{0,2},{1,3},{2,0},{3,1},{4,6},{5,7},{6,4},{7,5},{8,10},{9,11},{10,... | collective-permute-start | bytes 1572872 | tf_op jit(solution)/shard_map/ppermute | solution.py:474
  650.5 45.1 %collective-permute-start.45 = (bf16[1,256,1024]{2,1,0:T(8,128)(2,1)}, bf16[1,256,1024]{2,1,0:T(8,128)(2,1)}, u32[]{:S(2)}, u32[]{:S(2)}) collective-permute-start(bf16[1,256,1024]{2,1,0:T(8,128)(2,1)} %slice.296), channel_id=1, source_target_pairs={{0,2},{1,3},{2,0},{3,1},{4,6},{5,7},{6,4},{7,5},{8,10},{9,11},{10,... | collective-permute-start | bytes 1572872 | tf_op jit(solution)/shard_map/ppermute | solution.py:474
  696.5 25.5 %collective-permute-start.46 = (bf16[1,256,1024]{2,1,0:T(8,128)(2,1)}, bf16[1,256,1024]{2,1,0:T(8,128)(2,1)S(1)}, u32[]{:S(2)}, u32[]{:S(2)}) collective-permute-start(bf16[1,256,1024]{2,1,0:T(8,128)(2,1)} %slice.298), channel_id=1, source_target_pairs={{0,2},{1,3},{2,0},{3,1},{4,6},{5,7},{6,4},{7,5},{8,10},{9,11},{10,... | collective-permute-start | bytes 1572872 | tf_op jit(solution)/shard_map/ppermute | solution.py:474
  724.2 24.3 %collective-permute-start.47 = (f32[128]{0:T(128)S(1)}, f32[128]{0:T(128)S(1)}, u32[]{:S(2)}, u32[]{:S(2)}) collective-permute-start(f32[128]{0:T(128)S(1)} %add.473), channel_id=1, source_target_pairs={{0,2},{1,3},{2,0},{3,1},{4,6},{5,7},{6,4},{7,5},{8,10},{9,11},{10,... | collective-permute-start | bytes 1544 | tf_op jit(solution)/shard_map/ppermute | solution.py:474
  728.6 102.6 %collective-permute-start.43 = (bf16[512,2048]{1,0:T(8,128)(2,1)}, bf16[512,2048]{1,0:T(8,128)(2,1)}, u32[]{:S(2)}, u32[]{:S(2)}) collective-permute-start(bf16[512,2048]{1,0:T(8,128)(2,1)} %slice.293), channel_id=1, source_target_pairs={{0,4},{4,0},{8,12},{12,8},{16,20},{20,16},{24,28},{28,24},{1,5},{5... | collective-permute-start | bytes 6291464 | tf_op jit(solution)/shard_map/ppermute | solution.py:474
  753.2 27.6 %collective-permute-start.51 = (bf16[4,256,1536]{2,1,0:T(8,128)(2,1)}, bf16[4,256,1536]{2,1,0:T(8,128)(2,1)}, u32[]{:S(2)}, u32[]{:S(2)}) collective-permute-start(bf16[4,256,1536]{2,1,0:T(8,128)(2,1)} %slice.303), channel_id=1, source_target_pairs={{0,4},{4,0},{8,12},{12,8},{16,20},{20,16},{24,28},{28,24},{1,5},{5... | collective-permute-start | bytes 9437192 | tf_op jit(solution)/shard_map/ppermute | solution.py:474
  771.1 5.0 collective-permute-start.49
  772.7 13.5 %collective-permute-start.56 = (bf16[256,1024]{1,0:T(8,128)(2,1)S(1)}, bf16[256,1024]{1,0:T(8,128)(2,1)S(1)}, u32[]{:S(2)}, u32[]{:S(2)}) collective-permute-start(bf16[256,1024]{1,0:T(8,128)(2,1)S(1)} %slice_bitcast_fusion.3), channel_id=1, source_target_pairs={{0,4},{4,0},{8,12},{12,8},{16,20},{20,16},{24,28},{28,24},{1,5},{5... | collective-permute-start | bytes 1572872 | tf_op jit(solution)/shard_map/ppermute | solution.py:474
  776.2 4.7 collective-permute-start.50
  783.8 21.4 %collective-permute-start.55 = (bf16[1,256,1536]{2,1,0:T(8,128)(2,1)S(1)}, bf16[1,256,1536]{2,1,0:T(8,128)(2,1)}, u32[]{:S(2)}, u32[]{:S(2)}) collective-permute-start(bf16[1,256,1536]{2,1,0:T(8,128)(2,1)S(1)} %slice.311), channel_id=1, source_target_pairs={{0,16},{4,20},{8,24},{12,28},{16,0},{20,4},{24,8},{28,12},{1,17},{... | collective-permute-start | bytes 2359304 | tf_op jit(solution)/shard_map/ppermute | solution.py:474
  786.2 21.2 %collective-permute-start.58 = (bf16[256,1024]{1,0:T(8,128)(2,1)}, bf16[256,1024]{1,0:T(8,128)(2,1)}, u32[]{:S(2)}, u32[]{:S(2)}) collective-permute-start(bf16[256,1024]{1,0:T(8,128)(2,1)} %slice_bitcast_fusion.1), channel_id=1, source_target_pairs={{0,4},{4,0},{8,12},{12,8},{16,20},{20,16},{24,28},{28,24},{1,5},{5... | collective-permute-start | bytes 1572872 | tf_op jit(solution)/shard_map/ppermute | solution.py:474
  806.2 20.4 %collective-permute-start.57 = (bf16[1,256,1536]{2,1,0:T(8,128)(2,1)}, bf16[1,256,1536]{2,1,0:T(8,128)(2,1)}, u32[]{:S(2)}, u32[]{:S(2)}) collective-permute-start(bf16[1,256,1536]{2,1,0:T(8,128)(2,1)} %slice.316), channel_id=1, source_target_pairs={{0,16},{4,20},{8,24},{12,28},{16,0},{20,4},{24,8},{28,12},{1,17},{... | collective-permute-start | bytes 2359304 | tf_op jit(solution)/shard_map/ppermute | solution.py:474
  829.7 19.7 %collective-permute-start.59 = (bf16[1,256,1536]{2,1,0:T(8,128)(2,1)S(1)}, bf16[1,256,1536]{2,1,0:T(8,128)(2,1)S(1)}, u32[]{:S(2)}, u32[]{:S(2)}) collective-permute-start(bf16[1,256,1536]{2,1,0:T(8,128)(2,1)S(1)} %slice.350), channel_id=1, source_target_pairs={{0,8},{4,12},{8,0},{12,4},{16,24},{20,28},{24,16},{28,20},{1,9},{5... | collective-permute-start | bytes 2359304 | tf_op jit(solution)/shard_map/ppermute | solution.py:474
  869.0 6.7 collective-permute-start.60
  871.3 29.8 %collective-permute-start.54 = (bf16[256,512]{1,0:T(8,128)(2,1)S(1)}, bf16[256,512]{1,0:T(8,128)(2,1)S(1)}, u32[]{:S(2)}, u32[]{:S(2)}) collective-permute-start(bf16[256,512]{1,0:T(8,128)(2,1)S(1)} %get-tuple-element.642), channel_id=1, source_target_pairs={{0,3},{1,2},{2,1},{3,0},{4,7},{5,6},{6,5},{7,4},{8,11},{9,10},{10,... | collective-permute-start | bytes 786440 | tf_op jit(solution)/shard_map/ppermute | solution.py:474
  873.6 27.6 %collective-permute-start.53 = (bf16[256,512]{1,0:T(8,128)(2,1)S(1)}, bf16[256,512]{1,0:T(8,128)(2,1)S(1)}, u32[]{:S(2)}, u32[]{:S(2)}) collective-permute-start(bf16[256,512]{1,0:T(8,128)(2,1)S(1)} %get-tuple-element.643), channel_id=1, source_target_pairs={{0,2},{1,3},{2,0},{3,1},{4,6},{5,7},{6,4},{7,5},{8,10},{9,11},{10,... | collective-permute-start | bytes 786440 | tf_op jit(solution)/shard_map/ppermute | solution.py:474
  873.6 27.6 %collective-permute-start.52 = (bf16[256,512]{1,0:T(8,128)(2,1)S(1)}, bf16[256,512]{1,0:T(8,128)(2,1)S(1)}, u32[]{:S(2)}, u32[]{:S(2)}) collective-permute-start(bf16[256,512]{1,0:T(8,128)(2,1)S(1)} %get-tuple-element.641), channel_id=1, source_target_pairs={{0,1},{1,0},{2,3},{3,2},{4,5},{5,4},{6,7},{7,6},{8,9},{9,8},{10,11... | collective-permute-start | bytes 786440 | tf_op jit(solution)/shard_map/ppermute | solution.py:474
  875.7 23.9 %collective-permute-start.61 = (f32[24576]{0:T(1024)S(1)}, f32[24576]{0:T(1024)S(1)}, u32[]{:S(2)}, u32[]{:S(2)}) collective-permute-start(f32[24576]{0:T(1024)S(1)} %add.505), channel_id=1, source_target_pairs={{0,2},{1,3},{2,0},{3,1},{4,6},{5,7},{6,4},{7,5},{8,10},{9,11},{10,... | collective-permute-start | bytes 294920 | tf_op jit(solution)/shard_map/ppermute | solution.py:474
  (82 other events, 1119.4 us)
Sparse Core Ops, SparseCore 0:
  12.5 48.2 all-gather.10
  86.7 60.1 all-gather.12
  149.4 87.5 all-gather.6
  248.2 87.0 all-gather.8
  459.4 86.4 reduce-scatter.12
  549.1 86.3 reduce-scatter.14
  639.1 58.6 reduce-scatter.16
  722.1 143.2 reduce-scatter.10

commit v5 on v4

--- a/solution.py
+++ b/solution.py
@@ -301,31 +301,33 @@
 
 
 def matmul_kernel(terms, *refs):
-    lefts, rights, out_ref = refs[:terms], refs[terms : 2 * terms], refs[2 * terms]
+    lefts, rights, outs = refs[:terms], refs[terms : 2 * terms], refs[2 * terms :]
     total = dot_nt(lefts[0][...], rights[0][...])
     for left, right in zip(lefts[1:], rights[1:]):
         total = total + dot_nt(left[...], right[...])
-    out_ref[...] = total.astype(BF)
-
-
-def matmul_sum(lefts, rights):
+    rows = outs[0].shape[0]
+    outs[0][...] = total[:rows].astype(BF)
+    outs[1][...] = total[rows:].astype(BF)
+
+
+def matmul_sum(lefts, rights, seconds):
     terms = len(lefts)
     rows, depth = lefts[0].shape
     columns = rights[0].shape[0]
-    row_step, step = min(1024, rows), min(512, columns)
+    step = min(512, columns)
 
     def body(*refs):
         matmul_kernel(terms, *refs)
 
     return pl.pallas_call(
         body,
-        grid=(rows // row_step, columns // step),
-        in_specs=[pl.BlockSpec((row_step, depth), lambda m, n: (m, 0))] * terms
-        + [pl.BlockSpec((step, depth), lambda m, n: (n, 0))] * terms,
-        out_specs=pl.BlockSpec((row_step, step), lambda m, n: (m, n)),
-        out_shape=jax.ShapeDtypeStruct((rows, columns), BF),
+        grid=(columns // step,),
+        in_specs=[pl.BlockSpec((rows, depth), lambda n: (0, 0))] * terms
+        + [pl.BlockSpec((step, depth), lambda n: (n, 0))] * terms,
+        out_specs=[pl.BlockSpec((rows // 2, step), lambda n: (0, n))] * 2,
+        out_shape=[jax.ShapeDtypeStruct((rows // 2, columns), BF)] * 2,
         compiler_params=pltpu.CompilerParams(vmem_limit_bytes=VMEM_CAP),
-        cost_estimate=cost(2 * terms * rows * columns * depth / 8e14),
+        cost_estimate=cost(seconds),
         name="matmul_sum",
     )(*lefts, *rights)
 
@@ -702,7 +704,7 @@
     biases = [bias_up[j * half : (j + 1) * half] for j in range(slices)]
 
     def core_rows(partial):
-        return add_low(partial[:rows], shift(partial[rows:], "dp", 1))
+        return add_low(partial[0], shift(partial[1], "dp", 1))
 
     def chips_sum(blocks):
         blocks = blocks.reshape(dp_count // 2, 2, edge, blocks.shape[2])
@@ -742,11 +744,11 @@
         return work
 
     def far_result(state):
-        return dict(state, result_far=matmul_sum(state["act_far"], w_down))
+        return dict(state, result_far=matmul_sum(state["act_far"], w_down, 1e-5))
 
     def near_grad(state):
         return dict(
-            state, grad_near=matmul_sum(state["pre_near"], w_up), ffn_far=core_rows(state.pop("result_far"))
+            state, grad_near=matmul_sum(state["pre_near"], w_up, 1e-5), ffn_far=core_rows(state.pop("result_far"))
         )
 
     def down_blocks(state):
@@ -763,7 +765,7 @@
         return work
 
     def far_grad(state):
-        return dict(state, grad_far=matmul_sum(state["pre_far"], w_up))
+        return dict(state, grad_far=matmul_sum(state["pre_far"], w_up, 2e-6))
 
     def up_blocks(state):
         rights = [list(pair) for pair in zip(state["pre_near"], state["pre_far"])]
@@ -772,7 +774,7 @@
 
     def near_result(state):
         return dict(
-            state, result_near=matmul_sum(state["act_near"], w_down), near_rows=core_rows(state.pop("grad_near"))
+            state, result_near=matmul_sum(state["act_near"], w_down, 1e-5), near_rows=core_rows(state.pop("grad_near"))
         )
 
     def both(first, second):
@@ -812,7 +814,10 @@
     middle = rows // 2
     ffn_low, state = beside(state["ffn_far"][:middle], "tensor", 1, [(1, both(back_rows_in, down_blocks))], state)
     part_down = chips_sum(state.pop("down"))
-    steps = [(1, far_back(j)) for j in range(slices)] + [(slices, far_grad)]
+    work = far_back(0)
+    for j in range(1, slices):
+        work = both(work, far_back(j))
+    steps = [(1, both(work, far_grad))]
     ffn_high, state = beside(state.pop("ffn_far")[middle:], "tensor", 1, steps, state)
     ffn_across = jnp.concatenate([ffn_low, ffn_high], axis=0)
     far_rows = core_rows(state.pop("grad_far"))

time: 924 us -> 915 us (level)
  local copies, waits for them, and re-layouts: 63.6 us -> 52.5 us
  starting transfers between devices: 93.9 us -> 83.8 us
  waiting for transfers between devices: 240 us -> 250 us
    slice x4 -> x0, local copies, waits for them, and re-layouts: 10.4 us -> none  [core_rows(): return add_low(partial[:rows], shift(partial[rows:], 'dp', 1))]
    ppermute x54 -> x52, starting transfers between devices: 65.5 us -> 55.5 us  [shift(): lax.ppermute(value, axis, [(i, i ^ mask) for i in range(lax.axis_size(axi...]
    ppermute x54 -> x52, waiting for transfers between devices: 173 us -> 175 us  [shift(): lax.ppermute(value, axis, [(i, i ^ mask) for i in range(lax.axis_size(axi...]
  transfers between devices with their start and end apart: 70 -> 68, of which waited for: 25 -> 25; matrix products, arithmetic and copies ran while one was open for 25% -> 24% of each run, Pallas kernels for 34% -> 35%
where the time goes in v5:
time: 915 us; the launch traced here: 907 us
  Pallas kernels  326 us (36%)
  waiting for transfers between devices  250 us (27%)
  matrix products  93.1 us (10%)
  other arithmetic  85.5 us (9%)
  starting transfers between devices  83.8 us (9%)
  local copies, waits for them, and re-layouts  52.5 us (6%)
  between operations  16.1 us (2%)
    ppermute x52, waiting for transfers between devices, shift(): lax.ppermute(value, axis, [(i, i ^ mask) for i in range(lax.axis_size(axi...  175 us
    pallas_call x4, Pallas kernels, grad_blocks(): pl.pallas_call(body, grid_spec=pltpu.PrefetchScalarGridSpec(num_scalar_pr...  81.5 us
    ppermute x8, waiting for transfers between devices, move(): return lax.ppermute(value, axis, pairs)  62.4 us
    ppermute x52, starting transfers between devices, shift(): lax.ppermute(value, axis, [(i, i ^ mask) for i in range(lax.axis_size(axi...  55.5 us
    pallas_call x4, Pallas kernels, matmul_sum(): pl.pallas_call(body, grid=(columns // step,), in_specs=[pl.BlockSpec((row...  54.4 us
    pallas_call x4, Pallas kernels, update_tiles(): pl.pallas_call(body, grid=(count // group,), in_specs=[smem, smem, pl.Blo...  52.1 us
    pallas_call x1, Pallas kernels, attend_back(): pl.pallas_call(attend_back_kernel, grid=(heads,), in_specs=[pl.BlockSpec(...  44 us
    pallas_call x4, Pallas kernels, scatter_blocks(): pl.pallas_call(body, grid_spec=pltpu.PrefetchScalarGridSpec(num_scalar_pr...  37.8 us
  transfers between devices with their start and end apart: 68, of which 25 were waited for; matrix products, arithmetic and copies ran while one was open for 24% of the time, Pallas kernels for 35%

profile of v5, /device:TPU:0, one launch (start us, length us, event | category | flops | bytes accessed | tf_op | source)
XLA Modules:
  0.0 907.1 jit_solution(10519283653999288799)
XLA Ops:
  7.2 5.2 pack_weights.1
  16.7 7.0 collective-permute-start.1
  30.0 47.4 %collective-permute-done.2 = bf16[256,512]{1,0:T(8,128)(2,1)S(1)} collective-permute-done((bf16[256,512]{1,0:T(8,128)(2,1)S(1)}, bf16[256,512]{1,0:T(8,128)(2,1)S(1)}, u32[]{:S(2)}, u32[]{:S(2)}) %collective-permute-start.2) | collective-permute-done | bytes 262176 | tf_op jit(solution)/shard_map/ppermute | solution.py:476
  77.4 8.0 collective-permute-done.3
  89.9 49.6 %collective-permute-done.6.refs_6_.refs_4_ = bf16[512,2048]{1,0:T(8,128)(2,1)} collective-permute-done((bf16[512,2048]{1,0:T(8,128)(2,1)}, bf16[512,2048]{1,0:T(8,128)(2,1)}, u32[]{:S(2)}, u32[]{:S(2)}) %collective-permute-start.6) | collective-permute-done | bytes 2097184 | tf_op jit(solution)/shard_map/ppermute | solution.py:480
  142.9 11.7 %collective-permute-start.10 = (bf16[2,256,2048]{2,1,0:T(8,128)(2,1)}, bf16[2,256,2048]{2,1,0:T(8,128)(2,1)}, u32[]{:S(2)}, u32[]{:S(2)}) collective-permute-start(bf16[2,256,2048]{2,1,0:T(8,128)(2,1)} %pad_maximum_fusion.2), channel_id=1, source_target_pairs={{0,2},{3,1},{4,6},{7,5},{8,10},{11,9},{12,14},{15,13},{16,18},{19,... | collective-permute-start | bytes 6291464 | tf_op jit(solution)/shard_map/ppermute | solution.py:480
  157.8 8.6 scatter_blocks.4.refs_9_.refs_8_
  166.4 18.6 %project.2 = (bf16[2048,2048]{1,0:T(8,128)(2,1)}, bf16[2048,2048]{1,0:T(8,128)(2,1)}, bf16[2048,1536]{1,0:T(8,128)(2,1)}) custom-call(s32[3]{0:T(128)} %bitcast.217, s32[3]{0:T(128)} %bitcast.216, bf16[512,2048]{1,0:T(8,128)(2,1)} %fusion.5.refs_2_, bf16[512,2048]{1,0:T(8,128)(2,1)} %collective-permute-done.1.refs_3_, ...), custom_call_target="tpu_custom_call" | custom-call | bytes 63000000 | tf_op jit(solution)/shard_map/project/pallas_call | solution.py:453
  185.1 9.8 %scatter_blocks.5 = bf16[2048,2048]{1,0:T(8,128)(2,1)} custom-call(s32[8]{0:T(128)} %get-tuple-element.644.refs_0_, bf16[8,256,2048]{2,1,0:T(8,128)(2,1)} %bitcast.188), custom_call_target="tpu_custom_call" | custom-call | bytes 19573418 | tf_op jit(solution)/shard_map/scatter_blocks/pallas_call | solution.py:407
  199.6 11.5 %project.3 = (bf16[2048,2048]{1,0:T(8,128)(2,1)}, bf16[2048,2048]{1,0:T(8,128)(2,1)}, bf16[2048,1536]{1,0:T(8,128)(2,1)}) custom-call(s32[1]{0:T(128)} %slice.215.refs_0_, s32[1]{0:T(128)} %slice.216.refs_1_, bf16[512,2048]{1,0:T(8,128)(2,1)} %collective-permute-done.7.refs_4_.refs_2_, ...), custom_call_target="tpu_custom_call", output_to_operand_aliasing={{0}: (10, {}), {1}: (11, {}), {2}: (12, {})} | custom-call | bytes 21000000 | tf_op jit(solution)/shard_map/project/pallas_call | solution.py:453
  211.1 20.9 %attend.1 = (bf16[2048,512]{1,0:T(8,128)(2,1)}, f32[4,8,128]{2,1,0:T(8,128)}) custom-call(s32[1,2048]{1,0:T(1,128)} %compare_select_fusion.start_ref, bf16[2048,1536]{1,0:T(8,128)(2,1)} %get-tuple-element.329.qkv_ref), custom_call_target="tpu_custom_call" | custom-call | bytes 70000000 | tf_op jit(solution)/shard_map/attend/pallas_call | solution.py:91
  232.0 11.6 %collective-permute-done.11 = bf16[2,256,2048]{2,1,0:T(8,128)(2,1)} collective-permute-done((bf16[2,256,2048]{2,1,0:T(8,128)(2,1)}, bf16[2,256,2048]{2,1,0:T(8,128)(2,1)}, u32[]{:S(2)}, u32[]{:S(2)}) %collective-permute-start.11) | collective-permute-done | bytes 2097184 | tf_op jit(solution)/shard_map/ppermute | solution.py:480
  243.6 4.4 add.450
  263.3 4.8 pad_maximum_fusion.refs_1_
  268.1 9.7 %scatter_blocks.6 = (bf16[2048,1024]{1,0:T(8,128)(2,1)}, bf16[2048,1024]{1,0:T(8,128)(2,1)}) custom-call(s32[8]{0:T(128)} %gather_fusion, s32[8]{0:T(128)} %gather_fusion.1, bf16[8,256,2048]{2,1,0:T(8,128)(2,1)} %all-gather.7.cloned.1.call-done.refs_2_), custom_call_target="tpu_custom_call" | custom-call | bytes 19573418 | tf_op jit(solution)/shard_map/scatter_blocks/pallas_call | solution.py:407
  278.3 21.0 %collective-permute-done.13 = bf16[512,512]{1,0:T(8,128)(2,1)} collective-permute-done((bf16[512,512]{1,0:T(8,128)(2,1)}, bf16[512,512]{1,0:T(8,128)(2,1)}, u32[]{:S(2)}, u32[]{:S(2)}) %collective-permute-start.13) | collective-permute-done | bytes 524320 | tf_op jit(solution)/shard_map/ppermute | solution.py:476
  300.9 7.9 fusion.58
  311.1 8.0 convolution_convert_fusion.3
  319.0 4.2 pad_maximum_fusion.1.refs_1_
  323.3 8.0 fusion.18
  331.3 4.0 all-gather.9.cloned.1.call-done.refs_2_
  336.9 9.7 %scatter_blocks.7 = (bf16[2048,1024]{1,0:T(8,128)(2,1)}, bf16[2048,1024]{1,0:T(8,128)(2,1)}) custom-call(s32[8]{0:T(128)} %gather_fusion, s32[8]{0:T(128)} %gather_fusion.1, bf16[8,256,2048]{2,1,0:T(8,128)(2,1)} %all-gather.9.cloned.1.call-done.refs_2_), custom_call_target="tpu_custom_call" | custom-call | bytes 19573418 | tf_op jit(solution)/shard_map/scatter_blocks/pallas_call | solution.py:407
  349.3 7.8 convolution_convert_fusion.2
  357.1 7.7 fusion.24
  372.2 7.5 fusion.29
  379.7 7.4 fusion.34
  389.6 13.3 %matmul_sum.4 = (bf16[512,2048]{1,0:T(8,128)(2,1)}, bf16[512,2048]{1,0:T(8,128)(2,1)}) custom-call(bf16[1024,1024]{1,0:T(8,128)(2,1)} %get-tuple-element.405.refs_0_.refs_4_, bf16[1024,1024]{1,0:T(8,128)(2,1)} %get-tuple-element.406.refs_1_.refs_6_, bf16[2048,1024]{1,0:T(8,128)(2,1)} %get-tuple-element.344.refs_2_, bf16[2048,1024]{1,0:T(8,128)(2,1)} %get-tuple-element.358.refs_3_), custom_call_target="tpu_custom_call" | custom-call | bytes 35000000 | tf_op jit(solution)/shard_map/matmul_sum/pallas_call | solution.py:322
  402.9 3.4 collective-permute-done.25
  408.7 13.7 %matmul_sum.5 = (bf16[512,2048]{1,0:T(8,128)(2,1)}, bf16[512,2048]{1,0:T(8,128)(2,1)}) custom-call(bf16[1024,1024]{1,0:T(8,128)(2,1)} %get-tuple-element.537.refs_0_.refs_3_, bf16[1024,1024]{1,0:T(8,128)(2,1)} %get-tuple-element.539.refs_1_.refs_5_, bf16[2048,1024]{1,0:T(8,128)(2,1)} %get-tuple-element.340.refs_2_, bf16[2048,1024]{1,0:T(8,128)(2,1)} %get-tuple-element.356.refs_3_), custom_call_target="tpu_custom_call" | custom-call | bytes 35000000 | tf_op jit(solution)/shard_map/matmul_sum/pallas_call | solution.py:322
  432.7 24.7 %grad_blocks.4 = bf16[8,256,2048]{2,1,0:T(8,128)(2,1)} custom-call(s32[8]{0:T(128)} %gather_fusion.1, bf16[1024,2048]{1,0:T(8,128)(2,1)} %pad_maximum_fusion.refs_1_, bf16[1024,2048]{1,0:T(8,128)(2,1)} %copy-done.25, bf16[1024,1024]{1,0:T(8,128)(2,1)} %get-tuple-element.460.refs_3_.refs_0_, bf16[1024,1024]{1,0:T(8,128)(2,1)} %get-tuple-element.405.refs_0_.refs_4_, ...), custom_call_target="tpu_custom_call" | custom-call | bytes 75161928 | tf_op jit(solution)/shard_map/grad_blocks/pallas_call | solution.py:287
  459.1 10.6 %multiply_convert_fusion.1.refs_0_.refs_4_ = bf16[1024,1024]{1,0:T(8,128)(2,1)} fusion(bf16[1024,1024]{1,0:T(8,128)(2,1)} %get-tuple-element.425, bf16[1024,2048]{1,0:T(8,128)(2,1)} %copy-done.25, bf16[2048,1024]{1,0:T(8,128)(2,1)} %get-tuple-element.344.refs_2_), kind=kOutput, calls=%fused_computation.70 | convolution fusion | flops 4298113024 | bytes 12582912 | tf_op jit(solution)/shard_map/dot_general | solution.py:761
  469.7 5.8 multiply_convert_fusion.refs_1_.refs_6_
  475.5 13.5 %matmul_sum.6 = (bf16[512,2048]{1,0:T(8,128)(2,1)}, bf16[512,2048]{1,0:T(8,128)(2,1)}) custom-call(bf16[1024,1024]{1,0:T(8,128)(2,1)} %multiply_convert_fusion.1.refs_0_.refs_4_, bf16[1024,1024]{1,0:T(8,128)(2,1)} %multiply_convert_fusion.refs_1_.refs_6_, bf16[2048,1024]{1,0:T(8,128)(2,1)} %get-tuple-element.340.refs_2_, ...), custom_call_target="tpu_custom_call" | custom-call | bytes 7000000 | tf_op jit(solution)/shard_map/matmul_sum/pallas_call | solution.py:322
  489.1 4.4 collective-permute-done.31
  496.4 25.0 %grad_blocks.5 = bf16[8,256,2048]{2,1,0:T(8,128)(2,1)} custom-call(s32[8]{0:T(128)} %gather_fusion, bf16[1024,2048]{1,0:T(8,128)(2,1)} %pad_maximum_fusion.1.refs_1_, bf16[1024,2048]{1,0:T(8,128)(2,1)} %copy-done.24, bf16[1024,1024]{1,0:T(8,128)(2,1)} %get-tuple-element.537.refs_0_.refs_3_, bf16[1024,1024]{1,0:T(8,128)(2,1)} %multiply_convert_fusion.1.refs_0_.refs_4_, ...), custom_call_target="tpu_custom_call" | custom-call | bytes 75161928 | tf_op jit(solution)/shard_map/grad_blocks/pallas_call | solution.py:287
  521.3 5.5 collective-permute-done.32
  529.5 13.8 %matmul_sum.7 = (bf16[512,2048]{1,0:T(8,128)(2,1)}, bf16[512,2048]{1,0:T(8,128)(2,1)}) custom-call(bf16[1024,1024]{1,0:T(8,128)(2,1)} %get-tuple-element.460.refs_3_.refs_0_, bf16[1024,1024]{1,0:T(8,128)(2,1)} %get-tuple-element.461.refs_5_.refs_1_, bf16[2048,1024]{1,0:T(8,128)(2,1)} %get-tuple-element.344.refs_2_, bf16[2048,1024]{1,0:T(8,128)(2,1)} %get-tuple-element.358.refs_3_), custom_call_target="tpu_custom_call" | custom-call | bytes 35000000 | tf_op jit(solution)/shard_map/matmul_sum/pallas_call | solution.py:322
  552.0 4.7 multiply_reduce_fusion
  556.8 5.3 fusion.48
  562.1 4.8 convolution_convert_fusion.1
  567.0 11.2 %grad_blocks.6 = bf16[8,256,2048]{2,1,0:T(8,128)(2,1)} custom-call(s32[8]{0:T(128)} %gather_fusion.2, bf16[512,2048]{1,0:T(8,128)(2,1)} %copy-done.6, bf16[512,2048]{1,0:T(8,128)(2,1)} %copy-done.21), custom_call_target="tpu_custom_call" | custom-call | bytes 18790480 | tf_op jit(solution)/shard_map/grad_blocks/pallas_call | solution.py:287
  588.1 18.8 %collective-permute-done.37 = bf16[512,512]{1,0:T(8,128)(2,1)S(1)} collective-permute-done((bf16[512,512]{1,0:T(8,128)(2,1)S(1)}, bf16[512,512]{1,0:T(8,128)(2,1)S(1)}, u32[]{:S(2)}, u32[]{:S(2)}) %collective-permute-start.37) | collective-permute-done | bytes 524320 | tf_op jit(solution)/shard_map/ppermute | solution.py:476
  607.7 15.9 %collective-permute-done.38 = bf16[512,512]{1,0:T(8,128)(2,1)S(1)} collective-permute-done((bf16[512,512]{1,0:T(8,128)(2,1)S(1)}, bf16[512,512]{1,0:T(8,128)(2,1)S(1)}, u32[]{:S(2)}, u32[]{:S(2)}) %collective-permute-start.38) | collective-permute-done | bytes 524320 | tf_op jit(solution)/shard_map/ppermute | solution.py:476
  625.2 4.0 add_convert_fusion
  629.3 4.4 reduce-scatter.15.cloned.1.call-done
  634.0 4.9 collective-permute-start.42
  642.3 44.0 %attend_back.1.refs_2_ = bf16[2048,1536]{1,0:T(8,128)(2,1)} custom-call(s32[1,2048]{1,0:T(1,128)} %compare_select_fusion.start_ref, bf16[2048,1536]{1,0:T(8,128)(2,1)} %get-tuple-element.329.qkv_ref, bf16[2048,512]{1,0:T(8,128)(2,1)} %constant_dynamic-update-slice_fusion.17.back_ref), custom_call_target="tpu_custom_call" | custom-call | bytes 140000000 | tf_op jit(solution)/shard_map/attend_back/pallas_call | solution.py:146
  689.8 17.7 %convolution_convert_fusion = bf16[2048,2048]{1,0:T(8,128)(2,1)} fusion(bf16[2048,1536]{1,0:T(8,128)(2,1)} %attend_back.1.refs_2_, bf16[2048,1536]{1,0:T(8,128)(2,1)S(1)} %bitcast.178), kind=kOutput, calls=%fused_computation.10 | convolution fusion | flops 12889096192 | bytes 20971520 | tf_op jit(solution)/shard_map/dot_general | solution.py:31
  707.5 4.2 collective-permute-done.44
  715.1 20.7 %grad_blocks.7 = bf16[8,256,1536]{2,1,0:T(8,128)(2,1)} custom-call(s32[8]{0:T(128)} %gather_fusion.4, bf16[2048,2048]{1,0:T(8,128)(2,1)} %get-tuple-element.525.refs_1_, bf16[2048,1536]{1,0:T(8,128)(2,1)} %attend_back.1.refs_2_), custom_call_target="tpu_custom_call" | custom-call | bytes 56371444 | tf_op jit(solution)/shard_map/grad_blocks/pallas_call | solution.py:287
  736.8 3.8 slice.258
  741.8 10.6 %convert_reduce_fusion = (f32[2048]{0:T(1024)S(1)}, f32[2048]{0:T(1024)S(1)}) fusion(bf16[2048,2048]{1,0:T(8,128)(2,1)} %convolution_convert_fusion, bf16[2048,2048]{1,0:T(8,128)(2,1)} %get-tuple-element.536), kind=kLoop, calls=%fused_computation.5 | loop fusion | flops 20967424 | bytes 16793600 | tf_op jit(solution)/shard_map/reduce_sum | solution.py:919
  760.0 3.5 collective-permute-done.47
  775.8 16.8 %update_tiles.4 = (f32[96,128,128]{2,1,0:T(8,128)}, f32[96,128,128]{2,1,0:T(8,128)}, f32[96,128,128]{2,1,0:T(8,128)}, bf16[96,128,128]{2,1,0:T(8,128)(2,1)}, f32...) custom-call(f32[32]{0:T(128)} %get-tuple-element.647.refs_0_, ...), custom_call_target="tpu_custom_call" | custom-call | bytes 56000000 | tf_op jit(solution)/shard_map/update_tiles/pallas_call | solution.py:247
  797.8 16.1 %update_tiles.5 = (f32[96,128,128]{2,1,0:T(8,128)}, f32[96,128,128]{2,1,0:T(8,128)}, f32[96,128,128]{2,1,0:T(8,128)}, bf16[96,128,128]{2,1,0:T(8,128)(2,1)}, f32...) custom-call(f32[32]{0:T(128)} %get-tuple-element.646.refs_0_, ...), custom_call_target="tpu_custom_call", output_to_operand_aliasing={{0}: (10, {}), {1}: (11, {}), {2}: (12, {}), {3}: (13, {}),... | custom-call | bytes 56000000 | tf_op jit(solution)/shard_map/update_tiles/pallas_call | solution.py:247
  818.5 4.8 add_convert_fusion.2
  824.2 3.0 and_select_fusion.2
  827.3 9.8 %collective-permute-done.57 = bf16[1,256,1536]{2,1,0:T(8,128)(2,1)S(1)} collective-permute-done((bf16[1,256,1536]{2,1,0:T(8,128)(2,1)S(1)}, bf16[1,256,1536]{2,1,0:T(8,128)(2,1)S(1)}, u32[]{:S(2)}, u32[]{:S(2)}) %collective-permute-start.57) | collective-permute-done | bytes 786464 | tf_op jit(solution)/shard_map/ppermute | solution.py:476
  839.5 13.0 %update_tiles.6 = (f32[96,128,128]{2,1,0:T(8,128)}, f32[96,128,128]{2,1,0:T(8,128)}, f32[96,128,128]{2,1,0:T(8,128)}, bf16[96,128,128]{2,1,0:T(8,128)(2,1)}, f32...) custom-call(f32[24]{0:T(128)} %bitcast.215, ...), custom_call_target="tpu_custom_call", output_to_operand_aliasing={{0}: (10, {}), {1}: (11, {}), {2}: (12, {}), {3}: (13, {}),... | custom-call | bytes 42000000 | tf_op jit(solution)/shard_map/update_tiles/pallas_call | solution.py:247
  852.5 3.8 reduce-scatter.11.cloned.1.call-done
  861.1 3.4 collective-permute-start.52
  865.5 3.3 collective-permute-start.59
  871.7 18.9 %collective-permute-done.59 = f32[24576]{0:T(1024)S(1)} collective-permute-done((f32[24576]{0:T(1024)S(1)}, f32[24576]{0:T(1024)S(1)}, u32[]{:S(2)}, u32[]{:S(2)}) %collective-permute-start.59) | collective-permute-done | bytes 98336 | tf_op jit(solution)/shard_map/ppermute | solution.py:476
  893.5 6.3 update_tiles.7
  (436 shorter events, 157.9 us)
Async XLA Ops:
  7.2 150.6 %all-gather.11.cloned.1.call-start = ((), (), s32[]{:S(2)}) async-start(), calls=%async_computation.7 | async-start | bytes 7077888 | tf_op jit(solution)/shard_map/all_gather | solution.py:628
  12.4 172.6 %all-gather.13.cloned.1.call-start = ((), (), s32[]{:S(2)}) async-start(), calls=%async_computation.8 | async-start | bytes 9437184 | tf_op jit(solution)/shard_map/all_gather | solution.py:661
  15.4 70.0 %collective-permute-start = (bf16[512,2048]{1,0:T(8,128)(2,1)}, bf16[512,2048]{1,0:T(8,128)(2,1)}, u32[]{:S(2)}, u32[]{:S(2)}) collective-permute-start(bf16[512,2048]{1,0:T(8,128)(2,1)} %fusion.5.refs_2_), channel_id=1, source_target_pairs={{1,0},{2,1},{3,2},{5,4},{6,5},{7,6},{9,8},{10,9},{11,10},{13,12},{... | collective-permute-start | bytes 6291464 | tf_op jit(solution)/shard_map/ppermute | solution.py:480
  16.7 68.7 %collective-permute-start.1 = (bf16[512,2048]{1,0:T(8,128)(2,1)}, bf16[512,2048]{1,0:T(8,128)(2,1)}, u32[]{:S(2)}, u32[]{:S(2)}) collective-permute-start(bf16[512,2048]{1,0:T(8,128)(2,1)} %fusion.5.refs_2_), channel_id=1, source_target_pairs={{0,1},{1,2},{2,3},{4,5},{5,6},{6,7},{8,9},{9,10},{10,11},{12,13},{... | collective-permute-start | bytes 6291464 | tf_op jit(solution)/shard_map/ppermute | solution.py:480
  24.0 53.4 %collective-permute-start.2 = (bf16[256,512]{1,0:T(8,128)(2,1)S(1)}, bf16[256,512]{1,0:T(8,128)(2,1)S(1)}, u32[]{:S(2)}, u32[]{:S(2)}) collective-permute-start(bf16[256,512]{1,0:T(8,128)(2,1)S(1)} %copy-done.40), channel_id=1, source_target_pairs={{0,1},{1,0},{2,3},{3,2},{4,5},{5,4},{6,7},{7,6},{8,9},{9,8},{10,11... | collective-permute-start | bytes 786440 | tf_op jit(solution)/shard_map/ppermute | solution.py:476
  24.7 60.7 %collective-permute-start.3 = (bf16[256,512]{1,0:T(8,128)(2,1)S(1)}, bf16[256,512]{1,0:T(8,128)(2,1)S(1)}, u32[]{:S(2)}, u32[]{:S(2)}) collective-permute-start(bf16[256,512]{1,0:T(8,128)(2,1)S(1)} %copy-done.40), channel_id=1, source_target_pairs={{0,2},{1,3},{2,0},{3,1},{4,6},{5,7},{6,4},{7,5},{8,10},{9,11},{10,... | collective-permute-start | bytes 786440 | tf_op jit(solution)/shard_map/ppermute | solution.py:476
  27.1 58.4 %collective-permute-start.4 = (bf16[256,512]{1,0:T(8,128)(2,1)S(1)}, bf16[256,512]{1,0:T(8,128)(2,1)S(1)}, u32[]{:S(2)}, u32[]{:S(2)}) collective-permute-start(bf16[256,512]{1,0:T(8,128)(2,1)S(1)} %copy-done.40), channel_id=1, source_target_pairs={{0,3},{1,2},{2,1},{3,0},{4,7},{5,6},{6,5},{7,4},{8,11},{9,10},{10,... | collective-permute-start | bytes 786440 | tf_op jit(solution)/shard_map/ppermute | solution.py:476
  86.6 181.5 %all-gather.7.cloned.1.call-start = ((), (), s32[]{:S(2)}) async-start(), calls=%async_computation.4 | async-start | bytes 10485760 | tf_op jit(solution)/shard_map/all_gather | solution.py:622
  86.6 52.9 %collective-permute-start.6 = (bf16[512,2048]{1,0:T(8,128)(2,1)}, bf16[512,2048]{1,0:T(8,128)(2,1)}, u32[]{:S(2)}, u32[]{:S(2)}) collective-permute-start(bf16[512,2048]{1,0:T(8,128)(2,1)} %collective-permute-done.refs_5_), channel_id=1, source_target_pairs={{1,0},{2,1},{5,4},{6,5},{9,8},{10,9},{13,12},{14,13},{17,16},{18,1... | collective-permute-start | bytes 6291464 | tf_op jit(solution)/shard_map/ppermute | solution.py:480
  87.9 51.6 %collective-permute-start.7 = (bf16[512,2048]{1,0:T(8,128)(2,1)}, bf16[512,2048]{1,0:T(8,128)(2,1)}, u32[]{:S(2)}, u32[]{:S(2)}) collective-permute-start(bf16[512,2048]{1,0:T(8,128)(2,1)} %collective-permute-done.1.refs_3_), channel_id=1, source_target_pairs={{1,2},{2,3},{5,6},{6,7},{9,10},{10,11},{13,14},{14,15},{17,18},{18... | collective-permute-start | bytes 6291464 | tf_op jit(solution)/shard_map/ppermute | solution.py:480
  139.5 195.7 %all-gather.9.cloned.1.call-start = ((), (), s32[]{:S(2)}) async-start(), calls=%async_computation.5 | async-start | bytes 10485760 | tf_op jit(solution)/shard_map/all_gather | solution.py:622
  139.6 55.3 %collective-permute-start.8 = (bf16[512,2048]{1,0:T(8,128)(2,1)}, bf16[512,2048]{1,0:T(8,128)(2,1)}, u32[]{:S(2)}, u32[]{:S(2)}) collective-permute-start(bf16[512,2048]{1,0:T(8,128)(2,1)} %collective-permute-done.6.refs_6_.refs_4_), channel_id=1, source_target_pairs={{1,0},{5,4},{9,8},{13,12},{17,16},{21,20},{25,24},{29,28}} | collective-permute-start | bytes 6291464 | tf_op jit(solution)/shard_map/ppermute | solution.py:480
  140.9 54.0 %collective-permute-start.9 = (bf16[512,2048]{1,0:T(8,128)(2,1)}, bf16[512,2048]{1,0:T(8,128)(2,1)}, u32[]{:S(2)}, u32[]{:S(2)}) collective-permute-start(bf16[512,2048]{1,0:T(8,128)(2,1)} %collective-permute-done.7.refs_4_.refs_2_), channel_id=1, source_target_pairs={{2,3},{6,7},{10,11},{14,15},{18,19},{22,23},{26,27},{30,31}} | collective-permute-start | bytes 6291464 | tf_op jit(solution)/shard_map/ppermute | solution.py:480
  142.9 53.4 %collective-permute-start.10 = (bf16[2,256,2048]{2,1,0:T(8,128)(2,1)}, bf16[2,256,2048]{2,1,0:T(8,128)(2,1)}, u32[]{:S(2)}, u32[]{:S(2)}) collective-permute-start(bf16[2,256,2048]{2,1,0:T(8,128)(2,1)} %pad_maximum_fusion.2), channel_id=1, source_target_pairs={{0,2},{3,1},{4,6},{7,5},{8,10},{11,9},{12,14},{15,13},{16,18},{19,... | collective-permute-start | bytes 6291464 | tf_op jit(solution)/shard_map/ppermute | solution.py:480
  196.2 47.4 %collective-permute-start.11 = (bf16[2,256,2048]{2,1,0:T(8,128)(2,1)}, bf16[2,256,2048]{2,1,0:T(8,128)(2,1)}, u32[]{:S(2)}, u32[]{:S(2)}) collective-permute-start(bf16[2,256,2048]{2,1,0:T(8,128)(2,1)} %pad_maximum_fusion.2), channel_id=1, source_target_pairs={{1,3},{2,0},{5,7},{6,4},{9,11},{10,8},{13,15},{14,12},{17,19},{18,... | collective-permute-start | bytes 6291464 | tf_op jit(solution)/shard_map/ppermute | solution.py:480
  248.0 300.1 %reduce-scatter.13.cloned.1.call-start = ((), (), s32[]{:S(2)}) async-start(), calls=%async_computation.9 | async-start | bytes 10485760
  248.1 15.2 %collective-permute-start.15 = (bf16[512,2048]{1,0:T(8,128)(2,1)}, bf16[512,2048]{1,0:T(8,128)(2,1)}, u32[]{:S(2)}, u32[]{:S(2)}) collective-permute-start(bf16[512,2048]{1,0:T(8,128)(2,1)} %param.16), channel_id=1, source_target_pairs={{0,4},{4,0},{8,12},{12,8},{16,20},{20,16},{24,28},{28,24},{1,5},{5... | collective-permute-start | bytes 6291464 | tf_op jit(solution)/shard_map/ppermute | solution.py:476
  249.8 7.5 collective-permute-start.16
  253.0 25.4 %collective-permute-start.14 = (bf16[512,512]{1,0:T(8,128)(2,1)}, bf16[512,512]{1,0:T(8,128)(2,1)}, u32[]{:S(2)}, u32[]{:S(2)}) collective-permute-start(bf16[512,512]{1,0:T(8,128)(2,1)} %get-tuple-element.618), channel_id=1, source_target_pairs={{0,3},{1,2},{2,1},{3,0},{4,7},{5,6},{6,5},{7,4},{8,11},{9,10},{10,... | collective-permute-start | bytes 1572872 | tf_op jit(solution)/shard_map/ppermute | solution.py:476
  254.8 44.5 %collective-permute-start.13 = (bf16[512,512]{1,0:T(8,128)(2,1)}, bf16[512,512]{1,0:T(8,128)(2,1)}, u32[]{:S(2)}, u32[]{:S(2)}) collective-permute-start(bf16[512,512]{1,0:T(8,128)(2,1)} %get-tuple-element.619), channel_id=1, source_target_pairs={{0,2},{1,3},{2,0},{3,1},{4,6},{5,7},{6,4},{7,5},{8,10},{9,11},{10,... | collective-permute-start | bytes 1572872 | tf_op jit(solution)/shard_map/ppermute | solution.py:476
  254.8 44.5 %collective-permute-start.12 = (bf16[512,512]{1,0:T(8,128)(2,1)S(1)}, bf16[512,512]{1,0:T(8,128)(2,1)}, u32[]{:S(2)}, u32[]{:S(2)}) collective-permute-start(bf16[512,512]{1,0:T(8,128)(2,1)S(1)} %get-tuple-element.620), channel_id=1, source_target_pairs={{0,1},{1,0},{2,3},{3,2},{4,5},{5,4},{6,7},{7,6},{8,9},{9,8},{10,11... | collective-permute-start | bytes 1572872 | tf_op jit(solution)/shard_map/ppermute | solution.py:476
  261.8 16.0 %collective-permute-start.18 = (f32[128]{0:T(128)S(1)}, f32[128]{0:T(128)S(1)}, u32[]{:S(2)}, u32[]{:S(2)}) collective-permute-start(f32[128]{0:T(128)S(1)} %add.436), channel_id=1, source_target_pairs={{0,16},{4,20},{8,24},{12,28},{16,0},{20,4},{24,8},{28,12},{1,17},{... | collective-permute-start | bytes 1544 | tf_op jit(solution)/shard_map/ppermute | solution.py:476
  310.9 8.1 collective-permute-start.19
  311.0 20.3 %collective-permute-start.20 = (bf16[192,2048]{1,0:T(8,128)(2,1)S(1)}, bf16[192,2048]{1,0:T(8,128)(2,1)S(1)}, u32[]{:S(2)}, u32[]{:S(2)}) collective-permute-start(bf16[192,2048]{1,0:T(8,128)(2,1)S(1)} %slice.297), channel_id=1, source_target_pairs={{0,1},{1,0},{2,3},{3,2},{4,5},{5,4},{6,7},{7,6},{8,9},{9,8},{10,11... | collective-permute-start | bytes 2359304 | tf_op jit(solution)/shard_map/ppermute | solution.py:476
  335.3 12.3 %collective-permute-start.21 = (bf16[112,2048]{1,0:T(8,128)(2,1)S(1)}, bf16[112,2048]{1,0:T(8,128)(2,1)S(1)}, u32[]{:S(2)}, u32[]{:S(2)}) collective-permute-start(bf16[112,2048]{1,0:T(8,128)(2,1)S(1)} %slice.232), channel_id=1, source_target_pairs={{0,1},{1,0},{2,3},{3,2},{4,5},{5,4},{6,7},{7,6},{8,9},{9,8},{10,11... | collective-permute-start | bytes 1376264 | tf_op jit(solution)/shard_map/ppermute | solution.py:476
  347.7 19.9 %collective-permute-start.22 = (bf16[208,2048]{1,0:T(8,128)(2,1)S(1)}, bf16[208,2048]{1,0:T(8,128)(2,1)S(1)}, u32[]{:S(2)}, u32[]{:S(2)}) collective-permute-start(bf16[208,2048]{1,0:T(8,128)(2,1)S(1)} %slice.233), channel_id=1, source_target_pairs={{0,1},{1,0},{2,3},{3,2},{4,5},{5,4},{6,7},{7,6},{8,9},{9,8},{10,11... | collective-permute-start | bytes 2555912 | tf_op jit(solution)/shard_map/ppermute | solution.py:476
  367.8 4.2 collective-permute-start.23
  368.0 19.1 %collective-permute-start.24 = (bf16[160,2048]{1,0:T(8,128)(2,1)S(1)}, bf16[160,2048]{1,0:T(8,128)(2,1)S(1)}, u32[]{:S(2)}, u32[]{:S(2)}) collective-permute-start(bf16[160,2048]{1,0:T(8,128)(2,1)S(1)} %slice.234), channel_id=1, source_target_pairs={{0,1},{1,0},{2,3},{3,2},{4,5},{5,4},{6,7},{7,6},{8,9},{9,8},{10,11... | collective-permute-start | bytes 1966088 | tf_op jit(solution)/shard_map/ppermute | solution.py:476
  388.0 18.2 %collective-permute-start.25 = (bf16[176,2048]{1,0:T(8,128)(2,1)S(1)}, bf16[176,2048]{1,0:T(8,128)(2,1)S(1)}, u32[]{:S(2)}, u32[]{:S(2)}) collective-permute-start(bf16[176,2048]{1,0:T(8,128)(2,1)S(1)} %slice.235), channel_id=1, source_target_pairs={{0,1},{1,0},{2,3},{3,2},{4,5},{5,4},{6,7},{7,6},{8,9},{9,8},{10,11... | collective-permute-start | bytes 2162696 | tf_op jit(solution)/shard_map/ppermute | solution.py:476
  406.3 16.2 %collective-permute-start.26 = (bf16[512,2048]{1,0:T(8,128)(2,1)}, bf16[512,2048]{1,0:T(8,128)(2,1)S(1)}, u32[]{:S(2)}, u32[]{:S(2)}) collective-permute-start(bf16[512,2048]{1,0:T(8,128)(2,1)} %get-tuple-element.393), channel_id=1, source_target_pairs={{0,4},{4,0},{8,12},{12,8},{16,20},{20,16},{24,28},{28,24},{1,5},{5... | collective-permute-start | bytes 6291464 | tf_op jit(solution)/shard_map/ppermute | solution.py:476
  407.3 18.8 %collective-permute-start.27 = (bf16[176,2048]{1,0:T(8,128)(2,1)}, bf16[176,2048]{1,0:T(8,128)(2,1)S(1)}, u32[]{:S(2)}, u32[]{:S(2)}) collective-permute-start(bf16[176,2048]{1,0:T(8,128)(2,1)} %slice.236), channel_id=1, source_target_pairs={{0,1},{1,0},{2,3},{3,2},{4,5},{5,4},{6,7},{7,6},{8,9},{9,8},{10,11... | collective-permute-start | bytes 2162696 | tf_op jit(solution)/shard_map/ppermute | solution.py:476
  427.4 30.0 %collective-permute-start.29 = (bf16[256,2048]{1,0:T(8,128)(2,1)}, bf16[256,2048]{1,0:T(8,128)(2,1)}, u32[]{:S(2)}, u32[]{:S(2)}) collective-permute-start(bf16[256,2048]{1,0:T(8,128)(2,1)} %slice.237), channel_id=1, source_target_pairs={{0,1},{1,0},{2,3},{3,2},{4,5},{5,4},{6,7},{7,6},{8,9},{9,8},{10,11... | collective-permute-start | bytes 3145736 | tf_op jit(solution)/shard_map/ppermute | solution.py:476
  457.4 176.2 %reduce-scatter.15.cloned.1.call-start = ((), (), s32[]{:S(2)}) async-start(), calls=%async_computation.10 | async-start | bytes 10485760
  457.6 31.4 %collective-permute-start.30 = (bf16[256,2048]{1,0:T(8,128)(2,1)S(1)}, bf16[256,2048]{1,0:T(8,128)(2,1)S(1)}, u32[]{:S(2)}, u32[]{:S(2)}) collective-permute-start(bf16[256,2048]{1,0:T(8,128)(2,1)S(1)} %slice.238), channel_id=1, source_target_pairs={{0,1},{1,0},{2,3},{3,2},{4,5},{5,4},{6,7},{7,6},{8,9},{9,8},{10,11... | collective-permute-start | bytes 3145736 | tf_op jit(solution)/shard_map/ppermute | solution.py:476
  489.0 4.4 collective-permute-start.31
  495.9 30.9 %collective-permute-start.32 = (bf16[320,2048]{1,0:T(8,128)(2,1)S(1)}, bf16[320,2048]{1,0:T(8,128)(2,1)S(1)}, u32[]{:S(2)}, u32[]{:S(2)}) collective-permute-start(bf16[320,2048]{1,0:T(8,128)(2,1)S(1)} %slice.239), channel_id=1, source_target_pairs={{0,1},{1,0},{2,3},{3,2},{4,5},{5,4},{6,7},{7,6},{8,9},{9,8},{10,11... | collective-permute-start | bytes 3932168 | tf_op jit(solution)/shard_map/ppermute | solution.py:476
  526.8 184.9 %reduce-scatter.17.cloned.1.call-start = ((), (), s32[]{:S(2)}) async-start(), calls=%async_computation.11 | async-start | bytes 5242880
  526.9 16.4 %collective-permute-start.33 = (bf16[512,2048]{1,0:T(8,128)(2,1)}, bf16[512,2048]{1,0:T(8,128)(2,1)}, u32[]{:S(2)}, u32[]{:S(2)}) collective-permute-start(bf16[512,2048]{1,0:T(8,128)(2,1)} %get-tuple-element.463), channel_id=1, source_target_pairs={{0,4},{4,0},{8,12},{12,8},{16,20},{20,16},{24,28},{28,24},{1,5},{5... | collective-permute-start | bytes 6291464 | tf_op jit(solution)/shard_map/ppermute | solution.py:476
  527.9 20.3 %collective-permute-start.34 = (bf16[192,2048]{1,0:T(8,128)(2,1)}, bf16[192,2048]{1,0:T(8,128)(2,1)}, u32[]{:S(2)}, u32[]{:S(2)}) collective-permute-start(bf16[192,2048]{1,0:T(8,128)(2,1)} %slice.240), channel_id=1, source_target_pairs={{0,1},{1,0},{2,3},{3,2},{4,5},{5,4},{6,7},{7,6},{8,9},{9,8},{10,11... | collective-permute-start | bytes 2359304 | tf_op jit(solution)/shard_map/ppermute | solution.py:476
  549.3 29.0 %collective-permute-start.35 = (bf16[1,256,1024]{2,1,0:T(8,128)(2,1)S(1)}, bf16[1,256,1024]{2,1,0:T(8,128)(2,1)}, u32[]{:S(2)}, u32[]{:S(2)}) collective-permute-start(bf16[1,256,1024]{2,1,0:T(8,128)(2,1)S(1)} %slice.241), channel_id=1, source_target_pairs={{0,2},{1,3},{2,0},{3,1},{4,6},{5,7},{6,4},{7,5},{8,10},{9,11},{10,... | collective-permute-start | bytes 1572872 | tf_op jit(solution)/shard_map/ppermute | solution.py:476
  551.7 26.5 %collective-permute-start.36 = (f32[128]{0:T(128)S(1)}, f32[128]{0:T(128)S(1)}, u32[]{:S(2)}, u32[]{:S(2)}) collective-permute-start(f32[128]{0:T(128)S(1)} %copy-done.59), channel_id=1, source_target_pairs={{0,1},{1,0},{2,3},{3,2},{4,5},{5,4},{6,7},{7,6},{8,9},{9,8},{10,11... | collective-permute-start | bytes 1544 | tf_op jit(solution)/shard_map/ppermute | solution.py:476
  581.1 44.1 %collective-permute-start.40 = (bf16[4,256,2048]{2,1,0:T(8,128)(2,1)S(1)}, bf16[4,256,2048]{2,1,0:T(8,128)(2,1)S(1)}, u32[]{:S(2)}, u32[]{:S(2)}) collective-permute-start(bf16[4,256,2048]{2,1,0:T(8,128)(2,1)S(1)} %slice.248), channel_id=1, source_target_pairs={{0,4},{4,0},{8,12},{12,8},{16,20},{20,16},{24,28},{28,24},{1,5},{5... | collective-permute-start | bytes 12582920 | tf_op jit(solution)/shard_map/ppermute | solution.py:476
  583.7 23.2 %collective-permute-start.37 = (bf16[512,512]{1,0:T(8,128)(2,1)S(1)}, bf16[512,512]{1,0:T(8,128)(2,1)S(1)}, u32[]{:S(2)}, u32[]{:S(2)}) collective-permute-start(bf16[512,512]{1,0:T(8,128)(2,1)S(1)} %get-tuple-element.615), channel_id=1, source_target_pairs={{0,1},{1,0},{2,3},{3,2},{4,5},{5,4},{6,7},{7,6},{8,9},{9,8},{10,11... | collective-permute-start | bytes 1572872 | tf_op jit(solution)/shard_map/ppermute | solution.py:476
  585.4 38.2 %collective-permute-start.38 = (bf16[512,512]{1,0:T(8,128)(2,1)S(1)}, bf16[512,512]{1,0:T(8,128)(2,1)S(1)}, u32[]{:S(2)}, u32[]{:S(2)}) collective-permute-start(bf16[512,512]{1,0:T(8,128)(2,1)S(1)} %get-tuple-element.614), channel_id=1, source_target_pairs={{0,2},{1,3},{2,0},{3,1},{4,6},{5,7},{6,4},{7,5},{8,10},{9,11},{10,... | collective-permute-start | bytes 1572872 | tf_op jit(solution)/shard_map/ppermute | solution.py:476
  585.5 38.9 %collective-permute-start.39 = (bf16[512,512]{1,0:T(8,128)(2,1)S(1)}, bf16[512,512]{1,0:T(8,128)(2,1)S(1)}, u32[]{:S(2)}, u32[]{:S(2)}) collective-permute-start(bf16[512,512]{1,0:T(8,128)(2,1)S(1)} %get-tuple-element.613), channel_id=1, source_target_pairs={{0,3},{1,2},{2,1},{3,0},{4,7},{5,6},{6,5},{7,4},{8,11},{9,10},{10,... | collective-permute-start | bytes 1572872 | tf_op jit(solution)/shard_map/ppermute | solution.py:476
  633.7 222.7 %reduce-scatter.11.cloned.1.call-start = ((), (), s32[]{:S(2)}) async-start(), calls=%async_computation.6 | async-start | bytes 10485760 | tf_op jit(solution)/shard_map/reduce_scatter | solution.py:895
  634.0 52.3 %collective-permute-start.42 = (bf16[1,256,1024]{2,1,0:T(8,128)(2,1)S(1)}, bf16[1,256,1024]{2,1,0:T(8,128)(2,1)}, u32[]{:S(2)}, u32[]{:S(2)}) collective-permute-start(bf16[1,256,1024]{2,1,0:T(8,128)(2,1)S(1)} %slice.250), channel_id=1, source_target_pairs={{0,2},{1,3},{2,0},{3,1},{4,6},{5,7},{6,4},{7,5},{8,10},{9,11},{10,... | collective-permute-start | bytes 1572872 | tf_op jit(solution)/shard_map/ppermute | solution.py:476
  640.8 45.5 %collective-permute-start.43 = (bf16[1,256,1024]{2,1,0:T(8,128)(2,1)}, bf16[1,256,1024]{2,1,0:T(8,128)(2,1)}, u32[]{:S(2)}, u32[]{:S(2)}) collective-permute-start(bf16[1,256,1024]{2,1,0:T(8,128)(2,1)} %slice.251), channel_id=1, source_target_pairs={{0,2},{1,3},{2,0},{3,1},{4,6},{5,7},{6,4},{7,5},{8,10},{9,11},{10,... | collective-permute-start | bytes 1572872 | tf_op jit(solution)/shard_map/ppermute | solution.py:476
  687.1 24.6 %collective-permute-start.44 = (bf16[1,256,1024]{2,1,0:T(8,128)(2,1)}, bf16[1,256,1024]{2,1,0:T(8,128)(2,1)S(1)}, u32[]{:S(2)}, u32[]{:S(2)}) collective-permute-start(bf16[1,256,1024]{2,1,0:T(8,128)(2,1)} %slice.253), channel_id=1, source_target_pairs={{0,2},{1,3},{2,0},{3,1},{4,6},{5,7},{6,4},{7,5},{8,10},{9,11},{10,... | collective-permute-start | bytes 1572872 | tf_op jit(solution)/shard_map/ppermute | solution.py:476
  714.0 21.8 %collective-permute-start.45 = (f32[128]{0:T(128)S(1)}, f32[128]{0:T(128)S(1)}, u32[]{:S(2)}, u32[]{:S(2)}) collective-permute-start(f32[128]{0:T(128)S(1)} %add.473), channel_id=1, source_target_pairs={{0,2},{1,3},{2,0},{3,1},{4,6},{5,7},{6,4},{7,5},{8,10},{9,11},{10,... | collective-permute-start | bytes 1544 | tf_op jit(solution)/shard_map/ppermute | solution.py:476
  715.1 103.4 %collective-permute-start.41 = (bf16[512,2048]{1,0:T(8,128)(2,1)}, bf16[512,2048]{1,0:T(8,128)(2,1)}, u32[]{:S(2)}, u32[]{:S(2)}) collective-permute-start(bf16[512,2048]{1,0:T(8,128)(2,1)} %get-tuple-element.504), channel_id=1, source_target_pairs={{0,4},{4,0},{8,12},{12,8},{16,20},{20,16},{24,28},{28,24},{1,5},{5... | collective-permute-start | bytes 6291464 | tf_op jit(solution)/shard_map/ppermute | solution.py:476
  740.6 27.6 %collective-permute-start.49 = (bf16[4,256,1536]{2,1,0:T(8,128)(2,1)}, bf16[4,256,1536]{2,1,0:T(8,128)(2,1)}, u32[]{:S(2)}, u32[]{:S(2)}) collective-permute-start(bf16[4,256,1536]{2,1,0:T(8,128)(2,1)} %slice.258), channel_id=1, source_target_pairs={{0,4},{4,0},{8,12},{12,8},{16,20},{20,16},{24,28},{28,24},{1,5},{5... | collective-permute-start | bytes 9437192 | tf_op jit(solution)/shard_map/ppermute | solution.py:476
  758.4 5.1 collective-permute-start.47
  759.9 13.5 %collective-permute-start.54 = (bf16[256,1024]{1,0:T(8,128)(2,1)S(1)}, bf16[256,1024]{1,0:T(8,128)(2,1)S(1)}, u32[]{:S(2)}, u32[]{:S(2)}) collective-permute-start(bf16[256,1024]{1,0:T(8,128)(2,1)S(1)} %slice_bitcast_fusion.3), channel_id=1, source_target_pairs={{0,4},{4,0},{8,12},{12,8},{16,20},{20,16},{24,28},{28,24},{1,5},{5... | collective-permute-start | bytes 1572872 | tf_op jit(solution)/shard_map/ppermute | solution.py:476
  763.5 4.7 collective-permute-start.48
  771.1 21.6 %collective-permute-start.53 = (bf16[1,256,1536]{2,1,0:T(8,128)(2,1)S(1)}, bf16[1,256,1536]{2,1,0:T(8,128)(2,1)}, u32[]{:S(2)}, u32[]{:S(2)}) collective-permute-start(bf16[1,256,1536]{2,1,0:T(8,128)(2,1)S(1)} %slice.266), channel_id=1, source_target_pairs={{0,16},{4,20},{8,24},{12,28},{16,0},{20,4},{24,8},{28,12},{1,17},{... | collective-permute-start | bytes 2359304 | tf_op jit(solution)/shard_map/ppermute | solution.py:476
  773.4 21.3 %collective-permute-start.56 = (bf16[256,1024]{1,0:T(8,128)(2,1)}, bf16[256,1024]{1,0:T(8,128)(2,1)}, u32[]{:S(2)}, u32[]{:S(2)}) collective-permute-start(bf16[256,1024]{1,0:T(8,128)(2,1)} %slice_bitcast_fusion.1), channel_id=1, source_target_pairs={{0,4},{4,0},{8,12},{12,8},{16,20},{20,16},{24,28},{28,24},{1,5},{5... | collective-permute-start | bytes 1572872 | tf_op jit(solution)/shard_map/ppermute | solution.py:476
  793.6 20.3 %collective-permute-start.55 = (bf16[1,256,1536]{2,1,0:T(8,128)(2,1)}, bf16[1,256,1536]{2,1,0:T(8,128)(2,1)}, u32[]{:S(2)}, u32[]{:S(2)}) collective-permute-start(bf16[1,256,1536]{2,1,0:T(8,128)(2,1)} %slice.271), channel_id=1, source_target_pairs={{0,16},{4,20},{8,24},{12,28},{16,0},{20,4},{24,8},{28,12},{1,17},{... | collective-permute-start | bytes 2359304 | tf_op jit(solution)/shard_map/ppermute | solution.py:476
  817.1 20.0 %collective-permute-start.57 = (bf16[1,256,1536]{2,1,0:T(8,128)(2,1)S(1)}, bf16[1,256,1536]{2,1,0:T(8,128)(2,1)S(1)}, u32[]{:S(2)}, u32[]{:S(2)}) collective-permute-start(bf16[1,256,1536]{2,1,0:T(8,128)(2,1)S(1)} %slice.305), channel_id=1, source_target_pairs={{0,8},{4,12},{8,0},{12,4},{16,24},{20,28},{24,16},{28,20},{1,9},{5... | collective-permute-start | bytes 2359304 | tf_op jit(solution)/shard_map/ppermute | solution.py:476
  859.8 5.6 collective-permute-start.58
  861.1 31.0 %collective-permute-start.52 = (bf16[256,512]{1,0:T(8,128)(2,1)S(1)}, bf16[256,512]{1,0:T(8,128)(2,1)S(1)}, u32[]{:S(2)}, u32[]{:S(2)}) collective-permute-start(bf16[256,512]{1,0:T(8,128)(2,1)S(1)} %get-tuple-element.628), channel_id=1, source_target_pairs={{0,3},{1,2},{2,1},{3,0},{4,7},{5,6},{6,5},{7,4},{8,11},{9,10},{10,... | collective-permute-start | bytes 786440 | tf_op jit(solution)/shard_map/ppermute | solution.py:476
  864.5 27.5 %collective-permute-start.51 = (bf16[256,512]{1,0:T(8,128)(2,1)S(1)}, bf16[256,512]{1,0:T(8,128)(2,1)S(1)}, u32[]{:S(2)}, u32[]{:S(2)}) collective-permute-start(bf16[256,512]{1,0:T(8,128)(2,1)S(1)} %get-tuple-element.629), channel_id=1, source_target_pairs={{0,2},{1,3},{2,0},{3,1},{4,6},{5,7},{6,4},{7,5},{8,10},{9,11},{10,... | collective-permute-start | bytes 786440 | tf_op jit(solution)/shard_map/ppermute | solution.py:476
  864.5 27.5 %collective-permute-start.50 = (bf16[256,512]{1,0:T(8,128)(2,1)S(1)}, bf16[256,512]{1,0:T(8,128)(2,1)S(1)}, u32[]{:S(2)}, u32[]{:S(2)}) collective-permute-start(bf16[256,512]{1,0:T(8,128)(2,1)S(1)} %get-tuple-element.627), channel_id=1, source_target_pairs={{0,1},{1,0},{2,3},{3,2},{4,5},{5,4},{6,7},{7,6},{8,9},{9,8},{10,11... | collective-permute-start | bytes 786440 | tf_op jit(solution)/shard_map/ppermute | solution.py:476
  865.5 25.1 %collective-permute-start.59 = (f32[24576]{0:T(1024)S(1)}, f32[24576]{0:T(1024)S(1)}, u32[]{:S(2)}, u32[]{:S(2)}) collective-permute-start(f32[24576]{0:T(1024)S(1)} %add.505), channel_id=1, source_target_pairs={{0,2},{1,3},{2,0},{3,1},{4,6},{5,7},{6,4},{7,5},{8,10},{9,11},{10,... | collective-permute-start | bytes 294920 | tf_op jit(solution)/shard_map/ppermute | solution.py:476
  (75 other events, 1105.8 us)
Sparse Core Ops, SparseCore 0:
  12.5 48.2 all-gather.10
  86.7 60.1 all-gather.12
  149.4 87.5 all-gather.6
  248.2 87.0 all-gather.8
  457.5 86.4 reduce-scatter.12
  547.2 86.4 reduce-scatter.14
  637.2 52.6 reduce-scatter.16
  711.9 144.4 reduce-scatter.10

commit v6 on v5

--- a/solution.py
+++ b/solution.py
@@ -790,7 +790,7 @@
 
     steps = []
     for j in range(slices):
-        steps += [(1, arrive)] * (j > 0) + [(2, both(near_back(j), near_up(j)))]
+        steps += [(3, arrive)] * (j > 0) + [(6 if j else 7, both(near_back(j), near_up(j)))]
     normed_across, state = beside(normed_two, "tensor", 1, steps, state)
     state["normed_across"] = normed_across
 
@@ -807,8 +807,8 @@
     work = both(far_rows_in, far_up(0))
     for j in range(1, slices):
         work = both(work, far_up(j))
-    steps = [(slices, work)]
-    steps += [(slices, far_result), (slices, near_grad)]
+    steps = [(13, work)]
+    steps += [(9, far_result), (10, near_grad)]
     back_across, state = beside(cotangent, "tensor", 1, steps, state)
     state["back_across"] = back_across
     middle = rows // 2

time: 915 us -> 911 us (level)
  transfers between devices with their start and end apart: 68 -> 68, of which waited for: 25 -> 26; matrix products, arithmetic and copies ran while one was open for 24% -> 24% of each run, Pallas kernels for 35% -> 35%
where the time goes in v6:
time: 911 us; the launch traced here: 903 us
  Pallas kernels  326 us (36%)
  waiting for transfers between devices  245 us (27%)
  matrix products  92.7 us (10%)
  other arithmetic  86.6 us (10%)
  starting transfers between devices  83.1 us (9%)
  local copies, waits for them, and re-layouts  52.5 us (6%)
  between operations  16.1 us (2%)
    ppermute x52, waiting for transfers between devices, shift(): lax.ppermute(value, axis, [(i, i ^ mask) for i in range(lax.axis_size(axi...  174 us
    pallas_call x4, Pallas kernels, grad_blocks(): pl.pallas_call(body, grid_spec=pltpu.PrefetchScalarGridSpec(num_scalar_pr...  81.4 us
    ppermute x8, waiting for transfers between devices, move(): return lax.ppermute(value, axis, pairs)  62.4 us
    ppermute x52, starting transfers between devices, shift(): lax.ppermute(value, axis, [(i, i ^ mask) for i in range(lax.axis_size(axi...  55.1 us
    pallas_call x4, Pallas kernels, matmul_sum(): pl.pallas_call(body, grid=(columns // step,), in_specs=[pl.BlockSpec((row...  54.5 us
    pallas_call x4, Pallas kernels, update_tiles(): pl.pallas_call(body, grid=(count // group,), in_specs=[smem, smem, pl.Blo...  52.2 us
    pallas_call x1, Pallas kernels, attend_back(): pl.pallas_call(attend_back_kernel, grid=(heads,), in_specs=[pl.BlockSpec(...  44.1 us
    pallas_call x4, Pallas kernels, scatter_blocks(): pl.pallas_call(body, grid_spec=pltpu.PrefetchScalarGridSpec(num_scalar_pr...  37.8 us
  transfers between devices with their start and end apart: 68, of which 26 were waited for; matrix products, arithmetic and copies ran while one was open for 24% of the time, Pallas kernels for 35%

profile of v6, /device:TPU:0, one launch (start us, length us, event | category | flops | bytes accessed | tf_op | source)
XLA Modules:
  0.0 902.8 jit_solution(12070089061653814864)
XLA Ops:
  7.2 5.2 pack_weights.1
  16.7 7.0 collective-permute-start.1
  30.0 47.4 %collective-permute-done.2 = bf16[256,512]{1,0:T(8,128)(2,1)S(1)} collective-permute-done((bf16[256,512]{1,0:T(8,128)(2,1)S(1)}, bf16[256,512]{1,0:T(8,128)(2,1)S(1)}, u32[]{:S(2)}, u32[]{:S(2)}) %collective-permute-start.2) | collective-permute-done | bytes 262176 | tf_op jit(solution)/shard_map/ppermute | solution.py:476
  77.4 8.0 collective-permute-done.3
  89.9 49.6 %collective-permute-done.6.refs_6_.refs_4_ = bf16[512,2048]{1,0:T(8,128)(2,1)} collective-permute-done((bf16[512,2048]{1,0:T(8,128)(2,1)}, bf16[512,2048]{1,0:T(8,128)(2,1)}, u32[]{:S(2)}, u32[]{:S(2)}) %collective-permute-start.6) | collective-permute-done | bytes 2097184 | tf_op jit(solution)/shard_map/ppermute | solution.py:480
  142.9 11.7 %collective-permute-start.10 = (bf16[2,256,2048]{2,1,0:T(8,128)(2,1)}, bf16[2,256,2048]{2,1,0:T(8,128)(2,1)}, u32[]{:S(2)}, u32[]{:S(2)}) collective-permute-start(bf16[2,256,2048]{2,1,0:T(8,128)(2,1)} %pad_maximum_fusion.2), channel_id=1, source_target_pairs={{0,2},{3,1},{4,6},{7,5},{8,10},{11,9},{12,14},{15,13},{16,18},{19,... | collective-permute-start | bytes 6291464 | tf_op jit(solution)/shard_map/ppermute | solution.py:480
  157.9 8.6 scatter_blocks.4.refs_9_.refs_8_
  166.5 18.6 %project.2 = (bf16[2048,2048]{1,0:T(8,128)(2,1)}, bf16[2048,2048]{1,0:T(8,128)(2,1)}, bf16[2048,1536]{1,0:T(8,128)(2,1)}) custom-call(s32[3]{0:T(128)} %bitcast.217, s32[3]{0:T(128)} %bitcast.216, bf16[512,2048]{1,0:T(8,128)(2,1)} %fusion.5.refs_2_, bf16[512,2048]{1,0:T(8,128)(2,1)} %collective-permute-done.1.refs_3_, ...), custom_call_target="tpu_custom_call" | custom-call | bytes 63000000 | tf_op jit(solution)/shard_map/project/pallas_call | solution.py:453
  185.1 9.9 %scatter_blocks.5 = bf16[2048,2048]{1,0:T(8,128)(2,1)} custom-call(s32[8]{0:T(128)} %get-tuple-element.644.refs_0_, bf16[8,256,2048]{2,1,0:T(8,128)(2,1)} %bitcast.188), custom_call_target="tpu_custom_call" | custom-call | bytes 19573418 | tf_op jit(solution)/shard_map/scatter_blocks/pallas_call | solution.py:407
  199.6 11.5 %project.3 = (bf16[2048,2048]{1,0:T(8,128)(2,1)}, bf16[2048,2048]{1,0:T(8,128)(2,1)}, bf16[2048,1536]{1,0:T(8,128)(2,1)}) custom-call(s32[1]{0:T(128)} %slice.215.refs_0_, s32[1]{0:T(128)} %slice.216.refs_1_, bf16[512,2048]{1,0:T(8,128)(2,1)} %collective-permute-done.7.refs_4_.refs_2_, ...), custom_call_target="tpu_custom_call", output_to_operand_aliasing={{0}: (10, {}), {1}: (11, {}), {2}: (12, {})} | custom-call | bytes 21000000 | tf_op jit(solution)/shard_map/project/pallas_call | solution.py:453
  211.1 20.9 %attend.1 = (bf16[2048,512]{1,0:T(8,128)(2,1)}, f32[4,8,128]{2,1,0:T(8,128)}) custom-call(s32[1,2048]{1,0:T(1,128)} %compare_select_fusion.start_ref, bf16[2048,1536]{1,0:T(8,128)(2,1)} %get-tuple-element.329.qkv_ref), custom_call_target="tpu_custom_call" | custom-call | bytes 70000000 | tf_op jit(solution)/shard_map/attend/pallas_call | solution.py:91
  232.0 11.6 %collective-permute-done.11 = bf16[2,256,2048]{2,1,0:T(8,128)(2,1)} collective-permute-done((bf16[2,256,2048]{2,1,0:T(8,128)(2,1)}, bf16[2,256,2048]{2,1,0:T(8,128)(2,1)}, u32[]{:S(2)}, u32[]{:S(2)}) %collective-permute-start.11) | collective-permute-done | bytes 2097184 | tf_op jit(solution)/shard_map/ppermute | solution.py:480
  243.6 4.4 add.450
  263.3 4.8 pad_maximum_fusion.refs_1_
  268.1 9.7 %scatter_blocks.6 = (bf16[2048,1024]{1,0:T(8,128)(2,1)}, bf16[2048,1024]{1,0:T(8,128)(2,1)}) custom-call(s32[8]{0:T(128)} %gather_fusion, s32[8]{0:T(128)} %gather_fusion.1, bf16[8,256,2048]{2,1,0:T(8,128)(2,1)} %all-gather.7.cloned.1.call-done.refs_2_), custom_call_target="tpu_custom_call" | custom-call | bytes 19573418 | tf_op jit(solution)/shard_map/scatter_blocks/pallas_call | solution.py:407
  277.8 21.5 %collective-permute-done.13 = bf16[512,512]{1,0:T(8,128)(2,1)} collective-permute-done((bf16[512,512]{1,0:T(8,128)(2,1)}, bf16[512,512]{1,0:T(8,128)(2,1)}, u32[]{:S(2)}, u32[]{:S(2)}) %collective-permute-start.13) | collective-permute-done | bytes 524320 | tf_op jit(solution)/shard_map/ppermute | solution.py:476
  300.9 7.9 fusion.58
  311.0 8.0 convolution_convert_fusion.3
  319.0 4.2 pad_maximum_fusion.1.refs_1_
  323.2 8.0 fusion.18
  336.9 9.7 %scatter_blocks.7 = (bf16[2048,1024]{1,0:T(8,128)(2,1)}, bf16[2048,1024]{1,0:T(8,128)(2,1)}) custom-call(s32[8]{0:T(128)} %gather_fusion, s32[8]{0:T(128)} %gather_fusion.1, bf16[8,256,2048]{2,1,0:T(8,128)(2,1)} %all-gather.9.cloned.1.call-done.refs_2_), custom_call_target="tpu_custom_call" | custom-call | bytes 19573418 | tf_op jit(solution)/shard_map/scatter_blocks/pallas_call | solution.py:407
  347.9 7.7 convolution_convert_fusion.2
  355.6 7.7 fusion.24
  367.0 3.0 collective-permute-done.23
  370.2 7.5 fusion.29
  377.7 7.4 fusion.34
  388.4 13.3 %matmul_sum.4 = (bf16[512,2048]{1,0:T(8,128)(2,1)}, bf16[512,2048]{1,0:T(8,128)(2,1)}) custom-call(bf16[1024,1024]{1,0:T(8,128)(2,1)} %get-tuple-element.405.refs_0_.refs_4_, bf16[1024,1024]{1,0:T(8,128)(2,1)} %get-tuple-element.406.refs_1_.refs_6_, bf16[2048,1024]{1,0:T(8,128)(2,1)} %get-tuple-element.344.refs_2_, bf16[2048,1024]{1,0:T(8,128)(2,1)} %get-tuple-element.358.refs_3_), custom_call_target="tpu_custom_call" | custom-call | bytes 35000000 | tf_op jit(solution)/shard_map/matmul_sum/pallas_call | solution.py:322
  404.3 13.7 %matmul_sum.5 = (bf16[512,2048]{1,0:T(8,128)(2,1)}, bf16[512,2048]{1,0:T(8,128)(2,1)}) custom-call(bf16[1024,1024]{1,0:T(8,128)(2,1)} %get-tuple-element.537.refs_0_.refs_3_, bf16[1024,1024]{1,0:T(8,128)(2,1)} %get-tuple-element.539.refs_1_.refs_5_, bf16[2048,1024]{1,0:T(8,128)(2,1)} %get-tuple-element.340.refs_2_, bf16[2048,1024]{1,0:T(8,128)(2,1)} %get-tuple-element.356.refs_3_), custom_call_target="tpu_custom_call" | custom-call | bytes 35000000 | tf_op jit(solution)/shard_map/matmul_sum/pallas_call | solution.py:322
  428.6 24.7 %grad_blocks.4 = bf16[8,256,2048]{2,1,0:T(8,128)(2,1)} custom-call(s32[8]{0:T(128)} %gather_fusion.1, bf16[1024,2048]{1,0:T(8,128)(2,1)} %pad_maximum_fusion.refs_1_, bf16[1024,2048]{1,0:T(8,128)(2,1)} %copy-done.25, bf16[1024,1024]{1,0:T(8,128)(2,1)} %get-tuple-element.460.refs_3_.refs_0_, bf16[1024,1024]{1,0:T(8,128)(2,1)} %get-tuple-element.405.refs_0_.refs_4_, ...), custom_call_target="tpu_custom_call" | custom-call | bytes 75161928 | tf_op jit(solution)/shard_map/grad_blocks/pallas_call | solution.py:287
  454.4 10.3 %multiply_convert_fusion.1.refs_0_.refs_4_ = bf16[1024,1024]{1,0:T(8,128)(2,1)} fusion(bf16[1024,1024]{1,0:T(8,128)(2,1)} %get-tuple-element.425, bf16[1024,2048]{1,0:T(8,128)(2,1)} %copy-done.25, bf16[2048,1024]{1,0:T(8,128)(2,1)} %get-tuple-element.344.refs_2_), kind=kOutput, calls=%fused_computation.70 | convolution fusion | flops 4298113024 | bytes 12582912 | tf_op jit(solution)/shard_map/dot_general | solution.py:761
  464.7 5.8 multiply_convert_fusion.refs_1_.refs_6_
  470.5 13.6 %matmul_sum.6 = (bf16[512,2048]{1,0:T(8,128)(2,1)}, bf16[512,2048]{1,0:T(8,128)(2,1)}) custom-call(bf16[1024,1024]{1,0:T(8,128)(2,1)} %multiply_convert_fusion.1.refs_0_.refs_4_, bf16[1024,1024]{1,0:T(8,128)(2,1)} %multiply_convert_fusion.refs_1_.refs_6_, bf16[2048,1024]{1,0:T(8,128)(2,1)} %get-tuple-element.340.refs_2_, ...), custom_call_target="tpu_custom_call" | custom-call | bytes 7000000 | tf_op jit(solution)/shard_map/matmul_sum/pallas_call | solution.py:322
  484.2 4.4 collective-permute-done.31
  492.5 25.0 %grad_blocks.5 = bf16[8,256,2048]{2,1,0:T(8,128)(2,1)} custom-call(s32[8]{0:T(128)} %gather_fusion, bf16[1024,2048]{1,0:T(8,128)(2,1)} %pad_maximum_fusion.1.refs_1_, bf16[1024,2048]{1,0:T(8,128)(2,1)} %copy-done.24, bf16[1024,1024]{1,0:T(8,128)(2,1)} %get-tuple-element.537.refs_0_.refs_3_, bf16[1024,1024]{1,0:T(8,128)(2,1)} %multiply_convert_fusion.1.refs_0_.refs_4_, ...), custom_call_target="tpu_custom_call" | custom-call | bytes 75161928 | tf_op jit(solution)/shard_map/grad_blocks/pallas_call | solution.py:287
  517.5 4.3 collective-permute-done.32
  525.7 13.8 %matmul_sum.7 = (bf16[512,2048]{1,0:T(8,128)(2,1)}, bf16[512,2048]{1,0:T(8,128)(2,1)}) custom-call(bf16[1024,1024]{1,0:T(8,128)(2,1)} %get-tuple-element.460.refs_3_.refs_0_, bf16[1024,1024]{1,0:T(8,128)(2,1)} %get-tuple-element.461.refs_5_.refs_1_, bf16[2048,1024]{1,0:T(8,128)(2,1)} %get-tuple-element.344.refs_2_, bf16[2048,1024]{1,0:T(8,128)(2,1)} %get-tuple-element.358.refs_3_), custom_call_target="tpu_custom_call" | custom-call | bytes 35000000 | tf_op jit(solution)/shard_map/matmul_sum/pallas_call | solution.py:322
  548.2 5.2 multiply_reduce_fusion
  553.5 5.3 fusion.48
  558.8 4.8 convolution_convert_fusion.1
  563.8 10.9 %grad_blocks.6 = bf16[8,256,2048]{2,1,0:T(8,128)(2,1)} custom-call(s32[8]{0:T(128)} %gather_fusion.2, bf16[512,2048]{1,0:T(8,128)(2,1)} %copy-done.6, bf16[512,2048]{1,0:T(8,128)(2,1)} %copy-done.21), custom_call_target="tpu_custom_call" | custom-call | bytes 18790480 | tf_op jit(solution)/shard_map/grad_blocks/pallas_call | solution.py:287
  581.0 3.4 collective-permute-start.39
  584.4 19.6 %collective-permute-done.37 = bf16[512,512]{1,0:T(8,128)(2,1)S(1)} collective-permute-done((bf16[512,512]{1,0:T(8,128)(2,1)S(1)}, bf16[512,512]{1,0:T(8,128)(2,1)S(1)}, u32[]{:S(2)}, u32[]{:S(2)}) %collective-permute-start.37) | collective-permute-done | bytes 524320 | tf_op jit(solution)/shard_map/ppermute | solution.py:476
  604.8 13.7 %collective-permute-done.38 = bf16[512,512]{1,0:T(8,128)(2,1)S(1)} collective-permute-done((bf16[512,512]{1,0:T(8,128)(2,1)S(1)}, bf16[512,512]{1,0:T(8,128)(2,1)S(1)}, u32[]{:S(2)}, u32[]{:S(2)}) %collective-permute-start.38) | collective-permute-done | bytes 524320 | tf_op jit(solution)/shard_map/ppermute | solution.py:476
  620.2 4.0 add_convert_fusion
  624.3 4.7 reduce-scatter.15.cloned.1.call-done
  629.0 5.6 collective-permute-start.42
  638.0 44.1 %attend_back.1.refs_2_ = bf16[2048,1536]{1,0:T(8,128)(2,1)} custom-call(s32[1,2048]{1,0:T(1,128)} %compare_select_fusion.start_ref, bf16[2048,1536]{1,0:T(8,128)(2,1)} %get-tuple-element.329.qkv_ref, bf16[2048,512]{1,0:T(8,128)(2,1)} %constant_dynamic-update-slice_fusion.17.back_ref), custom_call_target="tpu_custom_call" | custom-call | bytes 140000000 | tf_op jit(solution)/shard_map/attend_back/pallas_call | solution.py:146
  685.7 17.7 %convolution_convert_fusion = bf16[2048,2048]{1,0:T(8,128)(2,1)} fusion(bf16[2048,1536]{1,0:T(8,128)(2,1)} %attend_back.1.refs_2_, bf16[2048,1536]{1,0:T(8,128)(2,1)S(1)} %bitcast.178), kind=kOutput, calls=%fused_computation.10 | convolution fusion | flops 12889096192 | bytes 20971520 | tf_op jit(solution)/shard_map/dot_general | solution.py:31
  703.4 5.2 collective-permute-done.44
  712.0 20.7 %grad_blocks.7 = bf16[8,256,1536]{2,1,0:T(8,128)(2,1)} custom-call(s32[8]{0:T(128)} %gather_fusion.4, bf16[2048,2048]{1,0:T(8,128)(2,1)} %get-tuple-element.525.refs_1_, bf16[2048,1536]{1,0:T(8,128)(2,1)} %attend_back.1.refs_2_), custom_call_target="tpu_custom_call" | custom-call | bytes 56371444 | tf_op jit(solution)/shard_map/grad_blocks/pallas_call | solution.py:287
  733.7 3.8 slice.258
  738.6 10.6 %convert_reduce_fusion = (f32[2048]{0:T(1024)S(1)}, f32[2048]{0:T(1024)S(1)}) fusion(bf16[2048,2048]{1,0:T(8,128)(2,1)} %convolution_convert_fusion, bf16[2048,2048]{1,0:T(8,128)(2,1)} %get-tuple-element.536), kind=kLoop, calls=%fused_computation.5 | loop fusion | flops 20967424 | bytes 16793600 | tf_op jit(solution)/shard_map/reduce_sum | solution.py:919
  756.6 3.7 collective-permute-done.47
  772.4 16.8 %update_tiles.4 = (f32[96,128,128]{2,1,0:T(8,128)}, f32[96,128,128]{2,1,0:T(8,128)}, f32[96,128,128]{2,1,0:T(8,128)}, bf16[96,128,128]{2,1,0:T(8,128)(2,1)}, f32...) custom-call(f32[32]{0:T(128)} %get-tuple-element.647.refs_0_, ...), custom_call_target="tpu_custom_call" | custom-call | bytes 56000000 | tf_op jit(solution)/shard_map/update_tiles/pallas_call | solution.py:247
  794.8 16.1 %update_tiles.5 = (f32[96,128,128]{2,1,0:T(8,128)}, f32[96,128,128]{2,1,0:T(8,128)}, f32[96,128,128]{2,1,0:T(8,128)}, bf16[96,128,128]{2,1,0:T(8,128)(2,1)}, f32...) custom-call(f32[32]{0:T(128)} %get-tuple-element.646.refs_0_, ...), custom_call_target="tpu_custom_call", output_to_operand_aliasing={{0}: (10, {}), {1}: (11, {}), {2}: (12, {}), {3}: (13, {}),... | custom-call | bytes 56000000 | tf_op jit(solution)/shard_map/update_tiles/pallas_call | solution.py:247
  815.3 4.9 add_convert_fusion.2
  821.1 3.1 and_select_fusion.2
  824.2 9.4 %collective-permute-done.57 = bf16[1,256,1536]{2,1,0:T(8,128)(2,1)S(1)} collective-permute-done((bf16[1,256,1536]{2,1,0:T(8,128)(2,1)S(1)}, bf16[1,256,1536]{2,1,0:T(8,128)(2,1)S(1)}, u32[]{:S(2)}, u32[]{:S(2)}) %collective-permute-start.57) | collective-permute-done | bytes 786464 | tf_op jit(solution)/shard_map/ppermute | solution.py:476
  836.1 13.0 %update_tiles.6 = (f32[96,128,128]{2,1,0:T(8,128)}, f32[96,128,128]{2,1,0:T(8,128)}, f32[96,128,128]{2,1,0:T(8,128)}, bf16[96,128,128]{2,1,0:T(8,128)(2,1)}, f32...) custom-call(f32[24]{0:T(128)} %bitcast.215, ...), custom_call_target="tpu_custom_call", output_to_operand_aliasing={{0}: (10, {}), {1}: (11, {}), {2}: (12, {}), {3}: (13, {}),... | custom-call | bytes 42000000 | tf_op jit(solution)/shard_map/update_tiles/pallas_call | solution.py:247
  849.1 2.9 reduce-scatter.11.cloned.1.call-done
  856.7 3.4 collective-permute-start.52
  861.1 3.3 collective-permute-start.59
  867.3 18.9 %collective-permute-done.59 = f32[24576]{0:T(1024)S(1)} collective-permute-done((f32[24576]{0:T(1024)S(1)}, f32[24576]{0:T(1024)S(1)}, u32[]{:S(2)}, u32[]{:S(2)}) %collective-permute-start.59) | collective-permute-done | bytes 98336 | tf_op jit(solution)/shard_map/ppermute | solution.py:476
  889.2 6.3 update_tiles.7
  (430 shorter events, 155.0 us)
Async XLA Ops:
  7.2 150.7 %all-gather.11.cloned.1.call-start = ((), (), s32[]{:S(2)}) async-start(), calls=%async_computation.7 | async-start | bytes 7077888 | tf_op jit(solution)/shard_map/all_gather | solution.py:628
  12.4 172.7 %all-gather.13.cloned.1.call-start = ((), (), s32[]{:S(2)}) async-start(), calls=%async_computation.8 | async-start | bytes 9437184 | tf_op jit(solution)/shard_map/all_gather | solution.py:661
  15.4 70.0 %collective-permute-start = (bf16[512,2048]{1,0:T(8,128)(2,1)}, bf16[512,2048]{1,0:T(8,128)(2,1)}, u32[]{:S(2)}, u32[]{:S(2)}) collective-permute-start(bf16[512,2048]{1,0:T(8,128)(2,1)} %fusion.5.refs_2_), channel_id=1, source_target_pairs={{1,0},{2,1},{3,2},{5,4},{6,5},{7,6},{9,8},{10,9},{11,10},{13,12},{... | collective-permute-start | bytes 6291464 | tf_op jit(solution)/shard_map/ppermute | solution.py:480
  16.7 68.7 %collective-permute-start.1 = (bf16[512,2048]{1,0:T(8,128)(2,1)}, bf16[512,2048]{1,0:T(8,128)(2,1)}, u32[]{:S(2)}, u32[]{:S(2)}) collective-permute-start(bf16[512,2048]{1,0:T(8,128)(2,1)} %fusion.5.refs_2_), channel_id=1, source_target_pairs={{0,1},{1,2},{2,3},{4,5},{5,6},{6,7},{8,9},{9,10},{10,11},{12,13},{... | collective-permute-start | bytes 6291464 | tf_op jit(solution)/shard_map/ppermute | solution.py:480
  24.0 53.4 %collective-permute-start.2 = (bf16[256,512]{1,0:T(8,128)(2,1)S(1)}, bf16[256,512]{1,0:T(8,128)(2,1)S(1)}, u32[]{:S(2)}, u32[]{:S(2)}) collective-permute-start(bf16[256,512]{1,0:T(8,128)(2,1)S(1)} %copy-done.38), channel_id=1, source_target_pairs={{0,1},{1,0},{2,3},{3,2},{4,5},{5,4},{6,7},{7,6},{8,9},{9,8},{10,11... | collective-permute-start | bytes 786440 | tf_op jit(solution)/shard_map/ppermute | solution.py:476
  24.7 60.7 %collective-permute-start.3 = (bf16[256,512]{1,0:T(8,128)(2,1)S(1)}, bf16[256,512]{1,0:T(8,128)(2,1)S(1)}, u32[]{:S(2)}, u32[]{:S(2)}) collective-permute-start(bf16[256,512]{1,0:T(8,128)(2,1)S(1)} %copy-done.38), channel_id=1, source_target_pairs={{0,2},{1,3},{2,0},{3,1},{4,6},{5,7},{6,4},{7,5},{8,10},{9,11},{10,... | collective-permute-start | bytes 786440 | tf_op jit(solution)/shard_map/ppermute | solution.py:476
  27.1 58.3 %collective-permute-start.4 = (bf16[256,512]{1,0:T(8,128)(2,1)S(1)}, bf16[256,512]{1,0:T(8,128)(2,1)S(1)}, u32[]{:S(2)}, u32[]{:S(2)}) collective-permute-start(bf16[256,512]{1,0:T(8,128)(2,1)S(1)} %copy-done.38), channel_id=1, source_target_pairs={{0,3},{1,2},{2,1},{3,0},{4,7},{5,6},{6,5},{7,4},{8,11},{9,10},{10,... | collective-permute-start | bytes 786440 | tf_op jit(solution)/shard_map/ppermute | solution.py:476
  86.6 181.5 %all-gather.7.cloned.1.call-start = ((), (), s32[]{:S(2)}) async-start(), calls=%async_computation.4 | async-start | bytes 10485760 | tf_op jit(solution)/shard_map/all_gather | solution.py:622
  86.6 52.9 %collective-permute-start.6 = (bf16[512,2048]{1,0:T(8,128)(2,1)}, bf16[512,2048]{1,0:T(8,128)(2,1)}, u32[]{:S(2)}, u32[]{:S(2)}) collective-permute-start(bf16[512,2048]{1,0:T(8,128)(2,1)} %collective-permute-done.refs_5_), channel_id=1, source_target_pairs={{1,0},{2,1},{5,4},{6,5},{9,8},{10,9},{13,12},{14,13},{17,16},{18,1... | collective-permute-start | bytes 6291464 | tf_op jit(solution)/shard_map/ppermute | solution.py:480
  87.9 51.6 %collective-permute-start.7 = (bf16[512,2048]{1,0:T(8,128)(2,1)}, bf16[512,2048]{1,0:T(8,128)(2,1)}, u32[]{:S(2)}, u32[]{:S(2)}) collective-permute-start(bf16[512,2048]{1,0:T(8,128)(2,1)} %collective-permute-done.1.refs_3_), channel_id=1, source_target_pairs={{1,2},{2,3},{5,6},{6,7},{9,10},{10,11},{13,14},{14,15},{17,18},{18... | collective-permute-start | bytes 6291464 | tf_op jit(solution)/shard_map/ppermute | solution.py:480
  139.6 195.7 %all-gather.9.cloned.1.call-start = ((), (), s32[]{:S(2)}) async-start(), calls=%async_computation.5 | async-start | bytes 10485760 | tf_op jit(solution)/shard_map/all_gather | solution.py:622
  139.6 55.4 %collective-permute-start.8 = (bf16[512,2048]{1,0:T(8,128)(2,1)}, bf16[512,2048]{1,0:T(8,128)(2,1)}, u32[]{:S(2)}, u32[]{:S(2)}) collective-permute-start(bf16[512,2048]{1,0:T(8,128)(2,1)} %collective-permute-done.6.refs_6_.refs_4_), channel_id=1, source_target_pairs={{1,0},{5,4},{9,8},{13,12},{17,16},{21,20},{25,24},{29,28}} | collective-permute-start | bytes 6291464 | tf_op jit(solution)/shard_map/ppermute | solution.py:480
  140.9 54.1 %collective-permute-start.9 = (bf16[512,2048]{1,0:T(8,128)(2,1)}, bf16[512,2048]{1,0:T(8,128)(2,1)}, u32[]{:S(2)}, u32[]{:S(2)}) collective-permute-start(bf16[512,2048]{1,0:T(8,128)(2,1)} %collective-permute-done.7.refs_4_.refs_2_), channel_id=1, source_target_pairs={{2,3},{6,7},{10,11},{14,15},{18,19},{22,23},{26,27},{30,31}} | collective-permute-start | bytes 6291464 | tf_op jit(solution)/shard_map/ppermute | solution.py:480
  142.9 53.4 %collective-permute-start.10 = (bf16[2,256,2048]{2,1,0:T(8,128)(2,1)}, bf16[2,256,2048]{2,1,0:T(8,128)(2,1)}, u32[]{:S(2)}, u32[]{:S(2)}) collective-permute-start(bf16[2,256,2048]{2,1,0:T(8,128)(2,1)} %pad_maximum_fusion.2), channel_id=1, source_target_pairs={{0,2},{3,1},{4,6},{7,5},{8,10},{11,9},{12,14},{15,13},{16,18},{19,... | collective-permute-start | bytes 6291464 | tf_op jit(solution)/shard_map/ppermute | solution.py:480
  196.2 47.4 %collective-permute-start.11 = (bf16[2,256,2048]{2,1,0:T(8,128)(2,1)}, bf16[2,256,2048]{2,1,0:T(8,128)(2,1)}, u32[]{:S(2)}, u32[]{:S(2)}) collective-permute-start(bf16[2,256,2048]{2,1,0:T(8,128)(2,1)} %pad_maximum_fusion.2), channel_id=1, source_target_pairs={{1,3},{2,0},{5,7},{6,4},{9,11},{10,8},{13,15},{14,12},{17,19},{18,... | collective-permute-start | bytes 6291464 | tf_op jit(solution)/shard_map/ppermute | solution.py:480
  248.0 295.2 %reduce-scatter.13.cloned.1.call-start = ((), (), s32[]{:S(2)}) async-start(), calls=%async_computation.9 | async-start | bytes 10485760
  248.1 15.2 %collective-permute-start.15 = (bf16[512,2048]{1,0:T(8,128)(2,1)}, bf16[512,2048]{1,0:T(8,128)(2,1)}, u32[]{:S(2)}, u32[]{:S(2)}) collective-permute-start(bf16[512,2048]{1,0:T(8,128)(2,1)} %param.16), channel_id=1, source_target_pairs={{0,4},{4,0},{8,12},{12,8},{16,20},{20,16},{24,28},{28,24},{1,5},{5... | collective-permute-start | bytes 6291464 | tf_op jit(solution)/shard_map/ppermute | solution.py:476
  249.8 7.5 collective-permute-start.16
  252.9 24.8 %collective-permute-start.14 = (bf16[512,512]{1,0:T(8,128)(2,1)}, bf16[512,512]{1,0:T(8,128)(2,1)}, u32[]{:S(2)}, u32[]{:S(2)}) collective-permute-start(bf16[512,512]{1,0:T(8,128)(2,1)} %get-tuple-element.618), channel_id=1, source_target_pairs={{0,3},{1,2},{2,1},{3,0},{4,7},{5,6},{6,5},{7,4},{8,11},{9,10},{10,... | collective-permute-start | bytes 1572872 | tf_op jit(solution)/shard_map/ppermute | solution.py:476
  254.8 44.5 %collective-permute-start.13 = (bf16[512,512]{1,0:T(8,128)(2,1)}, bf16[512,512]{1,0:T(8,128)(2,1)}, u32[]{:S(2)}, u32[]{:S(2)}) collective-permute-start(bf16[512,512]{1,0:T(8,128)(2,1)} %get-tuple-element.619), channel_id=1, source_target_pairs={{0,2},{1,3},{2,0},{3,1},{4,6},{5,7},{6,4},{7,5},{8,10},{9,11},{10,... | collective-permute-start | bytes 1572872 | tf_op jit(solution)/shard_map/ppermute | solution.py:476
  254.8 44.5 %collective-permute-start.12 = (bf16[512,512]{1,0:T(8,128)(2,1)S(1)}, bf16[512,512]{1,0:T(8,128)(2,1)}, u32[]{:S(2)}, u32[]{:S(2)}) collective-permute-start(bf16[512,512]{1,0:T(8,128)(2,1)S(1)} %get-tuple-element.620), channel_id=1, source_target_pairs={{0,1},{1,0},{2,3},{3,2},{4,5},{5,4},{6,7},{7,6},{8,9},{9,8},{10,11... | collective-permute-start | bytes 1572872 | tf_op jit(solution)/shard_map/ppermute | solution.py:476
  261.7 16.0 %collective-permute-start.18 = (f32[128]{0:T(128)S(1)}, f32[128]{0:T(128)S(1)}, u32[]{:S(2)}, u32[]{:S(2)}) collective-permute-start(f32[128]{0:T(128)S(1)} %add.436), channel_id=1, source_target_pairs={{0,16},{4,20},{8,24},{12,28},{16,0},{20,4},{24,8},{28,12},{1,17},{... | collective-permute-start | bytes 1544 | tf_op jit(solution)/shard_map/ppermute | solution.py:476
  310.9 8.1 collective-permute-start.19
  310.9 22.8 %collective-permute-start.20 = (bf16[224,2048]{1,0:T(8,128)(2,1)S(1)}, bf16[224,2048]{1,0:T(8,128)(2,1)S(1)}, u32[]{:S(2)}, u32[]{:S(2)}) collective-permute-start(bf16[224,2048]{1,0:T(8,128)(2,1)S(1)} %slice.297), channel_id=1, source_target_pairs={{0,1},{1,0},{2,3},{3,2},{4,5},{5,4},{6,7},{7,6},{8,9},{9,8},{10,11... | collective-permute-start | bytes 2752520 | tf_op jit(solution)/shard_map/ppermute | solution.py:476
  335.3 11.2 %collective-permute-start.21 = (bf16[96,2048]{1,0:T(8,128)(2,1)S(1)}, bf16[96,2048]{1,0:T(8,128)(2,1)S(1)}, u32[]{:S(2)}, u32[]{:S(2)}) collective-permute-start(bf16[96,2048]{1,0:T(8,128)(2,1)S(1)} %slice.232), channel_id=1, source_target_pairs={{0,1},{1,0},{2,3},{3,2},{4,5},{5,4},{6,7},{7,6},{8,9},{9,8},{10,11... | collective-permute-start | bytes 1179656 | tf_op jit(solution)/shard_map/ppermute | solution.py:476
  346.6 19.1 %collective-permute-start.22 = (bf16[192,2048]{1,0:T(8,128)(2,1)S(1)}, bf16[192,2048]{1,0:T(8,128)(2,1)S(1)}, u32[]{:S(2)}, u32[]{:S(2)}) collective-permute-start(bf16[192,2048]{1,0:T(8,128)(2,1)S(1)} %slice.233), channel_id=1, source_target_pairs={{0,1},{1,0},{2,3},{3,2},{4,5},{5,4},{6,7},{7,6},{8,9},{9,8},{10,11... | collective-permute-start | bytes 2359304 | tf_op jit(solution)/shard_map/ppermute | solution.py:476
  365.8 4.2 collective-permute-start.23
  366.0 21.5 %collective-permute-start.24 = (bf16[208,2048]{1,0:T(8,128)(2,1)S(1)}, bf16[208,2048]{1,0:T(8,128)(2,1)}, u32[]{:S(2)}, u32[]{:S(2)}) collective-permute-start(bf16[208,2048]{1,0:T(8,128)(2,1)S(1)} %slice.234), channel_id=1, source_target_pairs={{0,1},{1,0},{2,3},{3,2},{4,5},{5,4},{6,7},{7,6},{8,9},{9,8},{10,11... | collective-permute-start | bytes 2555912 | tf_op jit(solution)/shard_map/ppermute | solution.py:476
  387.6 15.0 %collective-permute-start.25 = (bf16[144,2048]{1,0:T(8,128)(2,1)S(1)}, bf16[144,2048]{1,0:T(8,128)(2,1)S(1)}, u32[]{:S(2)}, u32[]{:S(2)}) collective-permute-start(bf16[144,2048]{1,0:T(8,128)(2,1)S(1)} %slice.235), channel_id=1, source_target_pairs={{0,1},{1,0},{2,3},{3,2},{4,5},{5,4},{6,7},{7,6},{8,9},{9,8},{10,11... | collective-permute-start | bytes 1769480 | tf_op jit(solution)/shard_map/ppermute | solution.py:476
  402.6 15.5 %collective-permute-start.26 = (bf16[512,2048]{1,0:T(8,128)(2,1)}, bf16[512,2048]{1,0:T(8,128)(2,1)S(1)}, u32[]{:S(2)}, u32[]{:S(2)}) collective-permute-start(bf16[512,2048]{1,0:T(8,128)(2,1)} %get-tuple-element.393), channel_id=1, source_target_pairs={{0,4},{4,0},{8,12},{12,8},{16,20},{20,16},{24,28},{28,24},{1,5},{5... | collective-permute-start | bytes 6291464 | tf_op jit(solution)/shard_map/ppermute | solution.py:476
  403.5 17.4 %collective-permute-start.27 = (bf16[160,2048]{1,0:T(8,128)(2,1)}, bf16[160,2048]{1,0:T(8,128)(2,1)S(1)}, u32[]{:S(2)}, u32[]{:S(2)}) collective-permute-start(bf16[160,2048]{1,0:T(8,128)(2,1)} %slice.236), channel_id=1, source_target_pairs={{0,1},{1,0},{2,3},{3,2},{4,5},{5,4},{6,7},{7,6},{8,9},{9,8},{10,11... | collective-permute-start | bytes 1966088 | tf_op jit(solution)/shard_map/ppermute | solution.py:476
  423.4 30.0 %collective-permute-start.29 = (bf16[256,2048]{1,0:T(8,128)(2,1)}, bf16[256,2048]{1,0:T(8,128)(2,1)}, u32[]{:S(2)}, u32[]{:S(2)}) collective-permute-start(bf16[256,2048]{1,0:T(8,128)(2,1)} %slice.237), channel_id=1, source_target_pairs={{0,1},{1,0},{2,3},{3,2},{4,5},{5,4},{6,7},{7,6},{8,9},{9,8},{10,11... | collective-permute-start | bytes 3145736 | tf_op jit(solution)/shard_map/ppermute | solution.py:476
  453.4 175.5 %reduce-scatter.15.cloned.1.call-start = ((), (), s32[]{:S(2)}) async-start(), calls=%async_computation.10 | async-start | bytes 10485760
  453.6 30.5 %collective-permute-start.30 = (bf16[256,2048]{1,0:T(8,128)(2,1)S(1)}, bf16[256,2048]{1,0:T(8,128)(2,1)S(1)}, u32[]{:S(2)}, u32[]{:S(2)}) collective-permute-start(bf16[256,2048]{1,0:T(8,128)(2,1)S(1)} %slice.238), channel_id=1, source_target_pairs={{0,1},{1,0},{2,3},{3,2},{4,5},{5,4},{6,7},{7,6},{8,9},{9,8},{10,11... | collective-permute-start | bytes 3145736 | tf_op jit(solution)/shard_map/ppermute | solution.py:476
  484.1 4.4 collective-permute-start.31
  491.0 30.9 %collective-permute-start.32 = (bf16[320,2048]{1,0:T(8,128)(2,1)S(1)}, bf16[320,2048]{1,0:T(8,128)(2,1)S(1)}, u32[]{:S(2)}, u32[]{:S(2)}) collective-permute-start(bf16[320,2048]{1,0:T(8,128)(2,1)S(1)} %slice.239), channel_id=1, source_target_pairs={{0,1},{1,0},{2,3},{3,2},{4,5},{5,4},{6,7},{7,6},{8,9},{9,8},{10,11... | collective-permute-start | bytes 3932168 | tf_op jit(solution)/shard_map/ppermute | solution.py:476
  521.9 186.7 %reduce-scatter.17.cloned.1.call-start = ((), (), s32[]{:S(2)}) async-start(), calls=%async_computation.11 | async-start | bytes 5242880
  521.9 17.6 %collective-permute-start.33 = (bf16[512,2048]{1,0:T(8,128)(2,1)}, bf16[512,2048]{1,0:T(8,128)(2,1)}, u32[]{:S(2)}, u32[]{:S(2)}) collective-permute-start(bf16[512,2048]{1,0:T(8,128)(2,1)} %get-tuple-element.463), channel_id=1, source_target_pairs={{0,4},{4,0},{8,12},{12,8},{16,20},{20,16},{24,28},{28,24},{1,5},{5... | collective-permute-start | bytes 6291464 | tf_op jit(solution)/shard_map/ppermute | solution.py:476
  523.0 20.2 %collective-permute-start.34 = (bf16[192,2048]{1,0:T(8,128)(2,1)}, bf16[192,2048]{1,0:T(8,128)(2,1)}, u32[]{:S(2)}, u32[]{:S(2)}) collective-permute-start(bf16[192,2048]{1,0:T(8,128)(2,1)} %slice.240), channel_id=1, source_target_pairs={{0,1},{1,0},{2,3},{3,2},{4,5},{5,4},{6,7},{7,6},{8,9},{9,8},{10,11... | collective-permute-start | bytes 2359304 | tf_op jit(solution)/shard_map/ppermute | solution.py:476
  544.3 30.4 %collective-permute-start.35 = (bf16[1,256,1024]{2,1,0:T(8,128)(2,1)S(1)}, bf16[1,256,1024]{2,1,0:T(8,128)(2,1)}, u32[]{:S(2)}, u32[]{:S(2)}) collective-permute-start(bf16[1,256,1024]{2,1,0:T(8,128)(2,1)S(1)} %slice.241), channel_id=1, source_target_pairs={{0,2},{1,3},{2,0},{3,1},{4,6},{5,7},{6,4},{7,5},{8,10},{9,11},{10,... | collective-permute-start | bytes 1572872 | tf_op jit(solution)/shard_map/ppermute | solution.py:476
  546.8 27.9 %collective-permute-start.36 = (f32[128]{0:T(128)S(1)}, f32[128]{0:T(128)S(1)}, u32[]{:S(2)}, u32[]{:S(2)}) collective-permute-start(f32[128]{0:T(128)S(1)} %add.437), channel_id=1, source_target_pairs={{0,1},{1,0},{2,3},{3,2},{4,5},{5,4},{6,7},{7,6},{8,9},{9,8},{10,11... | collective-permute-start | bytes 1544 | tf_op jit(solution)/shard_map/ppermute | solution.py:476
  577.5 42.7 %collective-permute-start.40 = (bf16[4,256,2048]{2,1,0:T(8,128)(2,1)S(1)}, bf16[4,256,2048]{2,1,0:T(8,128)(2,1)S(1)}, u32[]{:S(2)}, u32[]{:S(2)}) collective-permute-start(bf16[4,256,2048]{2,1,0:T(8,128)(2,1)S(1)} %slice.248), channel_id=1, source_target_pairs={{0,4},{4,0},{8,12},{12,8},{16,20},{20,16},{24,28},{28,24},{1,5},{5... | collective-permute-start | bytes 12582920 | tf_op jit(solution)/shard_map/ppermute | solution.py:476
  580.0 24.0 %collective-permute-start.37 = (bf16[512,512]{1,0:T(8,128)(2,1)S(1)}, bf16[512,512]{1,0:T(8,128)(2,1)S(1)}, u32[]{:S(2)}, u32[]{:S(2)}) collective-permute-start(bf16[512,512]{1,0:T(8,128)(2,1)S(1)} %get-tuple-element.615), channel_id=1, source_target_pairs={{0,1},{1,0},{2,3},{3,2},{4,5},{5,4},{6,7},{7,6},{8,9},{9,8},{10,11... | collective-permute-start | bytes 1572872 | tf_op jit(solution)/shard_map/ppermute | solution.py:476
  580.4 38.2 %collective-permute-start.38 = (bf16[512,512]{1,0:T(8,128)(2,1)S(1)}, bf16[512,512]{1,0:T(8,128)(2,1)S(1)}, u32[]{:S(2)}, u32[]{:S(2)}) collective-permute-start(bf16[512,512]{1,0:T(8,128)(2,1)S(1)} %get-tuple-element.614), channel_id=1, source_target_pairs={{0,2},{1,3},{2,0},{3,1},{4,6},{5,7},{6,4},{7,5},{8,10},{9,11},{10,... | collective-permute-start | bytes 1572872 | tf_op jit(solution)/shard_map/ppermute | solution.py:476
  581.0 38.3 %collective-permute-start.39 = (bf16[512,512]{1,0:T(8,128)(2,1)S(1)}, bf16[512,512]{1,0:T(8,128)(2,1)S(1)}, u32[]{:S(2)}, u32[]{:S(2)}) collective-permute-start(bf16[512,512]{1,0:T(8,128)(2,1)S(1)} %get-tuple-element.613), channel_id=1, source_target_pairs={{0,3},{1,2},{2,1},{3,0},{4,7},{5,6},{6,5},{7,4},{8,11},{9,10},{10,... | collective-permute-start | bytes 1572872 | tf_op jit(solution)/shard_map/ppermute | solution.py:476
  628.9 223.0 %reduce-scatter.11.cloned.1.call-start = ((), (), s32[]{:S(2)}) async-start(), calls=%async_computation.6 | async-start | bytes 10485760 | tf_op jit(solution)/shard_map/reduce_scatter | solution.py:895
  629.0 53.1 %collective-permute-start.42 = (bf16[1,256,1024]{2,1,0:T(8,128)(2,1)S(1)}, bf16[1,256,1024]{2,1,0:T(8,128)(2,1)}, u32[]{:S(2)}, u32[]{:S(2)}) collective-permute-start(bf16[1,256,1024]{2,1,0:T(8,128)(2,1)S(1)} %slice.250), channel_id=1, source_target_pairs={{0,2},{1,3},{2,0},{3,1},{4,6},{5,7},{6,4},{7,5},{8,10},{9,11},{10,... | collective-permute-start | bytes 1572872 | tf_op jit(solution)/shard_map/ppermute | solution.py:476
  636.5 45.6 %collective-permute-start.43 = (bf16[1,256,1024]{2,1,0:T(8,128)(2,1)}, bf16[1,256,1024]{2,1,0:T(8,128)(2,1)}, u32[]{:S(2)}, u32[]{:S(2)}) collective-permute-start(bf16[1,256,1024]{2,1,0:T(8,128)(2,1)} %slice.251), channel_id=1, source_target_pairs={{0,2},{1,3},{2,0},{3,1},{4,6},{5,7},{6,4},{7,5},{8,10},{9,11},{10,... | collective-permute-start | bytes 1572872 | tf_op jit(solution)/shard_map/ppermute | solution.py:476
  682.9 25.7 %collective-permute-start.44 = (bf16[1,256,1024]{2,1,0:T(8,128)(2,1)}, bf16[1,256,1024]{2,1,0:T(8,128)(2,1)S(1)}, u32[]{:S(2)}, u32[]{:S(2)}) collective-permute-start(bf16[1,256,1024]{2,1,0:T(8,128)(2,1)} %slice.253), channel_id=1, source_target_pairs={{0,2},{1,3},{2,0},{3,1},{4,6},{5,7},{6,4},{7,5},{8,10},{9,11},{10,... | collective-permute-start | bytes 1572872 | tf_op jit(solution)/shard_map/ppermute | solution.py:476
  710.8 21.8 %collective-permute-start.45 = (f32[128]{0:T(128)S(1)}, f32[128]{0:T(128)S(1)}, u32[]{:S(2)}, u32[]{:S(2)}) collective-permute-start(f32[128]{0:T(128)S(1)} %add.473), channel_id=1, source_target_pairs={{0,2},{1,3},{2,0},{3,1},{4,6},{5,7},{6,4},{7,5},{8,10},{9,11},{10,... | collective-permute-start | bytes 1544 | tf_op jit(solution)/shard_map/ppermute | solution.py:476
  712.0 103.3 %collective-permute-start.41 = (bf16[512,2048]{1,0:T(8,128)(2,1)}, bf16[512,2048]{1,0:T(8,128)(2,1)}, u32[]{:S(2)}, u32[]{:S(2)}) collective-permute-start(bf16[512,2048]{1,0:T(8,128)(2,1)} %get-tuple-element.504), channel_id=1, source_target_pairs={{0,4},{4,0},{8,12},{12,8},{16,20},{20,16},{24,28},{28,24},{1,5},{5... | collective-permute-start | bytes 6291464 | tf_op jit(solution)/shard_map/ppermute | solution.py:476
  737.4 27.6 %collective-permute-start.49 = (bf16[4,256,1536]{2,1,0:T(8,128)(2,1)}, bf16[4,256,1536]{2,1,0:T(8,128)(2,1)}, u32[]{:S(2)}, u32[]{:S(2)}) collective-permute-start(bf16[4,256,1536]{2,1,0:T(8,128)(2,1)} %slice.258), channel_id=1, source_target_pairs={{0,4},{4,0},{8,12},{12,8},{16,20},{20,16},{24,28},{28,24},{1,5},{5... | collective-permute-start | bytes 9437192 | tf_op jit(solution)/shard_map/ppermute | solution.py:476
  755.3 5.1 collective-permute-start.47
  756.5 13.5 %collective-permute-start.54 = (bf16[256,1024]{1,0:T(8,128)(2,1)S(1)}, bf16[256,1024]{1,0:T(8,128)(2,1)S(1)}, u32[]{:S(2)}, u32[]{:S(2)}) collective-permute-start(bf16[256,1024]{1,0:T(8,128)(2,1)S(1)} %slice_bitcast_fusion.3), channel_id=1, source_target_pairs={{0,4},{4,0},{8,12},{12,8},{16,20},{20,16},{24,28},{28,24},{1,5},{5... | collective-permute-start | bytes 1572872 | tf_op jit(solution)/shard_map/ppermute | solution.py:476
  760.4 4.7 collective-permute-start.48
  767.9 21.3 %collective-permute-start.53 = (bf16[1,256,1536]{2,1,0:T(8,128)(2,1)S(1)}, bf16[1,256,1536]{2,1,0:T(8,128)(2,1)}, u32[]{:S(2)}, u32[]{:S(2)}) collective-permute-start(bf16[1,256,1536]{2,1,0:T(8,128)(2,1)S(1)} %slice.266), channel_id=1, source_target_pairs={{0,16},{4,20},{8,24},{12,28},{16,0},{20,4},{24,8},{28,12},{1,17},{... | collective-permute-start | bytes 2359304 | tf_op jit(solution)/shard_map/ppermute | solution.py:476
  770.0 21.7 %collective-permute-start.56 = (bf16[256,1024]{1,0:T(8,128)(2,1)}, bf16[256,1024]{1,0:T(8,128)(2,1)}, u32[]{:S(2)}, u32[]{:S(2)}) collective-permute-start(bf16[256,1024]{1,0:T(8,128)(2,1)} %slice_bitcast_fusion.1), channel_id=1, source_target_pairs={{0,4},{4,0},{8,12},{12,8},{16,20},{20,16},{24,28},{28,24},{1,5},{5... | collective-permute-start | bytes 1572872 | tf_op jit(solution)/shard_map/ppermute | solution.py:476
  790.2 20.8 %collective-permute-start.55 = (bf16[1,256,1536]{2,1,0:T(8,128)(2,1)}, bf16[1,256,1536]{2,1,0:T(8,128)(2,1)}, u32[]{:S(2)}, u32[]{:S(2)}) collective-permute-start(bf16[1,256,1536]{2,1,0:T(8,128)(2,1)} %slice.271), channel_id=1, source_target_pairs={{0,16},{4,20},{8,24},{12,28},{16,0},{20,4},{24,8},{28,12},{1,17},{... | collective-permute-start | bytes 2359304 | tf_op jit(solution)/shard_map/ppermute | solution.py:476
  814.1 19.5 %collective-permute-start.57 = (bf16[1,256,1536]{2,1,0:T(8,128)(2,1)S(1)}, bf16[1,256,1536]{2,1,0:T(8,128)(2,1)S(1)}, u32[]{:S(2)}, u32[]{:S(2)}) collective-permute-start(bf16[1,256,1536]{2,1,0:T(8,128)(2,1)S(1)} %slice.305), channel_id=1, source_target_pairs={{0,8},{4,12},{8,0},{12,4},{16,24},{20,28},{24,16},{28,20},{1,9},{5... | collective-permute-start | bytes 2359304 | tf_op jit(solution)/shard_map/ppermute | solution.py:476
  855.5 5.6 collective-permute-start.58
  856.7 31.0 %collective-permute-start.52 = (bf16[256,512]{1,0:T(8,128)(2,1)S(1)}, bf16[256,512]{1,0:T(8,128)(2,1)S(1)}, u32[]{:S(2)}, u32[]{:S(2)}) collective-permute-start(bf16[256,512]{1,0:T(8,128)(2,1)S(1)} %get-tuple-element.628), channel_id=1, source_target_pairs={{0,3},{1,2},{2,1},{3,0},{4,7},{5,6},{6,5},{7,4},{8,11},{9,10},{10,... | collective-permute-start | bytes 786440 | tf_op jit(solution)/shard_map/ppermute | solution.py:476
  860.1 27.6 %collective-permute-start.51 = (bf16[256,512]{1,0:T(8,128)(2,1)S(1)}, bf16[256,512]{1,0:T(8,128)(2,1)S(1)}, u32[]{:S(2)}, u32[]{:S(2)}) collective-permute-start(bf16[256,512]{1,0:T(8,128)(2,1)S(1)} %get-tuple-element.629), channel_id=1, source_target_pairs={{0,2},{1,3},{2,0},{3,1},{4,6},{5,7},{6,4},{7,5},{8,10},{9,11},{10,... | collective-permute-start | bytes 786440 | tf_op jit(solution)/shard_map/ppermute | solution.py:476
  860.1 27.6 %collective-permute-start.50 = (bf16[256,512]{1,0:T(8,128)(2,1)S(1)}, bf16[256,512]{1,0:T(8,128)(2,1)S(1)}, u32[]{:S(2)}, u32[]{:S(2)}) collective-permute-start(bf16[256,512]{1,0:T(8,128)(2,1)S(1)} %get-tuple-element.627), channel_id=1, source_target_pairs={{0,1},{1,0},{2,3},{3,2},{4,5},{5,4},{6,7},{7,6},{8,9},{9,8},{10,11... | collective-permute-start | bytes 786440 | tf_op jit(solution)/shard_map/ppermute | solution.py:476
  861.1 25.1 %collective-permute-start.59 = (f32[24576]{0:T(1024)S(1)}, f32[24576]{0:T(1024)S(1)}, u32[]{:S(2)}, u32[]{:S(2)}) collective-permute-start(f32[24576]{0:T(1024)S(1)} %add.505), channel_id=1, source_target_pairs={{0,2},{1,3},{2,0},{3,1},{4,6},{5,7},{6,4},{7,5},{8,10},{9,11},{10,... | collective-permute-start | bytes 294920 | tf_op jit(solution)/shard_map/ppermute | solution.py:476
  (72 other events, 1084.7 us)
Sparse Core Ops, SparseCore 0:
  12.5 48.2 all-gather.10
  86.7 60.1 all-gather.12
  149.4 87.6 all-gather.6
  248.2 87.0 all-gather.8
  453.5 85.7 reduce-scatter.12
  542.5 86.3 reduce-scatter.14
  632.5 52.6 reduce-scatter.16
  708.8 143.1 reduce-scatter.10
